TPU v7x, 32 devices: a whole 2x2x4 slice. The times are simulated.
32 devices in a mesh: rows: 2 (over core), cols: 16 (over z, y, x).
Axes of the slice: x: 2, y: 2, z: 4, core: 2. Of those that a mesh axis runs over, the one named last changes fastest.
Arguments:
- wind_speed: float32 [16, 2048], P('rows', 'cols'), may hold values from 3 to 25
- wind_dir: float32 [16, 2048], P('rows', 'cols'), may hold values from -3.140625 to 3.140625
- depth_class: int32 [16, 2048], P('rows', 'cols'), may hold values from 0 to 3
- group_speed: float32 [4, 24], replicated, may hold values from 0.3 to 3
- dissipation: float32 [4, 24], replicated, may hold values from 0.02 to 1
- input_rate: float32 [24], replicated, may hold values from 0.02 to 0.2
- outer_spectra: float32 [8192, 864], P(('rows', 'cols')), may hold values from -6 to 6
- dest_cell: int32 [8192], P(('rows', 'cols')), may hold values from 0 to 32767, as said below
- refraction_inverse: float32 [4, 216, 216], replicated, as said below
- sweep_order: int32 [2, 4], replicated, may hold values from 0 to 3, as said below
Outputs:
- wave_action: float32 [864, 16, 2048], P(None, 'rows', 'cols')
Inputs may be any that keep to these rules, and one draw needn't show every extreme that they name: `dest_cell`: every boundary point feeds a cell on the grid's outermost rows or columns. Among the points held by one device, at most 16 feed cells held by any one device, and in every draw one device receives exactly 16 points from every device. `refraction_inverse`: each matrix has a diagonal between 0.75 and 1 and off-diagonal entries below 1.2 / 216 in magnitude. `sweep_order`: each row names each of the four quadrants once.
All inputs are finite; a program needn't handle non-finite values.
Results may differ from a plain program's by a relative error of at most 0.0003.
Values sent between devices are 32-bit elements; how exact they have to be, the bound alone decides.
No kernel may reach another device: no remote copies, remote signals or barrier semaphores. Data moves between devices by JAX's collectives and lax.ppermute only.
A program may use at most 192 MiB of HBM per device.

v0:
```python
from functools import partial
import math

import jax
import jax.numpy as jnp
from jax import lax
from jax.sharding import PartitionSpec as P

NDIR = 36
NFREQ = 24
CAP = 16
ITERS = 2


whitecap_rate = 0.5


def passed_along(block, axis, distance):
    devices = range(lax.axis_size(axis))
    route = [(i - distance, i) for i in devices if i - distance in devices]
    return lax.ppermute(block, axis, route)


def class_table(table, onehot):
    return jnp.sum(table[:, :, None, None] * onehot[:, None], axis=0)


def boundary_forcing(outer_spectra, dest_cell, rows_dev, cols_dev):
    row_count = lax.axis_size("rows")
    col_count = lax.axis_size("cols")
    devices = row_count * col_count
    total_cols = cols_dev * col_count
    point_count = dest_cell.shape[0]
    components = outer_spectra.shape[1]
    grid_row = dest_cell // total_cols
    grid_col = dest_cell % total_cols
    owner_dev = grid_row // rows_dev * col_count + grid_col // cols_dev
    local_cell = grid_row % rows_dev * cols_dev + grid_col % cols_dev
    position = jnp.arange(point_count, dtype=jnp.int32)
    earlier = (owner_dev[:, None] == owner_dev[None, :]) & (position[:, None] > position[None, :])
    slot_index = owner_dev * CAP + jnp.sum(earlier.astype(jnp.int32), axis=1)
    outgoing = jnp.zeros((devices * CAP, components), jnp.float32).at[slot_index].set(outer_spectra)
    targets = (
        jnp.full((devices * CAP,), rows_dev * cols_dev, jnp.int32).at[slot_index].set(local_cell)
    )
    arrived, arrived_cells = (
        lax.all_to_all(
            outgoing.reshape(devices, CAP * components),
            ("rows", "cols"),
            split_axis=0,
            concat_axis=0,
            tiled=True,
        ),
        lax.all_to_all(
            targets.reshape(devices, CAP), ("rows", "cols"), split_axis=0, concat_axis=0, tiled=True
        ),
    )
    points = arrived.reshape(devices * CAP, components)
    summed = jax.ops.segment_sum(
        points, arrived_cells.reshape(-1), num_segments=rows_dev * cols_dev + 1
    )
    return summed[: rows_dev * cols_dev].T.reshape(components, rows_dev, cols_dev)


def sweep(state, quadrant, speeds, losses, source, cos_abs, sin_abs, inverse, blocks):
    step_x = (1, -1, -1, 1)[quadrant]
    step_y = (1, 1, -1, -1)[quadrant]
    quarter = cos_abs.shape[0] // 4
    freq_count = speeds.shape[0]
    quad_size = quarter * freq_count
    comp_low = quadrant * quad_size
    comp_high = comp_low + quad_size
    rows_dev = state.shape[1]
    cols_dev = state.shape[2]
    energy = jnp.mean(state * state, axis=0)
    damping = losses + whitecap_rate * energy / (1.0 + energy)
    dir_cos = cos_abs[quadrant * quarter : (quadrant + 1) * quarter]
    dir_sin = sin_abs[quadrant * quarter : (quadrant + 1) * quarter]
    along_x4 = dir_cos[:, None, None, None] * speeds[None]
    along_y4 = dir_sin[:, None, None, None] * speeds[None]
    denominator = (along_x4 + along_y4 + damping[None]).reshape(quad_size, rows_dev, cols_dev)
    along_x = along_x4.reshape(quad_size, rows_dev, cols_dev)
    along_y = along_y4.reshape(quad_size, rows_dev, cols_dev)
    previous = state[comp_low:comp_high]
    if step_y == 1:
        edge_col = previous[:, :, cols_dev - 1]
    else:
        edge_col = previous[:, :, 0]
    arrived = passed_along(edge_col, "cols", step_y)
    if step_y == 1:
        beside = jnp.concatenate([arrived[:, :, None], previous[:, :, :-1]], axis=2)
    else:
        beside = jnp.concatenate([previous[:, :, 1:], arrived[:, :, None]], axis=2)
    known = along_y * beside + source[comp_low:comp_high]
    matrix = inverse[quadrant]
    if step_x == 1:
        row_order = list(range(rows_dev))
    else:
        row_order = list(range(rows_dev - 1, -1, -1))
    row_count = lax.axis_size("rows")
    if step_x == 1:
        position = lax.axis_index("rows")
    else:
        position = row_count - 1 - lax.axis_index("rows")
    block_cols = cols_dev // blocks

    def advance(section_id, carry):
        updated, front_row = carry
        incoming = passed_along(front_row, "rows", step_x)
        block_id = section_id - position
        active = (block_id >= 0) & (block_id < blocks)
        col_start = jnp.clip(block_id, 0, blocks - 1) * block_cols

        def compute(operands):
            current, upwind = operands
            block_x = lax.dynamic_slice_in_dim(along_x, col_start, block_cols, 2)
            block_known = lax.dynamic_slice_in_dim(known, col_start, block_cols, 2)
            block_den = lax.dynamic_slice_in_dim(denominator, col_start, block_cols, 2)
            rows_out = [None] * rows_dev
            for row_id in row_order:
                balance = (block_x[:, row_id] * upwind + block_known[:, row_id]) / block_den[
                    :, row_id
                ]
                upwind = jnp.dot(
                    matrix,
                    balance,
                    precision=lax.Precision.HIGHEST,
                    preferred_element_type=jnp.float32,
                )
                rows_out[row_id] = upwind
            result = jnp.stack(rows_out, axis=1)
            return (lax.dynamic_update_slice_in_dim(current, result, col_start, 2), upwind)

        def skip_block(operands):
            return (operands[0], front_row)

        return lax.cond(active, compute, skip_block, (updated, incoming))

    initial = (jnp.zeros_like(previous), jnp.zeros((quad_size, block_cols), jnp.float32))
    updated, front_row = lax.fori_loop(0, row_count + blocks - 1, advance, initial)
    return state.at[comp_low:comp_high].set(updated)


def body(
    wind_speed,
    wind_dir,
    depth_class,
    group_speed,
    dissipation,
    input_rate,
    outer_spectra,
    dest_cell,
    refraction_inverse,
    sweep_order,
):
    rows_dev, cols_dev = wind_speed.shape
    class_count = group_speed.shape[0]
    onehot = (depth_class[None] == jnp.arange(class_count, dtype=jnp.int32)[:, None, None]).astype(
        jnp.float32
    )
    speeds = class_table(group_speed, onehot)
    losses = class_table(dissipation, onehot)
    angle = (jnp.arange(NDIR, dtype=jnp.float32) + 0.5) * (2.0 * math.pi / NDIR)
    spread = jnp.maximum(jnp.cos(angle[:, None, None] - wind_dir[None]), 0.0)
    strength = (wind_speed * 0.1) ** 2
    wind_input = (
        input_rate[None, :, None, None] * strength[None, None] * (spread * spread)[:, None]
    ).reshape(NDIR * NFREQ, rows_dev, cols_dev)
    source = wind_input + boundary_forcing(outer_spectra, dest_cell, rows_dev, cols_dev)
    cos_abs = jnp.abs(jnp.cos(angle))
    sin_abs = jnp.abs(jnp.sin(angle))
    blocks = 1
    branches = [
        partial(
            sweep,
            quadrant=quad,
            speeds=speeds,
            losses=losses,
            source=source,
            cos_abs=cos_abs,
            sin_abs=sin_abs,
            inverse=refraction_inverse,
            blocks=blocks,
        )
        for quad in range(4)
    ]
    state = jnp.zeros(source.shape, jnp.float32)
    for sweep_round in range(ITERS):
        for turn in range(4):
            state = lax.switch(sweep_order[sweep_round, turn], branches, state)
    return state


def solution(mesh):
    placed = (
        P("rows", "cols"),
        P("rows", "cols"),
        P("rows", "cols"),
        P(),
        P(),
        P(),
        P(("rows", "cols"), None),
        P(("rows", "cols")),
        P(),
        P(),
    )
    return jax.shard_map(
        body, mesh=mesh, in_specs=placed, out_specs=P(None, "rows", "cols"), check_vma=False
    )
```

profile of v0, /device:TPU:17, one launch (start us, length us, event | category | flops | bytes accessed | tf_op | source)
XLA Modules:
  0.0 829.6 jit_solution(9251791245155383073)
XLA Ops:
  34.3 29.8 %all-to-all-done.1 = f32[32,1,13824]{2,1,0:T(1,128)S(1)} async-done(((f32[32,1,13824]{2,1,0:T(1,128)}), f32[32,1,13824]{2,1,0:T(1,128)S(1)}, u32[]{:S(2)}, u32[]{:S(2)}) %all-to-all-start.1) | async-done | bytes 1769504 | tf_op jit(solution)/shard_map/all_to_all | solution.py:47
  70.9 7.8 scatter_custom_fusion.2
  91.0 55.4 %conditional.40 = (f32[864,8,128]{2,0,1:T(8,128)}) conditional(s32[]{:T(128)} %bitcast.1411, (f32[36]{0:T(128)S(1)}, f32[24,8,128]{2,1,0:T(8,128)}, f32[36]{0:T(128)S(1)}, f32[864,8,128]{2,1,0:T(8,128)S(1)}, f32[24,8,128]{2,1,0:T(8,128)}, /*index=5*/f32[4,216,216]{2,1,0:T(8,128)S(1)}) %tuple.2335, (f32[36]{0:T(128)S(1)}, ...), branch_computations={%region_6.11_spmd, %region_11.0_spmd, %region_16.21_spmd, %region_... | conditional | flops 575520768 | bytes 36032432 | solution.py:190
  107.3 30.2 %while.544 = (s32[]{:T(128)}, f32[216,8,128]{2,0,1:T(8,128)}, f32[216,128]{1,0:T(8,128)}, s32[]{:T(128)}, f32[216,8,128]{2,0,1:T(8,128)}, /*index=5*/f32[216,216...) while((s32[]{:T(128)}, f32[216,8,128]{2,0,1:T(8,128)}, ...), condition=%wide.region_10.10_spmd.clone.clone, body=%wide.region_7.9_spmd.clone.clone.sunk | while | flops 574857216 | bytes 25373796 | solution.py:140
  118.0 8.2 collective-permute-done.62
  146.4 89.8 %conditional.41 = (f32[864,8,128]{0,1,2:T(8,128)}) conditional(s32[]{:T(128)} %bitcast.1410, (f32[36]{0:T(128)S(1)}, f32[24,8,128]{2,1,0:T(8,128)}, f32[36]{0:T(128)S(1)}, f32[864,8,128]{2,0,1:T(8,128)}, f32[864,8,128]{2,1,0:T(8,128)S(1)}, /*index=5*/f32[24,8,128]{2,1,0:T(8,128)}, ...), branch_computations={%region_26.32_spmd, %region_32.38_spmd, %region_38.44_spmd, %regio... | conditional | flops 577539072 | bytes 53737900 | solution.py:190
  178.3 23.0 %while.549 = (s32[]{:T(128)}, f32[216,8,128]{2,0,1:T(8,128)}, f32[216,128]{1,0:T(8,128)}, s32[]{:T(128)}, f32[216,8,128]{2,0,1:T(8,128)}, /*index=5*/f32[216,216...) while((s32[]{:T(128)}, f32[216,8,128]{2,0,1:T(8,128)}, ...), condition=%wide.region_37.37_spmd.clone.clone, body=%wide.region_34.36_spmd.clone.clone.sunk | while | flops 574857216 | bytes 26147940 | solution.py:140
  203.9 22.5 %scatter.83 = f32[864,8,128]{0,1,2:T(8,128)} dynamic-update-slice(f32[864,8,128]{0,1,2:T(8,128)} %copy.1000, f32[216,8,128]{0,1,2:T(8,128)} %copy.826, s32[]{:T(128)} %constant.2101.clone, s32[]{:T(128)} %constant.2093.clone, s32[]{:T(128)} %constant.2093.clone) | dynamic-update-slice | bytes 1769476 | tf_op jit(solution)/shard_map/cond/branch_1_fun/scatter | solution.py:141
  236.3 104.7 %conditional.42 = (f32[864,8,128]{0,1,2:T(8,128)}) conditional(s32[]{:T(128)} %bitcast.1409, (f32[36]{0:T(128)S(1)}, f32[24,8,128]{2,1,0:T(8,128)}, f32[36]{0:T(128)S(1)}, f32[864,8,128]{0,1,2:T(8,128)}, f32[864,8,128]{2,1,0:T(8,128)S(1)}, /*index=5*/f32[24,8,128]{2,1,0:T(8,128)}, ...), branch_computations={%region_50.56_spmd, %region_56.62_spmd, %region_62.68_spmd, %regio... | conditional | flops 577539072 | bytes 53737900 | solution.py:190
  280.2 36.1 %while.555 = (s32[]{:T(128)}, f32[216,8,128]{2,0,1:T(8,128)}, f32[216,128]{1,0:T(8,128)}, s32[]{:T(128)}, f32[216,8,128]{2,0,1:T(8,128)}, /*index=5*/f32[216,216...) while((s32[]{:T(128)}, f32[216,8,128]{2,0,1:T(8,128)}, ...), condition=%wide.region_73.73_spmd.clone.clone, body=%wide.region_70.72_spmd.clone.clone.sunk | while | flops 574857216 | bytes 25373796 | solution.py:140
  296.7 8.3 collective-permute-done.40
  318.9 21.8 %scatter.95 = f32[864,8,128]{0,1,2:T(8,128)} dynamic-update-slice(f32[864,8,128]{0,1,2:T(8,128)} %get-tuple-element.6233, f32[216,8,128]{0,1,2:T(8,128)} %copy.862, s32[]{:T(128)} %constant.2169.clone, s32[]{:T(128)} %constant.2162.clone, s32[]{:T(128)} %constant.2162.clone) | dynamic-update-slice | bytes 1769476 | tf_op jit(solution)/shard_map/cond/branch_3_fun/scatter | solution.py:141
  341.0 95.9 %conditional.43 = (f32[864,8,128]{0,1,2:T(8,128)}) conditional(s32[]{:T(128)} %bitcast.1408, (f32[36]{0:T(128)S(1)}, f32[24,8,128]{2,1,0:T(8,128)}, f32[36]{0:T(128)S(1)}, f32[864,8,128]{0,1,2:T(8,128)}, f32[864,8,128]{2,1,0:T(8,128)S(1)}, /*index=5*/f32[24,8,128]{2,1,0:T(8,128)}, ...), branch_computations={%region_74.80_spmd, %region_80.86_spmd, %region_86.92_spmd, %regio... | conditional | flops 577539072 | bytes 53737900 | solution.py:190
  383.7 23.0 %while.558 = (s32[]{:T(128)}, f32[216,8,128]{2,0,1:T(8,128)}, f32[216,128]{1,0:T(8,128)}, s32[]{:T(128)}, f32[216,8,128]{2,0,1:T(8,128)}, /*index=5*/f32[216,216...) while((s32[]{:T(128)}, f32[216,8,128]{2,0,1:T(8,128)}, ...), condition=%wide.region_91.91_spmd.clone.clone, body=%wide.region_88.90_spmd.clone.clone.sunk | while | flops 574857216 | bytes 26147940 | solution.py:140
  391.3 7.7 conditional.161
  409.2 22.5 %scatter.101 = f32[864,8,128]{0,1,2:T(8,128)} dynamic-update-slice(f32[864,8,128]{0,1,2:T(8,128)} %get-tuple-element.6305, f32[216,8,128]{0,1,2:T(8,128)} %copy.880, s32[]{:T(128)} %constant.2203.clone, s32[]{:T(128)} %constant.2195.clone, s32[]{:T(128)} %constant.2195.clone) | dynamic-update-slice | bytes 1769476 | tf_op jit(solution)/shard_map/cond/branch_2_fun/scatter | solution.py:141
  436.9 102.8 %conditional.44 = (f32[864,8,128]{0,1,2:T(8,128)}) conditional(s32[]{:T(128)} %bitcast.1407, (f32[36]{0:T(128)S(1)}, f32[24,8,128]{2,1,0:T(8,128)}, f32[36]{0:T(128)S(1)}, f32[864,8,128]{0,1,2:T(8,128)}, f32[864,8,128]{2,1,0:T(8,128)S(1)}, /*index=5*/f32[24,8,128]{2,1,0:T(8,128)}, ...), branch_computations={%region_98.104_spmd, %region_104.110_spmd, %region_110.116_spmd, %... | conditional | flops 577539072 | bytes 53737900 | solution.py:190
  478.5 30.7 %while.562 = (s32[]{:T(128)}, f32[216,8,128]{2,0,1:T(8,128)}, f32[216,128]{1,0:T(8,128)}, s32[]{:T(128)}, f32[216,8,128]{2,0,1:T(8,128)}, /*index=5*/f32[216,216...) while((s32[]{:T(128)}, f32[216,8,128]{2,0,1:T(8,128)}, ...), condition=%wide.region_115.115_spmd.clone.clone, body=%wide.region_112.114_spmd.clone.clone.sunk | while | flops 574857216 | bytes 26147940 | solution.py:140
  478.5 9.6 %collective-permute-start.26 = (f32[216,128]{1,0:T(8,128)}, f32[216,128]{1,0:T(8,128)}, u32[]{:S(2)}, u32[]{:S(2)}) collective-permute-start(f32[216,128]{1,0:T(8,128)} %get-tuple-element.13807), channel_id=1, source_target_pairs={{16,0},{17,1},{18,2},{19,3},{20,4},{21,5},{22,6},{23,7},{24,8},{25... | collective-permute-start | bytes 331784 | tf_op jit(solution)/shard_map/cond/branch_2_fun/while/body/eval_jaxpr/ppermute | solution.py:21
  511.8 22.5 %scatter.110 = f32[864,8,128]{0,1,2:T(8,128)} dynamic-update-slice(f32[864,8,128]{0,1,2:T(8,128)} %get-tuple-element.6401, f32[216,8,128]{0,1,2:T(8,128)} %copy.904, s32[]{:T(128)} %constant.2248.clone, s32[]{:T(128)} %constant.2240.clone, s32[]{:T(128)} %constant.2240.clone) | dynamic-update-slice | bytes 1769476 | tf_op jit(solution)/shard_map/cond/branch_2_fun/scatter | solution.py:141
  539.7 98.5 %conditional.45 = (f32[864,8,128]{0,1,2:T(8,128)}) conditional(s32[]{:T(128)} %bitcast.1406, (f32[36]{0:T(128)S(1)}, f32[24,8,128]{2,1,0:T(8,128)}, f32[36]{0:T(128)S(1)}, f32[864,8,128]{0,1,2:T(8,128)}, f32[864,8,128]{2,1,0:T(8,128)S(1)}, /*index=5*/f32[24,8,128]{2,1,0:T(8,128)}, ...), branch_computations={%region_122.128_spmd, %region_128.134_spmd, %region_134.140_spmd, ... | conditional | flops 577539072 | bytes 53737900 | solution.py:190
  572.2 30.4 %while.565 = (s32[]{:T(128)}, f32[216,8,128]{2,0,1:T(8,128)}, f32[216,128]{1,0:T(8,128)}, s32[]{:T(128)}, f32[216,8,128]{2,0,1:T(8,128)}, /*index=5*/f32[216,216...) while((s32[]{:T(128)}, f32[216,8,128]{2,0,1:T(8,128)}, ...), condition=%wide.region_133.133_spmd.clone.clone, body=%wide.region_130.132_spmd.clone.clone.sunk | while | flops 574857216 | bytes 26147940 | solution.py:140
  572.2 9.3 %collective-permute-start.20 = (f32[216,128]{1,0:T(8,128)}, f32[216,128]{1,0:T(8,128)}, u32[]{:S(2)}, u32[]{:S(2)}) collective-permute-start(f32[216,128]{1,0:T(8,128)} %get-tuple-element.13687), channel_id=1, source_target_pairs={{16,0},{17,1},{18,2},{19,3},{20,4},{21,5},{22,6},{23,7},{24,8},{25... | collective-permute-start | bytes 331784 | tf_op jit(solution)/shard_map/cond/branch_1_fun/while/body/eval_jaxpr/ppermute | solution.py:21
  605.1 22.5 %scatter.116 = f32[864,8,128]{0,1,2:T(8,128)} dynamic-update-slice(f32[864,8,128]{0,1,2:T(8,128)} %get-tuple-element.6473, f32[216,8,128]{0,1,2:T(8,128)} %copy.922, s32[]{:T(128)} %constant.2281.clone, s32[]{:T(128)} %constant.2273.clone, s32[]{:T(128)} %constant.2273.clone) | dynamic-update-slice | bytes 1769476 | tf_op jit(solution)/shard_map/cond/branch_1_fun/scatter | solution.py:141
  638.2 93.0 %conditional.46 = (f32[864,8,128]{0,1,2:T(8,128)}) conditional(s32[]{:T(128)} %bitcast.1405, (f32[36]{0:T(128)S(1)}, f32[24,8,128]{2,1,0:T(8,128)}, f32[36]{0:T(128)S(1)}, f32[864,8,128]{0,1,2:T(8,128)}, f32[864,8,128]{2,1,0:T(8,128)S(1)}, /*index=5*/f32[24,8,128]{2,1,0:T(8,128)}, ...), branch_computations={%region_146.152_spmd, %region_152.158_spmd, %region_158.164_spmd, ... | conditional | flops 577539072 | bytes 53737900 | solution.py:190
  669.7 36.1 %while.568 = (s32[]{:T(128)}, f32[216,8,128]{2,0,1:T(8,128)}, f32[216,128]{1,0:T(8,128)}, s32[]{:T(128)}, f32[216,8,128]{2,0,1:T(8,128)}, /*index=5*/f32[216,216...) while((s32[]{:T(128)}, f32[216,8,128]{2,0,1:T(8,128)}, ...), condition=%wide.region_151.151_spmd.clone.clone, body=%wide.region_148.150_spmd.clone.clone.sunk | while | flops 574857216 | bytes 25373796 | solution.py:140
  686.2 8.2 collective-permute-done.14
  731.2 96.3 %conditional.47 = (f32[864,8,128]{2,1,0:T(8,128)S(1)}) conditional(s32[]{:T(128)} %bitcast.1404, (f32[36]{0:T(128)S(1)}, f32[24,8,128]{2,1,0:T(8,128)}, f32[36]{0:T(128)S(1)}, f32[864,8,128]{0,1,2:T(8,128)}, f32[864,8,128]{2,1,0:T(8,128)S(1)}, /*index=5*/f32[24,8,128]{2,1,0:T(8,128)}, ...), branch_computations={%region_170.176_spmd, %region_176.182_spmd, %region_182.188_spmd, ... | conditional | flops 577539072 | bytes 54524332 | solution.py:190
  771.0 28.9 %while.575 = (s32[]{:T(128)}, f32[216,8,128]{2,0,1:T(8,128)}, f32[216,128]{1,0:T(8,128)}, s32[]{:T(128)}, f32[216,8,128]{2,0,1:T(8,128)}, /*index=5*/f32[216,216...) while((s32[]{:T(128)}, f32[216,8,128]{2,0,1:T(8,128)}, ...), condition=%wide.region_193.193_spmd.clone.clone, body=%wide.region_190.192_spmd.clone.clone.sunk | while | flops 574857216 | bytes 17549328 | solution.py:140
  776.9 11.5 %collective-permute-done = f32[216,128]{1,0:T(8,128)S(1)} collective-permute-done((f32[216,128]{1,0:T(8,128)}, f32[216,128]{1,0:T(8,128)S(1)}, u32[]{:S(2)}, u32[]{:S(2)}) %collective-permute-start) | collective-permute-done | bytes 110624 | tf_op jit(solution)/shard_map/cond/branch_3_fun/while/body/eval_jaxpr/ppermute | solution.py:21
  789.4 10.5 %conditional.144 = ((f32[216,8,128]{2,0,1:T(8,128)}, f32[216,128]{1,0:T(8,128)})) conditional(s32[]{:T(128)} %convert_element_type.334, (f32[216,8,128]{2,0,1:T(8,128)}, f32[216,128]{1,0:T(8,128)}) %tuple.1916, (f32[216,8,128]{2,0,1:T(8,128)S(1)}, f32[216,128]{1,0:T(8,128)S(1)}, f32[216,8,128]{2,0,1:T(8,128)}, f32[216,8,128]{2,0,1:T(8,128)S(1)}, ...), branch_computations={%region_191.190_spmd, %region_192.191_spmd} | conditional | flops 574636032 | bytes 14156692 | solution.py:137
  801.5 22.0 %scatter.136 = f32[864,8,128]{0,1,2:T(8,128)} dynamic-update-slice(f32[864,8,128]{0,1,2:T(8,128)} %get-tuple-element.6713, f32[216,8,128]{0,1,2:T(8,128)S(1)} %copy.982, s32[]{:T(128)} %constant.2394.clone, s32[]{:T(128)} %constant.2387.clone, s32[]{:T(128)} %constant.2387.clone) | dynamic-update-slice | bytes 1769476 | tf_op jit(solution)/shard_map/cond/branch_3_fun/scatter | solution.py:141
  (476 shorter events, 546.9 us)
Async XLA Ops:
  3.7 13.6 %all-to-all-start = ((s32[32,1,16]{2,1,0:T(1,128)}), s32[32,1,16]{2,1,0:T(1,128)S(1)}, u32[]{:S(2)}, u32[]{:S(2)}) async-start(s32[32,1,16]{2,1,0:T(1,128)} %bitcast.1413), calls=%async_computation | async-start | bytes 32768 | tf_op jit(solution)/shard_map/all_to_all | solution.py:54
  13.3 16.0 %copy-start.131 = (s32[8,128]{1,0:T(8,128)S(1)}, s32[8,128]{1,0:T(8,128)}, u32[]{:S(2)}) copy-start(s32[8,128]{1,0:T(8,128)} %param.236) | copy-start | bytes 12292
  13.3 16.0 %copy-start.134 = (f32[4,24]{1,0:T(4,128)S(1)}, f32[4,24]{1,0:T(4,128)}, u32[]{:S(2)}) copy-start(f32[4,24]{1,0:T(4,128)} %param.238) | copy-start | bytes 1156
  13.3 16.0 %copy-start.135 = (f32[4,24]{1,0:T(4,128)S(1)}, f32[4,24]{1,0:T(4,128)}, u32[]{:S(2)}) copy-start(f32[4,24]{1,0:T(4,128)} %param.237) | copy-start | bytes 1156
  13.3 16.9 %copy-start.133 = (f32[8,128]{1,0:T(8,128)S(1)}, f32[8,128]{1,0:T(8,128)}, u32[]{:S(2)}) copy-start(f32[8,128]{1,0:T(8,128)} %param.234) | copy-start | bytes 12292
  13.3 16.9 %copy-start.136 = (f32[24]{0:T(128)S(1)}, f32[24]{0:T(128)}, u32[]{:S(2)}) copy-start(f32[24]{0:T(128)} %param.239) | copy-start | bytes 292
  13.4 17.0 %copy-start.132 = (f32[8,128]{1,0:T(8,128)S(1)}, f32[8,128]{1,0:T(8,128)}, u32[]{:S(2)}) copy-start(f32[8,128]{1,0:T(8,128)} %param.235) | copy-start | bytes 12292
  17.3 46.9 %all-to-all-start.1 = ((f32[32,1,13824]{2,1,0:T(1,128)}), f32[32,1,13824]{2,1,0:T(1,128)S(1)}, u32[]{:S(2)}, u32[]{:S(2)}) async-start(f32[32,1,13824]{2,1,0:T(1,128)} %all_to_all.16), calls=%async_computation.1 | async-start | bytes 3538944 | tf_op jit(solution)/shard_map/all_to_all | solution.py:47
  91.6 9.6 %collective-permute-start.63 = (f32[216,8]{0,1:T(8,128)}, f32[216,8]{0,1:T(8,128)}, u32[]{:S(2)}, u32[]{:S(2)}) collective-permute-start(f32[216,8]{0,1:T(8,128)} %broadcast.2016), channel_id=1, source_target_pairs={{0,1},{1,2},{2,3},{3,4},{4,5},{5,6},{6,7},{7,8},{8,9},{9,10},{10,1... | collective-permute-start | bytes 20744 | tf_op jit(solution)/shard_map/cond/branch_0_fun/ppermute | solution.py:21
  107.3 3.5 collective-permute-start.62
  114.7 11.5 %collective-permute-start.62 = (f32[216,128]{1,0:T(8,128)}, f32[216,128]{1,0:T(8,128)}, u32[]{:S(2)}, u32[]{:S(2)}) collective-permute-start(f32[216,128]{1,0:T(8,128)} %get-tuple-element.14527), channel_id=1, source_target_pairs={{0,16},{1,17},{2,18},{3,19},{4,20},{5,21},{6,22},{7,23},{8,24},{9,... | collective-permute-start | bytes 331784 | tf_op jit(solution)/shard_map/cond/branch_0_fun/while/body/eval_jaxpr/ppermute | solution.py:21
  152.4 19.3 %collective-permute-start.53 = (f32[216,8]{0,1:T(8,128)}, f32[216,8]{0,1:T(8,128)}, u32[]{:S(2)}, u32[]{:S(2)}) collective-permute-start(f32[216,8]{0,1:T(8,128)} %slice_bitcast_fusion.263), channel_id=1, source_target_pairs={{0,1},{1,2},{2,3},{3,4},{4,5},{5,6},{6,7},{7,8},{8,9},{9,10},{10,1... | collective-permute-start | bytes 20744 | tf_op jit(solution)/shard_map/cond/branch_1_fun/ppermute | solution.py:21
  178.3 3.9 collective-permute-start.52
  193.7 3.9 collective-permute-start.52
  248.0 25.6 %collective-permute-start.41 = (f32[216,8]{0,1:T(8,128)}, f32[216,8]{0,1:T(8,128)}, u32[]{:S(2)}, u32[]{:S(2)}) collective-permute-start(f32[216,8]{0,1:T(8,128)} %slice_bitcast_fusion.275), channel_id=1, source_target_pairs={{1,0},{2,1},{3,2},{4,3},{5,4},{6,5},{7,6},{8,7},{9,8},{10,9},{11,1... | collective-permute-start | bytes 20744 | tf_op jit(solution)/shard_map/cond/branch_3_fun/ppermute | solution.py:21
  280.2 9.5 %collective-permute-start.40 = (f32[216,128]{1,0:T(8,128)}, f32[216,128]{1,0:T(8,128)}, u32[]{:S(2)}, u32[]{:S(2)}) collective-permute-start(f32[216,128]{1,0:T(8,128)} %get-tuple-element.14087), channel_id=1, source_target_pairs={{0,16},{1,17},{2,18},{3,19},{4,20},{5,21},{6,22},{7,23},{8,24},{9,... | collective-permute-start | bytes 331784 | tf_op jit(solution)/shard_map/cond/branch_3_fun/while/body/eval_jaxpr/ppermute | solution.py:21
  293.5 11.5 %collective-permute-start.40 = (f32[216,128]{1,0:T(8,128)}, f32[216,128]{1,0:T(8,128)}, u32[]{:S(2)}, u32[]{:S(2)}) collective-permute-start(f32[216,128]{1,0:T(8,128)} %get-tuple-element.14087), channel_id=1, source_target_pairs={{0,16},{1,17},{2,18},{3,19},{4,20},{5,21},{6,22},{7,23},{8,24},{9,... | collective-permute-start | bytes 331784 | tf_op jit(solution)/shard_map/cond/branch_3_fun/while/body/eval_jaxpr/ppermute | solution.py:21
  352.8 24.3 %collective-permute-start.35 = (f32[216,8]{0,1:T(8,128)}, f32[216,8]{0,1:T(8,128)}, u32[]{:S(2)}, u32[]{:S(2)}) collective-permute-start(f32[216,8]{0,1:T(8,128)} %slice_bitcast_fusion.281), channel_id=1, source_target_pairs={{1,0},{2,1},{3,2},{4,3},{5,4},{6,5},{7,6},{8,7},{9,8},{10,9},{11,1... | collective-permute-start | bytes 20744 | tf_op jit(solution)/shard_map/cond/branch_2_fun/ppermute | solution.py:21
  383.7 3.9 collective-permute-start.34
  399.1 3.9 collective-permute-start.34
  448.4 23.5 %collective-permute-start.27 = (f32[216,8]{0,1:T(8,128)}, f32[216,8]{0,1:T(8,128)}, u32[]{:S(2)}, u32[]{:S(2)}) collective-permute-start(f32[216,8]{0,1:T(8,128)} %slice_bitcast_fusion.289), channel_id=1, source_target_pairs={{1,0},{2,1},{3,2},{4,3},{5,4},{6,5},{7,6},{8,7},{9,8},{10,9},{11,1... | collective-permute-start | bytes 20744 | tf_op jit(solution)/shard_map/cond/branch_2_fun/ppermute | solution.py:21
  478.5 11.6 %collective-permute-start.26 = (f32[216,128]{1,0:T(8,128)}, f32[216,128]{1,0:T(8,128)}, u32[]{:S(2)}, u32[]{:S(2)}) collective-permute-start(f32[216,128]{1,0:T(8,128)} %get-tuple-element.13807), channel_id=1, source_target_pairs={{16,0},{17,1},{18,2},{19,3},{20,4},{21,5},{22,6},{23,7},{24,8},{25... | collective-permute-start | bytes 331784 | tf_op jit(solution)/shard_map/cond/branch_2_fun/while/body/eval_jaxpr/ppermute | solution.py:21
  501.6 3.9 collective-permute-start.26
  541.1 24.5 %collective-permute-start.21 = (f32[216,8]{0,1:T(8,128)}, f32[216,8]{0,1:T(8,128)}, u32[]{:S(2)}, u32[]{:S(2)}) collective-permute-start(f32[216,8]{0,1:T(8,128)} %slice_bitcast_fusion.295), channel_id=1, source_target_pairs={{0,1},{1,2},{2,3},{3,4},{4,5},{5,6},{6,7},{7,8},{8,9},{9,10},{10,1... | collective-permute-start | bytes 20744 | tf_op jit(solution)/shard_map/cond/branch_1_fun/ppermute | solution.py:21
  572.2 11.3 %collective-permute-start.20 = (f32[216,128]{1,0:T(8,128)}, f32[216,128]{1,0:T(8,128)}, u32[]{:S(2)}, u32[]{:S(2)}) collective-permute-start(f32[216,128]{1,0:T(8,128)} %get-tuple-element.13687), channel_id=1, source_target_pairs={{16,0},{17,1},{18,2},{19,3},{20,4},{21,5},{22,6},{23,7},{24,8},{25... | collective-permute-start | bytes 331784 | tf_op jit(solution)/shard_map/cond/branch_1_fun/while/body/eval_jaxpr/ppermute | solution.py:21
  595.0 3.9 collective-permute-start.20
  639.5 23.6 %collective-permute-start.15 = (f32[216,8]{0,1:T(8,128)}, f32[216,8]{0,1:T(8,128)}, u32[]{:S(2)}, u32[]{:S(2)}) collective-permute-start(f32[216,8]{0,1:T(8,128)} %slice_bitcast_fusion.301), channel_id=1, source_target_pairs={{0,1},{1,2},{2,3},{3,4},{4,5},{5,6},{6,7},{7,8},{8,9},{9,10},{10,1... | collective-permute-start | bytes 20744 | tf_op jit(solution)/shard_map/cond/branch_0_fun/ppermute | solution.py:21
  669.7 9.5 %collective-permute-start.14 = (f32[216,128]{1,0:T(8,128)}, f32[216,128]{1,0:T(8,128)}, u32[]{:S(2)}, u32[]{:S(2)}) collective-permute-start(f32[216,128]{1,0:T(8,128)} %get-tuple-element.13567), channel_id=1, source_target_pairs={{0,16},{1,17},{2,18},{3,19},{4,20},{5,21},{6,22},{7,23},{8,24},{9,... | collective-permute-start | bytes 331784 | tf_op jit(solution)/shard_map/cond/branch_0_fun/while/body/eval_jaxpr/ppermute | solution.py:21
  683.0 11.5 %collective-permute-start.14 = (f32[216,128]{1,0:T(8,128)}, f32[216,128]{1,0:T(8,128)}, u32[]{:S(2)}, u32[]{:S(2)}) collective-permute-start(f32[216,128]{1,0:T(8,128)} %get-tuple-element.13567), channel_id=1, source_target_pairs={{0,16},{1,17},{2,18},{3,19},{4,20},{5,21},{6,22},{7,23},{8,24},{9,... | collective-permute-start | bytes 331784 | tf_op jit(solution)/shard_map/cond/branch_0_fun/while/body/eval_jaxpr/ppermute | solution.py:21
  743.8 22.0 %collective-permute-start.1 = (f32[216,8]{0,1:T(8,128)}, f32[216,8]{0,1:T(8,128)}, u32[]{:S(2)}, u32[]{:S(2)}) collective-permute-start(f32[216,8]{0,1:T(8,128)} %slice_bitcast_fusion.315), channel_id=1, source_target_pairs={{1,0},{2,1},{3,2},{4,3},{5,4},{6,5},{7,6},{8,7},{9,8},{10,9},{11,1... | collective-permute-start | bytes 20744 | tf_op jit(solution)/shard_map/cond/branch_3_fun/ppermute | solution.py:21
  771.0 3.4 collective-permute-start
  775.4 12.9 %collective-permute-start = (f32[216,128]{1,0:T(8,128)}, f32[216,128]{1,0:T(8,128)S(1)}, u32[]{:S(2)}, u32[]{:S(2)}) collective-permute-start(f32[216,128]{1,0:T(8,128)} %get-tuple-element.13287), channel_id=1, source_target_pairs={{0,16},{1,17},{2,18},{3,19},{4,20},{5,21},{6,22},{7,23},{8,24},{9,... | collective-permute-start | bytes 331784 | tf_op jit(solution)/shard_map/cond/branch_3_fun/while/body/eval_jaxpr/ppermute | solution.py:21
  (35 other events, 107.6 us)
where the time goes:
time: 835 us; the launch traced here: 830 us
  local copies, waits for them, and re-layouts  408 us (49%)
  other arithmetic  118 us (14%)
  loops' own time  96.4 us (12%)
  waiting for transfers between devices  80.8 us (10%)
  starting transfers between devices  79.9 us (10%)
  matrix products  40.6 us (5%)
    scatter x8, local copies, waits for them, and re-layouts, sweep(): return state.at[comp_low:comp_high].set(updated)  144 us
    another operation x8, loops' own time, body(): state = lax.switch(sweep_order[sweep_round, turn], branches, state)  95.3 us
    another operation x40, local copies, waits for them, and re-layouts  77.1 us
    ppermute x24, starting transfers between devices, passed_along(): return lax.ppermute(block, axis, route)  67.5 us
    ppermute x24, waiting for transfers between devices, passed_along(): return lax.ppermute(block, axis, route)  51 us
    dot_general x64, matrix products, compute(): jnp.dot(matrix, balance, precision=lax.Precision.HIGHEST, preferred_eleme...  40.6 us
    mul x32, local copies, waits for them, and re-layouts, sweep(): along_x4 = dir_cos[:, None, None, None] * speeds[None]  38.8 us
    all_to_all x1, waiting for transfers between devices, boundary_forcing(): lax.all_to_all(outgoing.reshape(devices, CAP * components), ('rows', 'col...  29.8 us
  transfers between devices with their start and end apart: 26, of which 9 were waited for; matrix products, arithmetic and copies ran while one was open for 22% of the time, Pallas kernels for 0%

commit v1 on v0

v1 whole, which is shorter than its diff:
```python
import math

import jax
import jax.numpy as jnp
import numpy as np
from jax import lax
from jax.experimental import pallas as pl
from jax.experimental.pallas import tpu as pltpu
from jax.sharding import PartitionSpec as P

NDIR = 36
NFREQ = 24
CAP = 16
ITERS = 2
QUADS = 4
LANES = 128
HALO = 8

whitecap_rate = 0.5


def split_bf16(value):
    high = value.astype(jnp.bfloat16)
    low = (value - high.astype(jnp.float32)).astype(jnp.bfloat16)
    return high, low


def split_rounded(value):
    rounded = lax.reduce_precision(value, 8, 7)
    return rounded.astype(jnp.bfloat16), (value - rounded).astype(jnp.bfloat16)


def pad_to(array, axis, size, value=0.0):
    widths = [(0, 0)] * array.ndim
    widths[axis] = (0, size - array.shape[axis])
    return jnp.pad(array, widths, constant_values=value)


def sweeps_kernel(rows, own, cells, quad_size, info, ax_ref, ay_ref, base_ref, wind_ref, mt_ref,
                  own_ref, par_ref, same_ref, cross_ref, keep_ref, send_ref,
                  state, power, rim, side):
    turn = pl.program_id(0)
    quad = info[turn]
    half = info[ITERS * QUADS]
    width = mt_ref.shape[2]
    rows_dev = rows // 2
    down = (quad == 0) | (quad == 3)
    step_x = jnp.where(down, 1, -1)
    first_row = jnp.where(down, 0, rows - 1)
    up_y = quad < 2

    @pl.when(turn == 0)
    def _():
        power[...] = jnp.zeros_like(power)

    rim[0] = own_ref[0, 0:cells]
    rim[0, own:cells] = own_ref[0, own:cells] + same_ref[0]
    rim[1] = par_ref[0, 0:cells]
    rim[1, own:cells] = par_ref[0, own:cells] + cross_ref[0]
    edge_at = jnp.where(half == 0, 0, 2 * HALO - 1)
    at_edge = lax.broadcasted_iota(jnp.int32, (2 * HALO, width), 0) == edge_at
    for j in range(rows_dev):
        mine = jnp.where(at_edge, own_ref[0, cells + j:cells + j + 1], 0.0)
        theirs = jnp.where(at_edge, par_ref[0, cells + j:cells + j + 1], 0.0)
        side[j + rows_dev * half] = mine
        side[j + rows_dev * (1 - half)] = theirs

    def run(count, second):
        def factors(i):
            row = first_row + i * step_x
            total = power[0, row, :count]
            for other in range(1, QUADS):
                total = total + power[other, row, :count]
            level = total * (1.0 / (QUADS * quad_size))
            damping = whitecap_rate * level / (1.0 + level)
            den = base_ref[0, row, :count] + jnp.concatenate([damping] * (width // LANES), axis=1)
            inverse = 1.0 / den
            source = wind_ref[0, row, :count]
            edge = side[row]
            parts = [source[:HALO] + edge[:HALO], source[HALO:own - HALO],
                     source[own - HALO:own] + edge[HALO:]]
            if count > own:
                parts.append(source[own:])
            source = jnp.concatenate(parts, axis=0)
            if i == 0 or i == rows - 1:
                here = jnp.where(row // rows_dev == half, 0, 1)
                source = source + rim[here, :count]
            if second:
                before = state[quad, row]
                shifted = jnp.where(up_y, pltpu.roll(before, 1, 0), pltpu.roll(before, cells - 1, 0))
                source = source + ay_ref[0, row, :count] * shifted[:count]
            return row, ax_ref[0, row, :count] * inverse, source * inverse

        row, along, known = factors(0)
        upwind = None
        for i in range(rows):
            balance = known if upwind is None else along * upwind + known
            high, low = split_bf16(balance)
            updated = jnp.dot(jnp.concatenate([high, high, low], axis=1), mt_ref[0],
                              preferred_element_type=jnp.float32)
            here = row
            if i + 1 < rows:
                row, along, known = factors(i + 1)
            square = updated * updated
            folded = square[:, :LANES]
            for lane in range(LANES, width, LANES):
                folded = folded + square[:, lane:lane + LANES]
            state[quad, here, :count] = updated
            power[quad, here, :count] = jnp.broadcast_to(
                jnp.sum(folded, axis=1, keepdims=True), (count, LANES))
            upwind = updated

    @pl.when(turn < QUADS)
    def _():
        run(cells, False)

    @pl.when(turn >= QUADS)
    def _():
        run(own, True)

    @pl.when(turn == ITERS * QUADS - 1)
    def _():
        for pair in range(QUADS // 2):
            for j in range(rows_dev):
                for out_ref, side_at in ((keep_ref, half), (send_ref, 1 - half)):
                    row = rows_dev * side_at + j
                    both = jnp.concatenate(
                        [state[2 * pair, row, :own], state[2 * pair + 1, row, :own]], axis=0)
                    out_ref[pair, :, j, :] = both.T[:quad_size]


def merge_kernel(own, info, keep_ref, got_ref, out_ref):
    half = info[ITERS * QUADS]
    keep = keep_ref[0]
    got = got_ref[0]
    left = jnp.where(half == 0, keep, got)
    right = jnp.where(half == 0, got, keep)
    low = lax.broadcasted_iota(jnp.int32, keep.shape, 2) < own
    axis = keep.ndim - 1
    out_ref[0, 0] = jnp.where(low, left, pltpu.roll(right, own, axis))
    out_ref[0, 1] = jnp.where(low, pltpu.roll(left, own, axis), right)


def body(
    wind_speed,
    wind_dir,
    depth_class,
    group_speed,
    dissipation,
    input_rate,
    outer_spectra,
    dest_cell,
    refraction_inverse,
    sweep_order,
):
    rows_dev, cols_dev = wind_speed.shape
    row_count = lax.axis_size("rows")
    col_count = lax.axis_size("cols")
    assert row_count == 2
    devices = row_count * col_count
    rows = rows_dev * row_count
    own = cols_dev // 2
    cells = own + HALO
    class_count = group_speed.shape[0]
    comps = outer_spectra.shape[1]
    quad_size = refraction_inverse.shape[1]
    quarter = NDIR // QUADS
    width = -(-quad_size // LANES) * LANES
    axes = ("rows", "cols")
    half = lax.axis_index("rows")

    def device(row_at, col_at):
        return row_at * col_count + col_at

    span = range(col_count)
    swap_route = [(device(1 - h, c), device(h, c)) for h in range(2) for c in span]
    same_route = [(device(0, c - 1), device(0, c)) for c in span if c > 0]
    same_route += [(device(1, c + 1), device(1, c)) for c in span if c + 1 < col_count]
    cross_route = [(device(1, c - 1), device(0, c)) for c in span if c > 0]
    cross_route += [(device(0, c + 1), device(1, c)) for c in span if c + 1 < col_count]

    points = dest_cell.shape[0]
    total_cols = cols_dev * col_count
    grid_row = dest_cell // total_cols
    grid_col = dest_cell % total_cols
    owner = grid_row // rows_dev * col_count + grid_col // cols_dev
    local_row = grid_row % rows_dev
    local_col = grid_col % cols_dev
    rim_code = jnp.where(
        (grid_row == 0) | (grid_row == rows - 1),
        local_col,
        jnp.where(grid_col == 0, cols_dev + local_row, cols_dev + rows_dev + local_row),
    )
    position = jnp.arange(points, dtype=jnp.int32)
    earlier = (owner[:, None] == owner[None, :]) & (position[:, None] > position[None, :])
    slot = owner * CAP + jnp.sum(earlier.astype(jnp.int32), axis=1)
    load = -(-(comps + 1) // LANES) * LANES
    payload = pad_to(
        jnp.concatenate([outer_spectra, (rim_code + 1).astype(jnp.float32)[:, None]], axis=1), 1, load)
    place = (jnp.arange(devices * CAP, dtype=jnp.int32)[:, None] == slot[None, :]).astype(jnp.float32)
    outgoing = jnp.dot(place, payload, precision=lax.Precision.HIGHEST,
                       preferred_element_type=jnp.float32)
    arrived = lax.all_to_all(outgoing.reshape(devices, CAP, load), axes, split_axis=0,
                             concat_axis=0, tiled=True).reshape(devices * CAP, load)

    held = jnp.stack([wind_speed, wind_dir, depth_class.astype(jnp.float32)])
    partner = lax.ppermute(held, axes, swap_route)
    beside_same = lax.ppermute(held, axes, same_route)
    beside_cross = lax.ppermute(held, axes, cross_route)
    is_low = half == 0
    chip = jnp.concatenate(
        [jnp.where(is_low, held, partner), jnp.where(is_low, partner, held)], axis=1)
    near = jnp.concatenate(
        [jnp.where(is_low, beside_same, beside_cross), jnp.where(is_low, beside_cross, beside_same)],
        axis=1)
    mine = jnp.where(is_low, chip[:, :, :own], chip[:, :, own:])
    right = jnp.where(is_low, chip[:, :, own], near[:, :, 0])
    left = jnp.where(is_low, near[:, :, cols_dev - 1], chip[:, :, own - 1])
    grid = jnp.concatenate(
        [mine, right[:, :, None], jnp.zeros((3, rows, HALO - 2), jnp.float32), left[:, :, None]], axis=2)
    speed_here, dir_here, class_here = grid[0], grid[1], grid[2]
    strength = (speed_here * 0.1) ** 2
    cos_here, sin_here = jnp.cos(dir_here), jnp.sin(dir_here)

    angle = (jnp.arange(NDIR, dtype=jnp.float32) + 0.5) * (2.0 * math.pi / NDIR)
    cos_lane = pad_to(jnp.repeat(jnp.cos(angle), NFREQ).reshape(QUADS, quad_size), 1, width)
    sin_lane = pad_to(jnp.repeat(jnp.sin(angle), NFREQ).reshape(QUADS, quad_size), 1, width)
    rate_lane = pad_to(jnp.tile(input_rate, quarter), 0, width)
    speed_lane = pad_to(jnp.tile(group_speed, (1, quarter)), 1, width)
    loss_lane = pad_to(jnp.tile(dissipation, (1, quarter)), 1, width, 1.0)
    ax_table = jnp.abs(cos_lane)[:, None] * speed_lane[None]
    ay_table = jnp.abs(sin_lane)[:, None] * speed_lane[None]
    base_table = ax_table + ay_table + loss_lane[None]

    def by_class(table):
        chosen = jnp.broadcast_to(table[:, None, None, 0], (QUADS, rows, cells, width))
        for kind in range(1, class_count):
            chosen = jnp.where((class_here == kind)[None, :, :, None], table[:, None, None, kind], chosen)
        return chosen

    ax = by_class(ax_table)
    ay = by_class(ay_table)
    base = by_class(base_table)
    spread = jnp.maximum(
        cos_here[None, :, :, None] * cos_lane[:, None, None]
        + sin_here[None, :, :, None] * sin_lane[:, None, None], 0.0)
    wind = (rate_lane[None, None, None] * strength[None, :, :, None]) * (spread * spread)

    flipped = pad_to(pad_to(jnp.swapaxes(refraction_inverse, 1, 2), 1, width), 2, width)
    flip_high, flip_low = split_rounded(flipped)
    matrices = jnp.concatenate([flip_high, flip_low, flip_high], axis=1)

    code = arrived[:, comps].astype(jnp.int32) - 1

    def place_in(side_at):
        col = code - own * side_at
        spot = jnp.where((code < cols_dev) & (code >= 0) & (col >= 0) & (col < own), col, -1)
        spot = jnp.where((side_at == 0) & (code == own), own, spot)
        spot = jnp.where((side_at == 1) & (code == own - 1), cells - 1, spot)
        along = code - cols_dev - rows_dev * side_at
        return jnp.where((along >= 0) & (along < rows_dev) & (code >= cols_dev), cells + along, spot)

    block = cells + rows_dev
    slots = jnp.arange(2 * block + 2 * HALO, dtype=jnp.int32)[:, None]
    to_own = place_in(half)[None, :]
    to_partner = place_in(1 - half)[None, :]
    out_right = code[None, :] == cols_dev - 1
    out_left = code[None, :] == 0
    to_same = jnp.where(is_low, jnp.where(out_right, HALO - 1, -1), jnp.where(out_left, 0, -1))
    to_cross = jnp.where(is_low, jnp.where(out_left, 0, -1), jnp.where(out_right, HALO - 1, -1))
    gather = (
        ((slots == to_own) & (to_own >= 0))
        | ((slots == to_partner + block) & (to_partner >= 0))
        | ((slots == to_same + 2 * block) & (to_same >= 0))
        | ((slots == to_cross + 2 * block + HALO) & (to_cross >= 0))
    ).astype(jnp.float32)
    summed = jnp.dot(gather, arrived, precision=lax.Precision.HIGHEST,
                     preferred_element_type=jnp.float32)[:, :comps]
    summed = jnp.swapaxes(summed.reshape(-1, QUADS, quad_size), 0, 1)
    summed = pad_to(summed, 2, width)
    rim_own = summed[:, :block]
    rim_partner = lax.ppermute(summed[:, block:2 * block], axes, swap_route)
    rim_same = lax.ppermute(summed[:, 2 * block:2 * block + HALO], axes, same_route)
    rim_cross = lax.ppermute(summed[:, 2 * block + HALO:], axes, cross_route)

    info = jnp.concatenate([sweep_order.reshape(-1), half[None].astype(jnp.int32)])
    turns = ITERS * QUADS

    def quad_block(shape):
        zeros = (0,) * len(shape)
        return pl.BlockSpec((1,) + shape, lambda t, info: (info[t],) + zeros)

    packed = (QUADS // 2, quad_size, rows_dev, cols_dev)
    whole = pl.BlockSpec(packed, lambda t, info: (0, 0, 0, 0))
    keep, send = pl.pallas_call(
        lambda *refs: sweeps_kernel(rows, own, cells, quad_size, *refs),
        grid_spec=pltpu.PrefetchScalarGridSpec(
            num_scalar_prefetch=1,
            grid=(turns,),
            in_specs=[quad_block((rows, cells, width))] * 4
            + [quad_block((3 * width, width))]
            + [quad_block((block, width))] * 2
            + [quad_block((HALO, width))] * 2,
            out_specs=[whole, whole],
            scratch_shapes=[
                pltpu.VMEM((QUADS, rows, cells, width), jnp.float32),
                pltpu.VMEM((QUADS, rows, cells, LANES), jnp.float32),
                pltpu.VMEM((2, cells, width), jnp.float32),
                pltpu.VMEM((rows, 2 * HALO, width), jnp.float32),
            ],
        ),
        out_shape=[jax.ShapeDtypeStruct(packed, jnp.float32)] * 2,
        compiler_params=pltpu.CompilerParams(
            dimension_semantics=("arbitrary",), vmem_limit_bytes=44 * 2**20),
    )(info, ax, ay, base, wind, matrices, rim_own, rim_partner, rim_same, rim_cross)

    got = lax.ppermute(send, axes, swap_route)
    chunks = 4
    part = quad_size // chunks
    half_block = pl.BlockSpec((1, part, rows_dev, cols_dev), lambda p, c, info: (p, c, 0, 0))
    merged = pl.pallas_call(
        lambda *refs: merge_kernel(own, *refs),
        grid_spec=pltpu.PrefetchScalarGridSpec(
            num_scalar_prefetch=1,
            grid=(QUADS // 2, chunks),
            in_specs=[half_block, half_block],
            out_specs=pl.BlockSpec(
                (1, 2, part, rows_dev, cols_dev), lambda p, c, info: (p, 0, c, 0, 0)),
        ),
        out_shape=jax.ShapeDtypeStruct((QUADS // 2, 2, quad_size, rows_dev, cols_dev), jnp.float32),
        compiler_params=pltpu.CompilerParams(vmem_limit_bytes=16 * 2**20),
    )(info, keep, got)
    return merged.reshape(comps, rows_dev, cols_dev)


def solution(mesh):
    placed = (
        P("rows", "cols"),
        P("rows", "cols"),
        P("rows", "cols"),
        P(),
        P(),
        P(),
        P(("rows", "cols"), None),
        P(("rows", "cols")),
        P(),
        P(),
    )
    return jax.shard_map(
        body, mesh=mesh, in_specs=placed, out_specs=P(None, "rows", "cols"), check_vma=False
    )
```

time: 835 us -> 120 us (0.14)
  local copies, waits for them, and re-layouts: 408 us -> 4.14 us
  other arithmetic: 118 us -> 17.4 us
  loops' own time: 96.4 us -> 0 us
  starting transfers between devices: 79.9 us -> 20.7 us
  waiting for transfers between devices: 80.8 us -> 34.6 us
  Pallas kernels: 0 us -> 36 us
  matrix products: 40.6 us -> 5.45 us
    scatter x10 -> x0, local copies, waits for them, and re-layouts: 147 us -> none  [the longest x8 144 us: sweep(): return state.at[comp_low:comp_high].set(updated)]
    another operation x32 -> x0, loops' own time: 96.4 us -> none  [the longest x8 95.3 us: body(): state = lax.switch(sweep_order[sweep_round, turn], branches, state)]
    another operation x45 -> x6, local copies, waits for them, and re-layouts: 77.2 us -> 0.25 us  [the longest x2 0.08 us: body(): rate_lane = pad_to(jnp.tile(input_rate, quarter), 0, width)]
    ppermute x24 -> x7, starting transfers between devices: 67.5 us -> 15.9 us  [the longest x1 4.39 us: body(): lax.ppermute(summed[:, 2 * block:2 * block + HALO], axes, same_route)]
    add x26 -> x5, other arithmetic: 53.2 us -> 1.65 us  [the longest x1 0.7 us: body(): slot = owner * CAP + jnp.sum(earlier.astype(jnp.int32), axis=1)]
    mul x48 -> x0, local copies, waits for them, and re-layouts: 49 us -> none  [the longest x32 38.8 us: sweep(): along_x4 = dir_cos[:, None, None, None] * speeds[None]]
    ppermute x24 -> x7, waiting for transfers between devices: 51 us -> 3.33 us  [the longest x1 3.32 us: body(): got = lax.ppermute(send, axes, swap_route)]
    pallas_call x0 -> x2, Pallas kernels: none -> 36 us  [the longest x1 31.4 us: body(): pl.pallas_call(lambda *refs: sweeps_kernel(rows, own, cells, quad_size, *...]
  transfers between devices with their start and end apart: 26 -> 8, of which waited for: 9 -> 2; matrix products, arithmetic and copies ran while one was open for 22% -> 17% of each run, Pallas kernels for 0% -> 0%
where the time goes in v1:
time: 120 us; the launch traced here: 119 us
  Pallas kernels  36 us (30%)
  waiting for transfers between devices  34.6 us (29%)
  starting transfers between devices  20.7 us (17%)
  other arithmetic  17.4 us (14%)
  matrix products  5.45 us (5%)
  local copies, waits for them, and re-layouts  4.14 us (3%)
    pallas_call x1, Pallas kernels, body(): pl.pallas_call(lambda *refs: sweeps_kernel(rows, own, cells, quad_size, *...  31.4 us
    all_to_all x1, waiting for transfers between devices, body(): lax.all_to_all(outgoing.reshape(devices, CAP, load), axes, split_axis=0,...  31.2 us
    select_n x1, other arithmetic, by_class(): jnp.where((class_here == kind)[None, :, :, None], table[:, None, None, ki...  6.64 us
    all_to_all x1, starting transfers between devices, body(): lax.all_to_all(outgoing.reshape(devices, CAP, load), axes, split_axis=0,...  4.77 us
    pallas_call x1, Pallas kernels, body(): pl.pallas_call(lambda *refs: merge_kernel(own, *refs), grid_spec=pltpu.Pr...  4.63 us
    ppermute x1, starting transfers between devices, body(): lax.ppermute(summed[:, 2 * block:2 * block + HALO], axes, same_route)  4.39 us
    ppermute x1, starting transfers between devices, body(): beside_same = lax.ppermute(held, axes, same_route)  3.96 us
    mul x1, other arithmetic, body(): rate_lane[None, None, None] * strength[None, :, :, None] * (spread * spread)  3.73 us
  transfers between devices with their start and end apart: 8, of which 2 were waited for; matrix products, arithmetic and copies ran while one was open for 17% of the time, Pallas kernels for 0%

profile of v1, /device:TPU:17, one launch (start us, length us, event | category | flops | bytes accessed | tf_op | source)
XLA Modules:
  0.0 118.6 jit_solution(1175134630672791834)
XLA Ops:
  0.0 0.7 convert_bitcast_fusion
  0.7 0.7 pad_maximum_fusion.4
  1.4 3.7 %collective-permute-start.2 = (f32[3,8,128]{2,1,0:T(8,128)S(1)}, f32[3,8,128]{2,1,0:T(8,128)S(1)}, u32[]{:S(2)}, u32[]{:S(2)}) collective-permute-start(f32[3,8,128]{2,1,0:T(8,128)S(1)} %pad_maximum_fusion.4), channel_id=1, source_target_pairs={{16,1},{17,2},{18,3},{19,4},{20,5},{21,6},{22,7},{23,8},{24,9},{25... | collective-permute-start | bytes 36872 | tf_op jit(solution)/shard_map/ppermute | solution.py:209
  5.1 4.0 %collective-permute-start.1 = (f32[3,8,128]{2,1,0:T(8,128)S(1)}, f32[3,8,128]{2,1,0:T(8,128)S(1)}, u32[]{:S(2)}, u32[]{:S(2)}) collective-permute-start(f32[3,8,128]{2,1,0:T(8,128)S(1)} %pad_maximum_fusion.4), channel_id=1, source_target_pairs={{0,1},{1,2},{2,3},{3,4},{4,5},{5,6},{6,7},{7,8},{8,9},{9,10},{10,1... | collective-permute-start | bytes 36872 | tf_op jit(solution)/shard_map/ppermute | solution.py:208
  9.2 0.7 fusion.50
  9.9 0.2 convert_reduce_fusion
  10.0 0.7 multiply_add_fusion
  10.8 3.5 %fusion.3 = f32[512,896]{1,0:T(8,128)} fusion(f32[256,1]{0,1:T(1,128)S(1)} %bitcast.60, f32[256,864]{0,1:T(8,128)} %param.16, s32[256]{0:T(256)S(1)} %get-tuple-element.84), kind=kOutput, calls=%fused_computation.11 | convolution fusion | flops 1410334720 | bytes 2721792 | tf_op jit(solution)/shard_map/dot_general | solution.py:201
  14.2 4.8 %all-to-all-start = ((f32[32,16,896]{2,1,0:T(8,128)}), f32[32,16,896]{2,1,0:T(8,128)S(1)}, u32[]{:S(2)}, u32[]{:S(2)}) async-start(f32[32,16,896]{2,1,0:T(8,128)} %bitcast.52), calls=%async_computation | async-start | bytes 3670016 | tf_op jit(solution)/shard_map/all_to_all | solution.py:203
  19.2 0.1 broadcast_in_dim.213
  19.3 0.1 broadcast_in_dim.201
  19.7 1.5 %copy.17 = f32[4,216,216]{1,2,0:T(8,128)S(1)} copy(f32[4,216,216]{2,1,0:T(8,128)} %param.18) | data formatting | bytes 1492992 | tf_op args[8]
  21.2 0.1 fusion.2
  21.4 0.2 pad_maximum_fusion.refs_5_
  22.2 1.3 %broadcast_multiply_fusion = f32[16,72,256]{2,1,0:T(8,128)} fusion(f32[16,72]{1,0:T(8,128)S(1)} %get-tuple-element.48, f32[256]{0:T(256)S(1)} %pad.37), kind=kLoop, calls=%fused_computation.21 | loop fusion | flops 294912 | bytes 1185280 | tf_op jit(solution)/shard_map/mul | solution.py:247
  23.5 6.6 %select_select_fusion = (f32[4,16,72,256]{3,2,1,0:T(8,128)}, f32[4,16,72,256]{3,2,1,0:T(8,128)}, f32[4,16,72,256]{3,2,1,0:T(8,128)}) fusion(f32[4,256]{1,0:T(4,128)S(1)} %get-tuple-element.59, f32[4,256]{1,0:T(4,128)S(1)} %get-tuple-element.60, f32[4,256]{1,0:T(4,128)S(1)} %get-tuple-element.61, f32[4,256]{1,0:T(4,128)S(1)} %get-tuple-element.58, ...), kind=kLoop, calls=%fused_computation.1 | loop fusion | flops 10616832 | bytes 14208384 | tf_op jit(solution)/shard_map/jit(_where)/select_n | solution.py:238
  30.1 31.2 %all-to-all-done = f32[32,16,896]{2,1,0:T(8,128)S(1)} async-done(((f32[32,16,896]{2,1,0:T(8,128)}), f32[32,16,896]{2,1,0:T(8,128)S(1)}, u32[]{:S(2)}, u32[]{:S(2)}) %all-to-all-start) | async-done | bytes 1835040 | tf_op jit(solution)/shard_map/all_to_all | solution.py:203
  61.4 0.8 and_reduce_fusion.1
  62.2 0.5 subtract_reduce_fusion.1
  62.6 0.2 and_reduce_fusion.5
  62.9 0.2 and_reduce_fusion.6
  63.1 0.2 fusion.24
  63.4 2.0 %fusion = f32[176,864]{1,0:T(8,128)} fusion(f32[512,896]{1,0:T(8,128)S(1)} %bitcast.51, s32[512]{0:T(512)S(1)} %get-tuple-element.19, s32[512]{0:T(512)S(1)} %get-tuple-element.18, s32[512]{0:T(512)S(1)} %broadcast_add_fusion, s32[512]{0:T(512)S(1)} %get-tuple-element.25, pred[512]{0:T(512)(128)(4,1)S(1)} %get-tuple-element.36, ...), kind=kOutput, calls=%fused_computation.4 | convolution fusion | flops 935272448 | bytes 2453504 | tf_op jit(solution)/shard_map/dot_general | solution.py:277
  65.4 1.7 %reshape.251 = f32[176,4,216]{2,1,0:T(4,128)S(1)} reshape(f32[176,864]{1,0:T(8,128)} %fusion) | data formatting | bytes 1216512 | tf_op jit(solution)/shard_map/reshape | solution.py:279
  67.0 0.1 copy.20
  67.3 3.2 %collective-permute-start.5 = (f32[4,8,256]{2,1,0:T(8,128)S(1)}, f32[4,8,256]{2,1,0:T(8,128)S(1)}, u32[]{:S(2)}, u32[]{:S(2)}) collective-permute-start(f32[4,8,256]{2,1,0:T(8,128)S(1)} %get-tuple-element.42), channel_id=1, source_target_pairs={{16,1},{17,2},{18,3},{19,4},{20,5},{21,6},{22,7},{23,8},{24,9},{25... | collective-permute-start | bytes 98312 | tf_op jit(solution)/shard_map/ppermute | solution.py:284
  70.5 4.4 %collective-permute-start.4 = (f32[4,8,256]{2,1,0:T(8,128)S(1)}, f32[4,8,256]{2,1,0:T(8,128)S(1)}, u32[]{:S(2)}, u32[]{:S(2)}) collective-permute-start(f32[4,8,256]{2,1,0:T(8,128)S(1)} %get-tuple-element.43), channel_id=1, source_target_pairs={{0,1},{1,2},{2,3},{3,4},{4,5},{5,6},{6,7},{7,8},{8,9},{9,10},{10,1... | collective-permute-start | bytes 98312 | tf_op jit(solution)/shard_map/ppermute | solution.py:283
  74.9 3.7 %multiply_multiply_fusion.refs_4_ = f32[4,16,72,256]{3,2,1,0:T(8,128)} fusion(f32[4,256]{1,0:T(4,128)S(1)} %get-tuple-element.83, f32[16,72]{1,0:T(8,128)S(1)} %get-tuple-element.49, f32[4,256]{1,0:T(4,128)S(1)} %get-tuple-element.76, f32[16,72]{1,0:T(8,128)S(1)} %get-tuple-element.50, f32[16,72,256]{2,1,0:T(8,128)} %broadcast_multiply_fusion), kind=kLoop, calls=%fused_computation | loop fusion | flops 7077888 | bytes 5915648 | tf_op jit(solution)/shard_map/mul | solution.py:247
  78.7 31.4 %shard_map.100 = (f32[2,216,8,128]{3,2,1,0:T(8,128)S(1)}, f32[2,216,8,128]{3,2,1,0:T(8,128)S(1)}) custom-call(s32[9]{0:T(128)S(1)} %pad_add_fusion.refs_0_, f32[4,16,72,256]{3,2,1,0:T(8,128)} %get-tuple-element.75.refs_1_, f32[4,16,72,256]{3,2,1,0:T(8,128)} %get-tuple-element.74.refs_2_, f32[4,16,72,256]{3,2,1,0:T(8,128)} %get-tuple-element.73.refs_3_, ...), custom_call_target="tpu_custom_call" | custom-call | tf_op jit(solution)/shard_map/pallas_call | solution.py:295
  110.1 0.5 collective-permute-start.6
  110.6 3.3 %collective-permute-done.6.refs_2_ = f32[2,216,8,128]{3,2,1,0:T(8,128)S(1)} collective-permute-done((f32[2,216,8,128]{3,2,1,0:T(8,128)S(1)}, f32[2,216,8,128]{3,2,1,0:T(8,128)S(1)}, u32[]{:S(2)}, u32[]{:S(2)}) %collective-permute-start.6) | collective-permute-done | bytes 1769504 | tf_op jit(solution)/shard_map/ppermute | solution.py:317
  113.9 4.6 %shard_map.101 = f32[2,2,216,8,128]{4,3,2,1,0:T(8,128)} custom-call(s32[9]{0:T(128)S(1)} %pad_add_fusion.refs_0_, f32[2,216,8,128]{3,2,1,0:T(8,128)S(1)} %get-tuple-element.7.refs_1_, f32[2,216,8,128]{3,2,1,0:T(8,128)S(1)} %collective-permute-done.6.refs_2_), custom_call_target="tpu_custom_call" | custom-call | tf_op jit(solution)/shard_map/pallas_call | solution.py:321
  (53 shorter events, 1.3 us)
Async XLA Ops:
  0.0 19.4 %copy-start.5 = (s32[2,4]{1,0:T(2,128)S(1)}, s32[2,4]{1,0:T(2,128)}, u32[]{:S(2)}) copy-start(s32[2,4]{1,0:T(2,128)} %param.19) | copy-start | bytes 100
  0.0 19.5 %copy-start.2 = (f32[4,24]{1,0:T(4,128)S(1)}, f32[4,24]{1,0:T(4,128)}, u32[]{:S(2)}) copy-start(f32[4,24]{1,0:T(4,128)} %param.13) | copy-start | bytes 1156
  0.0 19.6 %copy-start.3 = (f32[4,24]{1,0:T(4,128)S(1)}, f32[4,24]{1,0:T(4,128)}, u32[]{:S(2)}) copy-start(f32[4,24]{1,0:T(4,128)} %param.14) | copy-start | bytes 1156
  1.4 20.5 %collective-permute-start.2 = (f32[3,8,128]{2,1,0:T(8,128)S(1)}, f32[3,8,128]{2,1,0:T(8,128)S(1)}, u32[]{:S(2)}, u32[]{:S(2)}) collective-permute-start(f32[3,8,128]{2,1,0:T(8,128)S(1)} %pad_maximum_fusion.4), channel_id=1, source_target_pairs={{16,1},{17,2},{18,3},{19,4},{20,5},{21,6},{22,7},{23,8},{24,9},{25... | collective-permute-start | bytes 36872 | tf_op jit(solution)/shard_map/ppermute | solution.py:209
  5.1 16.9 %collective-permute-start.1 = (f32[3,8,128]{2,1,0:T(8,128)S(1)}, f32[3,8,128]{2,1,0:T(8,128)S(1)}, u32[]{:S(2)}, u32[]{:S(2)}) collective-permute-start(f32[3,8,128]{2,1,0:T(8,128)S(1)} %pad_maximum_fusion.4), channel_id=1, source_target_pairs={{0,1},{1,2},{2,3},{3,4},{4,5},{5,6},{6,7},{7,8},{8,9},{9,10},{10,1... | collective-permute-start | bytes 36872 | tf_op jit(solution)/shard_map/ppermute | solution.py:208
  9.1 12.8 %collective-permute-start = (f32[3,8,128]{2,1,0:T(8,128)S(1)}, f32[3,8,128]{2,1,0:T(8,128)S(1)}, u32[]{:S(2)}, u32[]{:S(2)}) collective-permute-start(f32[3,8,128]{2,1,0:T(8,128)S(1)} %pad_maximum_fusion.4), channel_id=1, source_target_pairs={{16,0},{17,1},{18,2},{19,3},{20,4},{21,5},{22,6},{23,7},{24,8},{25... | collective-permute-start | bytes 36872 | tf_op jit(solution)/shard_map/ppermute | solution.py:207
  14.2 7.5 %copy-start.4 = (f32[24]{0:T(128)S(1)}, f32[24]{0:T(128)}, u32[]{:S(2)}) copy-start(f32[24]{0:T(128)} %param.15) | copy-start | bytes 292
  14.2 7.7 %copy-start = (f32[8,128]{1,0:T(8,128)S(1)}, f32[8,128]{1,0:T(8,128)}, u32[]{:S(2)}) copy-start(f32[8,128]{1,0:T(8,128)} %param.11) | copy-start | bytes 12292
  14.2 7.7 %copy-start.1 = (f32[8,128]{1,0:T(8,128)S(1)}, f32[8,128]{1,0:T(8,128)}, u32[]{:S(2)}) copy-start(f32[8,128]{1,0:T(8,128)} %param.10) | copy-start | bytes 12292
  14.2 47.2 %all-to-all-start = ((f32[32,16,896]{2,1,0:T(8,128)}), f32[32,16,896]{2,1,0:T(8,128)S(1)}, u32[]{:S(2)}, u32[]{:S(2)}) async-start(f32[32,16,896]{2,1,0:T(8,128)} %bitcast.52), calls=%async_computation | async-start | bytes 3670016 | tf_op jit(solution)/shard_map/all_to_all | solution.py:203
  67.3 11.4 %collective-permute-start.5 = (f32[4,8,256]{2,1,0:T(8,128)S(1)}, f32[4,8,256]{2,1,0:T(8,128)S(1)}, u32[]{:S(2)}, u32[]{:S(2)}) collective-permute-start(f32[4,8,256]{2,1,0:T(8,128)S(1)} %get-tuple-element.42), channel_id=1, source_target_pairs={{16,1},{17,2},{18,3},{19,4},{20,5},{21,6},{22,7},{23,8},{24,9},{25... | collective-permute-start | bytes 98312 | tf_op jit(solution)/shard_map/ppermute | solution.py:284
  70.5 8.2 %collective-permute-start.4 = (f32[4,8,256]{2,1,0:T(8,128)S(1)}, f32[4,8,256]{2,1,0:T(8,128)S(1)}, u32[]{:S(2)}, u32[]{:S(2)}) collective-permute-start(f32[4,8,256]{2,1,0:T(8,128)S(1)} %get-tuple-element.43), channel_id=1, source_target_pairs={{0,1},{1,2},{2,3},{3,4},{4,5},{5,6},{6,7},{7,8},{8,9},{9,10},{10,1... | collective-permute-start | bytes 98312 | tf_op jit(solution)/shard_map/ppermute | solution.py:283
  74.9 3.8 %collective-permute-start.3 = (f32[4,80,256]{2,1,0:T(8,128)S(1)}, f32[4,80,256]{2,1,0:T(8,128)S(1)}, u32[]{:S(2)}, u32[]{:S(2)}) collective-permute-start(f32[4,80,256]{2,1,0:T(8,128)S(1)} %get-tuple-element.44), channel_id=1, source_target_pairs={{16,0},{17,1},{18,2},{19,3},{20,4},{21,5},{22,6},{23,7},{24,8},{25... | collective-permute-start | bytes 983048 | tf_op jit(solution)/shard_map/ppermute | solution.py:282
  110.1 3.9 %collective-permute-start.6 = (f32[2,216,8,128]{3,2,1,0:T(8,128)S(1)}, f32[2,216,8,128]{3,2,1,0:T(8,128)S(1)}, u32[]{:S(2)}, u32[]{:S(2)}) collective-permute-start(f32[2,216,8,128]{3,2,1,0:T(8,128)S(1)} %get-tuple-element.8), channel_id=1, source_target_pairs={{16,0},{17,1},{18,2},{19,3},{20,4},{21,5},{22,6},{23,7},{24,8},{25... | collective-permute-start | bytes 5308424 | tf_op jit(solution)/shard_map/ppermute | solution.py:317

commit v2 on v1

--- a/solution.py
+++ b/solution.py
@@ -34,6 +34,83 @@
     widths = [(0, 0)] * array.ndim
     widths[axis] = (0, size - array.shape[axis])
     return jnp.pad(array, widths, constant_values=value)
+
+
+def pack_kernel(shifts, col_count, rows, comps, dest_ref, spectra_ref, out_ref, high, low, slots):
+    step = pl.program_id(0)
+    points = dest_ref.shape[1]
+    load = out_ref.shape[1]
+    total_bits, row_bits, col_bits = shifts
+
+    @pl.when(step == 0)
+    def _():
+        dest = dest_ref[...]
+        grid_row = lax.shift_right_logical(dest, total_bits)
+        grid_col = dest & (2**total_bits - 1)
+        local_row = grid_row & (2**row_bits - 1)
+        local_col = grid_col & (2**col_bits - 1)
+        owner = (lax.shift_right_logical(grid_row, row_bits) * col_count
+                 + lax.shift_right_logical(grid_col, col_bits))
+        on_row = (grid_row == 0) | (grid_row == rows - 1)
+        on_left = jnp.where(grid_col == 0, 2**col_bits, 2**col_bits + 2**row_bits) + local_row
+        code = jnp.where(on_row, local_col, on_left) + 1
+        lanes = jnp.concatenate(
+            [owner.astype(jnp.float32), code.astype(jnp.float32), jnp.zeros((6, points), jnp.float32)],
+            axis=0)
+        columns = lanes.T
+        same = columns[:, 0:1] == lanes[0:1]
+        above = (lax.broadcasted_iota(jnp.int32, (points, points), 0)
+                 < lax.broadcasted_iota(jnp.int32, (points, points), 1))
+        rank = jnp.sum(jnp.where(same & above, 1.0, 0.0), axis=0, keepdims=True)
+        slots[...] = owner * CAP + rank.astype(jnp.int32)
+        spectra = jnp.concatenate(
+            [spectra_ref[...], jnp.broadcast_to(columns[:, 1:2], (points, load - comps))], axis=1)
+        high[...], low[...] = split_bf16(spectra)
+
+    place = jnp.where(
+        lax.broadcasted_iota(jnp.int32, (out_ref.shape[0], points), 0) + step * out_ref.shape[0]
+        == slots[...], 1.0, 0.0).astype(jnp.bfloat16)
+    out_ref[...] = (jnp.dot(place, high[...], preferred_element_type=jnp.float32)
+                    + jnp.dot(place, low[...], preferred_element_type=jnp.float32))
+
+
+def rim_kernel(own, rows_dev, comps, quad_size, info, arrived_ref, own_ref, send_ref, same_ref,
+               cross_ref):
+    half = info[ITERS * QUADS]
+    cols_dev = 2 * own
+    cells = own + HALO
+    block = cells + rows_dev
+    width = own_ref.shape[2]
+    load = arrived_ref.shape[1]
+    spots = -(-(2 * block + 2 * HALO) // LANES) * LANES
+    lane = lax.broadcasted_iota(jnp.int32, (1, spots), 1)
+    at_send = lane >= block
+    spot = jnp.where(at_send, lane - block, lane)
+    side_at = jnp.where(at_send, 1 - half, half)
+    want = jnp.where(spot < own, own * side_at + spot, -1)
+    want = jnp.where((spot == own) & (side_at == 0), own, want)
+    want = jnp.where((spot == cells - 1) & (side_at == 1), own - 1, want)
+    want = jnp.where(spot >= cells, cols_dev + rows_dev * side_at + spot - cells, want)
+    rest = lane - 2 * block
+    to_left = jnp.where((rest == HALO - 1) & (half == 0), cols_dev - 1, -1)
+    to_left = jnp.where((rest == 0) & (half == 1), 0, to_left)
+    to_left = jnp.where((rest == HALO) & (half == 0), 0, to_left)
+    to_left = jnp.where((rest == 2 * HALO - 1) & (half == 1), cols_dev - 1, to_left)
+    want = jnp.where(rest >= 0, to_left, want)
+    code = arrived_ref[:, comps:comps + 1]
+    gather = jnp.where(code == (want + 1).astype(jnp.float32), 1.0, 0.0)
+    gather = jnp.where(want >= 0, gather, 0.0).astype(jnp.bfloat16)
+    high, low = split_bf16(arrived_ref[...])
+    over_points = (((0,), (0,)), ((), ()))
+    summed = (lax.dot_general(gather, high, over_points, preferred_element_type=jnp.float32)
+              + lax.dot_general(gather, low, over_points, preferred_element_type=jnp.float32))
+    for quad in range(QUADS):
+        start = quad * quad_size
+        part = summed if quad == 0 else pltpu.roll(summed, load - start, 1)
+        own_ref[quad] = part[:block, :width]
+        send_ref[quad] = part[block:2 * block, :width]
+        same_ref[quad] = part[2 * block:2 * block + HALO, :width]
+        cross_ref[quad] = part[2 * block + HALO:2 * block + 2 * HALO, :width]
 
 
 def sweeps_kernel(rows, own, cells, quad_size, info, ax_ref, ay_ref, base_ref, wind_ref, mt_ref,
@@ -66,48 +143,55 @@
         side[j + rows_dev * (1 - half)] = theirs
 
     def run(count, second):
-        def factors(i):
+        chains = [(0, own // 2), (own // 2, count)]
+
+        def factors(i, low, high):
             row = first_row + i * step_x
-            total = power[0, row, :count]
+            total = power[0, row, low:high]
             for other in range(1, QUADS):
-                total = total + power[other, row, :count]
+                total = total + power[other, row, low:high]
             level = total * (1.0 / (QUADS * quad_size))
             damping = whitecap_rate * level / (1.0 + level)
-            den = base_ref[0, row, :count] + jnp.concatenate([damping] * (width // LANES), axis=1)
+            den = base_ref[0, row, low:high] + jnp.concatenate([damping] * (width // LANES), axis=1)
             inverse = 1.0 / den
-            source = wind_ref[0, row, :count]
-            edge = side[row]
-            parts = [source[:HALO] + edge[:HALO], source[HALO:own - HALO],
-                     source[own - HALO:own] + edge[HALO:]]
-            if count > own:
-                parts.append(source[own:])
-            source = jnp.concatenate(parts, axis=0)
+            source = wind_ref[0, row, low:high]
+            if low == 0:
+                source = jnp.concatenate([source[:HALO] + side[row, :HALO], source[HALO:]], axis=0)
+            else:
+                last = own - HALO - low
+                parts = [source[:last], source[last:own - low] + side[row, HALO:]]
+                if high > own:
+                    parts.append(source[own - low:])
+                source = jnp.concatenate(parts, axis=0)
             if i == 0 or i == rows - 1:
                 here = jnp.where(row // rows_dev == half, 0, 1)
-                source = source + rim[here, :count]
+                source = source + rim[here, low:high]
             if second:
                 before = state[quad, row]
                 shifted = jnp.where(up_y, pltpu.roll(before, 1, 0), pltpu.roll(before, cells - 1, 0))
-                source = source + ay_ref[0, row, :count] * shifted[:count]
-            return row, ax_ref[0, row, :count] * inverse, source * inverse
-
-        row, along, known = factors(0)
-        upwind = None
+                source = source + ay_ref[0, row, low:high] * shifted[low:high]
+            return ax_ref[0, row, low:high] * inverse, source * inverse
+
+        ready = [factors(0, *chain) for chain in chains]
+        upwind = [None] * len(chains)
         for i in range(rows):
-            balance = known if upwind is None else along * upwind + known
-            high, low = split_bf16(balance)
-            updated = jnp.dot(jnp.concatenate([high, high, low], axis=1), mt_ref[0],
-                              preferred_element_type=jnp.float32)
-            here = row
+            updated = []
+            for (along, known), before in zip(ready, upwind):
+                balance = known if before is None else along * before + known
+                high, low = split_bf16(balance)
+                updated.append(jnp.dot(jnp.concatenate([high, high, low], axis=1), mt_ref[0],
+                                       preferred_element_type=jnp.float32))
             if i + 1 < rows:
-                row, along, known = factors(i + 1)
-            square = updated * updated
-            folded = square[:, :LANES]
-            for lane in range(LANES, width, LANES):
-                folded = folded + square[:, lane:lane + LANES]
-            state[quad, here, :count] = updated
-            power[quad, here, :count] = jnp.broadcast_to(
-                jnp.sum(folded, axis=1, keepdims=True), (count, LANES))
+                ready = [factors(i + 1, *chain) for chain in chains]
+            row = first_row + i * step_x
+            for (start, stop), value in zip(chains, updated):
+                square = value * value
+                folded = square[:, :LANES]
+                for lane in range(LANES, width, LANES):
+                    folded = folded + square[:, lane:lane + LANES]
+                state[quad, row, start:stop] = value
+                power[quad, row, start:stop] = jnp.broadcast_to(
+                    jnp.sum(folded, axis=1, keepdims=True), (stop - start, LANES))
             upwind = updated
 
     @pl.when(turn < QUADS)
@@ -180,30 +264,31 @@
     cross_route += [(device(0, c + 1), device(1, c)) for c in span if c + 1 < col_count]
 
     points = dest_cell.shape[0]
-    total_cols = cols_dev * col_count
-    grid_row = dest_cell // total_cols
-    grid_col = dest_cell % total_cols
-    owner = grid_row // rows_dev * col_count + grid_col // cols_dev
-    local_row = grid_row % rows_dev
-    local_col = grid_col % cols_dev
-    rim_code = jnp.where(
-        (grid_row == 0) | (grid_row == rows - 1),
-        local_col,
-        jnp.where(grid_col == 0, cols_dev + local_row, cols_dev + rows_dev + local_row),
-    )
-    position = jnp.arange(points, dtype=jnp.int32)
-    earlier = (owner[:, None] == owner[None, :]) & (position[:, None] > position[None, :])
-    slot = owner * CAP + jnp.sum(earlier.astype(jnp.int32), axis=1)
     load = -(-(comps + 1) // LANES) * LANES
-    payload = pad_to(
-        jnp.concatenate([outer_spectra, (rim_code + 1).astype(jnp.float32)[:, None]], axis=1), 1, load)
-    place = (jnp.arange(devices * CAP, dtype=jnp.int32)[:, None] == slot[None, :]).astype(jnp.float32)
-    outgoing = jnp.dot(place, payload, precision=lax.Precision.HIGHEST,
-                       preferred_element_type=jnp.float32)
+    sizes = (cols_dev * col_count, rows_dev, cols_dev)
+    shifts = tuple(size.bit_length() - 1 for size in sizes)
+    assert all(size == 2**shift for size, shift in zip(sizes, shifts))
+    slot_total = devices * CAP
+    steps = 4
+    outgoing = pl.pallas_call(
+        lambda *refs: pack_kernel(shifts, col_count, rows, comps, *refs),
+        grid=(steps,),
+        in_specs=[pl.BlockSpec((1, points), lambda s: (0, 0)),
+                  pl.BlockSpec((points, comps), lambda s: (0, 0))],
+        out_specs=pl.BlockSpec((slot_total // steps, load), lambda s: (s, 0)),
+        scratch_shapes=[pltpu.VMEM((points, load), jnp.bfloat16),
+                        pltpu.VMEM((points, load), jnp.bfloat16),
+                        pltpu.VMEM((1, points), jnp.int32)],
+        out_shape=jax.ShapeDtypeStruct((slot_total, load), jnp.float32),
+        compiler_params=pltpu.CompilerParams(
+            dimension_semantics=("arbitrary",), vmem_limit_bytes=48 * 2**20),
+    )(dest_cell.reshape(1, points), outer_spectra)
+    held = jnp.stack([wind_speed, wind_dir, depth_class.astype(jnp.float32)])
+    outgoing, held, refraction_inverse = lax.optimization_barrier(
+        (outgoing, held, refraction_inverse))
     arrived = lax.all_to_all(outgoing.reshape(devices, CAP, load), axes, split_axis=0,
-                             concat_axis=0, tiled=True).reshape(devices * CAP, load)
-
-    held = jnp.stack([wind_speed, wind_dir, depth_class.astype(jnp.float32)])
+                             concat_axis=0, tiled=True).reshape(slot_total, load)
+
     partner = lax.ppermute(held, axes, swap_route)
     beside_same = lax.ppermute(held, axes, same_route)
     beside_cross = lax.ppermute(held, axes, cross_route)
@@ -250,40 +335,28 @@
     flip_high, flip_low = split_rounded(flipped)
     matrices = jnp.concatenate([flip_high, flip_low, flip_high], axis=1)
 
-    code = arrived[:, comps].astype(jnp.int32) - 1
-
-    def place_in(side_at):
-        col = code - own * side_at
-        spot = jnp.where((code < cols_dev) & (code >= 0) & (col >= 0) & (col < own), col, -1)
-        spot = jnp.where((side_at == 0) & (code == own), own, spot)
-        spot = jnp.where((side_at == 1) & (code == own - 1), cells - 1, spot)
-        along = code - cols_dev - rows_dev * side_at
-        return jnp.where((along >= 0) & (along < rows_dev) & (code >= cols_dev), cells + along, spot)
-
+    arrived, ax, ay, base, wind, matrices = lax.optimization_barrier(
+        (arrived, ax, ay, base, wind, matrices))
+
+    info = jnp.concatenate([sweep_order.reshape(-1), half[None].astype(jnp.int32)])
     block = cells + rows_dev
-    slots = jnp.arange(2 * block + 2 * HALO, dtype=jnp.int32)[:, None]
-    to_own = place_in(half)[None, :]
-    to_partner = place_in(1 - half)[None, :]
-    out_right = code[None, :] == cols_dev - 1
-    out_left = code[None, :] == 0
-    to_same = jnp.where(is_low, jnp.where(out_right, HALO - 1, -1), jnp.where(out_left, 0, -1))
-    to_cross = jnp.where(is_low, jnp.where(out_left, 0, -1), jnp.where(out_right, HALO - 1, -1))
-    gather = (
-        ((slots == to_own) & (to_own >= 0))
-        | ((slots == to_partner + block) & (to_partner >= 0))
-        | ((slots == to_same + 2 * block) & (to_same >= 0))
-        | ((slots == to_cross + 2 * block + HALO) & (to_cross >= 0))
-    ).astype(jnp.float32)
-    summed = jnp.dot(gather, arrived, precision=lax.Precision.HIGHEST,
-                     preferred_element_type=jnp.float32)[:, :comps]
-    summed = jnp.swapaxes(summed.reshape(-1, QUADS, quad_size), 0, 1)
-    summed = pad_to(summed, 2, width)
-    rim_own = summed[:, :block]
-    rim_partner = lax.ppermute(summed[:, block:2 * block], axes, swap_route)
-    rim_same = lax.ppermute(summed[:, 2 * block:2 * block + HALO], axes, same_route)
-    rim_cross = lax.ppermute(summed[:, 2 * block + HALO:], axes, cross_route)
-
-    info = jnp.concatenate([sweep_order.reshape(-1), half[None].astype(jnp.int32)])
+    rim_shapes = [jax.ShapeDtypeStruct((QUADS, size, width), jnp.float32)
+                  for size in (block, block, HALO, HALO)]
+    rim_own, rim_send, out_same, out_cross = pl.pallas_call(
+        lambda *refs: rim_kernel(own, rows_dev, comps, quad_size, *refs),
+        grid_spec=pltpu.PrefetchScalarGridSpec(
+            num_scalar_prefetch=1,
+            grid=(1,),
+            in_specs=[pl.BlockSpec((slot_total, load), lambda s, info: (0, 0))],
+            out_specs=[pl.BlockSpec(shape.shape, lambda s, info: (0, 0, 0)) for shape in rim_shapes],
+        ),
+        out_shape=rim_shapes,
+        compiler_params=pltpu.CompilerParams(vmem_limit_bytes=48 * 2**20),
+    )(info, arrived)
+    rim_partner = lax.ppermute(rim_send, axes, swap_route)
+    rim_same = lax.ppermute(out_same, axes, same_route)
+    rim_cross = lax.ppermute(out_cross, axes, cross_route)
+
     turns = ITERS * QUADS
 
     def quad_block(shape):

time: 120 us -> 116 us (0.967)
  Pallas kernels: 36 us -> 42.5 us
  matrix products: 5.45 us -> 0 us
  other arithmetic: 17.4 us -> 14.1 us
  waiting for transfers between devices: 34.6 us -> 32 us
    dot_general x2 -> x0, matrix products: 5.45 us -> none  [the longest x1 3.46 us: body(): jnp.dot(place, payload, precision=lax.Precision.HIGHEST, preferred_elemen...]
    pallas_call x0 -> x2, Pallas kernels: none -> 4.47 us  [the longest x1 2.98 us: body(): pl.pallas_call(lambda *refs: pack_kernel(shifts, col_count, rows, comps,...]
    all_to_all x1, waiting for transfers between devices: 31.2 us -> 27.3 us  [body(): lax.all_to_all(outgoing.reshape(devices, CAP, load), axes, split_axis=0,...]
    ppermute x1, starting transfers between devices: 0.55 us -> 2.84 us  [body(): got = lax.ppermute(send, axes, swap_route)]
    pallas_call x1, Pallas kernels: 31.4 us -> 33.4 us  [body(): pl.pallas_call(lambda *refs: sweeps_kernel(rows, own, cells, quad_size, *...]
    reshape x2 -> x0, local copies, waits for them, and re-layouts: 1.82 us -> none  [body(): summed = jnp.swapaxes(summed.reshape(-1, QUADS, quad_size), 0, 1)]
    add x4 -> x0, other arithmetic: 1.64 us -> none  [the longest x1 0.7 us: body(): slot = owner * CAP + jnp.sum(earlier.astype(jnp.int32), axis=1)]
    optimization_barrier x0 -> x1, local copies, waits for them, and re-layouts: none -> 1.49 us  [body(): lax.optimization_barrier((outgoing, held, refraction_inverse))]
  transfers between devices with their start and end apart: 8 -> 8, of which waited for: 2 -> 3; matrix products, arithmetic and copies ran while one was open for 17% -> 13% of each run, Pallas kernels for 0% -> 0%
where the time goes in v2:
time: 116 us; the launch traced here: 115 us
  Pallas kernels  42.5 us (37%)
  waiting for transfers between devices  32 us (28%)
  starting transfers between devices  21.6 us (19%)
  other arithmetic  14.1 us (12%)
  local copies, waits for them, and re-layouts  4.4 us (4%)
    pallas_call x1, Pallas kernels, body(): pl.pallas_call(lambda *refs: sweeps_kernel(rows, own, cells, quad_size, *...  33.4 us
    all_to_all x1, waiting for transfers between devices, body(): lax.all_to_all(outgoing.reshape(devices, CAP, load), axes, split_axis=0,...  27.3 us
    select_n x1, other arithmetic, by_class(): jnp.where((class_here == kind)[None, :, :, None], table[:, None, None, ki...  6.67 us
    all_to_all x1, starting transfers between devices, body(): lax.all_to_all(outgoing.reshape(devices, CAP, load), axes, split_axis=0,...  5.11 us
    pallas_call x1, Pallas kernels, body(): pl.pallas_call(lambda *refs: merge_kernel(own, *refs), grid_spec=pltpu.Pr...  4.63 us
    ppermute x1, starting transfers between devices, body(): rim_cross = lax.ppermute(out_cross, axes, cross_route)  4.13 us
    ppermute x1, starting transfers between devices, body(): beside_same = lax.ppermute(held, axes, same_route)  3.95 us
    ppermute x1, waiting for transfers between devices, body(): got = lax.ppermute(send, axes, swap_route)  3.32 us
  transfers between devices with their start and end apart: 8, of which 3 were waited for; matrix products, arithmetic and copies ran while one was open for 13% of the time, Pallas kernels for 0%

profile of v2, /device:TPU:17, one launch (start us, length us, event | category | flops | bytes accessed | tf_op | source)
XLA Modules:
  0.0 114.9 jit_solution(15701454849715454413)
XLA Ops:
  0.0 0.7 convert_bitcast_fusion
  0.7 1.5 %copy.13.refs_1_ = f32[256,864]{1,0:T(8,128)S(1)} copy(f32[256,864]{0,1:T(8,128)} %param.16) | data formatting | bytes 1769472 | tf_op args[6]
  2.2 0.7 copy-done
  2.9 3.0 %shard_map.100 = f32[512,896]{1,0:T(8,128)} custom-call(s32[1,256]{1,0:T(1,128)S(1)} %bitcast.47, f32[256,864]{1,0:T(8,128)S(1)} %copy.13.refs_1_), custom_call_target="tpu_custom_call" | custom-call | tf_op jit(solution)/shard_map/pallas_call | solution.py:273
  5.9 0.7 pad_maximum_fusion.4
  6.6 3.9 %collective-permute-start.1 = (f32[3,8,128]{2,1,0:T(8,128)S(1)}, f32[3,8,128]{2,1,0:T(8,128)S(1)}, u32[]{:S(2)}, u32[]{:S(2)}) collective-permute-start(f32[3,8,128]{2,1,0:T(8,128)S(1)} %pad_maximum_fusion.4), channel_id=1, source_target_pairs={{0,1},{1,2},{2,3},{3,4},{4,5},{5,6},{6,7},{7,8},{8,9},{9,10},{10,1... | collective-permute-start | bytes 36872 | tf_op jit(solution)/shard_map/ppermute | solution.py:293
  10.5 3.1 %collective-permute-start.2 = (f32[3,8,128]{2,1,0:T(8,128)S(1)}, f32[3,8,128]{2,1,0:T(8,128)S(1)}, u32[]{:S(2)}, u32[]{:S(2)}) collective-permute-start(f32[3,8,128]{2,1,0:T(8,128)S(1)} %pad_maximum_fusion.4), channel_id=1, source_target_pairs={{16,1},{17,2},{18,3},{19,4},{20,5},{21,6},{22,7},{23,8},{24,9},{25... | collective-permute-start | bytes 36872 | tf_op jit(solution)/shard_map/ppermute | solution.py:294
  13.7 5.1 %all-to-all-start = ((f32[32,16,896]{2,1,0:T(8,128)}), f32[32,16,896]{2,1,0:T(8,128)S(1)}, u32[]{:S(2)}, u32[]{:S(2)}) async-start(f32[32,16,896]{2,1,0:T(8,128)} %bitcast.5), calls=%async_computation | async-start | bytes 3670016 | tf_op jit(solution)/shard_map/all_to_all | solution.py:289
  19.0 0.1 broadcast_in_dim.177
  19.2 0.1 broadcast_in_dim.165
  19.3 0.1 tile.13
  19.5 1.5 %copy.14 = f32[4,216,216]{1,2,0:T(8,128)S(1)} copy(f32[4,216,216]{2,1,0:T(8,128)} %param.18) | data formatting | bytes 1492992 | tf_op jit(solution)/shard_map/optimization_barrier | solution.py:287
  21.0 1.2 %fusion = (bf16[4,256,256]{2,1,0:T(8,128)(2,1)}, bf16[4,256,256]{2,1,0:T(8,128)(2,1)}) fusion(f32[4,216,216]{2,1,0:T(8,128)S(1)} %bitcast.48), kind=kLoop, calls=%fused_computation.7 | loop fusion | flops 1048576 | bytes 1795072 | tf_op jit(solution)/shard_map/convert_element_type | solution.py:30
  22.2 0.1 reshape.97
  22.3 1.5 %pad_maximum_fusion.refs_5_ = bf16[4,768,256]{2,1,0:T(8,128)(2,1)S(1)} fusion(bf16[4,256,256]{2,1,0:T(8,128)(2,1)} %get-tuple-element.36, bf16[4,256,256]{2,1,0:T(8,128)(2,1)} %get-tuple-element.35), kind=kLoop, calls=%fused_computation.4 | loop fusion | flops 4718592 | bytes 2621440 | tf_op jit(solution)/shard_map/concatenate | solution.py:336
  23.8 0.1 pad_add_fusion.refs_0_
  23.9 0.1 tile.32
  24.2 0.1 fusion.2
  24.3 0.1 pad_maximum_fusion.3
  24.4 0.2 broadcast_multiply_fusion
  24.6 2.7 %multiply_multiply_fusion.refs_4_ = f32[4,16,72,256]{3,2,1,0:T(8,128)} fusion(f32[4,256]{1,0:T(4,128)S(1)} %get-tuple-element.72, f32[16,72]{1,0:T(8,128)S(1)} %get-tuple-element.40, f32[4,256]{1,0:T(4,128)S(1)} %get-tuple-element.67, f32[16,72]{1,0:T(8,128)S(1)} %get-tuple-element.41, f32[16,72,256]{2,1,0:T(8,128)S(1)} %broadcast_multiply_fusion), kind=kLoop, calls=%fused_computation | loop fusion | flops 7077888 | bytes 5915648 | tf_op jit(solution)/shard_map/mul | solution.py:332
  27.3 6.7 %select_select_fusion = (f32[4,16,72,256]{3,2,1,0:T(8,128)}, f32[4,16,72,256]{3,2,1,0:T(8,128)}, f32[4,16,72,256]{3,2,1,0:T(8,128)}) fusion(f32[4,256]{1,0:T(4,128)S(1)} %get-tuple-element.50, f32[4,256]{1,0:T(4,128)S(1)} %get-tuple-element.51, f32[4,256]{1,0:T(4,128)S(1)} %get-tuple-element.52, f32[4,256]{1,0:T(4,128)S(1)} %get-tuple-element.49, ...), kind=kLoop, calls=%fused_computation.1 | loop fusion | flops 10616832 | bytes 14208384 | tf_op jit(solution)/shard_map/jit(_where)/select_n | solution.py:323
  34.0 27.3 %all-to-all-done = f32[32,16,896]{2,1,0:T(8,128)S(1)} async-done(((f32[32,16,896]{2,1,0:T(8,128)}), f32[32,16,896]{2,1,0:T(8,128)S(1)}, u32[]{:S(2)}, u32[]{:S(2)}) %all-to-all-start) | async-done | bytes 1835040 | tf_op jit(solution)/shard_map/all_to_all | solution.py:289
  61.2 1.5 %shard_map.101 = (f32[4,80,256]{2,1,0:T(8,128)S(1)}, f32[4,80,256]{2,1,0:T(8,128)S(1)}, f32[4,8,256]{2,1,0:T(8,128)S(1)}, f32[4,8,256]{2,1,0:T(8,128)S(1)}) custom-call(s32[9]{0:T(128)S(1)} %pad_add_fusion.refs_0_, f32[512,896]{1,0:T(8,128)S(1)} %bitcast.46), custom_call_target="tpu_custom_call" | custom-call | tf_op jit(solution)/shard_map/pallas_call | solution.py:345
  62.7 0.5 collective-permute-start.3
  63.2 1.9 %collective-permute-start.4 = (f32[4,8,256]{2,1,0:T(8,128)S(1)}, f32[4,8,256]{2,1,0:T(8,128)S(1)}, u32[]{:S(2)}, u32[]{:S(2)}) collective-permute-start(f32[4,8,256]{2,1,0:T(8,128)S(1)} %get-tuple-element.31), channel_id=1, source_target_pairs={{0,1},{1,2},{2,3},{3,4},{4,5},{5,6},{6,7},{7,8},{8,9},{9,10},{10,1... | collective-permute-start | bytes 98312 | tf_op jit(solution)/shard_map/ppermute | solution.py:357
  65.2 4.1 %collective-permute-start.5 = (f32[4,8,256]{2,1,0:T(8,128)S(1)}, f32[4,8,256]{2,1,0:T(8,128)S(1)}, u32[]{:S(2)}, u32[]{:S(2)}) collective-permute-start(f32[4,8,256]{2,1,0:T(8,128)S(1)} %get-tuple-element.32), channel_id=1, source_target_pairs={{16,1},{17,2},{18,3},{19,4},{20,5},{21,6},{22,7},{23,8},{24,9},{25... | collective-permute-start | bytes 98312 | tf_op jit(solution)/shard_map/ppermute | solution.py:358
  69.3 1.4 %collective-permute-done.5.refs_9_ = f32[4,8,256]{2,1,0:T(8,128)S(1)} collective-permute-done((f32[4,8,256]{2,1,0:T(8,128)S(1)}, f32[4,8,256]{2,1,0:T(8,128)S(1)}, u32[]{:S(2)}, u32[]{:S(2)}) %collective-permute-start.5) | collective-permute-done | bytes 32800 | tf_op jit(solution)/shard_map/ppermute | solution.py:358
  70.7 33.4 %shard_map.102 = (f32[2,216,8,128]{3,2,1,0:T(8,128)S(1)}, f32[2,216,8,128]{3,2,1,0:T(8,128)S(1)}) custom-call(s32[9]{0:T(128)S(1)} %pad_add_fusion.refs_0_, f32[4,16,72,256]{3,2,1,0:T(8,128)} %get-tuple-element.23.refs_1_, f32[4,16,72,256]{3,2,1,0:T(8,128)} %get-tuple-element.24.refs_2_, f32[4,16,72,256]{3,2,1,0:T(8,128)} %get-tuple-element.25.refs_3_, ...), custom_call_target="tpu_custom_call" | custom-call | tf_op jit(solution)/shard_map/pallas_call | solution.py:368
  104.1 2.8 %collective-permute-start.6 = (f32[2,216,8,128]{3,2,1,0:T(8,128)S(1)}, f32[2,216,8,128]{3,2,1,0:T(8,128)S(1)}, u32[]{:S(2)}, u32[]{:S(2)}) collective-permute-start(f32[2,216,8,128]{3,2,1,0:T(8,128)S(1)} %get-tuple-element.34), channel_id=1, source_target_pairs={{16,0},{17,1},{18,2},{19,3},{20,4},{21,5},{22,6},{23,7},{24,8},{25... | collective-permute-start | bytes 5308424 | tf_op jit(solution)/shard_map/ppermute | solution.py:390
  106.9 3.3 %collective-permute-done.6.refs_2_ = f32[2,216,8,128]{3,2,1,0:T(8,128)S(1)} collective-permute-done((f32[2,216,8,128]{3,2,1,0:T(8,128)S(1)}, f32[2,216,8,128]{3,2,1,0:T(8,128)S(1)}, u32[]{:S(2)}, u32[]{:S(2)}) %collective-permute-start.6) | collective-permute-done | bytes 1769504 | tf_op jit(solution)/shard_map/ppermute | solution.py:390
  110.2 4.6 %shard_map.103 = f32[2,2,216,8,128]{4,3,2,1,0:T(8,128)} custom-call(s32[9]{0:T(128)S(1)} %pad_add_fusion.refs_0_, f32[2,216,8,128]{3,2,1,0:T(8,128)S(1)} %get-tuple-element.33.refs_1_, f32[2,216,8,128]{3,2,1,0:T(8,128)S(1)} %collective-permute-done.6.refs_2_), custom_call_target="tpu_custom_call" | custom-call | tf_op jit(solution)/shard_map/pallas_call | solution.py:394
  (38 shorter events, 0.7 us)
Async XLA Ops:
  0.0 19.3 %copy-start.1 = (f32[4,24]{1,0:T(4,128)S(1)}, f32[4,24]{1,0:T(4,128)}, u32[]{:S(2)}) copy-start(f32[4,24]{1,0:T(4,128)} %param.13) | copy-start | bytes 1156
  0.0 19.4 %copy-start.2 = (f32[4,24]{1,0:T(4,128)S(1)}, f32[4,24]{1,0:T(4,128)}, u32[]{:S(2)}) copy-start(f32[4,24]{1,0:T(4,128)} %param.14) | copy-start | bytes 1156
  2.2 0.7 copy-start
  2.9 19.3 %copy-start.4 = (s32[2,4]{1,0:T(2,128)S(1)}, s32[2,4]{1,0:T(2,128)}, u32[]{:S(2)}) copy-start(s32[2,4]{1,0:T(2,128)} %param.19) | copy-start | bytes 100
  6.6 17.6 %collective-permute-start.1 = (f32[3,8,128]{2,1,0:T(8,128)S(1)}, f32[3,8,128]{2,1,0:T(8,128)S(1)}, u32[]{:S(2)}, u32[]{:S(2)}) collective-permute-start(f32[3,8,128]{2,1,0:T(8,128)S(1)} %pad_maximum_fusion.4), channel_id=1, source_target_pairs={{0,1},{1,2},{2,3},{3,4},{4,5},{5,6},{6,7},{7,8},{8,9},{9,10},{10,1... | collective-permute-start | bytes 36872 | tf_op jit(solution)/shard_map/ppermute | solution.py:293
  10.5 13.6 %collective-permute-start.2 = (f32[3,8,128]{2,1,0:T(8,128)S(1)}, f32[3,8,128]{2,1,0:T(8,128)S(1)}, u32[]{:S(2)}, u32[]{:S(2)}) collective-permute-start(f32[3,8,128]{2,1,0:T(8,128)S(1)} %pad_maximum_fusion.4), channel_id=1, source_target_pairs={{16,1},{17,2},{18,3},{19,4},{20,5},{21,6},{22,7},{23,8},{24,9},{25... | collective-permute-start | bytes 36872 | tf_op jit(solution)/shard_map/ppermute | solution.py:294
  13.6 10.4 %collective-permute-start = (f32[3,8,128]{2,1,0:T(8,128)S(1)}, f32[3,8,128]{2,1,0:T(8,128)S(1)}, u32[]{:S(2)}, u32[]{:S(2)}) collective-permute-start(f32[3,8,128]{2,1,0:T(8,128)S(1)} %pad_maximum_fusion.4), channel_id=1, source_target_pairs={{16,0},{17,1},{18,2},{19,3},{20,4},{21,5},{22,6},{23,7},{24,8},{25... | collective-permute-start | bytes 36872 | tf_op jit(solution)/shard_map/ppermute | solution.py:292
  13.7 10.2 %copy-start.3 = (f32[24]{0:T(128)S(1)}, f32[24]{0:T(128)}, u32[]{:S(2)}) copy-start(f32[24]{0:T(128)} %param.15) | copy-start | bytes 292
  13.7 47.5 %all-to-all-start = ((f32[32,16,896]{2,1,0:T(8,128)}), f32[32,16,896]{2,1,0:T(8,128)S(1)}, u32[]{:S(2)}, u32[]{:S(2)}) async-start(f32[32,16,896]{2,1,0:T(8,128)} %bitcast.5), calls=%async_computation | async-start | bytes 3670016 | tf_op jit(solution)/shard_map/all_to_all | solution.py:289
  62.7 8.0 %collective-permute-start.3 = (f32[4,80,256]{2,1,0:T(8,128)S(1)}, f32[4,80,256]{2,1,0:T(8,128)S(1)}, u32[]{:S(2)}, u32[]{:S(2)}) collective-permute-start(f32[4,80,256]{2,1,0:T(8,128)S(1)} %get-tuple-element.30), channel_id=1, source_target_pairs={{16,0},{17,1},{18,2},{19,3},{20,4},{21,5},{22,6},{23,7},{24,8},{25... | collective-permute-start | bytes 983048 | tf_op jit(solution)/shard_map/ppermute | solution.py:356
  63.2 6.1 %collective-permute-start.4 = (f32[4,8,256]{2,1,0:T(8,128)S(1)}, f32[4,8,256]{2,1,0:T(8,128)S(1)}, u32[]{:S(2)}, u32[]{:S(2)}) collective-permute-start(f32[4,8,256]{2,1,0:T(8,128)S(1)} %get-tuple-element.31), channel_id=1, source_target_pairs={{0,1},{1,2},{2,3},{3,4},{4,5},{5,6},{6,7},{7,8},{8,9},{9,10},{10,1... | collective-permute-start | bytes 98312 | tf_op jit(solution)/shard_map/ppermute | solution.py:357
  65.2 5.5 %collective-permute-start.5 = (f32[4,8,256]{2,1,0:T(8,128)S(1)}, f32[4,8,256]{2,1,0:T(8,128)S(1)}, u32[]{:S(2)}, u32[]{:S(2)}) collective-permute-start(f32[4,8,256]{2,1,0:T(8,128)S(1)} %get-tuple-element.32), channel_id=1, source_target_pairs={{16,1},{17,2},{18,3},{19,4},{20,5},{21,6},{22,7},{23,8},{24,9},{25... | collective-permute-start | bytes 98312 | tf_op jit(solution)/shard_map/ppermute | solution.py:358
  104.1 6.2 %collective-permute-start.6 = (f32[2,216,8,128]{3,2,1,0:T(8,128)S(1)}, f32[2,216,8,128]{3,2,1,0:T(8,128)S(1)}, u32[]{:S(2)}, u32[]{:S(2)}) collective-permute-start(f32[2,216,8,128]{3,2,1,0:T(8,128)S(1)} %get-tuple-element.34), channel_id=1, source_target_pairs={{16,0},{17,1},{18,2},{19,3},{20,4},{21,5},{22,6},{23,7},{24,8},{25... | collective-permute-start | bytes 5308424 | tf_op jit(solution)/shard_map/ppermute | solution.py:390

commit v3 on v2

--- a/solution.py
+++ b/solution.py
@@ -1,3 +1,4 @@
+from functools import partial
 import math
 
 import jax
@@ -119,7 +120,7 @@
     turn = pl.program_id(0)
     quad = info[turn]
     half = info[ITERS * QUADS]
-    width = mt_ref.shape[2]
+    width = mt_ref.shape[3]
     rows_dev = rows // 2
     down = (quad == 0) | (quad == 3)
     step_x = jnp.where(down, 1, -1)
@@ -143,7 +144,7 @@
         side[j + rows_dev * (1 - half)] = theirs
 
     def run(count, second):
-        chains = [(0, own // 2), (own // 2, count)]
+        chains = [(0, count)]
 
         def factors(i, low, high):
             row = first_row + i * step_x
@@ -155,14 +156,12 @@
             den = base_ref[0, row, low:high] + jnp.concatenate([damping] * (width // LANES), axis=1)
             inverse = 1.0 / den
             source = wind_ref[0, row, low:high]
-            if low == 0:
-                source = jnp.concatenate([source[:HALO] + side[row, :HALO], source[HALO:]], axis=0)
-            else:
-                last = own - HALO - low
-                parts = [source[:last], source[last:own - low] + side[row, HALO:]]
-                if high > own:
-                    parts.append(source[own - low:])
-                source = jnp.concatenate(parts, axis=0)
+            edge = side[row]
+            parts = [source[:HALO] + edge[:HALO], source[HALO:own - HALO],
+                     source[own - HALO:own] + edge[HALO:]]
+            if high > own:
+                parts.append(source[own:])
+            source = jnp.concatenate(parts, axis=0)
             if i == 0 or i == rows - 1:
                 here = jnp.where(row // rows_dev == half, 0, 1)
                 source = source + rim[here, low:high]
@@ -179,8 +178,9 @@
             for (along, known), before in zip(ready, upwind):
                 balance = known if before is None else along * before + known
                 high, low = split_bf16(balance)
-                updated.append(jnp.dot(jnp.concatenate([high, high, low], axis=1), mt_ref[0],
-                                       preferred_element_type=jnp.float32))
+                product = partial(jnp.dot, preferred_element_type=jnp.float32)
+                fine = product(high, mt_ref[0, 1]) + product(low, mt_ref[0, 0])
+                updated.append(product(high, mt_ref[0, 0]) + fine)
             if i + 1 < rows:
                 ready = [factors(i + 1, *chain) for chain in chains]
             row = first_row + i * step_x
@@ -283,9 +283,12 @@
         compiler_params=pltpu.CompilerParams(
             dimension_semantics=("arbitrary",), vmem_limit_bytes=48 * 2**20),
     )(dest_cell.reshape(1, points), outer_spectra)
+    outgoing, refraction_inverse = lax.optimization_barrier((outgoing, refraction_inverse))
+    flipped = pad_to(pad_to(jnp.swapaxes(refraction_inverse, 1, 2), 1, width), 2, width)
+    flip_high, flip_low = split_rounded(flipped)
+    matrices = jnp.stack([flip_high, flip_low], axis=1)
     held = jnp.stack([wind_speed, wind_dir, depth_class.astype(jnp.float32)])
-    outgoing, held, refraction_inverse = lax.optimization_barrier(
-        (outgoing, held, refraction_inverse))
+    held, matrices = lax.optimization_barrier((held, matrices))
     arrived = lax.all_to_all(outgoing.reshape(devices, CAP, load), axes, split_axis=0,
                              concat_axis=0, tiled=True).reshape(slot_total, load)
 
@@ -330,10 +333,6 @@
         cos_here[None, :, :, None] * cos_lane[:, None, None]
         + sin_here[None, :, :, None] * sin_lane[:, None, None], 0.0)
     wind = (rate_lane[None, None, None] * strength[None, :, :, None]) * (spread * spread)
-
-    flipped = pad_to(pad_to(jnp.swapaxes(refraction_inverse, 1, 2), 1, width), 2, width)
-    flip_high, flip_low = split_rounded(flipped)
-    matrices = jnp.concatenate([flip_high, flip_low, flip_high], axis=1)
 
     arrived, ax, ay, base, wind, matrices = lax.optimization_barrier(
         (arrived, ax, ay, base, wind, matrices))
@@ -371,7 +370,7 @@
             num_scalar_prefetch=1,
             grid=(turns,),
             in_specs=[quad_block((rows, cells, width))] * 4
-            + [quad_block((3 * width, width))]
+            + [quad_block((2, width, width))]
             + [quad_block((block, width))] * 2
             + [quad_block((HALO, width))] * 2,
             out_specs=[whole, whole],

time: 116 us -> 116 us (level)
  waiting for transfers between devices: 32 us -> 36 us
  other arithmetic: 14.1 us -> 11.2 us
  Pallas kernels: 42.5 us -> 40.3 us
  local copies, waits for them, and re-layouts: 4.4 us -> 5.57 us
    all_to_all x1, waiting for transfers between devices: 27.3 us -> 31.3 us  [body(): lax.all_to_all(outgoing.reshape(devices, CAP, load), axes, split_axis=0,...]
    unnamed x11 -> x19, local copies, waits for them, and re-layouts: 2.16 us -> 4.51 us
    pallas_call x1, Pallas kernels: 33.4 us -> 31.3 us  [body(): pl.pallas_call(lambda *refs: sweeps_kernel(rows, own, cells, quad_size, *...]
    concatenate x1 -> x0, other arithmetic: 1.46 us -> none  [body(): matrices = jnp.concatenate([flip_high, flip_low, flip_high], axis=1)]
    convert_element_type x1 -> x0, other arithmetic: 1.17 us -> none  [split_rounded(): (value - rounded).astype(jnp.bfloat16)]
    optimization_barrier x1, local copies, waits for them, and re-layouts: 1.49 us -> 0.32 us  [body(): lax.optimization_barrier((outgoing, refraction_inverse))]
  transfers between devices with their start and end apart: 8 -> 8, of which waited for: 3 -> 3; matrix products, arithmetic and copies ran while one was open for 13% -> 9% of each run, Pallas kernels for 0% -> 0%
where the time goes in v3:
time: 116 us; the launch traced here: 115 us
  Pallas kernels  40.3 us (35%)
  waiting for transfers between devices  36 us (31%)
  starting transfers between devices  21.6 us (19%)
  other arithmetic  11.2 us (10%)
  local copies, waits for them, and re-layouts  5.57 us (5%)
    all_to_all x1, waiting for transfers between devices, body(): lax.all_to_all(outgoing.reshape(devices, CAP, load), axes, split_axis=0,...  31.3 us
    pallas_call x1, Pallas kernels, body(): pl.pallas_call(lambda *refs: sweeps_kernel(rows, own, cells, quad_size, *...  31.3 us
    select_n x1, other arithmetic, by_class(): jnp.where((class_here == kind)[None, :, :, None], table[:, None, None, ki...  6.71 us
    all_to_all x1, starting transfers between devices, body(): lax.all_to_all(outgoing.reshape(devices, CAP, load), axes, split_axis=0,...  5.12 us
    pallas_call x1, Pallas kernels, body(): pl.pallas_call(lambda *refs: merge_kernel(own, *refs), grid_spec=pltpu.Pr...  4.58 us
    unnamed x19, local copies, waits for them, and re-layouts  4.51 us
    ppermute x1, starting transfers between devices, body(): rim_cross = lax.ppermute(out_cross, axes, cross_route)  4.13 us
    ppermute x1, starting transfers between devices, body(): beside_same = lax.ppermute(held, axes, same_route)  3.96 us
  transfers between devices with their start and end apart: 8, of which 3 were waited for; matrix products, arithmetic and copies ran while one was open for 9% of the time, Pallas kernels for 0%

profile of v3, /device:TPU:17, one launch (start us, length us, event | category | flops | bytes accessed | tf_op | source)
XLA Modules:
  0.0 115.1 jit_solution(13152680919638504184)
XLA Ops:
  0.0 0.8 convert_bitcast_fusion
  0.8 1.5 %copy.14.refs_1_ = f32[256,864]{1,0:T(8,128)S(1)} copy(f32[256,864]{0,1:T(8,128)} %param.16) | data formatting | bytes 1769472 | tf_op args[6]
  2.3 0.7 copy-done.1
  2.9 3.0 %shard_map.100 = f32[512,896]{1,0:T(8,128)} custom-call(s32[1,256]{1,0:T(1,128)S(1)} %bitcast.53, f32[256,864]{1,0:T(8,128)S(1)} %copy.14.refs_1_), custom_call_target="tpu_custom_call" | custom-call | tf_op jit(solution)/shard_map/pallas_call | solution.py:273
  5.9 0.3 copy.15
  6.3 0.1 fusion.2
  6.4 0.1 pad_maximum_fusion.refs_5_
  6.6 4.0 %collective-permute-start.1 = (f32[3,8,128]{2,1,0:T(8,128)S(1)}, f32[3,8,128]{2,1,0:T(8,128)S(1)}, u32[]{:S(2)}, u32[]{:S(2)}) collective-permute-start(f32[3,8,128]{2,1,0:T(8,128)S(1)} %pad_maximum_fusion.4), channel_id=1, source_target_pairs={{0,1},{1,2},{2,3},{3,4},{4,5},{5,6},{6,7},{7,8},{8,9},{9,10},{10,1... | collective-permute-start | bytes 36872 | tf_op jit(solution)/shard_map/ppermute | solution.py:296
  10.5 3.1 %collective-permute-start.2 = (f32[3,8,128]{2,1,0:T(8,128)S(1)}, f32[3,8,128]{2,1,0:T(8,128)S(1)}, u32[]{:S(2)}, u32[]{:S(2)}) collective-permute-start(f32[3,8,128]{2,1,0:T(8,128)S(1)} %pad_maximum_fusion.4), channel_id=1, source_target_pairs={{16,1},{17,2},{18,3},{19,4},{20,5},{21,6},{22,7},{23,8},{24,9},{25... | collective-permute-start | bytes 36872 | tf_op jit(solution)/shard_map/ppermute | solution.py:297
  13.7 5.1 %all-to-all-start = ((f32[32,16,896]{2,1,0:T(8,128)}), f32[32,16,896]{2,1,0:T(8,128)S(1)}, u32[]{:S(2)}, u32[]{:S(2)}) async-start(f32[32,16,896]{2,1,0:T(8,128)} %bitcast.2), calls=%async_computation | async-start | bytes 3670016 | tf_op jit(solution)/shard_map/all_to_all | solution.py:292
  19.0 0.1 reshape.97
  19.1 0.1 broadcast_in_dim.177
  19.3 0.1 broadcast_in_dim.165
  19.4 0.1 tile.13
  19.5 0.1 tile.30
  19.7 0.1 tile.32
  20.0 0.1 fusion.4
  20.1 0.1 pad_maximum_fusion.3
  20.3 0.2 broadcast_multiply_fusion
  20.5 2.7 %multiply_multiply_fusion.refs_4_ = f32[4,16,72,256]{3,2,1,0:T(8,128)} fusion(f32[4,256]{1,0:T(4,128)S(1)} %get-tuple-element.74, f32[16,72]{1,0:T(8,128)S(1)} %get-tuple-element.42, f32[4,256]{1,0:T(4,128)S(1)} %get-tuple-element.69, f32[16,72]{1,0:T(8,128)S(1)} %get-tuple-element.43, f32[16,72,256]{2,1,0:T(8,128)S(1)} %broadcast_multiply_fusion), kind=kLoop, calls=%fused_computation | loop fusion | flops 7077888 | bytes 5915648 | tf_op jit(solution)/shard_map/mul | solution.py:335
  23.2 6.7 %select_select_fusion = (f32[4,16,72,256]{3,2,1,0:T(8,128)}, f32[4,16,72,256]{3,2,1,0:T(8,128)}, f32[4,16,72,256]{3,2,1,0:T(8,128)}) fusion(f32[4,256]{1,0:T(4,128)S(1)} %get-tuple-element.52, f32[4,256]{1,0:T(4,128)S(1)} %get-tuple-element.53, f32[4,256]{1,0:T(4,128)S(1)} %get-tuple-element.54, f32[4,256]{1,0:T(4,128)S(1)} %get-tuple-element.51, ...), kind=kLoop, calls=%fused_computation.1 | loop fusion | flops 10616832 | bytes 14208384 | tf_op jit(solution)/shard_map/jit(_where)/select_n | solution.py:326
  29.9 31.3 %all-to-all-done = f32[32,16,896]{2,1,0:T(8,128)S(1)} async-done(((f32[32,16,896]{2,1,0:T(8,128)}), f32[32,16,896]{2,1,0:T(8,128)S(1)}, u32[]{:S(2)}, u32[]{:S(2)}) %all-to-all-start) | async-done | bytes 1835040 | tf_op jit(solution)/shard_map/all_to_all | solution.py:292
  61.2 1.5 %shard_map.101 = (f32[4,80,256]{2,1,0:T(8,128)S(1)}, f32[4,80,256]{2,1,0:T(8,128)S(1)}, f32[4,8,256]{2,1,0:T(8,128)S(1)}, f32[4,8,256]{2,1,0:T(8,128)S(1)}) custom-call(s32[9]{0:T(128)S(1)} %pad_add_fusion.refs_0_, f32[512,896]{1,0:T(8,128)S(1)} %bitcast.52), custom_call_target="tpu_custom_call" | custom-call | tf_op jit(solution)/shard_map/pallas_call | solution.py:344
  62.7 0.5 collective-permute-start.3
  63.2 1.9 %collective-permute-start.4 = (f32[4,8,256]{2,1,0:T(8,128)S(1)}, f32[4,8,256]{2,1,0:T(8,128)S(1)}, u32[]{:S(2)}, u32[]{:S(2)}) collective-permute-start(f32[4,8,256]{2,1,0:T(8,128)S(1)} %get-tuple-element.33), channel_id=1, source_target_pairs={{0,1},{1,2},{2,3},{3,4},{4,5},{5,6},{6,7},{7,8},{8,9},{9,10},{10,1... | collective-permute-start | bytes 98312 | tf_op jit(solution)/shard_map/ppermute | solution.py:356
  65.2 4.1 %collective-permute-start.5 = (f32[4,8,256]{2,1,0:T(8,128)S(1)}, f32[4,8,256]{2,1,0:T(8,128)S(1)}, u32[]{:S(2)}, u32[]{:S(2)}) collective-permute-start(f32[4,8,256]{2,1,0:T(8,128)S(1)} %get-tuple-element.34), channel_id=1, source_target_pairs={{16,1},{17,2},{18,3},{19,4},{20,5},{21,6},{22,7},{23,8},{24,9},{25... | collective-permute-start | bytes 98312 | tf_op jit(solution)/shard_map/ppermute | solution.py:357
  69.3 1.4 %collective-permute-done.5.refs_9_ = f32[4,8,256]{2,1,0:T(8,128)S(1)} collective-permute-done((f32[4,8,256]{2,1,0:T(8,128)S(1)}, f32[4,8,256]{2,1,0:T(8,128)S(1)}, u32[]{:S(2)}, u32[]{:S(2)}) %collective-permute-start.5) | collective-permute-done | bytes 32800 | tf_op jit(solution)/shard_map/ppermute | solution.py:357
  70.7 2.3 %copy-done = f32[4,16,72,256]{3,2,1,0:T(8,128)S(1)} copy-done((f32[4,16,72,256]{3,2,1,0:T(8,128)S(1)}, f32[4,16,72,256]{3,2,1,0:T(8,128)}, u32[]{:S(2)}) %copy-start) | copy-done | bytes 4718616
  73.0 31.3 %shard_map.102 = (f32[2,216,8,128]{3,2,1,0:T(8,128)S(1)}, f32[2,216,8,128]{3,2,1,0:T(8,128)S(1)}) custom-call(s32[9]{0:T(128)S(1)} %pad_add_fusion.refs_0_, f32[4,16,72,256]{3,2,1,0:T(8,128)S(1)} %copy-done, f32[4,16,72,256]{3,2,1,0:T(8,128)} %get-tuple-element.26.refs_2_, f32[4,16,72,256]{3,2,1,0:T(8,128)} %get-tuple-element.27.refs_3_, ...), custom_call_target="tpu_custom_call" | custom-call | tf_op jit(solution)/shard_map/pallas_call | solution.py:367
  104.3 2.8 %collective-permute-start.6 = (f32[2,216,8,128]{3,2,1,0:T(8,128)S(1)}, f32[2,216,8,128]{3,2,1,0:T(8,128)S(1)}, u32[]{:S(2)}, u32[]{:S(2)}) collective-permute-start(f32[2,216,8,128]{3,2,1,0:T(8,128)S(1)} %get-tuple-element.36), channel_id=1, source_target_pairs={{16,0},{17,1},{18,2},{19,3},{20,4},{21,5},{22,6},{23,7},{24,8},{25... | collective-permute-start | bytes 5308424 | tf_op jit(solution)/shard_map/ppermute | solution.py:389
  107.2 3.3 %collective-permute-done.6.refs_2_ = f32[2,216,8,128]{3,2,1,0:T(8,128)S(1)} collective-permute-done((f32[2,216,8,128]{3,2,1,0:T(8,128)S(1)}, f32[2,216,8,128]{3,2,1,0:T(8,128)S(1)}, u32[]{:S(2)}, u32[]{:S(2)}) %collective-permute-start.6) | collective-permute-done | bytes 1769504 | tf_op jit(solution)/shard_map/ppermute | solution.py:389
  110.5 4.6 %shard_map.103 = f32[2,2,216,8,128]{4,3,2,1,0:T(8,128)} custom-call(s32[9]{0:T(128)S(1)} %pad_add_fusion.refs_0_, f32[2,216,8,128]{3,2,1,0:T(8,128)S(1)} %get-tuple-element.35.refs_1_, f32[2,216,8,128]{3,2,1,0:T(8,128)S(1)} %collective-permute-done.6.refs_2_), custom_call_target="tpu_custom_call" | custom-call | tf_op jit(solution)/shard_map/pallas_call | solution.py:393
  (46 shorter events, 0.7 us)
Async XLA Ops:
  0.0 5.9 %copy-start.2 = (f32[4,216,216]{2,1,0:T(8,128)S(1)}, f32[4,216,216]{2,1,0:T(8,128)}, u32[]{:S(2)}) copy-start(f32[4,216,216]{2,1,0:T(8,128)} %param.18) | copy-start | bytes 2239492
  2.2 0.7 copy-start.1
  2.9 3.6 %copy-start.3 = (f32[8,128]{1,0:T(8,128)S(1)}, f32[8,128]{1,0:T(8,128)}, u32[]{:S(2)}) copy-start(f32[8,128]{1,0:T(8,128)} %param.11) | copy-start | bytes 12292
  2.9 3.6 %copy-start.4 = (f32[8,128]{1,0:T(8,128)S(1)}, f32[8,128]{1,0:T(8,128)}, u32[]{:S(2)}) copy-start(f32[8,128]{1,0:T(8,128)} %param.10) | copy-start | bytes 12292
  5.9 13.1 %copy-start.8 = (s32[2,4]{1,0:T(2,128)S(1)}, s32[2,4]{1,0:T(2,128)}, u32[]{:S(2)}) copy-start(s32[2,4]{1,0:T(2,128)} %param.19) | copy-start | bytes 100
  5.9 13.5 %copy-start.5 = (f32[4,24]{1,0:T(4,128)S(1)}, f32[4,24]{1,0:T(4,128)}, u32[]{:S(2)}) copy-start(f32[4,24]{1,0:T(4,128)} %param.13) | copy-start | bytes 1156
  5.9 13.6 %copy-start.6 = (f32[4,24]{1,0:T(4,128)S(1)}, f32[4,24]{1,0:T(4,128)}, u32[]{:S(2)}) copy-start(f32[4,24]{1,0:T(4,128)} %param.14) | copy-start | bytes 1156
  5.9 13.8 %copy-start.7 = (f32[24]{0:T(128)S(1)}, f32[24]{0:T(128)}, u32[]{:S(2)}) copy-start(f32[24]{0:T(128)} %param.15) | copy-start | bytes 292
  6.6 13.5 %collective-permute-start.1 = (f32[3,8,128]{2,1,0:T(8,128)S(1)}, f32[3,8,128]{2,1,0:T(8,128)S(1)}, u32[]{:S(2)}, u32[]{:S(2)}) collective-permute-start(f32[3,8,128]{2,1,0:T(8,128)S(1)} %pad_maximum_fusion.4), channel_id=1, source_target_pairs={{0,1},{1,2},{2,3},{3,4},{4,5},{5,6},{6,7},{7,8},{8,9},{9,10},{10,1... | collective-permute-start | bytes 36872 | tf_op jit(solution)/shard_map/ppermute | solution.py:296
  10.5 9.5 %collective-permute-start.2 = (f32[3,8,128]{2,1,0:T(8,128)S(1)}, f32[3,8,128]{2,1,0:T(8,128)S(1)}, u32[]{:S(2)}, u32[]{:S(2)}) collective-permute-start(f32[3,8,128]{2,1,0:T(8,128)S(1)} %pad_maximum_fusion.4), channel_id=1, source_target_pairs={{16,1},{17,2},{18,3},{19,4},{20,5},{21,6},{22,7},{23,8},{24,9},{25... | collective-permute-start | bytes 36872 | tf_op jit(solution)/shard_map/ppermute | solution.py:297
  13.6 6.3 %collective-permute-start = (f32[3,8,128]{2,1,0:T(8,128)S(1)}, f32[3,8,128]{2,1,0:T(8,128)S(1)}, u32[]{:S(2)}, u32[]{:S(2)}) collective-permute-start(f32[3,8,128]{2,1,0:T(8,128)S(1)} %pad_maximum_fusion.4), channel_id=1, source_target_pairs={{16,0},{17,1},{18,2},{19,3},{20,4},{21,5},{22,6},{23,7},{24,8},{25... | collective-permute-start | bytes 36872 | tf_op jit(solution)/shard_map/ppermute | solution.py:295
  13.7 47.5 %all-to-all-start = ((f32[32,16,896]{2,1,0:T(8,128)}), f32[32,16,896]{2,1,0:T(8,128)S(1)}, u32[]{:S(2)}, u32[]{:S(2)}) async-start(f32[32,16,896]{2,1,0:T(8,128)} %bitcast.2), calls=%async_computation | async-start | bytes 3670016 | tf_op jit(solution)/shard_map/all_to_all | solution.py:292
  62.7 8.0 %collective-permute-start.3 = (f32[4,80,256]{2,1,0:T(8,128)S(1)}, f32[4,80,256]{2,1,0:T(8,128)S(1)}, u32[]{:S(2)}, u32[]{:S(2)}) collective-permute-start(f32[4,80,256]{2,1,0:T(8,128)S(1)} %get-tuple-element.32), channel_id=1, source_target_pairs={{16,0},{17,1},{18,2},{19,3},{20,4},{21,5},{22,6},{23,7},{24,8},{25... | collective-permute-start | bytes 983048 | tf_op jit(solution)/shard_map/ppermute | solution.py:355
  63.2 6.1 %collective-permute-start.4 = (f32[4,8,256]{2,1,0:T(8,128)S(1)}, f32[4,8,256]{2,1,0:T(8,128)S(1)}, u32[]{:S(2)}, u32[]{:S(2)}) collective-permute-start(f32[4,8,256]{2,1,0:T(8,128)S(1)} %get-tuple-element.33), channel_id=1, source_target_pairs={{0,1},{1,2},{2,3},{3,4},{4,5},{5,6},{6,7},{7,8},{8,9},{9,10},{10,1... | collective-permute-start | bytes 98312 | tf_op jit(solution)/shard_map/ppermute | solution.py:356
  65.2 5.5 %collective-permute-start.5 = (f32[4,8,256]{2,1,0:T(8,128)S(1)}, f32[4,8,256]{2,1,0:T(8,128)S(1)}, u32[]{:S(2)}, u32[]{:S(2)}) collective-permute-start(f32[4,8,256]{2,1,0:T(8,128)S(1)} %get-tuple-element.34), channel_id=1, source_target_pairs={{16,1},{17,2},{18,3},{19,4},{20,5},{21,6},{22,7},{23,8},{24,9},{25... | collective-permute-start | bytes 98312 | tf_op jit(solution)/shard_map/ppermute | solution.py:357
  70.7 2.3 %copy-start = (f32[4,16,72,256]{3,2,1,0:T(8,128)S(1)}, f32[4,16,72,256]{3,2,1,0:T(8,128)}, u32[]{:S(2)}) copy-start(f32[4,16,72,256]{3,2,1,0:T(8,128)} %get-tuple-element.25.refs_1_) | copy-start | bytes 14155780
  104.3 6.2 %collective-permute-start.6 = (f32[2,216,8,128]{3,2,1,0:T(8,128)S(1)}, f32[2,216,8,128]{3,2,1,0:T(8,128)S(1)}, u32[]{:S(2)}, u32[]{:S(2)}) collective-permute-start(f32[2,216,8,128]{3,2,1,0:T(8,128)S(1)} %get-tuple-element.36), channel_id=1, source_target_pairs={{16,0},{17,1},{18,2},{19,3},{20,4},{21,5},{22,6},{23,7},{24,8},{25... | collective-permute-start | bytes 5308424 | tf_op jit(solution)/shard_map/ppermute | solution.py:389

commit v4 on v3

--- a/solution.py
+++ b/solution.py
@@ -65,14 +65,15 @@
         rank = jnp.sum(jnp.where(same & above, 1.0, 0.0), axis=0, keepdims=True)
         slots[...] = owner * CAP + rank.astype(jnp.int32)
         spectra = jnp.concatenate(
-            [spectra_ref[...], jnp.broadcast_to(columns[:, 1:2], (points, load - comps))], axis=1)
+            [spectra_ref[...], jnp.broadcast_to(lanes[1:2], (load - comps, points))], axis=0)
         high[...], low[...] = split_bf16(spectra)
 
     place = jnp.where(
         lax.broadcasted_iota(jnp.int32, (out_ref.shape[0], points), 0) + step * out_ref.shape[0]
         == slots[...], 1.0, 0.0).astype(jnp.bfloat16)
-    out_ref[...] = (jnp.dot(place, high[...], preferred_element_type=jnp.float32)
-                    + jnp.dot(place, low[...], preferred_element_type=jnp.float32))
+    over_points = (((1,), (1,)), ((), ()))
+    out_ref[...] = (lax.dot_general(place, high[...], over_points, preferred_element_type=jnp.float32)
+                    + lax.dot_general(place, low[...], over_points, preferred_element_type=jnp.float32))
 
 
 def rim_kernel(own, rows_dev, comps, quad_size, info, arrived_ref, own_ref, send_ref, same_ref,
@@ -144,55 +145,62 @@
         side[j + rows_dev * (1 - half)] = theirs
 
     def run(count, second):
-        chains = [(0, count)]
-
-        def factors(i, low, high):
+        def factors(i, at_rim):
             row = first_row + i * step_x
-            total = power[0, row, low:high]
+            total = power[0, row, :count]
             for other in range(1, QUADS):
-                total = total + power[other, row, low:high]
+                total = total + power[other, row, :count]
             level = total * (1.0 / (QUADS * quad_size))
             damping = whitecap_rate * level / (1.0 + level)
-            den = base_ref[0, row, low:high] + jnp.concatenate([damping] * (width // LANES), axis=1)
+            den = base_ref[0, row, :count] + jnp.concatenate([damping] * (width // LANES), axis=1)
             inverse = 1.0 / den
-            source = wind_ref[0, row, low:high]
+            source = wind_ref[0, row, :count]
             edge = side[row]
             parts = [source[:HALO] + edge[:HALO], source[HALO:own - HALO],
                      source[own - HALO:own] + edge[HALO:]]
-            if high > own:
+            if count > own:
                 parts.append(source[own:])
             source = jnp.concatenate(parts, axis=0)
-            if i == 0 or i == rows - 1:
+            if at_rim:
                 here = jnp.where(row // rows_dev == half, 0, 1)
-                source = source + rim[here, low:high]
+                source = source + rim[here, :count]
             if second:
                 before = state[quad, row]
                 shifted = jnp.where(up_y, pltpu.roll(before, 1, 0), pltpu.roll(before, cells - 1, 0))
-                source = source + ay_ref[0, row, low:high] * shifted[low:high]
-            return ax_ref[0, row, low:high] * inverse, source * inverse
-
-        ready = [factors(0, *chain) for chain in chains]
-        upwind = [None] * len(chains)
-        for i in range(rows):
-            updated = []
-            for (along, known), before in zip(ready, upwind):
-                balance = known if before is None else along * before + known
-                high, low = split_bf16(balance)
-                product = partial(jnp.dot, preferred_element_type=jnp.float32)
-                fine = product(high, mt_ref[0, 1]) + product(low, mt_ref[0, 0])
-                updated.append(product(high, mt_ref[0, 0]) + fine)
-            if i + 1 < rows:
-                ready = [factors(i + 1, *chain) for chain in chains]
+                source = source + ay_ref[0, row, :count] * shifted[:count]
+            return ax_ref[0, row, :count] * inverse, source * inverse
+
+        def times_matrix(balance):
+            high, low = split_bf16(balance)
+            product = partial(jnp.dot, preferred_element_type=jnp.float32)
+            fine = product(high, mt_ref[0, 1]) + product(low, mt_ref[0, 0])
+            return product(high, mt_ref[0, 0]) + fine
+
+        def store(i, value):
             row = first_row + i * step_x
-            for (start, stop), value in zip(chains, updated):
-                square = value * value
-                folded = square[:, :LANES]
-                for lane in range(LANES, width, LANES):
-                    folded = folded + square[:, lane:lane + LANES]
-                state[quad, row, start:stop] = value
-                power[quad, row, start:stop] = jnp.broadcast_to(
-                    jnp.sum(folded, axis=1, keepdims=True), (stop - start, LANES))
-            upwind = updated
+            square = value * value
+            folded = square[:, :LANES]
+            for lane in range(LANES, width, LANES):
+                folded = folded + square[:, lane:lane + LANES]
+            state[quad, row, :count] = value
+            power[quad, row, :count] = jnp.broadcast_to(
+                jnp.sum(folded, axis=1, keepdims=True), (count, LANES))
+
+        def step(i, carry):
+            along, known, before = carry
+            value = times_matrix(along * before + known)
+            along, known = factors(i + 1, False)
+            store(i - 1, before)
+            return along, known, value
+
+        first = times_matrix(factors(0, True)[1])
+        along, known, before = lax.fori_loop(1, rows - 2, step, (*factors(1, False), first))
+        value = times_matrix(along * before + known)
+        along, known = factors(rows - 1, True)
+        store(rows - 3, before)
+        last = times_matrix(along * value + known)
+        store(rows - 2, value)
+        store(rows - 1, last)
 
     @pl.when(turn < QUADS)
     def _():
@@ -274,33 +282,35 @@
         lambda *refs: pack_kernel(shifts, col_count, rows, comps, *refs),
         grid=(steps,),
         in_specs=[pl.BlockSpec((1, points), lambda s: (0, 0)),
-                  pl.BlockSpec((points, comps), lambda s: (0, 0))],
+                  pl.BlockSpec((comps, points), lambda s: (0, 0))],
         out_specs=pl.BlockSpec((slot_total // steps, load), lambda s: (s, 0)),
-        scratch_shapes=[pltpu.VMEM((points, load), jnp.bfloat16),
-                        pltpu.VMEM((points, load), jnp.bfloat16),
+        scratch_shapes=[pltpu.VMEM((load, points), jnp.bfloat16),
+                        pltpu.VMEM((load, points), jnp.bfloat16),
                         pltpu.VMEM((1, points), jnp.int32)],
         out_shape=jax.ShapeDtypeStruct((slot_total, load), jnp.float32),
         compiler_params=pltpu.CompilerParams(
             dimension_semantics=("arbitrary",), vmem_limit_bytes=48 * 2**20),
-    )(dest_cell.reshape(1, points), outer_spectra)
+    )(dest_cell.reshape(1, points), outer_spectra.T)
     outgoing, refraction_inverse = lax.optimization_barrier((outgoing, refraction_inverse))
     flipped = pad_to(pad_to(jnp.swapaxes(refraction_inverse, 1, 2), 1, width), 2, width)
     flip_high, flip_low = split_rounded(flipped)
     matrices = jnp.stack([flip_high, flip_low], axis=1)
     held = jnp.stack([wind_speed, wind_dir, depth_class.astype(jnp.float32)])
-    held, matrices = lax.optimization_barrier((held, matrices))
     arrived = lax.all_to_all(outgoing.reshape(devices, CAP, load), axes, split_axis=0,
                              concat_axis=0, tiled=True).reshape(slot_total, load)
 
-    partner = lax.ppermute(held, axes, swap_route)
-    beside_same = lax.ppermute(held, axes, same_route)
-    beside_cross = lax.ppermute(held, axes, cross_route)
+    everywhere = lax.all_gather(held, axes).reshape((row_count, col_count) + held.shape)
     is_low = half == 0
-    chip = jnp.concatenate(
-        [jnp.where(is_low, held, partner), jnp.where(is_low, partner, held)], axis=1)
-    near = jnp.concatenate(
-        [jnp.where(is_low, beside_same, beside_cross), jnp.where(is_low, beside_cross, beside_same)],
-        axis=1)
+    col_at = lax.axis_index("cols")
+    near_at = jnp.where(is_low, col_at - 1, col_at + 1)
+    inside = (near_at >= 0) & (near_at < col_count)
+
+    def chip_at(index):
+        both = lax.dynamic_index_in_dim(everywhere, index, axis=1, keepdims=False)
+        return jnp.concatenate([both[0], both[1]], axis=1)
+
+    chip = chip_at(col_at)
+    near = jnp.where(inside, chip_at(jnp.clip(near_at, 0, col_count - 1)), 0.0)
     mine = jnp.where(is_low, chip[:, :, :own], chip[:, :, own:])
     right = jnp.where(is_low, chip[:, :, own], near[:, :, 0])
     left = jnp.where(is_low, near[:, :, cols_dev - 1], chip[:, :, own - 1])
@@ -383,7 +393,7 @@
         ),
         out_shape=[jax.ShapeDtypeStruct(packed, jnp.float32)] * 2,
         compiler_params=pltpu.CompilerParams(
-            dimension_semantics=("arbitrary",), vmem_limit_bytes=44 * 2**20),
+            dimension_semantics=("arbitrary",), vmem_limit_bytes=56 * 2**20),
     )(info, ax, ay, base, wind, matrices, rim_own, rim_partner, rim_same, rim_cross)
 
     got = lax.ppermute(send, axes, swap_route)

time: 116 us -> 180 us (1.55)
  blocking collectives: 0 us -> 81.9 us
  waiting for transfers between devices: 36 us -> 6.18 us
  starting transfers between devices: 21.6 us -> 27.1 us
  Pallas kernels: 40.3 us -> 45.7 us
    all_gather x0 -> x1, blocking collectives: none -> 81.9 us  [body(): lax.all_gather(held, axes).reshape((row_count, col_count) + held.shape)]
    all_to_all x1, waiting for transfers between devices: 31.3 us -> 0.01 us  [body(): lax.all_to_all(outgoing.reshape(devices, CAP, load), axes, split_axis=0,...]
    ppermute x1, starting transfers between devices: 0.51 us -> 14.2 us  [body(): rim_partner = lax.ppermute(rim_send, axes, swap_route)]
    ppermute x3 -> x0, starting transfers between devices: 7.14 us -> none  [the longest x1 3.96 us: body(): beside_same = lax.ppermute(held, axes, same_route)]
    pallas_call x1, Pallas kernels: 31.3 us -> 36.3 us  [body(): pl.pallas_call(lambda *refs: sweeps_kernel(rows, own, cells, quad_size, *...]
    unnamed x19 -> x32, local copies, waits for them, and re-layouts: 4.51 us -> 4.88 us
  transfers between devices with their start and end apart: 8 -> 5, of which waited for: 3 -> 3; matrix products, arithmetic and copies ran while one was open for 9% -> 8% of each run, Pallas kernels for 0% -> 0%
where the time goes in v4:
time: 180 us
  blocking collectives  81.9 us (46%)
  Pallas kernels  45.7 us (25%)
  starting transfers between devices  27.1 us (15%)
  other arithmetic  11.3 us (6%)
  local copies, waits for them, and re-layouts  7.12 us (4%)
  waiting for transfers between devices  6.18 us (3%)
    all_gather x1, blocking collectives, body(): lax.all_gather(held, axes).reshape((row_count, col_count) + held.shape)  81.9 us
    pallas_call x1, Pallas kernels, body(): pl.pallas_call(lambda *refs: sweeps_kernel(rows, own, cells, quad_size, *...  36.3 us
    ppermute x1, starting transfers between devices, body(): rim_partner = lax.ppermute(rim_send, axes, swap_route)  14.2 us
    select_n x1, other arithmetic, by_class(): jnp.where((class_here == kind)[None, :, :, None], table[:, None, None, ki...  6.66 us
    all_to_all x1, starting transfers between devices, body(): lax.all_to_all(outgoing.reshape(devices, CAP, load), axes, split_axis=0,...  6.25 us
    unnamed x32, local copies, waits for them, and re-layouts  4.88 us
    pallas_call x1, Pallas kernels, body(): pl.pallas_call(lambda *refs: merge_kernel(own, *refs), grid_spec=pltpu.Pr...  4.59 us
  transfers between devices with their start and end apart: 5, of which 3 were waited for; matrix products, arithmetic and copies ran while one was open for 8% of the time, Pallas kernels for 0%

profile of v4, /device:TPU:17, one launch (start us, length us, event | category | flops | bytes accessed | tf_op | source)
XLA Modules:
  0.0 179.7 jit_solution(5712267218635389406)
XLA Ops:
  0.0 1.2 copy-done.1
  1.2 0.7 copy-done.5
  1.9 3.3 %shard_map.100 = f32[512,896]{1,0:T(8,128)} custom-call(s32[1,256]{1,0:T(1,128)S(1)} %bitcast.64, f32[864,256]{1,0:T(8,128)S(1)} %bitcast.63), custom_call_target="tpu_custom_call" | custom-call | tf_op jit(solution)/shard_map/pallas_call | solution.py:281
  5.2 6.3 %all-to-all-start = ((f32[32,16,896]{2,1,0:T(8,128)}), f32[32,16,896]{2,1,0:T(8,128)S(1)}, u32[]{:S(2)}, u32[]{:S(2)}) async-start(f32[32,16,896]{2,1,0:T(8,128)} %bitcast.3), calls=%async_computation | async-start | bytes 3670016 | tf_op jit(solution)/shard_map/all_to_all | solution.py:299
  11.6 0.1 reshape.108
  11.7 0.1 tile.32
  11.9 0.1 broadcast_in_dim.182
  12.0 0.1 broadcast_in_dim.170
  12.2 0.1 tile.13
  12.4 81.9 %all-gather = f32[96,8,128]{2,1,0:T(8,128)S(1)} all-gather(f32[3,8,128]{2,1,0:T(8,128)S(1)} %pad_maximum_fusion.3), channel_id=2, replica_groups=mesh['rows'=2,'cols'=16] {'rows','cols'}, dimensions={0}, use_global_device_ids=true | all-gather | bytes 405504 | tf_op jit(solution)/shard_map/all_gather | solution.py:302
  94.3 1.5 copy.15
  96.1 0.2 fusion.2
  96.3 1.1 pad_maximum_fusion.refs_5_
  97.3 0.1 fusion.4
  97.4 0.1 pad_maximum_fusion.2
  97.6 0.2 broadcast_multiply_fusion
  97.9 2.7 %multiply_multiply_fusion.refs_4_ = f32[4,16,72,256]{3,2,1,0:T(8,128)} fusion(f32[4,256]{1,0:T(4,128)S(1)} %get-tuple-element.70, f32[16,72]{1,0:T(8,128)S(1)} %get-tuple-element.42, f32[4,256]{1,0:T(4,128)S(1)} %get-tuple-element.65, f32[16,72]{1,0:T(8,128)S(1)} %get-tuple-element.43, f32[16,72,256]{2,1,0:T(8,128)S(1)} %broadcast_multiply_fusion), kind=kLoop, calls=%fused_computation | loop fusion | flops 7077888 | bytes 5915648 | tf_op jit(solution)/shard_map/mul | solution.py:345
  100.6 6.7 %select_select_fusion = (f32[4,16,72,256]{3,2,1,0:T(8,128)}, f32[4,16,72,256]{3,2,1,0:T(8,128)}, f32[4,16,72,256]{3,2,1,0:T(8,128)}) fusion(f32[4,256]{1,0:T(4,128)S(1)} %get-tuple-element.48, f32[4,256]{1,0:T(4,128)S(1)} %get-tuple-element.49, f32[4,256]{1,0:T(4,128)S(1)} %get-tuple-element.50, f32[4,256]{1,0:T(4,128)S(1)} %get-tuple-element.47, ...), kind=kLoop, calls=%fused_computation.1 | loop fusion | flops 10616832 | bytes 14208384 | tf_op jit(solution)/shard_map/jit(_where)/select_n | solution.py:336
  107.2 1.5 shard_map.101
  108.7 0.8 copy-done.2
  109.5 14.2 %collective-permute-start = (f32[4,80,256]{2,1,0:T(8,128)S(1)}, f32[4,80,256]{2,1,0:T(8,128)S(1)}, u32[]{:S(2)}, u32[]{:S(2)}) collective-permute-start(f32[4,80,256]{2,1,0:T(8,128)S(1)} %get-tuple-element.28), channel_id=1, source_target_pairs={{16,0},{17,1},{18,2},{19,3},{20,4},{21,5},{22,6},{23,7},{24,8},{25... | collective-permute-start | bytes 983048 | tf_op jit(solution)/shard_map/ppermute | solution.py:365
  123.7 2.0 %collective-permute-start.1 = (f32[4,8,256]{2,1,0:T(8,128)S(1)}, f32[4,8,256]{2,1,0:T(8,128)S(1)}, u32[]{:S(2)}, u32[]{:S(2)}) collective-permute-start(f32[4,8,256]{2,1,0:T(8,128)S(1)} %get-tuple-element.29), channel_id=1, source_target_pairs={{0,1},{1,2},{2,3},{3,4},{4,5},{5,6},{6,7},{7,8},{8,9},{9,10},{10,1... | collective-permute-start | bytes 98312 | tf_op jit(solution)/shard_map/ppermute | solution.py:366
  125.7 2.6 %collective-permute-start.2 = (f32[4,8,256]{2,1,0:T(8,128)S(1)}, f32[4,8,256]{2,1,0:T(8,128)S(1)}, u32[]{:S(2)}, u32[]{:S(2)}) collective-permute-start(f32[4,8,256]{2,1,0:T(8,128)S(1)} %get-tuple-element.30), channel_id=1, source_target_pairs={{16,1},{17,2},{18,3},{19,4},{20,5},{21,6},{22,7},{23,8},{24,9},{25... | collective-permute-start | bytes 98312 | tf_op jit(solution)/shard_map/ppermute | solution.py:367
  128.3 0.1 collective-permute-done.1.refs_8_
  128.4 2.6 %collective-permute-done.2.refs_9_ = f32[4,8,256]{2,1,0:T(8,128)S(1)} collective-permute-done((f32[4,8,256]{2,1,0:T(8,128)S(1)}, f32[4,8,256]{2,1,0:T(8,128)S(1)}, u32[]{:S(2)}, u32[]{:S(2)}) %collective-permute-start.2) | collective-permute-done | bytes 32800 | tf_op jit(solution)/shard_map/ppermute | solution.py:367
  131.0 0.6 copy-done.8
  131.6 0.1 copy-done.6
  131.7 36.3 %shard_map.102 = (f32[2,216,8,128]{3,2,1,0:T(8,128)}, f32[2,216,8,128]{3,2,1,0:T(8,128)}) custom-call(s32[9]{0:T(128)} %copy-done.3, f32[4,16,72,256]{3,2,1,0:T(8,128)} %get-tuple-element.21.refs_1_, f32[4,16,72,256]{3,2,1,0:T(8,128)} %get-tuple-element.22.refs_2_, f32[4,16,72,256]{3,2,1,0:T(8,128)} %get-tuple-element.23.refs_3_, ...), custom_call_target="tpu_custom_call" | custom-call | tf_op jit(solution)/shard_map/pallas_call | solution.py:377
  168.0 2.1 %collective-permute-start.3 = (f32[2,216,8,128]{3,2,1,0:T(8,128)}, f32[2,216,8,128]{3,2,1,0:T(8,128)S(1)}, u32[]{:S(2)}, u32[]{:S(2)}) collective-permute-start(f32[2,216,8,128]{3,2,1,0:T(8,128)} %get-tuple-element.32), channel_id=1, source_target_pairs={{16,0},{17,1},{18,2},{19,3},{20,4},{21,5},{22,6},{23,7},{24,8},{25... | collective-permute-start | bytes 5308424 | tf_op jit(solution)/shard_map/ppermute | solution.py:399
  170.1 3.5 %collective-permute-done.3.refs_2_ = f32[2,216,8,128]{3,2,1,0:T(8,128)S(1)} collective-permute-done((f32[2,216,8,128]{3,2,1,0:T(8,128)}, f32[2,216,8,128]{3,2,1,0:T(8,128)S(1)}, u32[]{:S(2)}, u32[]{:S(2)}) %collective-permute-start.3) | collective-permute-done | bytes 1769504 | tf_op jit(solution)/shard_map/ppermute | solution.py:399
  173.6 1.5 copy-done
  175.1 4.6 %shard_map.103 = f32[2,2,216,8,128]{4,3,2,1,0:T(8,128)} custom-call(s32[9]{0:T(128)S(1)} %copy-done.4, f32[2,216,8,128]{3,2,1,0:T(8,128)S(1)} %copy-done, f32[2,216,8,128]{3,2,1,0:T(8,128)S(1)} %collective-permute-done.3.refs_2_), custom_call_target="tpu_custom_call" | custom-call | tf_op jit(solution)/shard_map/pallas_call | solution.py:403
  (54 shorter events, 0.7 us)
Async XLA Ops:
  0.0 11.6 %copy-start.15 = (s32[2,4]{1,0:T(2,128)S(1)}, s32[2,4]{1,0:T(2,128)}, u32[]{:S(2)}) copy-start(s32[2,4]{1,0:T(2,128)} %param.19) | copy-start | bytes 100
  0.0 11.7 %copy-start.14 = (f32[24]{0:T(128)S(1)}, f32[24]{0:T(128)}, u32[]{:S(2)}) copy-start(f32[24]{0:T(128)} %param.15) | copy-start | bytes 292
  0.0 12.1 %copy-start.12 = (f32[4,24]{1,0:T(4,128)S(1)}, f32[4,24]{1,0:T(4,128)}, u32[]{:S(2)}) copy-start(f32[4,24]{1,0:T(4,128)} %param.13) | copy-start | bytes 1156
  0.0 1.2 copy-start.1
  1.2 0.7 copy-start.5
  1.9 9.8 %copy-start.9 = (s32[8,128]{1,0:T(8,128)S(1)}, s32[8,128]{1,0:T(8,128)}, u32[]{:S(2)}) copy-start(s32[8,128]{1,0:T(8,128)} %param.12) | copy-start | bytes 12292
  1.9 10.4 %copy-start.13 = (f32[4,24]{1,0:T(4,128)S(1)}, f32[4,24]{1,0:T(4,128)}, u32[]{:S(2)}) copy-start(f32[4,24]{1,0:T(4,128)} %param.14) | copy-start | bytes 1156
  1.9 10.5 %copy-start.10 = (f32[8,128]{1,0:T(8,128)S(1)}, f32[8,128]{1,0:T(8,128)}, u32[]{:S(2)}) copy-start(f32[8,128]{1,0:T(8,128)} %param.11) | copy-start | bytes 12292
  1.9 10.5 %copy-start.11 = (f32[8,128]{1,0:T(8,128)S(1)}, f32[8,128]{1,0:T(8,128)}, u32[]{:S(2)}) copy-start(f32[8,128]{1,0:T(8,128)} %param.10) | copy-start | bytes 12292
  5.2 102.0 %all-to-all-start = ((f32[32,16,896]{2,1,0:T(8,128)}), f32[32,16,896]{2,1,0:T(8,128)S(1)}, u32[]{:S(2)}, u32[]{:S(2)}) async-start(f32[32,16,896]{2,1,0:T(8,128)} %bitcast.3), calls=%async_computation | async-start | bytes 3670016 | tf_op jit(solution)/shard_map/all_to_all | solution.py:299
  96.1 11.1 %copy-start.3 = (s32[9]{0:T(128)}, s32[9]{0:T(128)S(1)}, u32[]{:S(2)}) copy-start(s32[9]{0:T(128)S(1)} %pad_add_fusion.refs_0_) | copy-start | bytes 112
  108.7 0.8 copy-start.2
  109.5 21.5 %collective-permute-start = (f32[4,80,256]{2,1,0:T(8,128)S(1)}, f32[4,80,256]{2,1,0:T(8,128)S(1)}, u32[]{:S(2)}, u32[]{:S(2)}) collective-permute-start(f32[4,80,256]{2,1,0:T(8,128)S(1)} %get-tuple-element.28), channel_id=1, source_target_pairs={{16,0},{17,1},{18,2},{19,3},{20,4},{21,5},{22,6},{23,7},{24,8},{25... | collective-permute-start | bytes 983048 | tf_op jit(solution)/shard_map/ppermute | solution.py:365
  123.7 4.6 %collective-permute-start.1 = (f32[4,8,256]{2,1,0:T(8,128)S(1)}, f32[4,8,256]{2,1,0:T(8,128)S(1)}, u32[]{:S(2)}, u32[]{:S(2)}) collective-permute-start(f32[4,8,256]{2,1,0:T(8,128)S(1)} %get-tuple-element.29), channel_id=1, source_target_pairs={{0,1},{1,2},{2,3},{3,4},{4,5},{5,6},{6,7},{7,8},{8,9},{9,10},{10,1... | collective-permute-start | bytes 98312 | tf_op jit(solution)/shard_map/ppermute | solution.py:366
  125.7 5.2 %collective-permute-start.2 = (f32[4,8,256]{2,1,0:T(8,128)S(1)}, f32[4,8,256]{2,1,0:T(8,128)S(1)}, u32[]{:S(2)}, u32[]{:S(2)}) collective-permute-start(f32[4,8,256]{2,1,0:T(8,128)S(1)} %get-tuple-element.30), channel_id=1, source_target_pairs={{16,1},{17,2},{18,3},{19,4},{20,5},{21,6},{22,7},{23,8},{24,9},{25... | collective-permute-start | bytes 98312 | tf_op jit(solution)/shard_map/ppermute | solution.py:367
  128.4 2.6 %copy-start.7 = (f32[4,8,256]{2,1,0:T(8,128)}, f32[4,8,256]{2,1,0:T(8,128)S(1)}, u32[]{:S(2)}) copy-start(f32[4,8,256]{2,1,0:T(8,128)S(1)} %collective-permute-done.1.refs_8_) | copy-start | bytes 98308
  131.0 0.6 copy-start.8
  131.0 0.7 copy-start.6
  131.7 41.9 %copy-start.4 = (s32[9]{0:T(128)S(1)}, s32[9]{0:T(128)}, u32[]{:S(2)}) copy-start(s32[9]{0:T(128)} %copy-done.3) | copy-start | bytes 112
  168.0 5.6 %collective-permute-start.3 = (f32[2,216,8,128]{3,2,1,0:T(8,128)}, f32[2,216,8,128]{3,2,1,0:T(8,128)S(1)}, u32[]{:S(2)}, u32[]{:S(2)}) collective-permute-start(f32[2,216,8,128]{3,2,1,0:T(8,128)} %get-tuple-element.32), channel_id=1, source_target_pairs={{16,0},{17,1},{18,2},{19,3},{20,4},{21,5},{22,6},{23,7},{24,8},{25... | collective-permute-start | bytes 5308424 | tf_op jit(solution)/shard_map/ppermute | solution.py:399
  173.6 1.5 copy-start

commit v5 on v3

--- a/solution.py
+++ b/solution.py
@@ -1,4 +1,3 @@
-from functools import partial
 import math
 
 import jax
@@ -26,9 +25,9 @@
     return high, low
 
 
-def split_rounded(value):
-    rounded = lax.reduce_precision(value, 8, 7)
-    return rounded.astype(jnp.bfloat16), (value - rounded).astype(jnp.bfloat16)
+def lane_scale(width):
+    golden = (math.sqrt(5.0) - 1.0) / 2.0
+    return np.exp2(np.mod(np.arange(width) * golden, 1.0)).astype(np.float32)
 
 
 def pad_to(array, axis, size, value=0.0):
@@ -65,14 +64,15 @@
         rank = jnp.sum(jnp.where(same & above, 1.0, 0.0), axis=0, keepdims=True)
         slots[...] = owner * CAP + rank.astype(jnp.int32)
         spectra = jnp.concatenate(
-            [spectra_ref[...], jnp.broadcast_to(columns[:, 1:2], (points, load - comps))], axis=1)
+            [spectra_ref[...], jnp.broadcast_to(lanes[1:2], (load - comps, points))], axis=0)
         high[...], low[...] = split_bf16(spectra)
 
     place = jnp.where(
         lax.broadcasted_iota(jnp.int32, (out_ref.shape[0], points), 0) + step * out_ref.shape[0]
         == slots[...], 1.0, 0.0).astype(jnp.bfloat16)
-    out_ref[...] = (jnp.dot(place, high[...], preferred_element_type=jnp.float32)
-                    + jnp.dot(place, low[...], preferred_element_type=jnp.float32))
+    over_points = (((1,), (1,)), ((), ()))
+    out_ref[...] = (lax.dot_general(place, high[...], over_points, preferred_element_type=jnp.float32)
+                    + lax.dot_general(place, low[...], over_points, preferred_element_type=jnp.float32))
 
 
 def rim_kernel(own, rows_dev, comps, quad_size, info, arrived_ref, own_ref, send_ref, same_ref,
@@ -114,13 +114,13 @@
         cross_ref[quad] = part[2 * block + HALO:2 * block + 2 * HALO, :width]
 
 
-def sweeps_kernel(rows, own, cells, quad_size, info, ax_ref, ay_ref, base_ref, wind_ref, mt_ref,
+def sweeps_kernel(rows, own, cells, quad_size, info, ax_ref, ay_ref, base_ref, wind_ref, mt_ref, diag_ref, scale_ref,
                   own_ref, par_ref, same_ref, cross_ref, keep_ref, send_ref,
                   state, power, rim, side):
     turn = pl.program_id(0)
     quad = info[turn]
     half = info[ITERS * QUADS]
-    width = mt_ref.shape[3]
+    width = mt_ref.shape[2]
     rows_dev = rows // 2
     down = (quad == 0) | (quad == 3)
     step_x = jnp.where(down, 1, -1)
@@ -154,7 +154,7 @@
             level = total * (1.0 / (QUADS * quad_size))
             damping = whitecap_rate * level / (1.0 + level)
             den = base_ref[0, row, low:high] + jnp.concatenate([damping] * (width // LANES), axis=1)
-            inverse = 1.0 / den
+            inverse = scale_ref[...] / den
             source = wind_ref[0, row, low:high]
             edge = side[row]
             parts = [source[:HALO] + edge[:HALO], source[HALO:own - HALO],
@@ -177,10 +177,9 @@
             updated = []
             for (along, known), before in zip(ready, upwind):
                 balance = known if before is None else along * before + known
-                high, low = split_bf16(balance)
-                product = partial(jnp.dot, preferred_element_type=jnp.float32)
-                fine = product(high, mt_ref[0, 1]) + product(low, mt_ref[0, 0])
-                updated.append(product(high, mt_ref[0, 0]) + fine)
+                mixed = jnp.dot(balance.astype(jnp.bfloat16), mt_ref[0],
+                                preferred_element_type=jnp.float32)
+                updated.append(diag_ref[0] * balance + mixed)
             if i + 1 < rows:
                 ready = [factors(i + 1, *chain) for chain in chains]
             row = first_row + i * step_x
@@ -274,21 +273,23 @@
         lambda *refs: pack_kernel(shifts, col_count, rows, comps, *refs),
         grid=(steps,),
         in_specs=[pl.BlockSpec((1, points), lambda s: (0, 0)),
-                  pl.BlockSpec((points, comps), lambda s: (0, 0))],
+                  pl.BlockSpec((comps, points), lambda s: (0, 0))],
         out_specs=pl.BlockSpec((slot_total // steps, load), lambda s: (s, 0)),
-        scratch_shapes=[pltpu.VMEM((points, load), jnp.bfloat16),
-                        pltpu.VMEM((points, load), jnp.bfloat16),
+        scratch_shapes=[pltpu.VMEM((load, points), jnp.bfloat16),
+                        pltpu.VMEM((load, points), jnp.bfloat16),
                         pltpu.VMEM((1, points), jnp.int32)],
         out_shape=jax.ShapeDtypeStruct((slot_total, load), jnp.float32),
         compiler_params=pltpu.CompilerParams(
             dimension_semantics=("arbitrary",), vmem_limit_bytes=48 * 2**20),
-    )(dest_cell.reshape(1, points), outer_spectra)
+    )(dest_cell.reshape(1, points), outer_spectra.T)
     outgoing, refraction_inverse = lax.optimization_barrier((outgoing, refraction_inverse))
+    scale = jnp.asarray(lane_scale(width))
     flipped = pad_to(pad_to(jnp.swapaxes(refraction_inverse, 1, 2), 1, width), 2, width)
-    flip_high, flip_low = split_rounded(flipped)
-    matrices = jnp.stack([flip_high, flip_low], axis=1)
+    scaled = flipped / scale[None, :, None]
+    on_diag = jnp.eye(width, dtype=bool)[None]
+    matrices = jnp.where(on_diag, 0.0, scaled).astype(jnp.bfloat16)
+    diagonal = jnp.sum(jnp.where(on_diag, scaled, 0.0), axis=1, keepdims=True)
     held = jnp.stack([wind_speed, wind_dir, depth_class.astype(jnp.float32)])
-    held, matrices = lax.optimization_barrier((held, matrices))
     arrived = lax.all_to_all(outgoing.reshape(devices, CAP, load), axes, split_axis=0,
                              concat_axis=0, tiled=True).reshape(slot_total, load)
 
@@ -370,7 +371,8 @@
             num_scalar_prefetch=1,
             grid=(turns,),
             in_specs=[quad_block((rows, cells, width))] * 4
-            + [quad_block((2, width, width))]
+            + [quad_block((width, width)), quad_block((1, width))]
+            + [pl.BlockSpec((1, width), lambda t, info: (0, 0))]
             + [quad_block((block, width))] * 2
             + [quad_block((HALO, width))] * 2,
             out_specs=[whole, whole],
@@ -383,8 +385,8 @@
         ),
         out_shape=[jax.ShapeDtypeStruct(packed, jnp.float32)] * 2,
         compiler_params=pltpu.CompilerParams(
-            dimension_semantics=("arbitrary",), vmem_limit_bytes=44 * 2**20),
-    )(info, ax, ay, base, wind, matrices, rim_own, rim_partner, rim_same, rim_cross)
+            dimension_semantics=("arbitrary",), vmem_limit_bytes=56 * 2**20),
+    )(info, ax, ay, base, wind, matrices, diagonal, scale[None], rim_own, rim_partner, rim_same, rim_cross)
 
     got = lax.ppermute(send, axes, swap_route)
     chunks = 4

time: 116 us -> 112 us (0.966)
  Pallas kernels: 40.3 us -> 35 us
  waiting for transfers between devices: 36 us -> 33.3 us
  local copies, waits for them, and re-layouts: 5.57 us -> 7.68 us
  other arithmetic: 11.2 us -> 12.6 us
    pallas_call x1, Pallas kernels: 31.3 us -> 25.6 us  [body(): pl.pallas_call(lambda *refs: sweeps_kernel(rows, own, cells, quad_size, *...]
    all_to_all x1, waiting for transfers between devices: 31.3 us -> 28.8 us  [body(): lax.all_to_all(outgoing.reshape(devices, CAP, load), axes, split_axis=0,...]
    optimization_barrier x1, local copies, waits for them, and re-layouts: 0.32 us -> 1.49 us  [body(): lax.optimization_barrier((outgoing, refraction_inverse))]
    unnamed x19 -> x32, local copies, waits for them, and re-layouts: 4.51 us -> 4.84 us
  transfers between devices with their start and end apart: 8 -> 8, of which waited for: 3 -> 3; matrix products, arithmetic and copies ran while one was open for 9% -> 13% of each run, Pallas kernels for 0% -> 3%
where the time goes in v5:
time: 112 us; the launch traced here: 110 us
  Pallas kernels  35 us (31%)
  waiting for transfers between devices  33.3 us (30%)
  starting transfers between devices  21.6 us (19%)
  other arithmetic  12.6 us (11%)
  local copies, waits for them, and re-layouts  7.68 us (7%)
    all_to_all x1, waiting for transfers between devices, body(): lax.all_to_all(outgoing.reshape(devices, CAP, load), axes, split_axis=0,...  28.8 us
    pallas_call x1, Pallas kernels, body(): pl.pallas_call(lambda *refs: sweeps_kernel(rows, own, cells, quad_size, *...  25.6 us
    select_n x1, other arithmetic, by_class(): jnp.where((class_here == kind)[None, :, :, None], table[:, None, None, ki...  6.65 us
    unnamed x32, local copies, waits for them, and re-layouts  4.84 us
    all_to_all x1, starting transfers between devices, body(): lax.all_to_all(outgoing.reshape(devices, CAP, load), axes, split_axis=0,...  4.77 us
    pallas_call x1, Pallas kernels, body(): pl.pallas_call(lambda *refs: merge_kernel(own, *refs), grid_spec=pltpu.Pr...  4.59 us
    ppermute x1, starting transfers between devices, body(): beside_same = lax.ppermute(held, axes, same_route)  3.96 us
    ppermute x1, starting transfers between devices, body(): rim_cross = lax.ppermute(out_cross, axes, cross_route)  3.95 us
  transfers between devices with their start and end apart: 8, of which 3 were waited for; matrix products, arithmetic and copies ran while one was open for 13% of the time, Pallas kernels for 3%

profile of v5, /device:TPU:17, one launch (start us, length us, event | category | flops | bytes accessed | tf_op | source)
XLA Modules:
  0.0 110.4 jit_solution(1323094210602257396)
XLA Ops:
  0.0 0.7 convert_bitcast_fusion
  0.8 0.7 pad_maximum_fusion.3
  1.5 3.7 %collective-permute-start.2 = (f32[3,8,128]{2,1,0:T(8,128)S(1)}, f32[3,8,128]{2,1,0:T(8,128)S(1)}, u32[]{:S(2)}, u32[]{:S(2)}) collective-permute-start(f32[3,8,128]{2,1,0:T(8,128)S(1)} %pad_maximum_fusion.3), channel_id=1, source_target_pairs={{16,1},{17,2},{18,3},{19,4},{20,5},{21,6},{22,7},{23,8},{24,9},{25... | collective-permute-start | bytes 36872 | tf_op jit(solution)/shard_map/ppermute | solution.py:298
  5.1 4.0 %collective-permute-start.1 = (f32[3,8,128]{2,1,0:T(8,128)S(1)}, f32[3,8,128]{2,1,0:T(8,128)S(1)}, u32[]{:S(2)}, u32[]{:S(2)}) collective-permute-start(f32[3,8,128]{2,1,0:T(8,128)S(1)} %pad_maximum_fusion.3), channel_id=1, source_target_pairs={{0,1},{1,2},{2,3},{3,4},{4,5},{5,6},{6,7},{7,8},{8,9},{9,10},{10,1... | collective-permute-start | bytes 36872 | tf_op jit(solution)/shard_map/ppermute | solution.py:297
  9.2 1.2 %copy-done.1 = f32[256,864]{0,1:T(8,128)S(1)} copy-done((f32[256,864]{0,1:T(8,128)S(1)}, f32[256,864]{0,1:T(8,128)}, u32[]{:S(2)}) %copy-start.1) | copy-done | bytes 884760
  10.4 0.7 copy-done.5
  11.0 3.3 %shard_map.109 = f32[512,896]{1,0:T(8,128)} custom-call(s32[1,256]{1,0:T(1,128)S(1)} %bitcast.49, f32[864,256]{1,0:T(8,128)S(1)} %bitcast.48), custom_call_target="tpu_custom_call" | custom-call | tf_op jit(solution)/shard_map/pallas_call | solution.py:272
  14.3 4.8 %all-to-all-start = ((f32[32,16,896]{2,1,0:T(8,128)}), f32[32,16,896]{2,1,0:T(8,128)S(1)}, u32[]{:S(2)}, u32[]{:S(2)}) async-start(f32[32,16,896]{2,1,0:T(8,128)} %bitcast.3), calls=%async_computation | async-start | bytes 3670016 | tf_op jit(solution)/shard_map/all_to_all | solution.py:293
  19.3 0.1 broadcast_in_dim.207
  19.5 0.1 broadcast_in_dim.195
  19.9 1.5 %copy.13 = f32[4,216,216]{1,2,0:T(8,128)S(1)} copy(f32[4,216,216]{2,1,0:T(8,128)} %param.19) | data formatting | bytes 1492992 | tf_op jit(solution)/shard_map/optimization_barrier | solution.py:285
  21.5 1.0 select_reduce_fusion
  22.6 0.1 tile.32
  22.9 0.1 fusion.1
  23.1 0.2 broadcast_multiply_fusion
  23.4 2.7 %multiply_multiply_fusion.refs_4_ = f32[4,16,72,256]{3,2,1,0:T(8,128)} fusion(f32[4,256]{1,0:T(4,128)S(1)} %get-tuple-element.70, f32[16,72]{1,0:T(8,128)S(1)} %get-tuple-element.38, f32[4,256]{1,0:T(4,128)S(1)} %get-tuple-element.65, f32[16,72]{1,0:T(8,128)S(1)} %get-tuple-element.39, f32[16,72,256]{2,1,0:T(8,128)S(1)} %broadcast_multiply_fusion), kind=kLoop, calls=%fused_computation | loop fusion | flops 7077888 | bytes 5915648 | tf_op jit(solution)/shard_map/mul | solution.py:336
  26.1 6.7 %select_select_fusion = (f32[4,16,72,256]{3,2,1,0:T(8,128)}, f32[4,16,72,256]{3,2,1,0:T(8,128)}, f32[4,16,72,256]{3,2,1,0:T(8,128)}) fusion(f32[4,256]{1,0:T(4,128)S(1)} %get-tuple-element.48, f32[4,256]{1,0:T(4,128)S(1)} %get-tuple-element.49, f32[4,256]{1,0:T(4,128)S(1)} %get-tuple-element.50, f32[4,256]{1,0:T(4,128)S(1)} %get-tuple-element.47, ...), kind=kLoop, calls=%fused_computation.1 | loop fusion | flops 10616832 | bytes 14208384 | tf_op jit(solution)/shard_map/jit(_where)/select_n | solution.py:327
  32.7 28.8 %all-to-all-done = f32[32,16,896]{2,1,0:T(8,128)S(1)} async-done(((f32[32,16,896]{2,1,0:T(8,128)}), f32[32,16,896]{2,1,0:T(8,128)S(1)}, u32[]{:S(2)}, u32[]{:S(2)}) %all-to-all-start) | async-done | bytes 1835040 | tf_op jit(solution)/shard_map/all_to_all | solution.py:293
  61.5 1.5 %shard_map.110 = (f32[4,80,256]{2,1,0:T(8,128)S(1)}, f32[4,80,256]{2,1,0:T(8,128)S(1)}, f32[4,8,256]{2,1,0:T(8,128)S(1)}, f32[4,8,256]{2,1,0:T(8,128)S(1)}) custom-call(s32[9]{0:T(128)S(1)} %pad_add_fusion.refs_0_, f32[512,896]{1,0:T(8,128)S(1)} %bitcast.47), custom_call_target="tpu_custom_call" | custom-call | tf_op jit(solution)/shard_map/pallas_call | solution.py:345
  63.0 0.7 copy-done.2
  63.8 0.4 collective-permute-start.3
  64.2 1.9 %collective-permute-start.4 = (f32[4,8,256]{2,1,0:T(8,128)S(1)}, f32[4,8,256]{2,1,0:T(8,128)S(1)}, u32[]{:S(2)}, u32[]{:S(2)}) collective-permute-start(f32[4,8,256]{2,1,0:T(8,128)S(1)} %get-tuple-element.29), channel_id=1, source_target_pairs={{0,1},{1,2},{2,3},{3,4},{4,5},{5,6},{6,7},{7,8},{8,9},{9,10},{10,1... | collective-permute-start | bytes 98312 | tf_op jit(solution)/shard_map/ppermute | solution.py:357
  66.1 4.0 %collective-permute-start.5 = (f32[4,8,256]{2,1,0:T(8,128)S(1)}, f32[4,8,256]{2,1,0:T(8,128)S(1)}, u32[]{:S(2)}, u32[]{:S(2)}) collective-permute-start(f32[4,8,256]{2,1,0:T(8,128)S(1)} %get-tuple-element.30), channel_id=1, source_target_pairs={{16,1},{17,2},{18,3},{19,4},{20,5},{21,6},{22,7},{23,8},{24,9},{25... | collective-permute-start | bytes 98312 | tf_op jit(solution)/shard_map/ppermute | solution.py:358
  70.1 0.6 broadcast_in_dim.226.refs_6_
  70.7 1.0 collective-permute-done.5.refs_11_
  71.7 0.6 copy-done.8
  72.3 0.1 copy-done.6
  72.4 25.6 %shard_map.111 = (f32[2,216,8,128]{3,2,1,0:T(8,128)}, f32[2,216,8,128]{3,2,1,0:T(8,128)}) custom-call(s32[9]{0:T(128)} %copy-done.3, f32[4,16,72,256]{3,2,1,0:T(8,128)} %get-tuple-element.21.refs_1_, f32[4,16,72,256]{3,2,1,0:T(8,128)} %get-tuple-element.22.refs_2_, f32[4,16,72,256]{3,2,1,0:T(8,128)} %get-tuple-element.23.refs_3_, ...), custom_call_target="tpu_custom_call" | custom-call | tf_op jit(solution)/shard_map/pallas_call | solution.py:368
  98.0 2.8 %collective-permute-start.6 = (f32[2,216,8,128]{3,2,1,0:T(8,128)}, f32[2,216,8,128]{3,2,1,0:T(8,128)S(1)}, u32[]{:S(2)}, u32[]{:S(2)}) collective-permute-start(f32[2,216,8,128]{3,2,1,0:T(8,128)} %get-tuple-element.32), channel_id=1, source_target_pairs={{16,0},{17,1},{18,2},{19,3},{20,4},{21,5},{22,6},{23,7},{24,8},{25... | collective-permute-start | bytes 5308424 | tf_op jit(solution)/shard_map/ppermute | solution.py:391
  100.8 3.5 %collective-permute-done.6.refs_2_ = f32[2,216,8,128]{3,2,1,0:T(8,128)S(1)} collective-permute-done((f32[2,216,8,128]{3,2,1,0:T(8,128)}, f32[2,216,8,128]{3,2,1,0:T(8,128)S(1)}, u32[]{:S(2)}, u32[]{:S(2)}) %collective-permute-start.6) | collective-permute-done | bytes 1769504 | tf_op jit(solution)/shard_map/ppermute | solution.py:391
  104.3 1.5 %copy-done = f32[2,216,8,128]{3,2,1,0:T(8,128)S(1)} copy-done((f32[2,216,8,128]{3,2,1,0:T(8,128)S(1)}, f32[2,216,8,128]{3,2,1,0:T(8,128)}, u32[]{:S(2)}) %copy-start) | copy-done | bytes 1769496
  105.8 4.6 %shard_map.112 = f32[2,2,216,8,128]{4,3,2,1,0:T(8,128)} custom-call(s32[9]{0:T(128)S(1)} %copy-done.4, f32[2,216,8,128]{3,2,1,0:T(8,128)S(1)} %copy-done, f32[2,216,8,128]{3,2,1,0:T(8,128)S(1)} %collective-permute-done.6.refs_2_), custom_call_target="tpu_custom_call" | custom-call | tf_op jit(solution)/shard_map/pallas_call | solution.py:395
  (60 shorter events, 1.1 us)
Async XLA Ops:
  0.0 21.5 %copy-start.13 = (f32[256]{0:T(256)S(1)}, f32[256]{0:T(256)}, u32[]{:S(2)}) copy-start(f32[256]{0:T(256)} %constant.45) | copy-start | bytes 3076
  0.0 19.6 %copy-start.11 = (f32[4,24]{1,0:T(4,128)S(1)}, f32[4,24]{1,0:T(4,128)}, u32[]{:S(2)}) copy-start(f32[4,24]{1,0:T(4,128)} %param.14) | copy-start | bytes 1156
  0.0 19.7 %copy-start.12 = (f32[4,24]{1,0:T(4,128)S(1)}, f32[4,24]{1,0:T(4,128)}, u32[]{:S(2)}) copy-start(f32[4,24]{1,0:T(4,128)} %param.15) | copy-start | bytes 1156
  0.0 19.8 %copy-start.15 = (s32[2,4]{1,0:T(2,128)S(1)}, s32[2,4]{1,0:T(2,128)}, u32[]{:S(2)}) copy-start(s32[2,4]{1,0:T(2,128)} %param.20) | copy-start | bytes 100
  1.5 21.4 %collective-permute-start.2 = (f32[3,8,128]{2,1,0:T(8,128)S(1)}, f32[3,8,128]{2,1,0:T(8,128)S(1)}, u32[]{:S(2)}, u32[]{:S(2)}) collective-permute-start(f32[3,8,128]{2,1,0:T(8,128)S(1)} %pad_maximum_fusion.3), channel_id=1, source_target_pairs={{16,1},{17,2},{18,3},{19,4},{20,5},{21,6},{22,7},{23,8},{24,9},{25... | collective-permute-start | bytes 36872 | tf_op jit(solution)/shard_map/ppermute | solution.py:298
  5.1 17.7 %collective-permute-start.1 = (f32[3,8,128]{2,1,0:T(8,128)S(1)}, f32[3,8,128]{2,1,0:T(8,128)S(1)}, u32[]{:S(2)}, u32[]{:S(2)}) collective-permute-start(f32[3,8,128]{2,1,0:T(8,128)S(1)} %pad_maximum_fusion.3), channel_id=1, source_target_pairs={{0,1},{1,2},{2,3},{3,4},{4,5},{5,6},{6,7},{7,8},{8,9},{9,10},{10,1... | collective-permute-start | bytes 36872 | tf_op jit(solution)/shard_map/ppermute | solution.py:297
  9.1 13.7 %collective-permute-start = (f32[3,8,128]{2,1,0:T(8,128)S(1)}, f32[3,8,128]{2,1,0:T(8,128)S(1)}, u32[]{:S(2)}, u32[]{:S(2)}) collective-permute-start(f32[3,8,128]{2,1,0:T(8,128)S(1)} %pad_maximum_fusion.3), channel_id=1, source_target_pairs={{16,0},{17,1},{18,2},{19,3},{20,4},{21,5},{22,6},{23,7},{24,8},{25... | collective-permute-start | bytes 36872 | tf_op jit(solution)/shard_map/ppermute | solution.py:296
  9.2 1.2 %copy-start.1 = (f32[256,864]{0,1:T(8,128)S(1)}, f32[256,864]{0,1:T(8,128)}, u32[]{:S(2)}) copy-start(f32[256,864]{0,1:T(8,128)} %param.17) | copy-start | bytes 2654212
  10.4 0.7 copy-start.5
  11.0 11.6 %copy-start.14 = (f32[24]{0:T(128)S(1)}, f32[24]{0:T(128)}, u32[]{:S(2)}) copy-start(f32[24]{0:T(128)} %param.16) | copy-start | bytes 292
  11.0 11.7 %copy-start.9 = (f32[8,128]{1,0:T(8,128)S(1)}, f32[8,128]{1,0:T(8,128)}, u32[]{:S(2)}) copy-start(f32[8,128]{1,0:T(8,128)} %param.12) | copy-start | bytes 12292
  11.0 11.7 %copy-start.10 = (f32[8,128]{1,0:T(8,128)S(1)}, f32[8,128]{1,0:T(8,128)}, u32[]{:S(2)}) copy-start(f32[8,128]{1,0:T(8,128)} %param.11) | copy-start | bytes 12292
  14.3 47.2 %all-to-all-start = ((f32[32,16,896]{2,1,0:T(8,128)}), f32[32,16,896]{2,1,0:T(8,128)S(1)}, u32[]{:S(2)}, u32[]{:S(2)}) async-start(f32[32,16,896]{2,1,0:T(8,128)} %bitcast.3), calls=%async_computation | async-start | bytes 3670016 | tf_op jit(solution)/shard_map/all_to_all | solution.py:293
  22.6 38.9 %copy-start.3 = (s32[9]{0:T(128)}, s32[9]{0:T(128)S(1)}, u32[]{:S(2)}) copy-start(s32[9]{0:T(128)S(1)} %pad_add_fusion.refs_0_) | copy-start | bytes 112
  63.0 0.7 copy-start.2
  63.8 7.9 %collective-permute-start.3 = (f32[4,80,256]{2,1,0:T(8,128)S(1)}, f32[4,80,256]{2,1,0:T(8,128)S(1)}, u32[]{:S(2)}, u32[]{:S(2)}) collective-permute-start(f32[4,80,256]{2,1,0:T(8,128)S(1)} %get-tuple-element.28), channel_id=1, source_target_pairs={{16,0},{17,1},{18,2},{19,3},{20,4},{21,5},{22,6},{23,7},{24,8},{25... | collective-permute-start | bytes 983048 | tf_op jit(solution)/shard_map/ppermute | solution.py:356
  64.2 6.5 %collective-permute-start.4 = (f32[4,8,256]{2,1,0:T(8,128)S(1)}, f32[4,8,256]{2,1,0:T(8,128)S(1)}, u32[]{:S(2)}, u32[]{:S(2)}) collective-permute-start(f32[4,8,256]{2,1,0:T(8,128)S(1)} %get-tuple-element.29), channel_id=1, source_target_pairs={{0,1},{1,2},{2,3},{3,4},{4,5},{5,6},{6,7},{7,8},{8,9},{9,10},{10,1... | collective-permute-start | bytes 98312 | tf_op jit(solution)/shard_map/ppermute | solution.py:357
  66.1 5.5 %collective-permute-start.5 = (f32[4,8,256]{2,1,0:T(8,128)S(1)}, f32[4,8,256]{2,1,0:T(8,128)S(1)}, u32[]{:S(2)}, u32[]{:S(2)}) collective-permute-start(f32[4,8,256]{2,1,0:T(8,128)S(1)} %get-tuple-element.30), channel_id=1, source_target_pairs={{16,1},{17,2},{18,3},{19,4},{20,5},{21,6},{22,7},{23,8},{24,9},{25... | collective-permute-start | bytes 98312 | tf_op jit(solution)/shard_map/ppermute | solution.py:358
  70.7 1.0 copy-start.7
  71.7 0.6 copy-start.8
  71.7 0.8 copy-start.6
  72.4 31.9 %copy-start.4 = (s32[9]{0:T(128)S(1)}, s32[9]{0:T(128)}, u32[]{:S(2)}) copy-start(s32[9]{0:T(128)} %copy-done.3) | copy-start | bytes 112
  98.0 6.3 %collective-permute-start.6 = (f32[2,216,8,128]{3,2,1,0:T(8,128)}, f32[2,216,8,128]{3,2,1,0:T(8,128)S(1)}, u32[]{:S(2)}, u32[]{:S(2)}) collective-permute-start(f32[2,216,8,128]{3,2,1,0:T(8,128)} %get-tuple-element.32), channel_id=1, source_target_pairs={{16,0},{17,1},{18,2},{19,3},{20,4},{21,5},{22,6},{23,7},{24,8},{25... | collective-permute-start | bytes 5308424 | tf_op jit(solution)/shard_map/ppermute | solution.py:391
  104.3 1.5 %copy-start = (f32[2,216,8,128]{3,2,1,0:T(8,128)S(1)}, f32[2,216,8,128]{3,2,1,0:T(8,128)}, u32[]{:S(2)}) copy-start(f32[2,216,8,128]{3,2,1,0:T(8,128)} %get-tuple-element.31.refs_1_) | copy-start | bytes 5308420

commit v6 on v5

--- a/solution.py
+++ b/solution.py
@@ -1,3 +1,4 @@
+from functools import partial
 import math
 
 import jax
@@ -115,8 +116,10 @@
 
 
 def sweeps_kernel(rows, own, cells, quad_size, info, ax_ref, ay_ref, base_ref, wind_ref, mt_ref, diag_ref, scale_ref,
-                  own_ref, par_ref, same_ref, cross_ref, keep_ref, send_ref,
-                  state, power, rim, side):
+                  own_ref, par_ref, same_ref, cross_ref, *rest):
+    pairs = QUADS // 2
+    keep_refs, send_refs = rest[:pairs], rest[pairs:2 * pairs]
+    state, power, rim, side = rest[2 * pairs:]
     turn = pl.program_id(0)
     quad = info[turn]
     half = info[ITERS * QUADS]
@@ -144,7 +147,7 @@
         side[j + rows_dev * (1 - half)] = theirs
 
     def run(count, second):
-        chains = [(0, count)]
+        chains = [(0, own // 2), (own // 2, count)]
 
         def factors(i, low, high):
             row = first_row + i * step_x
@@ -156,12 +159,14 @@
             den = base_ref[0, row, low:high] + jnp.concatenate([damping] * (width // LANES), axis=1)
             inverse = scale_ref[...] / den
             source = wind_ref[0, row, low:high]
-            edge = side[row]
-            parts = [source[:HALO] + edge[:HALO], source[HALO:own - HALO],
-                     source[own - HALO:own] + edge[HALO:]]
-            if high > own:
-                parts.append(source[own:])
-            source = jnp.concatenate(parts, axis=0)
+            if low == 0:
+                source = jnp.concatenate([source[:HALO] + side[row, :HALO], source[HALO:]], axis=0)
+            else:
+                last = own - HALO - low
+                parts = [source[:last], source[last:own - low] + side[row, HALO:]]
+                if high > own:
+                    parts.append(source[own - low:])
+                source = jnp.concatenate(parts, axis=0)
             if i == 0 or i == rows - 1:
                 here = jnp.where(row // rows_dev == half, 0, 1)
                 source = source + rim[here, low:high]
@@ -203,25 +208,35 @@
 
     @pl.when(turn == ITERS * QUADS - 1)
     def _():
-        for pair in range(QUADS // 2):
+        for pair in range(pairs):
             for j in range(rows_dev):
-                for out_ref, side_at in ((keep_ref, half), (send_ref, 1 - half)):
+                for out_ref, side_at in ((keep_refs[pair], half), (send_refs[pair], 1 - half)):
                     row = rows_dev * side_at + j
                     both = jnp.concatenate(
                         [state[2 * pair, row, :own], state[2 * pair + 1, row, :own]], axis=0)
-                    out_ref[pair, :, j, :] = both.T[:quad_size]
-
-
-def merge_kernel(own, info, keep_ref, got_ref, out_ref):
+                    out_ref[:, j, :] = both.T[:quad_size]
+
+
+def merge_kernel(own, pair, chunks, info, keep_ref, got_ref, *rest):
+    out_ref, stage, sems = rest[-3:]
     half = info[ITERS * QUADS]
-    keep = keep_ref[0]
-    got = got_ref[0]
-    left = jnp.where(half == 0, keep, got)
-    right = jnp.where(half == 0, got, keep)
-    low = lax.broadcasted_iota(jnp.int32, keep.shape, 2) < own
-    axis = keep.ndim - 1
-    out_ref[0, 0] = jnp.where(low, left, pltpu.roll(right, own, axis))
-    out_ref[0, 1] = jnp.where(low, pltpu.roll(left, own, axis), right)
+    part = keep_ref.shape[0] // chunks
+    copies = []
+    for chunk in range(chunks):
+        span = pl.ds(chunk * part, part)
+        keep = keep_ref[span]
+        got = got_ref[span]
+        left = jnp.where(half == 0, keep, got)
+        right = jnp.where(half == 0, got, keep)
+        low = lax.broadcasted_iota(jnp.int32, keep.shape, 2) < own
+        stage[chunk, 0] = jnp.where(low, left, pltpu.roll(right, own, 2))
+        stage[chunk, 1] = jnp.where(low, pltpu.roll(left, own, 2), right)
+        for member in range(2):
+            copies.append(pltpu.make_async_copy(
+                stage.at[chunk, member], out_ref.at[2 * pair + member, span], sems.at[chunk, member]))
+            copies[-1].start()
+    for copy in copies:
+        copy.wait()
 
 
 def body(
@@ -294,14 +309,10 @@
                              concat_axis=0, tiled=True).reshape(slot_total, load)
 
     partner = lax.ppermute(held, axes, swap_route)
-    beside_same = lax.ppermute(held, axes, same_route)
-    beside_cross = lax.ppermute(held, axes, cross_route)
     is_low = half == 0
     chip = jnp.concatenate(
         [jnp.where(is_low, held, partner), jnp.where(is_low, partner, held)], axis=1)
-    near = jnp.concatenate(
-        [jnp.where(is_low, beside_same, beside_cross), jnp.where(is_low, beside_cross, beside_same)],
-        axis=1)
+    near = lax.ppermute(chip, axes, same_route)
     mine = jnp.where(is_low, chip[:, :, :own], chip[:, :, own:])
     right = jnp.where(is_low, chip[:, :, own], near[:, :, 0])
     left = jnp.where(is_low, near[:, :, cols_dev - 1], chip[:, :, own - 1])
@@ -363,9 +374,10 @@
         zeros = (0,) * len(shape)
         return pl.BlockSpec((1,) + shape, lambda t, info: (info[t],) + zeros)
 
-    packed = (QUADS // 2, quad_size, rows_dev, cols_dev)
-    whole = pl.BlockSpec(packed, lambda t, info: (0, 0, 0, 0))
-    keep, send = pl.pallas_call(
+    pairs = QUADS // 2
+    packed = jax.ShapeDtypeStruct((quad_size, rows_dev, cols_dev), jnp.float32)
+    in_vmem = pl.BlockSpec(memory_space=pltpu.VMEM)
+    halves = pl.pallas_call(
         lambda *refs: sweeps_kernel(rows, own, cells, quad_size, *refs),
         grid_spec=pltpu.PrefetchScalarGridSpec(
             num_scalar_prefetch=1,
@@ -375,7 +387,7 @@
             + [pl.BlockSpec((1, width), lambda t, info: (0, 0))]
             + [quad_block((block, width))] * 2
             + [quad_block((HALO, width))] * 2,
-            out_specs=[whole, whole],
+            out_specs=[in_vmem] * (2 * pairs),
             scratch_shapes=[
                 pltpu.VMEM((QUADS, rows, cells, width), jnp.float32),
                 pltpu.VMEM((QUADS, rows, cells, LANES), jnp.float32),
@@ -383,28 +395,28 @@
                 pltpu.VMEM((rows, 2 * HALO, width), jnp.float32),
             ],
         ),
-        out_shape=[jax.ShapeDtypeStruct(packed, jnp.float32)] * 2,
+        out_shape=[packed] * (2 * pairs),
         compiler_params=pltpu.CompilerParams(
             dimension_semantics=("arbitrary",), vmem_limit_bytes=56 * 2**20),
     )(info, ax, ay, base, wind, matrices, diagonal, scale[None], rim_own, rim_partner, rim_same, rim_cross)
 
-    got = lax.ppermute(send, axes, swap_route)
+    got = [lax.ppermute(half_out, axes, swap_route) for half_out in halves[pairs:]]
     chunks = 4
-    part = quad_size // chunks
-    half_block = pl.BlockSpec((1, part, rows_dev, cols_dev), lambda p, c, info: (p, c, 0, 0))
-    merged = pl.pallas_call(
-        lambda *refs: merge_kernel(own, *refs),
-        grid_spec=pltpu.PrefetchScalarGridSpec(
-            num_scalar_prefetch=1,
-            grid=(QUADS // 2, chunks),
-            in_specs=[half_block, half_block],
-            out_specs=pl.BlockSpec(
-                (1, 2, part, rows_dev, cols_dev), lambda p, c, info: (p, 0, c, 0, 0)),
-        ),
-        out_shape=jax.ShapeDtypeStruct((QUADS // 2, 2, quad_size, rows_dev, cols_dev), jnp.float32),
-        compiler_params=pltpu.CompilerParams(vmem_limit_bytes=16 * 2**20),
-    )(info, keep, got)
-    return merged.reshape(comps, rows_dev, cols_dev)
+    merged = []
+    for pair in range(pairs):
+        merged = [pl.pallas_call(
+            partial(merge_kernel, own, pair, chunks),
+            in_specs=[pl.BlockSpec(memory_space=pltpu.SMEM), in_vmem, in_vmem]
+            + [pl.BlockSpec(memory_space=pl.ANY)] * len(merged),
+            out_specs=pl.BlockSpec(memory_space=pl.ANY),
+            scratch_shapes=[
+                pltpu.VMEM((chunks, 2, quad_size // chunks, rows_dev, cols_dev), jnp.float32),
+                pltpu.SemaphoreType.DMA((chunks, 2))],
+            out_shape=jax.ShapeDtypeStruct((QUADS, quad_size, rows_dev, cols_dev), jnp.float32),
+            input_output_aliases={3: 0} if merged else {},
+            compiler_params=pltpu.CompilerParams(vmem_limit_bytes=16 * 2**20),
+        )(info, halves[pair], got[pair], *merged)]
+    return merged[0].reshape(comps, rows_dev, cols_dev)
 
 
 def solution(mesh):

time: 112 us -> 112 us (level); the launches traced: 110 us -> 112 us
  waiting for transfers between devices: 33.3 us -> 37.4 us
  starting transfers between devices: 21.6 us -> 19.3 us
    ppermute x3, waiting for transfers between devices: 3.53 us -> 34.6 us  [the longest x1 32.4 us: body(): near = lax.ppermute(chip, axes, same_route)]
    all_to_all x1, waiting for transfers between devices: 28.8 us -> 0.01 us  [body(): lax.all_to_all(outgoing.reshape(devices, CAP, load), axes, split_axis=0,...]
    ppermute x3, starting transfers between devices: 10.4 us -> 5.19 us  [the longest x1 3.99 us: body(): near = lax.ppermute(chip, axes, same_route)]
    ppermute x1, starting transfers between devices: 0.44 us -> 3.25 us  [body(): rim_partner = lax.ppermute(rim_send, axes, swap_route)]
    ppermute x1, starting transfers between devices: 3.95 us -> 2.1 us  [body(): rim_cross = lax.ppermute(out_cross, axes, cross_route)]
    ppermute x1, waiting for transfers between devices: 0.98 us -> 2.81 us  [body(): rim_cross = lax.ppermute(out_cross, axes, cross_route)]
    pallas_call x1 -> x2, Pallas kernels: 4.59 us -> 3.99 us  [body(): pl.pallas_call(partial(merge_kernel, own, pair, chunks), in_specs=[pl.Blo...]
    unnamed x32 -> x34, local copies, waits for them, and re-layouts: 4.84 us -> 4.53 us
  transfers between devices with their start and end apart: 8 -> 8, of which waited for: 3 -> 3; matrix products, arithmetic and copies ran while one was open for 13% -> 13% of each run, Pallas kernels for 3% -> 5%
where the time goes in v6:
time: 112 us
  waiting for transfers between devices  37.4 us (33%)
  Pallas kernels  34.6 us (31%)
  starting transfers between devices  19.3 us (17%)
  other arithmetic  12.6 us (11%)
  local copies, waits for them, and re-layouts  7.37 us (7%)
    ppermute x1, waiting for transfers between devices, body(): near = lax.ppermute(chip, axes, same_route)  32.4 us
    pallas_call x1, Pallas kernels, body(): pl.pallas_call(lambda *refs: sweeps_kernel(rows, own, cells, quad_size, *...  25.8 us
    select_n x1, other arithmetic, by_class(): jnp.where((class_here == kind)[None, :, :, None], table[:, None, None, ki...  6.65 us
    all_to_all x1, starting transfers between devices, body(): lax.all_to_all(outgoing.reshape(devices, CAP, load), axes, split_axis=0,...  5.69 us
    unnamed x34, local copies, waits for them, and re-layouts  4.53 us
    ppermute x1, starting transfers between devices, body(): near = lax.ppermute(chip, axes, same_route)  3.99 us
    pallas_call x2, Pallas kernels, body(): pl.pallas_call(partial(merge_kernel, own, pair, chunks), in_specs=[pl.Blo...  3.99 us
    pallas_call x1, Pallas kernels, body(): pl.pallas_call(lambda *refs: pack_kernel(shifts, col_count, rows, comps,...  3.31 us
  transfers between devices with their start and end apart: 8, of which 3 were waited for; matrix products, arithmetic and copies ran while one was open for 13% of the time, Pallas kernels for 5%

profile of v6, /device:TPU:17, one launch (start us, length us, event | category | flops | bytes accessed | tf_op | source)
XLA Modules:
  0.0 111.7 jit_solution(4903293840759139330)
XLA Ops:
  0.0 0.7 convert_bitcast_fusion
  0.8 0.7 pad_maximum_fusion.2
  1.5 0.7 collective-permute-start
  2.1 1.2 %copy-done.1 = f32[256,864]{0,1:T(8,128)S(1)} copy-done((f32[256,864]{0,1:T(8,128)S(1)}, f32[256,864]{0,1:T(8,128)}, u32[]{:S(2)}) %copy-start.1) | copy-done | bytes 884760
  3.3 0.7 copy-done.6
  4.0 3.3 %shard_map.109 = f32[512,896]{1,0:T(8,128)} custom-call(s32[1,256]{1,0:T(1,128)S(1)} %bitcast.49, f32[864,256]{1,0:T(8,128)S(1)} %bitcast.48), custom_call_target="tpu_custom_call" | custom-call | tf_op jit(solution)/shard_map/pallas_call | solution.py:287
  7.3 5.7 %all-to-all-start = ((f32[32,16,896]{2,1,0:T(8,128)}), f32[32,16,896]{2,1,0:T(8,128)S(1)}, u32[]{:S(2)}, u32[]{:S(2)}) async-start(f32[32,16,896]{2,1,0:T(8,128)} %bitcast.3), calls=%async_computation | async-start | bytes 3670016 | tf_op jit(solution)/shard_map/all_to_all | solution.py:308
  13.2 0.1 broadcast_in_dim.207
  13.3 0.1 broadcast_in_dim.195
  13.8 1.5 %copy.14 = f32[4,216,216]{1,2,0:T(8,128)S(1)} copy(f32[4,216,216]{2,1,0:T(8,128)} %param.19) | data formatting | bytes 1492992 | tf_op jit(solution)/shard_map/optimization_barrier | solution.py:300
  15.3 1.0 select_reduce_fusion
  16.5 0.1 tile.32
  16.7 4.0 %collective-permute-start.1 = (f32[3,16,128]{2,1,0:T(8,128)S(1)}, f32[3,16,128]{2,1,0:T(8,128)S(1)}, u32[]{:S(2)}, u32[]{:S(2)}) collective-permute-start(f32[3,16,128]{2,1,0:T(8,128)S(1)} %pad_maximum_fusion), channel_id=1, source_target_pairs={{0,1},{1,2},{2,3},{3,4},{4,5},{5,6},{6,7},{7,8},{8,9},{9,10},{10,1... | collective-permute-start | bytes 73736 | tf_op jit(solution)/shard_map/ppermute | solution.py:315
  20.7 32.4 %collective-permute-done.1 = f32[3,16,128]{2,1,0:T(8,128)S(1)} collective-permute-done((f32[3,16,128]{2,1,0:T(8,128)S(1)}, f32[3,16,128]{2,1,0:T(8,128)S(1)}, u32[]{:S(2)}, u32[]{:S(2)}) %collective-permute-start.1) | collective-permute-done | bytes 24608 | tf_op jit(solution)/shard_map/ppermute | solution.py:315
  53.4 0.2 broadcast_multiply_fusion
  53.6 2.7 %multiply_multiply_fusion.refs_4_ = f32[4,16,72,256]{3,2,1,0:T(8,128)} fusion(f32[4,256]{1,0:T(4,128)S(1)} %get-tuple-element.72, f32[16,72]{1,0:T(8,128)S(1)} %get-tuple-element.42, f32[4,256]{1,0:T(4,128)S(1)} %get-tuple-element.67, f32[16,72]{1,0:T(8,128)S(1)} %get-tuple-element.43, f32[16,72,256]{2,1,0:T(8,128)S(1)} %broadcast_multiply_fusion), kind=kLoop, calls=%fused_computation | loop fusion | flops 7077888 | bytes 5915648 | tf_op jit(solution)/shard_map/mul | solution.py:347
  56.4 6.7 %select_select_fusion = (f32[4,16,72,256]{3,2,1,0:T(8,128)}, f32[4,16,72,256]{3,2,1,0:T(8,128)}, f32[4,16,72,256]{3,2,1,0:T(8,128)}) fusion(f32[4,256]{1,0:T(4,128)S(1)} %get-tuple-element.50, f32[4,256]{1,0:T(4,128)S(1)} %get-tuple-element.51, f32[4,256]{1,0:T(4,128)S(1)} %get-tuple-element.52, f32[4,256]{1,0:T(4,128)S(1)} %get-tuple-element.49, ...), kind=kLoop, calls=%fused_computation.1 | loop fusion | flops 10616832 | bytes 14208384 | tf_op jit(solution)/shard_map/jit(_where)/select_n | solution.py:338
  63.0 1.5 %shard_map.110 = (f32[4,80,256]{2,1,0:T(8,128)S(1)}, f32[4,80,256]{2,1,0:T(8,128)S(1)}, f32[4,8,256]{2,1,0:T(8,128)S(1)}, f32[4,8,256]{2,1,0:T(8,128)S(1)}) custom-call(s32[9]{0:T(128)S(1)} %pad_add_fusion.refs_0_.info, f32[512,896]{1,0:T(8,128)S(1)} %bitcast.47), custom_call_target="tpu_custom_call" | custom-call | tf_op jit(solution)/shard_map/pallas_call | solution.py:356
  64.5 0.7 copy-done.3
  65.3 3.3 %collective-permute-start.2 = (f32[4,80,256]{2,1,0:T(8,128)S(1)}, f32[4,80,256]{2,1,0:T(8,128)S(1)}, u32[]{:S(2)}, u32[]{:S(2)}) collective-permute-start(f32[4,80,256]{2,1,0:T(8,128)S(1)} %get-tuple-element.30), channel_id=1, source_target_pairs={{16,0},{17,1},{18,2},{19,3},{20,4},{21,5},{22,6},{23,7},{24,8},{25... | collective-permute-start | bytes 983048 | tf_op jit(solution)/shard_map/ppermute | solution.py:367
  68.5 2.3 %collective-permute-start.3 = (f32[4,8,256]{2,1,0:T(8,128)S(1)}, f32[4,8,256]{2,1,0:T(8,128)S(1)}, u32[]{:S(2)}, u32[]{:S(2)}) collective-permute-start(f32[4,8,256]{2,1,0:T(8,128)S(1)} %get-tuple-element.31), channel_id=1, source_target_pairs={{0,1},{1,2},{2,3},{3,4},{4,5},{5,6},{6,7},{7,8},{8,9},{9,10},{10,1... | collective-permute-start | bytes 98312 | tf_op jit(solution)/shard_map/ppermute | solution.py:368
  70.9 2.1 %collective-permute-start.4 = (f32[4,8,256]{2,1,0:T(8,128)S(1)}, f32[4,8,256]{2,1,0:T(8,128)S(1)}, u32[]{:S(2)}, u32[]{:S(2)}) collective-permute-start(f32[4,8,256]{2,1,0:T(8,128)S(1)} %get-tuple-element.32), channel_id=1, source_target_pairs={{16,1},{17,2},{18,3},{19,4},{20,5},{21,6},{22,7},{23,8},{24,9},{25... | collective-permute-start | bytes 98312 | tf_op jit(solution)/shard_map/ppermute | solution.py:369
  73.0 0.6 broadcast_in_dim.226.refs_6_
  73.6 2.8 %collective-permute-done.4.refs_11_ = f32[4,8,256]{2,1,0:T(8,128)S(1)} collective-permute-done((f32[4,8,256]{2,1,0:T(8,128)S(1)}, f32[4,8,256]{2,1,0:T(8,128)S(1)}, u32[]{:S(2)}, u32[]{:S(2)}) %collective-permute-start.4) | collective-permute-done | bytes 32800 | tf_op jit(solution)/shard_map/ppermute | solution.py:369
  76.4 0.6 copy-done.9
  77.0 0.2 copy-done.7
  77.2 25.8 %shard_map.111 = (f32[216,8,128]{2,1,0:T(8,128)}, f32[216,8,128]{2,1,0:T(8,128)}, f32[216,8,128]{2,1,0:T(8,128)}, f32[216,8,128]{2,1,0:T(8,128)}) custom-call(s32[9]{0:T(128)} %copy-done.4, f32[4,16,72,256]{3,2,1,0:T(8,128)} %get-tuple-element.23.refs_1_, f32[4,16,72,256]{3,2,1,0:T(8,128)} %get-tuple-element.24.refs_2_, ...), custom_call_target="tpu_custom_call" | custom-call | tf_op jit(solution)/shard_map/pallas_call | solution.py:380
  103.0 1.1 %collective-permute-start.6 = (f32[216,8,128]{2,1,0:T(8,128)}, f32[216,8,128]{2,1,0:T(8,128)S(1)}, u32[]{:S(2)}, u32[]{:S(2)}) collective-permute-start(f32[216,8,128]{2,1,0:T(8,128)} %get-tuple-element.36), channel_id=1, source_target_pairs={{16,0},{17,1},{18,2},{19,3},{20,4},{21,5},{22,6},{23,7},{24,8},{25... | collective-permute-start | bytes 2654216 | tf_op jit(solution)/shard_map/ppermute | solution.py:403
  104.2 2.2 %collective-permute-done.6.got_ref = f32[216,8,128]{2,1,0:T(8,128)S(1)} collective-permute-done((f32[216,8,128]{2,1,0:T(8,128)}, f32[216,8,128]{2,1,0:T(8,128)S(1)}, u32[]{:S(2)}, u32[]{:S(2)}) %collective-permute-start.6) | collective-permute-done | bytes 884768 | tf_op jit(solution)/shard_map/ppermute | solution.py:403
  106.3 1.2 %copy-done.2 = f32[216,8,128]{2,1,0:T(8,128)S(1)} copy-done((f32[216,8,128]{2,1,0:T(8,128)S(1)}, f32[216,8,128]{2,1,0:T(8,128)}, u32[]{:S(2)}) %copy-start.2) | copy-done | bytes 884760
  107.5 2.0 %shard_map.112.rest_0_ = f32[4,216,8,128]{3,2,1,0:T(8,128)} custom-call(s32[9]{0:T(128)S(1)} %copy-done.5, f32[216,8,128]{2,1,0:T(8,128)S(1)} %copy-done.2, f32[216,8,128]{2,1,0:T(8,128)S(1)} %collective-permute-done.6.got_ref), custom_call_target="tpu_custom_call" | custom-call | tf_op jit(solution)/shard_map/pallas_call | solution.py:407
  109.5 2.0 %shard_map.113 = f32[4,216,8,128]{3,2,1,0:T(8,128)} custom-call(s32[9]{0:T(128)S(1)} %copy-done.5, f32[216,8,128]{2,1,0:T(8,128)S(1)} %copy-done, f32[216,8,128]{2,1,0:T(8,128)S(1)} %collective-permute-done.5.got_ref, f32[4,216,8,128]{3,2,1,0:T(8,128)} %shard_map.112.rest_0_), custom_call_target="tpu_custom_call", output_to_operand_aliasing={{}: (3, {})} | custom-call | tf_op jit(solution)/shard_map/pallas_call | solution.py:407
  (63 shorter events, 1.2 us)
Async XLA Ops:
  0.0 15.3 %copy-start.14 = (f32[256]{0:T(256)S(1)}, f32[256]{0:T(256)}, u32[]{:S(2)}) copy-start(f32[256]{0:T(256)} %constant.45) | copy-start | bytes 3076
  0.0 13.4 %copy-start.12 = (f32[4,24]{1,0:T(4,128)S(1)}, f32[4,24]{1,0:T(4,128)}, u32[]{:S(2)}) copy-start(f32[4,24]{1,0:T(4,128)} %param.14) | copy-start | bytes 1156
  0.0 13.5 %copy-start.13 = (f32[4,24]{1,0:T(4,128)S(1)}, f32[4,24]{1,0:T(4,128)}, u32[]{:S(2)}) copy-start(f32[4,24]{1,0:T(4,128)} %param.15) | copy-start | bytes 1156
  0.0 13.7 %copy-start.16 = (s32[2,4]{1,0:T(2,128)S(1)}, s32[2,4]{1,0:T(2,128)}, u32[]{:S(2)}) copy-start(s32[2,4]{1,0:T(2,128)} %param.20) | copy-start | bytes 100
  1.5 15.2 %collective-permute-start = (f32[3,8,128]{2,1,0:T(8,128)S(1)}, f32[3,8,128]{2,1,0:T(8,128)S(1)}, u32[]{:S(2)}, u32[]{:S(2)}) collective-permute-start(f32[3,8,128]{2,1,0:T(8,128)S(1)} %pad_maximum_fusion.2), channel_id=1, source_target_pairs={{16,0},{17,1},{18,2},{19,3},{20,4},{21,5},{22,6},{23,7},{24,8},{25... | collective-permute-start | bytes 36872 | tf_op jit(solution)/shard_map/ppermute | solution.py:311
  2.1 1.2 %copy-start.1 = (f32[256,864]{0,1:T(8,128)S(1)}, f32[256,864]{0,1:T(8,128)}, u32[]{:S(2)}) copy-start(f32[256,864]{0,1:T(8,128)} %param.17) | copy-start | bytes 2654212
  3.3 0.7 copy-start.6
  4.0 12.5 %copy-start.15 = (f32[24]{0:T(128)S(1)}, f32[24]{0:T(128)}, u32[]{:S(2)}) copy-start(f32[24]{0:T(128)} %param.16) | copy-start | bytes 292
  4.0 12.7 %copy-start.10 = (f32[8,128]{1,0:T(8,128)S(1)}, f32[8,128]{1,0:T(8,128)}, u32[]{:S(2)}) copy-start(f32[8,128]{1,0:T(8,128)} %param.12) | copy-start | bytes 12292
  4.0 12.7 %copy-start.11 = (f32[8,128]{1,0:T(8,128)S(1)}, f32[8,128]{1,0:T(8,128)}, u32[]{:S(2)}) copy-start(f32[8,128]{1,0:T(8,128)} %param.11) | copy-start | bytes 12292
  7.3 55.7 %all-to-all-start = ((f32[32,16,896]{2,1,0:T(8,128)}), f32[32,16,896]{2,1,0:T(8,128)S(1)}, u32[]{:S(2)}, u32[]{:S(2)}) async-start(f32[32,16,896]{2,1,0:T(8,128)} %bitcast.3), calls=%async_computation | async-start | bytes 3670016 | tf_op jit(solution)/shard_map/all_to_all | solution.py:308
  16.5 46.6 %copy-start.4 = (s32[9]{0:T(128)}, s32[9]{0:T(128)S(1)}, u32[]{:S(2)}) copy-start(s32[9]{0:T(128)S(1)} %pad_add_fusion.refs_0_.info) | copy-start | bytes 112
  16.7 36.5 %collective-permute-start.1 = (f32[3,16,128]{2,1,0:T(8,128)S(1)}, f32[3,16,128]{2,1,0:T(8,128)S(1)}, u32[]{:S(2)}, u32[]{:S(2)}) collective-permute-start(f32[3,16,128]{2,1,0:T(8,128)S(1)} %pad_maximum_fusion), channel_id=1, source_target_pairs={{0,1},{1,2},{2,3},{3,4},{4,5},{5,6},{6,7},{7,8},{8,9},{9,10},{10,1... | collective-permute-start | bytes 73736 | tf_op jit(solution)/shard_map/ppermute | solution.py:315
  64.5 0.7 copy-start.3
  65.3 11.1 %collective-permute-start.2 = (f32[4,80,256]{2,1,0:T(8,128)S(1)}, f32[4,80,256]{2,1,0:T(8,128)S(1)}, u32[]{:S(2)}, u32[]{:S(2)}) collective-permute-start(f32[4,80,256]{2,1,0:T(8,128)S(1)} %get-tuple-element.30), channel_id=1, source_target_pairs={{16,0},{17,1},{18,2},{19,3},{20,4},{21,5},{22,6},{23,7},{24,8},{25... | collective-permute-start | bytes 983048 | tf_op jit(solution)/shard_map/ppermute | solution.py:367
  68.5 5.1 %collective-permute-start.3 = (f32[4,8,256]{2,1,0:T(8,128)S(1)}, f32[4,8,256]{2,1,0:T(8,128)S(1)}, u32[]{:S(2)}, u32[]{:S(2)}) collective-permute-start(f32[4,8,256]{2,1,0:T(8,128)S(1)} %get-tuple-element.31), channel_id=1, source_target_pairs={{0,1},{1,2},{2,3},{3,4},{4,5},{5,6},{6,7},{7,8},{8,9},{9,10},{10,1... | collective-permute-start | bytes 98312 | tf_op jit(solution)/shard_map/ppermute | solution.py:368
  70.9 5.5 %collective-permute-start.4 = (f32[4,8,256]{2,1,0:T(8,128)S(1)}, f32[4,8,256]{2,1,0:T(8,128)S(1)}, u32[]{:S(2)}, u32[]{:S(2)}) collective-permute-start(f32[4,8,256]{2,1,0:T(8,128)S(1)} %get-tuple-element.32), channel_id=1, source_target_pairs={{16,1},{17,2},{18,3},{19,4},{20,5},{21,6},{22,7},{23,8},{24,9},{25... | collective-permute-start | bytes 98312 | tf_op jit(solution)/shard_map/ppermute | solution.py:369
  73.6 2.8 %copy-start.8 = (f32[4,8,256]{2,1,0:T(8,128)}, f32[4,8,256]{2,1,0:T(8,128)S(1)}, u32[]{:S(2)}) copy-start(f32[4,8,256]{2,1,0:T(8,128)S(1)} %collective-permute-done.3.refs_10_) | copy-start | bytes 98308
  76.4 0.6 copy-start.9
  76.4 0.8 copy-start.7
  77.2 29.2 %copy-start.5 = (s32[9]{0:T(128)S(1)}, s32[9]{0:T(128)}, u32[]{:S(2)}) copy-start(s32[9]{0:T(128)} %copy-done.4) | copy-start | bytes 112
  103.0 6.6 %copy-start = (f32[216,8,128]{2,1,0:T(8,128)S(1)}, f32[216,8,128]{2,1,0:T(8,128)}, u32[]{:S(2)}) copy-start(f32[216,8,128]{2,1,0:T(8,128)} %get-tuple-element.33.keep_ref) | copy-start | bytes 2654212
  103.0 3.4 %collective-permute-start.6 = (f32[216,8,128]{2,1,0:T(8,128)}, f32[216,8,128]{2,1,0:T(8,128)S(1)}, u32[]{:S(2)}, u32[]{:S(2)}) collective-permute-start(f32[216,8,128]{2,1,0:T(8,128)} %get-tuple-element.36), channel_id=1, source_target_pairs={{16,0},{17,1},{18,2},{19,3},{20,4},{21,5},{22,6},{23,7},{24,8},{25... | collective-permute-start | bytes 2654216 | tf_op jit(solution)/shard_map/ppermute | solution.py:403
  104.1 5.4 %collective-permute-start.5 = (f32[216,8,128]{2,1,0:T(8,128)}, f32[216,8,128]{2,1,0:T(8,128)S(1)}, u32[]{:S(2)}, u32[]{:S(2)}) collective-permute-start(f32[216,8,128]{2,1,0:T(8,128)} %get-tuple-element.34), channel_id=1, source_target_pairs={{16,0},{17,1},{18,2},{19,3},{20,4},{21,5},{22,6},{23,7},{24,8},{25... | collective-permute-start | bytes 2654216 | tf_op jit(solution)/shard_map/ppermute | solution.py:403
  106.3 1.2 %copy-start.2 = (f32[216,8,128]{2,1,0:T(8,128)S(1)}, f32[216,8,128]{2,1,0:T(8,128)}, u32[]{:S(2)}) copy-start(f32[216,8,128]{2,1,0:T(8,128)} %get-tuple-element.35.keep_ref) | copy-start | bytes 2654212

commit v7 on v6

--- a/solution.py
+++ b/solution.py
@@ -116,6 +116,7 @@
 
 
 def sweeps_kernel(rows, own, cells, quad_size, info, ax_ref, ay_ref, base_ref, wind_ref, mt_ref, diag_ref, scale_ref,
+                  ax_table, base_table, lane_table, far_ref,
                   own_ref, par_ref, same_ref, cross_ref, *rest):
     pairs = QUADS // 2
     keep_refs, send_refs = rest[:pairs], rest[pairs:2 * pairs]
@@ -138,6 +139,8 @@
     rim[0, own:cells] = own_ref[0, own:cells] + same_ref[0]
     rim[1] = par_ref[0, 0:cells]
     rim[1, own:cells] = par_ref[0, own:cells] + cross_ref[0]
+    far_at = jnp.where(half == 0, HALO - 1, 0)
+    at_far = lax.broadcasted_iota(jnp.int32, (HALO, width), 0) == far_at
     edge_at = jnp.where(half == 0, 0, 2 * HALO - 1)
     at_edge = lax.broadcasted_iota(jnp.int32, (2 * HALO, width), 0) == edge_at
     for j in range(rows_dev):
@@ -147,26 +150,38 @@
         side[j + rows_dev * (1 - half)] = theirs
 
     def run(count, second):
-        chains = [(0, own // 2), (own // 2, count)]
+        chains = [(0, count)]
+
+        def patched(block, far_row):
+            if second:
+                return block
+            return jnp.concatenate([block[:own], jnp.where(at_far, far_row, block[own:])], axis=0)
 
         def factors(i, low, high):
             row = first_row + i * step_x
+            kind = far_ref[0, row]
+            far_ax = jnp.zeros((1, width), jnp.float32)
+            far_base = jnp.zeros((1, width), jnp.float32)
+            for each in range(ax_table.shape[1]):
+                far_ax = jnp.where(kind == each, ax_table[0, each:each + 1], far_ax)
+                far_base = jnp.where(kind == each, base_table[0, each:each + 1], far_base)
+            spread = jnp.maximum(
+                far_ref[2, row] * lane_table[0, 1:2] + far_ref[3, row] * lane_table[0, 2:3], 0.0)
+            far_wind = (lane_table[0, 0:1] * far_ref[1, row]) * (spread * spread)
             total = power[0, row, low:high]
             for other in range(1, QUADS):
                 total = total + power[other, row, low:high]
             level = total * (1.0 / (QUADS * quad_size))
             damping = whitecap_rate * level / (1.0 + level)
-            den = base_ref[0, row, low:high] + jnp.concatenate([damping] * (width // LANES), axis=1)
+            den = patched(base_ref[0, row, low:high], far_base) + jnp.concatenate([damping] * (width // LANES), axis=1)
             inverse = scale_ref[...] / den
-            source = wind_ref[0, row, low:high]
-            if low == 0:
-                source = jnp.concatenate([source[:HALO] + side[row, :HALO], source[HALO:]], axis=0)
-            else:
-                last = own - HALO - low
-                parts = [source[:last], source[last:own - low] + side[row, HALO:]]
-                if high > own:
-                    parts.append(source[own - low:])
-                source = jnp.concatenate(parts, axis=0)
+            source = patched(wind_ref[0, row, low:high], far_wind)
+            edge = side[row]
+            parts = [source[:HALO] + edge[:HALO], source[HALO:own - HALO],
+                     source[own - HALO:own] + edge[HALO:]]
+            if high > own:
+                parts.append(source[own:])
+            source = jnp.concatenate(parts, axis=0)
             if i == 0 or i == rows - 1:
                 here = jnp.where(row // rows_dev == half, 0, 1)
                 source = source + rim[here, low:high]
@@ -174,7 +189,7 @@
                 before = state[quad, row]
                 shifted = jnp.where(up_y, pltpu.roll(before, 1, 0), pltpu.roll(before, cells - 1, 0))
                 source = source + ay_ref[0, row, low:high] * shifted[low:high]
-            return ax_ref[0, row, low:high] * inverse, source * inverse
+            return patched(ax_ref[0, row, low:high], far_ax) * inverse, source * inverse
 
         ready = [factors(0, *chain) for chain in chains]
         upwind = [None] * len(chains)
@@ -284,11 +299,11 @@
     assert all(size == 2**shift for size, shift in zip(sizes, shifts))
     slot_total = devices * CAP
     steps = 4
+    in_vmem = pl.BlockSpec(memory_space=pltpu.VMEM)
     outgoing = pl.pallas_call(
         lambda *refs: pack_kernel(shifts, col_count, rows, comps, *refs),
         grid=(steps,),
-        in_specs=[pl.BlockSpec((1, points), lambda s: (0, 0)),
-                  pl.BlockSpec((comps, points), lambda s: (0, 0))],
+        in_specs=[in_vmem, in_vmem],
         out_specs=pl.BlockSpec((slot_total // steps, load), lambda s: (s, 0)),
         scratch_shapes=[pltpu.VMEM((load, points), jnp.bfloat16),
                         pltpu.VMEM((load, points), jnp.bfloat16),
@@ -312,15 +327,16 @@
     is_low = half == 0
     chip = jnp.concatenate(
         [jnp.where(is_low, held, partner), jnp.where(is_low, partner, held)], axis=1)
-    near = lax.ppermute(chip, axes, same_route)
-    mine = jnp.where(is_low, chip[:, :, :own], chip[:, :, own:])
-    right = jnp.where(is_low, chip[:, :, own], near[:, :, 0])
-    left = jnp.where(is_low, near[:, :, cols_dev - 1], chip[:, :, own - 1])
+    strength = (chip[0] * 0.1) ** 2
+    feats = jnp.stack([chip[2], strength, jnp.cos(chip[1]), jnp.sin(chip[1])])
+    far = lax.ppermute(
+        jnp.where(is_low, feats[:, :, cols_dev - 1], feats[:, :, 0]), axes, same_route)
+    mine = jnp.where(is_low, feats[:, :, :own], feats[:, :, own:])
+    right = jnp.where(is_low, feats[:, :, own], 0.0)
+    left = jnp.where(is_low, 0.0, feats[:, :, own - 1])
     grid = jnp.concatenate(
-        [mine, right[:, :, None], jnp.zeros((3, rows, HALO - 2), jnp.float32), left[:, :, None]], axis=2)
-    speed_here, dir_here, class_here = grid[0], grid[1], grid[2]
-    strength = (speed_here * 0.1) ** 2
-    cos_here, sin_here = jnp.cos(dir_here), jnp.sin(dir_here)
+        [mine, right[:, :, None], jnp.zeros((4, rows, HALO - 2), jnp.float32), left[:, :, None]], axis=2)
+    class_here, strength, cos_here, sin_here = grid[0], grid[1], grid[2], grid[3]
 
     angle = (jnp.arange(NDIR, dtype=jnp.float32) + 0.5) * (2.0 * math.pi / NDIR)
     cos_lane = pad_to(jnp.repeat(jnp.cos(angle), NFREQ).reshape(QUADS, quad_size), 1, width)
@@ -332,6 +348,9 @@
     ay_table = jnp.abs(sin_lane)[:, None] * speed_lane[None]
     base_table = ax_table + ay_table + loss_lane[None]
 
+    lane_table = jnp.stack(
+        [jnp.broadcast_to(rate_lane, (QUADS, width)), cos_lane, sin_lane], axis=1)
+
     def by_class(table):
         chosen = jnp.broadcast_to(table[:, None, None, 0], (QUADS, rows, cells, width))
         for kind in range(1, class_count):
@@ -354,15 +373,11 @@
     rim_shapes = [jax.ShapeDtypeStruct((QUADS, size, width), jnp.float32)
                   for size in (block, block, HALO, HALO)]
     rim_own, rim_send, out_same, out_cross = pl.pallas_call(
-        lambda *refs: rim_kernel(own, rows_dev, comps, quad_size, *refs),
-        grid_spec=pltpu.PrefetchScalarGridSpec(
-            num_scalar_prefetch=1,
-            grid=(1,),
-            in_specs=[pl.BlockSpec((slot_total, load), lambda s, info: (0, 0))],
-            out_specs=[pl.BlockSpec(shape.shape, lambda s, info: (0, 0, 0)) for shape in rim_shapes],
-        ),
+        partial(rim_kernel, own, rows_dev, comps, quad_size),
+        in_specs=[pl.BlockSpec(memory_space=pltpu.SMEM), in_vmem],
+        out_specs=[in_vmem] * len(rim_shapes),
         out_shape=rim_shapes,
-        compiler_params=pltpu.CompilerParams(vmem_limit_bytes=48 * 2**20),
+        compiler_params=pltpu.CompilerParams(vmem_limit_bytes=40 * 2**20),
     )(info, arrived)
     rim_partner = lax.ppermute(rim_send, axes, swap_route)
     rim_same = lax.ppermute(out_same, axes, same_route)
@@ -376,7 +391,6 @@
 
     pairs = QUADS // 2
     packed = jax.ShapeDtypeStruct((quad_size, rows_dev, cols_dev), jnp.float32)
-    in_vmem = pl.BlockSpec(memory_space=pltpu.VMEM)
     halves = pl.pallas_call(
         lambda *refs: sweeps_kernel(rows, own, cells, quad_size, *refs),
         grid_spec=pltpu.PrefetchScalarGridSpec(
@@ -385,6 +399,8 @@
             in_specs=[quad_block((rows, cells, width))] * 4
             + [quad_block((width, width)), quad_block((1, width))]
             + [pl.BlockSpec((1, width), lambda t, info: (0, 0))]
+            + [quad_block((class_count, width))] * 2 + [quad_block((3, width))]
+            + [pl.BlockSpec(memory_space=pltpu.SMEM)]
             + [quad_block((block, width))] * 2
             + [quad_block((HALO, width))] * 2,
             out_specs=[in_vmem] * (2 * pairs),
@@ -397,8 +413,9 @@
         ),
         out_shape=[packed] * (2 * pairs),
         compiler_params=pltpu.CompilerParams(
-            dimension_semantics=("arbitrary",), vmem_limit_bytes=56 * 2**20),
-    )(info, ax, ay, base, wind, matrices, diagonal, scale[None], rim_own, rim_partner, rim_same, rim_cross)
+            dimension_semantics=("arbitrary",), vmem_limit_bytes=49 * 2**20),
+    )(info, ax, ay, base, wind, matrices, diagonal, scale[None], ax_table, base_table,
+      lane_table, far, rim_own, rim_partner, rim_same, rim_cross)
 
     got = [lax.ppermute(half_out, axes, swap_route) for half_out in halves[pairs:]]
     chunks = 4

time: 112 us -> 100 us (0.89)
  waiting for transfers between devices: 37.4 us -> 33.1 us
  local copies, waits for them, and re-layouts: 7.37 us -> 4.2 us
  Pallas kernels: 34.6 us -> 32 us
    ppermute x1, waiting for transfers between devices: 32.4 us -> 0.01 us  [body(): lax.ppermute(jnp.where(is_low, feats[:, :, cols_dev - 1], feats[:, :, 0])...]
    all_to_all x1, waiting for transfers between devices: 0.01 us -> 29.3 us  [body(): lax.all_to_all(outgoing.reshape(devices, CAP, load), axes, split_axis=0,...]
    ppermute x1, starting transfers between devices: 3.25 us -> 0.51 us  [body(): rim_partner = lax.ppermute(rim_send, axes, swap_route)]
    pallas_call x1, Pallas kernels: 25.8 us -> 23.2 us  [body(): pl.pallas_call(lambda *refs: sweeps_kernel(rows, own, cells, quad_size, *...]
    unnamed x34 -> x32, local copies, waits for them, and re-layouts: 4.53 us -> 1.91 us
    ppermute x2, starting transfers between devices: 1.2 us -> 3.75 us  [body(): lax.ppermute(half_out, axes, swap_route)]
    ppermute x1, starting transfers between devices: 3.99 us -> 1.92 us  [body(): lax.ppermute(jnp.where(is_low, feats[:, :, cols_dev - 1], feats[:, :, 0])...]
    ppermute x1, starting transfers between devices: 2.1 us -> 3.65 us  [body(): rim_cross = lax.ppermute(out_cross, axes, cross_route)]
where the time goes in v7:
time: 100 us
  waiting for transfers between devices  33.1 us (33%)
  Pallas kernels  32 us (32%)
  starting transfers between devices  18.4 us (18%)
  other arithmetic  11.9 us (12%)
  local copies, waits for them, and re-layouts  4.2 us (4%)
    all_to_all x1, waiting for transfers between devices, body(): lax.all_to_all(outgoing.reshape(devices, CAP, load), axes, split_axis=0,...  29.3 us
    pallas_call x1, Pallas kernels, body(): pl.pallas_call(lambda *refs: sweeps_kernel(rows, own, cells, quad_size, *...  23.2 us
    select_n x1, other arithmetic, by_class(): jnp.where((class_here == kind)[None, :, :, None], table[:, None, None, ki...  6.67 us
    all_to_all x1, starting transfers between devices, body(): lax.all_to_all(outgoing.reshape(devices, CAP, load), axes, split_axis=0,...  5.69 us
    pallas_call x2, Pallas kernels, body(): pl.pallas_call(partial(merge_kernel, own, pair, chunks), in_specs=[pl.Blo...  4 us
    ppermute x2, starting transfers between devices, body(): lax.ppermute(half_out, axes, swap_route)  3.75 us
    ppermute x1, starting transfers between devices, body(): rim_cross = lax.ppermute(out_cross, axes, cross_route)  3.65 us
    pallas_call x1, Pallas kernels, body(): pl.pallas_call(lambda *refs: pack_kernel(shifts, col_count, rows, comps,...  3.31 us
  transfers between devices with their start and end apart: 8, of which 3 were waited for; matrix products, arithmetic and copies ran while one was open for 13% of the time, Pallas kernels for 5%

profile of v7, /device:TPU:17, one launch (start us, length us, event | category | flops | bytes accessed | tf_op | source)
XLA Modules:
  0.0 100.0 jit_solution(7645286602517540425)
XLA Ops:
  0.0 0.7 convert_bitcast_fusion
  0.8 0.7 pad_maximum_fusion.3
  1.5 0.7 collective-permute-start
  2.1 1.2 %copy-done = f32[256,864]{0,1:T(8,128)S(1)} copy-done((f32[256,864]{0,1:T(8,128)S(1)}, f32[256,864]{0,1:T(8,128)}, u32[]{:S(2)}) %copy-start) | copy-done | bytes 884760
  3.3 0.7 copy-done.1
  4.0 3.3 %shard_map.109 = f32[512,896]{1,0:T(8,128)} custom-call(s32[1,256]{1,0:T(1,128)S(1)} %bitcast.61, f32[864,256]{1,0:T(8,128)S(1)} %bitcast.60), custom_call_target="tpu_custom_call" | custom-call | tf_op jit(solution)/shard_map/pallas_call | solution.py:303
  7.3 5.7 %all-to-all-start = ((f32[32,16,896]{2,1,0:T(8,128)}), f32[32,16,896]{2,1,0:T(8,128)S(1)}, u32[]{:S(2)}, u32[]{:S(2)}) async-start(f32[32,16,896]{2,1,0:T(8,128)} %bitcast.3), calls=%async_computation | async-start | bytes 3670016 | tf_op jit(solution)/shard_map/all_to_all | solution.py:323
  13.2 0.1 broadcast_in_dim.211
  13.3 0.1 broadcast_in_dim.199
  13.7 0.1 reshape.89
  13.8 1.5 %copy.14 = f32[4,216,216]{1,2,0:T(8,128)S(1)} copy(f32[4,216,216]{2,1,0:T(8,128)} %param.19) | data formatting | bytes 1492992 | tf_op jit(solution)/shard_map/optimization_barrier | solution.py:315
  15.4 0.3 select_reduce_fusion
  15.6 0.1 pad_add_fusion.info.refs_0_
  15.7 0.1 tile.32
  16.2 0.2 fusion
  16.3 0.1 pad_maximum_fusion.1
  16.5 0.2 broadcast_multiply_fusion
  16.7 2.7 %multiply_multiply_fusion.refs_4_ = f32[4,16,72,256]{3,2,1,0:T(8,128)} fusion(f32[4,256]{1,0:T(4,128)S(1)} %get-tuple-element.77, f32[16,72]{1,0:T(8,128)S(1)} %get-tuple-element.43, f32[4,256]{1,0:T(4,128)S(1)} %get-tuple-element.72, f32[16,72]{1,0:T(8,128)S(1)} %get-tuple-element.44, f32[16,72,256]{2,1,0:T(8,128)S(1)} %broadcast_multiply_fusion), kind=kLoop, calls=%fused_computation | loop fusion | flops 7077888 | bytes 5915648 | tf_op jit(solution)/shard_map/mul | solution.py:366
  19.4 6.7 %select_select_fusion = (f32[4,16,72,256]{3,2,1,0:T(8,128)}, f32[4,16,72,256]{3,2,1,0:T(8,128)}, f32[4,16,72,256]{3,2,1,0:T(8,128)}) fusion(f32[4,256]{1,0:T(4,128)S(1)} %bitcast.68, f32[4,256]{1,0:T(4,128)S(1)} %bitcast.69, f32[4,256]{1,0:T(4,128)S(1)} %bitcast.70, f32[4,256]{1,0:T(4,128)S(1)} %bitcast.67, pred[16,72]{1,0:T(8,128)(4,1)S(1)} %get-tuple-element.47, ...), kind=kLoop, calls=%fused_computation.1 | loop fusion | flops 10616832 | bytes 14208384 | tf_op jit(solution)/shard_map/jit(_where)/select_n | solution.py:357
  26.0 29.3 %all-to-all-done = f32[32,16,896]{2,1,0:T(8,128)S(1)} async-done(((f32[32,16,896]{2,1,0:T(8,128)}), f32[32,16,896]{2,1,0:T(8,128)S(1)}, u32[]{:S(2)}, u32[]{:S(2)}) %all-to-all-start) | async-done | bytes 1835040 | tf_op jit(solution)/shard_map/all_to_all | solution.py:323
  55.4 1.5 %shard_map.110 = (f32[4,80,256]{2,1,0:T(8,128)S(1)}, f32[4,80,256]{2,1,0:T(8,128)S(1)}, f32[4,8,256]{2,1,0:T(8,128)S(1)}, f32[4,8,256]{2,1,0:T(8,128)S(1)}) custom-call(s32[9]{0:T(128)S(1)} %pad_add_fusion.info.refs_0_, f32[512,896]{1,0:T(8,128)S(1)} %bitcast.59), custom_call_target="tpu_custom_call" | custom-call | tf_op jit(solution)/shard_map/pallas_call | solution.py:375
  56.9 0.5 collective-permute-start.2
  57.4 1.9 %collective-permute-start.1 = (f32[4,16]{1,0:T(4,128)S(1)}, f32[4,16]{1,0:T(4,128)S(1)}, u32[]{:S(2)}, u32[]{:S(2)}) collective-permute-start(f32[4,16]{1,0:T(4,128)S(1)} %get-tuple-element.39), channel_id=1, source_target_pairs={{0,1},{1,2},{2,3},{3,4},{4,5},{5,6},{6,7},{7,8},{8,9},{9,10},{10,1... | collective-permute-start | bytes 776 | tf_op jit(solution)/shard_map/ppermute | solution.py:332
  59.3 2.2 %collective-permute-start.3 = (f32[4,8,256]{2,1,0:T(8,128)S(1)}, f32[4,8,256]{2,1,0:T(8,128)S(1)}, u32[]{:S(2)}, u32[]{:S(2)}) collective-permute-start(f32[4,8,256]{2,1,0:T(8,128)S(1)} %get-tuple-element.31), channel_id=1, source_target_pairs={{0,1},{1,2},{2,3},{3,4},{4,5},{5,6},{6,7},{7,8},{8,9},{9,10},{10,1... | collective-permute-start | bytes 98312 | tf_op jit(solution)/shard_map/ppermute | solution.py:383
  61.6 3.6 %collective-permute-start.4 = (f32[4,8,256]{2,1,0:T(8,128)S(1)}, f32[4,8,256]{2,1,0:T(8,128)S(1)}, u32[]{:S(2)}, u32[]{:S(2)}) collective-permute-start(f32[4,8,256]{2,1,0:T(8,128)S(1)} %get-tuple-element.32), channel_id=1, source_target_pairs={{16,1},{17,2},{18,3},{19,4},{20,5},{21,6},{22,7},{23,8},{24,9},{25... | collective-permute-start | bytes 98312 | tf_op jit(solution)/shard_map/ppermute | solution.py:384
  65.3 1.8 %collective-permute-done.4.refs_15_ = f32[4,8,256]{2,1,0:T(8,128)S(1)} collective-permute-done((f32[4,8,256]{2,1,0:T(8,128)S(1)}, f32[4,8,256]{2,1,0:T(8,128)S(1)}, u32[]{:S(2)}, u32[]{:S(2)}) %collective-permute-start.4) | collective-permute-done | bytes 32800 | tf_op jit(solution)/shard_map/ppermute | solution.py:384
  67.1 23.2 %shard_map.111 = (f32[216,8,128]{2,1,0:T(8,128)S(1)}, f32[216,8,128]{2,1,0:T(8,128)S(1)}, f32[216,8,128]{2,1,0:T(8,128)S(1)}, f32[216,8,128]{2,1,0:T(8,128)S(1)}) custom-call(s32[9]{0:T(128)S(1)} %pad_add_fusion.info.refs_0_, f32[4,16,72,256]{3,2,1,0:T(8,128)} %get-tuple-element.23.refs_1_, f32[4,16,72,256]{3,2,1,0:T(8,128)} %get-tuple-element.24.refs_2_, ...), custom_call_target="tpu_custom_call" | custom-call | tf_op jit(solution)/shard_map/pallas_call | solution.py:394
  90.3 3.7 %collective-permute-start.6 = (f32[216,8,128]{2,1,0:T(8,128)S(1)}, f32[216,8,128]{2,1,0:T(8,128)S(1)}, u32[]{:S(2)}, u32[]{:S(2)}) collective-permute-start(f32[216,8,128]{2,1,0:T(8,128)S(1)} %get-tuple-element.36), channel_id=1, source_target_pairs={{16,0},{17,1},{18,2},{19,3},{20,4},{21,5},{22,6},{23,7},{24,8},{25... | collective-permute-start | bytes 2654216 | tf_op jit(solution)/shard_map/ppermute | solution.py:420
  93.9 0.1 collective-permute-start.5
  94.0 2.0 %collective-permute-done.6.got_ref = f32[216,8,128]{2,1,0:T(8,128)S(1)} collective-permute-done((f32[216,8,128]{2,1,0:T(8,128)S(1)}, f32[216,8,128]{2,1,0:T(8,128)S(1)}, u32[]{:S(2)}, u32[]{:S(2)}) %collective-permute-start.6) | collective-permute-done | bytes 884768 | tf_op jit(solution)/shard_map/ppermute | solution.py:420
  96.0 2.0 %shard_map.112.rest_0_ = f32[4,216,8,128]{3,2,1,0:T(8,128)} custom-call(s32[9]{0:T(128)S(1)} %pad_add_fusion.info.refs_0_, f32[216,8,128]{2,1,0:T(8,128)S(1)} %get-tuple-element.35.keep_ref, f32[216,8,128]{2,1,0:T(8,128)S(1)} %collective-permute-done.6.got_ref), custom_call_target="tpu_custom_call" | custom-call | tf_op jit(solution)/shard_map/pallas_call | solution.py:424
  98.0 2.0 %shard_map.113 = f32[4,216,8,128]{3,2,1,0:T(8,128)} custom-call(s32[9]{0:T(128)S(1)} %pad_add_fusion.info.refs_0_, f32[216,8,128]{2,1,0:T(8,128)S(1)} %get-tuple-element.33.keep_ref, f32[216,8,128]{2,1,0:T(8,128)S(1)} %collective-permute-done.5.got_ref, f32[4,216,8,128]{3,2,1,0:T(8,128)} %shard_map.112.rest_0_), custom_call_target="tpu_custom_call", output_to_operand_aliasing={{}: (3, {})} | custom-call | tf_op jit(solution)/shard_map/pallas_call | solution.py:424
  (66 shorter events, 0.9 us)
Async XLA Ops:
  0.0 15.4 %copy-start.7 = (f32[256]{0:T(256)S(1)}, f32[256]{0:T(256)}, u32[]{:S(2)}) copy-start(f32[256]{0:T(256)} %constant.45) | copy-start | bytes 3076
  0.0 13.4 %copy-start.5 = (f32[4,24]{1,0:T(4,128)S(1)}, f32[4,24]{1,0:T(4,128)}, u32[]{:S(2)}) copy-start(f32[4,24]{1,0:T(4,128)} %param.14) | copy-start | bytes 1156
  0.0 13.5 %copy-start.6 = (f32[4,24]{1,0:T(4,128)S(1)}, f32[4,24]{1,0:T(4,128)}, u32[]{:S(2)}) copy-start(f32[4,24]{1,0:T(4,128)} %param.15) | copy-start | bytes 1156
  0.0 13.7 %copy-start.9 = (s32[2,4]{1,0:T(2,128)S(1)}, s32[2,4]{1,0:T(2,128)}, u32[]{:S(2)}) copy-start(s32[2,4]{1,0:T(2,128)} %param.20) | copy-start | bytes 100
  1.5 14.6 %collective-permute-start = (f32[3,8,128]{2,1,0:T(8,128)S(1)}, f32[3,8,128]{2,1,0:T(8,128)S(1)}, u32[]{:S(2)}, u32[]{:S(2)}) collective-permute-start(f32[3,8,128]{2,1,0:T(8,128)S(1)} %pad_maximum_fusion.3), channel_id=1, source_target_pairs={{16,0},{17,1},{18,2},{19,3},{20,4},{21,5},{22,6},{23,7},{24,8},{25... | collective-permute-start | bytes 36872 | tf_op jit(solution)/shard_map/ppermute | solution.py:326
  2.1 1.2 %copy-start = (f32[256,864]{0,1:T(8,128)S(1)}, f32[256,864]{0,1:T(8,128)}, u32[]{:S(2)}) copy-start(f32[256,864]{0,1:T(8,128)} %param.17) | copy-start | bytes 2654212
  3.3 0.7 copy-start.1
  4.0 11.7 %copy-start.8 = (f32[24]{0:T(128)S(1)}, f32[24]{0:T(128)}, u32[]{:S(2)}) copy-start(f32[24]{0:T(128)} %param.16) | copy-start | bytes 292
  4.0 12.0 %copy-start.3 = (f32[8,128]{1,0:T(8,128)S(1)}, f32[8,128]{1,0:T(8,128)}, u32[]{:S(2)}) copy-start(f32[8,128]{1,0:T(8,128)} %param.12) | copy-start | bytes 12292
  4.0 12.0 %copy-start.4 = (f32[8,128]{1,0:T(8,128)S(1)}, f32[8,128]{1,0:T(8,128)}, u32[]{:S(2)}) copy-start(f32[8,128]{1,0:T(8,128)} %param.11) | copy-start | bytes 12292
  7.3 48.1 %all-to-all-start = ((f32[32,16,896]{2,1,0:T(8,128)}), f32[32,16,896]{2,1,0:T(8,128)S(1)}, u32[]{:S(2)}, u32[]{:S(2)}) async-start(f32[32,16,896]{2,1,0:T(8,128)} %bitcast.3), calls=%async_computation | async-start | bytes 3670016 | tf_op jit(solution)/shard_map/all_to_all | solution.py:323
  19.4 47.7 %copy-start.2 = (f32[1,256]{1,0:T(1,128)S(1)}, f32[1,256]{1,0:T(1,128)}, u32[]{:S(2)}) copy-start(f32[1,256]{1,0:T(1,128)} %constant.46.refs_7_) | copy-start | bytes 3076
  56.9 10.2 %collective-permute-start.2 = (f32[4,80,256]{2,1,0:T(8,128)S(1)}, f32[4,80,256]{2,1,0:T(8,128)S(1)}, u32[]{:S(2)}, u32[]{:S(2)}) collective-permute-start(f32[4,80,256]{2,1,0:T(8,128)S(1)} %get-tuple-element.30), channel_id=1, source_target_pairs={{16,0},{17,1},{18,2},{19,3},{20,4},{21,5},{22,6},{23,7},{24,8},{25... | collective-permute-start | bytes 983048 | tf_op jit(solution)/shard_map/ppermute | solution.py:382
  57.4 7.9 %collective-permute-start.1 = (f32[4,16]{1,0:T(4,128)S(1)}, f32[4,16]{1,0:T(4,128)S(1)}, u32[]{:S(2)}, u32[]{:S(2)}) collective-permute-start(f32[4,16]{1,0:T(4,128)S(1)} %get-tuple-element.39), channel_id=1, source_target_pairs={{0,1},{1,2},{2,3},{3,4},{4,5},{5,6},{6,7},{7,8},{8,9},{9,10},{10,1... | collective-permute-start | bytes 776 | tf_op jit(solution)/shard_map/ppermute | solution.py:332
  59.3 5.9 %collective-permute-start.3 = (f32[4,8,256]{2,1,0:T(8,128)S(1)}, f32[4,8,256]{2,1,0:T(8,128)S(1)}, u32[]{:S(2)}, u32[]{:S(2)}) collective-permute-start(f32[4,8,256]{2,1,0:T(8,128)S(1)} %get-tuple-element.31), channel_id=1, source_target_pairs={{0,1},{1,2},{2,3},{3,4},{4,5},{5,6},{6,7},{7,8},{8,9},{9,10},{10,1... | collective-permute-start | bytes 98312 | tf_op jit(solution)/shard_map/ppermute | solution.py:383
  61.6 5.5 %collective-permute-start.4 = (f32[4,8,256]{2,1,0:T(8,128)S(1)}, f32[4,8,256]{2,1,0:T(8,128)S(1)}, u32[]{:S(2)}, u32[]{:S(2)}) collective-permute-start(f32[4,8,256]{2,1,0:T(8,128)S(1)} %get-tuple-element.32), channel_id=1, source_target_pairs={{16,1},{17,2},{18,3},{19,4},{20,5},{21,6},{22,7},{23,8},{24,9},{25... | collective-permute-start | bytes 98312 | tf_op jit(solution)/shard_map/ppermute | solution.py:384
  90.3 5.7 %collective-permute-start.6 = (f32[216,8,128]{2,1,0:T(8,128)S(1)}, f32[216,8,128]{2,1,0:T(8,128)S(1)}, u32[]{:S(2)}, u32[]{:S(2)}) collective-permute-start(f32[216,8,128]{2,1,0:T(8,128)S(1)} %get-tuple-element.36), channel_id=1, source_target_pairs={{16,0},{17,1},{18,2},{19,3},{20,4},{21,5},{22,6},{23,7},{24,8},{25... | collective-permute-start | bytes 2654216 | tf_op jit(solution)/shard_map/ppermute | solution.py:420
  93.9 4.1 %collective-permute-start.5 = (f32[216,8,128]{2,1,0:T(8,128)S(1)}, f32[216,8,128]{2,1,0:T(8,128)S(1)}, u32[]{:S(2)}, u32[]{:S(2)}) collective-permute-start(f32[216,8,128]{2,1,0:T(8,128)S(1)} %get-tuple-element.34), channel_id=1, source_target_pairs={{16,0},{17,1},{18,2},{19,3},{20,4},{21,5},{22,6},{23,7},{24,8},{25... | collective-permute-start | bytes 2654216 | tf_op jit(solution)/shard_map/ppermute | solution.py:420

commit v8 on v7

--- a/solution.py
+++ b/solution.py
@@ -37,7 +37,8 @@
     return jnp.pad(array, widths, constant_values=value)
 
 
-def pack_kernel(shifts, col_count, rows, comps, dest_ref, spectra_ref, out_ref, high, low, slots):
+def pack_kernel(shifts, col_count, rows, comps, dest_hbm, spectra_hbm, wind_hbm, dir_hbm, class_hbm,
+                out_ref, held_ref, dest_ref, spectra_ref, class_ref, high, low, slots, sems):
     step = pl.program_id(0)
     points = dest_ref.shape[1]
     load = out_ref.shape[1]
@@ -45,6 +46,13 @@
 
     @pl.when(step == 0)
     def _():
+        pieces = ((dest_hbm, dest_ref), (spectra_hbm, spectra_ref), (wind_hbm, held_ref.at[0]),
+                  (dir_hbm, held_ref.at[1]), (class_hbm, class_ref))
+        copies = [pltpu.make_async_copy(source, target, sems.at[index])
+                  for index, (source, target) in enumerate(pieces)]
+        for copy in copies:
+            copy.start()
+        copies[0].wait()
         dest = dest_ref[...]
         grid_row = lax.shift_right_logical(dest, total_bits)
         grid_col = dest & (2**total_bits - 1)
@@ -64,6 +72,9 @@
                  < lax.broadcasted_iota(jnp.int32, (points, points), 1))
         rank = jnp.sum(jnp.where(same & above, 1.0, 0.0), axis=0, keepdims=True)
         slots[...] = owner * CAP + rank.astype(jnp.int32)
+        for copy in copies[1:]:
+            copy.wait()
+        held_ref[2] = class_ref[...].astype(jnp.float32)
         spectra = jnp.concatenate(
             [spectra_ref[...], jnp.broadcast_to(lanes[1:2], (load - comps, points))], axis=0)
         high[...], low[...] = split_bf16(spectra)
@@ -76,7 +87,7 @@
                     + lax.dot_general(place, low[...], over_points, preferred_element_type=jnp.float32))
 
 
-def rim_kernel(own, rows_dev, comps, quad_size, info, arrived_ref, own_ref, send_ref, same_ref,
+def rim_kernel(own, rows_dev, comps, quad_size, info, arrived_ref, far_ref, own_ref, send_ref, same_ref,
                cross_ref):
     half = info[ITERS * QUADS]
     cols_dev = 2 * own
@@ -111,13 +122,13 @@
         part = summed if quad == 0 else pltpu.roll(summed, load - start, 1)
         own_ref[quad] = part[:block, :width]
         send_ref[quad] = part[block:2 * block, :width]
-        same_ref[quad] = part[2 * block:2 * block + HALO, :width]
+        same_ref[quad, :HALO] = part[2 * block:2 * block + HALO, :width]
+        same_ref[quad, HALO:] = far_ref[quad]
         cross_ref[quad] = part[2 * block + HALO:2 * block + 2 * HALO, :width]
 
 
-def sweeps_kernel(rows, own, cells, quad_size, info, ax_ref, ay_ref, base_ref, wind_ref, mt_ref, diag_ref, scale_ref,
-                  ax_table, base_table, lane_table, far_ref,
-                  own_ref, par_ref, same_ref, cross_ref, *rest):
+def sweeps_kernel(rows, own, cells, quad_size, class_count, info, ax_ref, ay_ref, base_ref,
+                  wind_ref, mt_ref, const_ref, own_ref, par_ref, same_ref, cross_ref, *rest):
     pairs = QUADS // 2
     keep_refs, send_refs = rest[:pairs], rest[pairs:2 * pairs]
     state, power, rim, side = rest[2 * pairs:]
@@ -126,6 +137,10 @@
     half = info[ITERS * QUADS]
     width = mt_ref.shape[2]
     rows_dev = rows // 2
+    ax_table = const_ref[0, :class_count]
+    base_table = const_ref[0, class_count:2 * class_count]
+    rate_lane, cos_lane, sin_lane, scale_lane, diag_lane = [
+        const_ref[0, 2 * class_count + each:2 * class_count + each + 1] for each in range(5)]
     down = (quad == 0) | (quad == 3)
     step_x = jnp.where(down, 1, -1)
     first_row = jnp.where(down, 0, rows - 1)
@@ -135,23 +150,21 @@
     def _():
         power[...] = jnp.zeros_like(power)
 
-    rim[0] = own_ref[0, 0:cells]
-    rim[0, own:cells] = own_ref[0, own:cells] + same_ref[0]
-    rim[1] = par_ref[0, 0:cells]
-    rim[1, own:cells] = par_ref[0, own:cells] + cross_ref[0]
+    rim[0] = own_ref[quad, 0:cells]
+    rim[0, own:cells] = own_ref[quad, own:cells] + same_ref[quad, :HALO]
+    rim[1] = par_ref[quad, 0:cells]
+    rim[1, own:cells] = par_ref[quad, own:cells] + cross_ref[quad]
     far_at = jnp.where(half == 0, HALO - 1, 0)
     at_far = lax.broadcasted_iota(jnp.int32, (HALO, width), 0) == far_at
     edge_at = jnp.where(half == 0, 0, 2 * HALO - 1)
     at_edge = lax.broadcasted_iota(jnp.int32, (2 * HALO, width), 0) == edge_at
     for j in range(rows_dev):
-        mine = jnp.where(at_edge, own_ref[0, cells + j:cells + j + 1], 0.0)
-        theirs = jnp.where(at_edge, par_ref[0, cells + j:cells + j + 1], 0.0)
+        mine = jnp.where(at_edge, own_ref[quad, cells + j:cells + j + 1], 0.0)
+        theirs = jnp.where(at_edge, par_ref[quad, cells + j:cells + j + 1], 0.0)
         side[j + rows_dev * half] = mine
         side[j + rows_dev * (1 - half)] = theirs
 
     def run(count, second):
-        chains = [(0, count)]
-
         def patched(block, far_row):
             if second:
                 return block
@@ -159,22 +172,22 @@
 
         def factors(i, low, high):
             row = first_row + i * step_x
-            kind = far_ref[0, row]
+            kind, strength, far_cos, far_sin = [
+                same_ref[feat, pl.ds(HALO + row, 1), :] for feat in range(4)]
             far_ax = jnp.zeros((1, width), jnp.float32)
             far_base = jnp.zeros((1, width), jnp.float32)
-            for each in range(ax_table.shape[1]):
-                far_ax = jnp.where(kind == each, ax_table[0, each:each + 1], far_ax)
-                far_base = jnp.where(kind == each, base_table[0, each:each + 1], far_base)
-            spread = jnp.maximum(
-                far_ref[2, row] * lane_table[0, 1:2] + far_ref[3, row] * lane_table[0, 2:3], 0.0)
-            far_wind = (lane_table[0, 0:1] * far_ref[1, row]) * (spread * spread)
+            for each in range(class_count):
+                far_ax = jnp.where(kind == each, ax_table[each:each + 1], far_ax)
+                far_base = jnp.where(kind == each, base_table[each:each + 1], far_base)
+            spread = jnp.maximum(far_cos * cos_lane + far_sin * sin_lane, 0.0)
+            far_wind = (rate_lane * strength) * (spread * spread)
             total = power[0, row, low:high]
             for other in range(1, QUADS):
                 total = total + power[other, row, low:high]
             level = total * (1.0 / (QUADS * quad_size))
             damping = whitecap_rate * level / (1.0 + level)
             den = patched(base_ref[0, row, low:high], far_base) + jnp.concatenate([damping] * (width // LANES), axis=1)
-            inverse = scale_ref[...] / den
+            inverse = scale_lane / den
             source = patched(wind_ref[0, row, low:high], far_wind)
             edge = side[row]
             parts = [source[:HALO] + edge[:HALO], source[HALO:own - HALO],
@@ -191,27 +204,29 @@
                 source = source + ay_ref[0, row, low:high] * shifted[low:high]
             return patched(ax_ref[0, row, low:high], far_ax) * inverse, source * inverse
 
-        ready = [factors(0, *chain) for chain in chains]
-        upwind = [None] * len(chains)
+        def store(i, value):
+            row = first_row + i * step_x
+            square = value * value
+            folded = square[:, :LANES]
+            for lane in range(LANES, width, LANES):
+                folded = folded + square[:, lane:lane + LANES]
+            state[quad, row, :count] = value
+            power[quad, row, :count] = jnp.broadcast_to(
+                jnp.sum(folded, axis=1, keepdims=True), (count, LANES))
+
+        along, known = factors(0, 0, count)
+        upwind = None
         for i in range(rows):
-            updated = []
-            for (along, known), before in zip(ready, upwind):
-                balance = known if before is None else along * before + known
-                mixed = jnp.dot(balance.astype(jnp.bfloat16), mt_ref[0],
-                                preferred_element_type=jnp.float32)
-                updated.append(diag_ref[0] * balance + mixed)
+            balance = known if upwind is None else along * upwind + known
+            mixed = jnp.dot(balance.astype(jnp.bfloat16), mt_ref[0],
+                            preferred_element_type=jnp.float32)
+            updated = diag_lane * balance + mixed
             if i + 1 < rows:
-                ready = [factors(i + 1, *chain) for chain in chains]
-            row = first_row + i * step_x
-            for (start, stop), value in zip(chains, updated):
-                square = value * value
-                folded = square[:, :LANES]
-                for lane in range(LANES, width, LANES):
-                    folded = folded + square[:, lane:lane + LANES]
-                state[quad, row, start:stop] = value
-                power[quad, row, start:stop] = jnp.broadcast_to(
-                    jnp.sum(folded, axis=1, keepdims=True), (stop - start, LANES))
+                along, known = factors(i + 1, 0, count)
+            if i > 0:
+                store(i - 1, upwind)
             upwind = updated
+        store(rows - 1, upwind)
 
     @pl.when(turn < QUADS)
     def _():
@@ -300,18 +315,24 @@
     slot_total = devices * CAP
     steps = 4
     in_vmem = pl.BlockSpec(memory_space=pltpu.VMEM)
-    outgoing = pl.pallas_call(
-        lambda *refs: pack_kernel(shifts, col_count, rows, comps, *refs),
+    anywhere = pl.BlockSpec(memory_space=pl.ANY)
+    outgoing, held = pl.pallas_call(
+        partial(pack_kernel, shifts, col_count, rows, comps),
         grid=(steps,),
-        in_specs=[in_vmem, in_vmem],
-        out_specs=pl.BlockSpec((slot_total // steps, load), lambda s: (s, 0)),
-        scratch_shapes=[pltpu.VMEM((load, points), jnp.bfloat16),
+        in_specs=[anywhere] * 5,
+        out_specs=[pl.BlockSpec((slot_total // steps, load), lambda s: (s, 0)), in_vmem],
+        scratch_shapes=[pltpu.VMEM((1, points), jnp.int32),
+                        pltpu.VMEM((comps, points), jnp.float32),
+                        pltpu.VMEM((rows_dev, cols_dev), jnp.int32),
                         pltpu.VMEM((load, points), jnp.bfloat16),
-                        pltpu.VMEM((1, points), jnp.int32)],
-        out_shape=jax.ShapeDtypeStruct((slot_total, load), jnp.float32),
+                        pltpu.VMEM((load, points), jnp.bfloat16),
+                        pltpu.VMEM((1, points), jnp.int32),
+                        pltpu.SemaphoreType.DMA((5,))],
+        out_shape=[jax.ShapeDtypeStruct((slot_total, load), jnp.float32),
+                   jax.ShapeDtypeStruct((3, rows_dev, cols_dev), jnp.float32)],
         compiler_params=pltpu.CompilerParams(
             dimension_semantics=("arbitrary",), vmem_limit_bytes=48 * 2**20),
-    )(dest_cell.reshape(1, points), outer_spectra.T)
+    )(dest_cell.reshape(1, points), outer_spectra.T, wind_speed, wind_dir, depth_class)
     outgoing, refraction_inverse = lax.optimization_barrier((outgoing, refraction_inverse))
     scale = jnp.asarray(lane_scale(width))
     flipped = pad_to(pad_to(jnp.swapaxes(refraction_inverse, 1, 2), 1, width), 2, width)
@@ -319,7 +340,6 @@
     on_diag = jnp.eye(width, dtype=bool)[None]
     matrices = jnp.where(on_diag, 0.0, scaled).astype(jnp.bfloat16)
     diagonal = jnp.sum(jnp.where(on_diag, scaled, 0.0), axis=1, keepdims=True)
-    held = jnp.stack([wind_speed, wind_dir, depth_class.astype(jnp.float32)])
     arrived = lax.all_to_all(outgoing.reshape(devices, CAP, load), axes, split_axis=0,
                              concat_axis=0, tiled=True).reshape(slot_total, load)
 
@@ -329,8 +349,8 @@
         [jnp.where(is_low, held, partner), jnp.where(is_low, partner, held)], axis=1)
     strength = (chip[0] * 0.1) ** 2
     feats = jnp.stack([chip[2], strength, jnp.cos(chip[1]), jnp.sin(chip[1])])
-    far = lax.ppermute(
-        jnp.where(is_low, feats[:, :, cols_dev - 1], feats[:, :, 0]), axes, same_route)
+    far_out = jnp.broadcast_to(
+        jnp.where(is_low, feats[:, :, cols_dev - 1:], feats[:, :, :1]), (QUADS, rows, width))
     mine = jnp.where(is_low, feats[:, :, :own], feats[:, :, own:])
     right = jnp.where(is_low, feats[:, :, own], 0.0)
     left = jnp.where(is_low, 0.0, feats[:, :, own - 1])
@@ -348,8 +368,10 @@
     ay_table = jnp.abs(sin_lane)[:, None] * speed_lane[None]
     base_table = ax_table + ay_table + loss_lane[None]
 
-    lane_table = jnp.stack(
-        [jnp.broadcast_to(rate_lane, (QUADS, width)), cos_lane, sin_lane], axis=1)
+    lanes = jnp.stack([jnp.broadcast_to(rate_lane, (QUADS, width)), cos_lane, sin_lane,
+                       jnp.broadcast_to(scale, (QUADS, width))], axis=1)
+    consts = jnp.concatenate([ax_table, base_table, lanes, diagonal], axis=1)
+    consts = pad_to(consts, 1, -(-consts.shape[1] // 8) * 8)
 
     def by_class(table):
         chosen = jnp.broadcast_to(table[:, None, None, 0], (QUADS, rows, cells, width))
@@ -371,14 +393,14 @@
     info = jnp.concatenate([sweep_order.reshape(-1), half[None].astype(jnp.int32)])
     block = cells + rows_dev
     rim_shapes = [jax.ShapeDtypeStruct((QUADS, size, width), jnp.float32)
-                  for size in (block, block, HALO, HALO)]
+                  for size in (block, block, HALO + rows, HALO)]
     rim_own, rim_send, out_same, out_cross = pl.pallas_call(
         partial(rim_kernel, own, rows_dev, comps, quad_size),
-        in_specs=[pl.BlockSpec(memory_space=pltpu.SMEM), in_vmem],
+        in_specs=[pl.BlockSpec(memory_space=pltpu.SMEM), in_vmem, in_vmem],
         out_specs=[in_vmem] * len(rim_shapes),
         out_shape=rim_shapes,
         compiler_params=pltpu.CompilerParams(vmem_limit_bytes=40 * 2**20),
-    )(info, arrived)
+    )(info, arrived, far_out)
     rim_partner = lax.ppermute(rim_send, axes, swap_route)
     rim_same = lax.ppermute(out_same, axes, same_route)
     rim_cross = lax.ppermute(out_cross, axes, cross_route)
@@ -392,17 +414,13 @@
     pairs = QUADS // 2
     packed = jax.ShapeDtypeStruct((quad_size, rows_dev, cols_dev), jnp.float32)
     halves = pl.pallas_call(
-        lambda *refs: sweeps_kernel(rows, own, cells, quad_size, *refs),
+        partial(sweeps_kernel, rows, own, cells, quad_size, class_count),
         grid_spec=pltpu.PrefetchScalarGridSpec(
             num_scalar_prefetch=1,
             grid=(turns,),
             in_specs=[quad_block((rows, cells, width))] * 4
-            + [quad_block((width, width)), quad_block((1, width))]
-            + [pl.BlockSpec((1, width), lambda t, info: (0, 0))]
-            + [quad_block((class_count, width))] * 2 + [quad_block((3, width))]
-            + [pl.BlockSpec(memory_space=pltpu.SMEM)]
-            + [quad_block((block, width))] * 2
-            + [quad_block((HALO, width))] * 2,
+            + [quad_block((width, width)), quad_block(consts.shape[1:])]
+            + [in_vmem] * 4,
             out_specs=[in_vmem] * (2 * pairs),
             scratch_shapes=[
                 pltpu.VMEM((QUADS, rows, cells, width), jnp.float32),
@@ -414,8 +432,7 @@
         out_shape=[packed] * (2 * pairs),
         compiler_params=pltpu.CompilerParams(
             dimension_semantics=("arbitrary",), vmem_limit_bytes=49 * 2**20),
-    )(info, ax, ay, base, wind, matrices, diagonal, scale[None], ax_table, base_table,
-      lane_table, far, rim_own, rim_partner, rim_same, rim_cross)
+    )(info, ax, ay, base, wind, matrices, consts, rim_own, rim_partner, rim_same, rim_cross)
 
     got = [lax.ppermute(half_out, axes, swap_route) for half_out in halves[pairs:]]
     chunks = 4

time: 100 us -> 98.9 us (0.989); the launches traced: 100 us -> 97.6 us
  local copies, waits for them, and re-layouts: 4.2 us -> 7.65 us
  starting transfers between devices: 18.4 us -> 15.8 us
  other arithmetic: 11.9 us -> 10.4 us
  Pallas kernels: 32 us -> 30.6 us
    unnamed x32 -> x36, local copies, waits for them, and re-layouts: 1.91 us -> 5.2 us
    ppermute x1 -> x0, starting transfers between devices: 1.92 us -> none  [body(): lax.ppermute(jnp.where(is_low, feats[:, :, cols_dev - 1], feats[:, :, 0])...]
    another operation x3 -> x0, other arithmetic: 1.45 us -> none  [the longest x2 1.44 us: body(): held = jnp.stack([wind_speed, wind_dir, depth_class.astype(jnp.float32)])]
    pallas_call x2, Pallas kernels: 26.5 us -> 25.1 us  [the longest x1 22.7 us: body(): pl.pallas_call(partial(sweeps_kernel, rows, own, cells, quad_size, class_...]
    ppermute x2, starting transfers between devices: 3.75 us -> 2.62 us  [body(): lax.ppermute(half_out, axes, swap_route)]
  transfers between devices with their start and end apart: 8 -> 7, of which waited for: 3 -> 3; matrix products, arithmetic and copies ran while one was open for 13% -> 13% of each run, Pallas kernels for 5% -> 2%
where the time goes in v8:
time: 98.9 us; the launch traced here: 97.6 us
  waiting for transfers between devices  32.5 us (33%)
  Pallas kernels  30.6 us (31%)
  starting transfers between devices  15.8 us (16%)
  other arithmetic  10.4 us (11%)
  local copies, waits for them, and re-layouts  7.65 us (8%)
    all_to_all x1, waiting for transfers between devices, body(): lax.all_to_all(outgoing.reshape(devices, CAP, load), axes, split_axis=0,...  29 us
    pallas_call x1, Pallas kernels, body(): pl.pallas_call(partial(sweeps_kernel, rows, own, cells, quad_size, class_...  22.7 us
    select_n x1, other arithmetic, by_class(): jnp.where((class_here == kind)[None, :, :, None], table[:, None, None, ki...  6.65 us
    all_to_all x1, starting transfers between devices, body(): lax.all_to_all(outgoing.reshape(devices, CAP, load), axes, split_axis=0,...  6.25 us
    unnamed x36, local copies, waits for them, and re-layouts  5.2 us
    ppermute x1, starting transfers between devices, body(): rim_cross = lax.ppermute(out_cross, axes, cross_route)  4.13 us
    pallas_call x2, Pallas kernels, body(): pl.pallas_call(partial(merge_kernel, own, pair, chunks), in_specs=[pl.Blo...  4 us
    mul x1, other arithmetic, body(): rate_lane[None, None, None] * strength[None, :, :, None] * (spread * spread)  2.66 us
  transfers between devices with their start and end apart: 7, of which 3 were waited for; matrix products, arithmetic and copies ran while one was open for 13% of the time, Pallas kernels for 2%

profile of v8, /device:TPU:17, one launch (start us, length us, event | category | flops | bytes accessed | tf_op | source)
XLA Modules:
  0.0 97.6 jit_solution(17314520375831095303)
XLA Ops:
  0.0 1.2 %copy-done.1 = f32[256,864]{0,1:T(8,128)S(1)} copy-done((f32[256,864]{0,1:T(8,128)S(1)}, f32[256,864]{0,1:T(8,128)}, u32[]{:S(2)}) %copy-start.1) | copy-done | bytes 884760
  1.2 0.7 copy-done.2
  1.9 0.7 copy-done.3
  2.6 0.7 copy-done.4
  3.3 0.7 copy-done.5
  4.0 2.4 %shard_map.109 = (f32[512,896]{1,0:T(8,128)S(1)}, f32[3,8,128]{2,1,0:T(8,128)S(1)}) custom-call(s32[1,256]{1,0:T(1,128)S(1)} %bitcast.58, f32[864,256]{1,0:T(8,128)S(1)} %bitcast.57, f32[8,128]{1,0:T(8,128)S(1)} %copy-done.2, f32[8,128]{1,0:T(8,128)S(1)} %copy-done.3, s32[8,128]{1,0:T(8,128)S(1)} %copy-done.4), custom_call_target="tpu_custom_call" | custom-call | tf_op jit(solution)/shard_map/pallas_call | solution.py:319
  6.4 1.2 %copy-done = f32[512,896]{1,0:T(8,128)} copy-done((f32[512,896]{1,0:T(8,128)}, f32[512,896]{1,0:T(8,128)S(1)}, u32[]{:S(2)}) %copy-start) | copy-done | bytes 1835032
  7.6 6.2 %all-to-all-start = ((f32[32,16,896]{2,1,0:T(8,128)}), f32[32,16,896]{2,1,0:T(8,128)S(1)}, u32[]{:S(2)}, u32[]{:S(2)}) async-start(f32[32,16,896]{2,1,0:T(8,128)} %bitcast.56), calls=%async_computation | async-start | bytes 3670016 | tf_op jit(solution)/shard_map/all_to_all | solution.py:343
  13.8 0.4 collective-permute-start
  14.4 0.1 broadcast_in_dim.215
  14.6 0.1 broadcast_in_dim.203
  15.0 0.1 reshape.87
  15.1 1.5 %copy.14 = f32[4,216,216]{1,2,0:T(8,128)S(1)} copy(f32[4,216,216]{2,1,0:T(8,128)} %param.19) | data formatting | bytes 1492992 | tf_op jit(solution)/shard_map/optimization_barrier | solution.py:336
  16.7 0.2 select_reduce_fusion
  16.9 0.1 pad_add_fusion.info
  17.0 0.1 tile.32
  17.4 0.2 fusion
  17.6 0.1 pad_maximum_fusion.1
  17.7 0.2 broadcast_multiply_fusion
  18.0 2.7 %multiply_multiply_fusion.wind_ref = f32[4,16,72,256]{3,2,1,0:T(8,128)} fusion(f32[4,256]{1,0:T(4,128)S(1)} %get-tuple-element.81, f32[16,72]{1,0:T(8,128)S(1)} %get-tuple-element.47, f32[4,256]{1,0:T(4,128)S(1)} %get-tuple-element.76, f32[16,72]{1,0:T(8,128)S(1)} %get-tuple-element.48, f32[16,72,256]{2,1,0:T(8,128)S(1)} %broadcast_multiply_fusion), kind=kLoop, calls=%fused_computation | loop fusion | flops 7077888 | bytes 5915648 | tf_op jit(solution)/shard_map/mul | solution.py:388
  20.6 6.6 %select_select_fusion = (f32[4,16,72,256]{3,2,1,0:T(8,128)}, f32[4,16,72,256]{3,2,1,0:T(8,128)}, f32[4,16,72,256]{3,2,1,0:T(8,128)}) fusion(f32[4,256]{1,0:T(4,128)S(1)} %bitcast.65, f32[4,256]{1,0:T(4,128)S(1)} %bitcast.66, f32[4,256]{1,0:T(4,128)S(1)} %bitcast.67, f32[4,256]{1,0:T(4,128)S(1)} %bitcast.64, pred[16,72]{1,0:T(8,128)(4,1)S(1)} %get-tuple-element.51, ...), kind=kLoop, calls=%fused_computation.1 | loop fusion | flops 10616832 | bytes 14208384 | tf_op jit(solution)/shard_map/jit(_where)/select_n | solution.py:379
  27.3 29.0 %all-to-all-done = f32[32,16,896]{2,1,0:T(8,128)S(1)} async-done(((f32[32,16,896]{2,1,0:T(8,128)}), f32[32,16,896]{2,1,0:T(8,128)S(1)}, u32[]{:S(2)}, u32[]{:S(2)}) %all-to-all-start) | async-done | bytes 1835040 | tf_op jit(solution)/shard_map/all_to_all | solution.py:343
  56.3 1.5 %shard_map.110 = (f32[4,80,256]{2,1,0:T(8,128)S(1)}, f32[4,80,256]{2,1,0:T(8,128)S(1)}, f32[4,24,256]{2,1,0:T(8,128)S(1)}, f32[4,8,256]{2,1,0:T(8,128)S(1)}) custom-call(s32[9]{0:T(128)S(1)} %pad_add_fusion.info, f32[512,896]{1,0:T(8,128)S(1)} %bitcast.55, f32[4,16,256]{2,1,0:T(8,128)S(1)} %broadcast_in_dim.236.far_ref), custom_call_target="tpu_custom_call" | custom-call | tf_op jit(solution)/shard_map/pallas_call | solution.py:397
  57.8 0.5 collective-permute-start.1
  58.3 1.9 %collective-permute-start.2 = (f32[4,24,256]{2,1,0:T(8,128)S(1)}, f32[4,24,256]{2,1,0:T(8,128)S(1)}, u32[]{:S(2)}, u32[]{:S(2)}) collective-permute-start(f32[4,24,256]{2,1,0:T(8,128)S(1)} %get-tuple-element.35), channel_id=1, source_target_pairs={{0,1},{1,2},{2,3},{3,4},{4,5},{5,6},{6,7},{7,8},{8,9},{9,10},{10,1... | collective-permute-start | bytes 294920 | tf_op jit(solution)/shard_map/ppermute | solution.py:405
  60.2 4.1 %collective-permute-start.3 = (f32[4,8,256]{2,1,0:T(8,128)S(1)}, f32[4,8,256]{2,1,0:T(8,128)S(1)}, u32[]{:S(2)}, u32[]{:S(2)}) collective-permute-start(f32[4,8,256]{2,1,0:T(8,128)S(1)} %get-tuple-element.36), channel_id=1, source_target_pairs={{16,1},{17,2},{18,3},{19,4},{20,5},{21,6},{22,7},{23,8},{24,9},{25... | collective-permute-start | bytes 98312 | tf_op jit(solution)/shard_map/ppermute | solution.py:406
  64.5 1.5 %collective-permute-done.3.cross_ref = f32[4,8,256]{2,1,0:T(8,128)S(1)} collective-permute-done((f32[4,8,256]{2,1,0:T(8,128)S(1)}, f32[4,8,256]{2,1,0:T(8,128)S(1)}, u32[]{:S(2)}, u32[]{:S(2)}) %collective-permute-start.3) | collective-permute-done | bytes 32800 | tf_op jit(solution)/shard_map/ppermute | solution.py:406
  66.1 22.7 %shard_map.111 = (f32[216,8,128]{2,1,0:T(8,128)S(1)}, f32[216,8,128]{2,1,0:T(8,128)S(1)}, f32[216,8,128]{2,1,0:T(8,128)S(1)}, f32[216,8,128]{2,1,0:T(8,128)S(1)}) custom-call(s32[9]{0:T(128)S(1)} %pad_add_fusion.info, f32[4,16,72,256]{3,2,1,0:T(8,128)} %get-tuple-element.27.ax_ref, f32[4,16,72,256]{3,2,1,0:T(8,128)} %get-tuple-element.28.ay_ref, ...), custom_call_target="tpu_custom_call" | custom-call | tf_op jit(solution)/shard_map/pallas_call | solution.py:416
  88.8 2.5 %collective-permute-start.5 = (f32[216,8,128]{2,1,0:T(8,128)S(1)}, f32[216,8,128]{2,1,0:T(8,128)S(1)}, u32[]{:S(2)}, u32[]{:S(2)}) collective-permute-start(f32[216,8,128]{2,1,0:T(8,128)S(1)} %get-tuple-element.40), channel_id=1, source_target_pairs={{16,0},{17,1},{18,2},{19,3},{20,4},{21,5},{22,6},{23,7},{24,8},{25... | collective-permute-start | bytes 2654216 | tf_op jit(solution)/shard_map/ppermute | solution.py:437
  91.4 2.0 %collective-permute-done.5.got_ref = f32[216,8,128]{2,1,0:T(8,128)S(1)} collective-permute-done((f32[216,8,128]{2,1,0:T(8,128)S(1)}, f32[216,8,128]{2,1,0:T(8,128)S(1)}, u32[]{:S(2)}, u32[]{:S(2)}) %collective-permute-start.5) | collective-permute-done | bytes 884768 | tf_op jit(solution)/shard_map/ppermute | solution.py:437
  93.4 2.0 %shard_map.112.rest_0_ = f32[4,216,8,128]{3,2,1,0:T(8,128)} custom-call(s32[9]{0:T(128)S(1)} %pad_add_fusion.info, f32[216,8,128]{2,1,0:T(8,128)S(1)} %get-tuple-element.39.keep_ref, f32[216,8,128]{2,1,0:T(8,128)S(1)} %collective-permute-done.5.got_ref), custom_call_target="tpu_custom_call" | custom-call | tf_op jit(solution)/shard_map/pallas_call | solution.py:441
  95.4 2.0 %shard_map.113 = f32[4,216,8,128]{3,2,1,0:T(8,128)} custom-call(s32[9]{0:T(128)S(1)} %pad_add_fusion.info, f32[216,8,128]{2,1,0:T(8,128)S(1)} %get-tuple-element.37.keep_ref, f32[216,8,128]{2,1,0:T(8,128)S(1)} %collective-permute-done.4.got_ref, f32[4,216,8,128]{3,2,1,0:T(8,128)} %shard_map.112.rest_0_), custom_call_target="tpu_custom_call", output_to_operand_aliasing={{}: (3, {})} | custom-call | tf_op jit(solution)/shard_map/pallas_call | solution.py:441
  (69 shorter events, 1.1 us)
Async XLA Ops:
  0.0 16.6 %copy-start.8 = (f32[256]{0:T(256)S(1)}, f32[256]{0:T(256)}, u32[]{:S(2)}) copy-start(f32[256]{0:T(256)} %constant.47) | copy-start | bytes 3076
  0.0 14.7 %copy-start.6 = (f32[4,24]{1,0:T(4,128)S(1)}, f32[4,24]{1,0:T(4,128)}, u32[]{:S(2)}) copy-start(f32[4,24]{1,0:T(4,128)} %param.14) | copy-start | bytes 1156
  0.0 15.0 %copy-start.11 = (s32[2,4]{1,0:T(2,128)S(1)}, s32[2,4]{1,0:T(2,128)}, u32[]{:S(2)}) copy-start(s32[2,4]{1,0:T(2,128)} %param.20) | copy-start | bytes 100
  0.0 17.0 %copy-start.10 = (f32[24]{0:T(128)S(1)}, f32[24]{0:T(128)}, u32[]{:S(2)}) copy-start(f32[24]{0:T(128)} %param.16) | copy-start | bytes 292
  0.0 1.2 %copy-start.1 = (f32[256,864]{0,1:T(8,128)S(1)}, f32[256,864]{0,1:T(8,128)}, u32[]{:S(2)}) copy-start(f32[256,864]{0,1:T(8,128)} %param.17) | copy-start | bytes 2654212
  1.2 0.7 copy-start.2
  1.9 0.7 copy-start.3
  2.6 0.7 copy-start.4
  3.3 0.7 copy-start.5
  4.0 10.8 %copy-start.7 = (f32[4,24]{1,0:T(4,128)S(1)}, f32[4,24]{1,0:T(4,128)}, u32[]{:S(2)}) copy-start(f32[4,24]{1,0:T(4,128)} %param.15) | copy-start | bytes 1156
  6.4 1.2 %copy-start = (f32[512,896]{1,0:T(8,128)}, f32[512,896]{1,0:T(8,128)S(1)}, u32[]{:S(2)}) copy-start(f32[512,896]{1,0:T(8,128)S(1)} %get-tuple-element.24) | copy-start | bytes 5505028
  7.6 48.6 %all-to-all-start = ((f32[32,16,896]{2,1,0:T(8,128)}), f32[32,16,896]{2,1,0:T(8,128)S(1)}, u32[]{:S(2)}, u32[]{:S(2)}) async-start(f32[32,16,896]{2,1,0:T(8,128)} %bitcast.56), calls=%async_computation | async-start | bytes 3670016 | tf_op jit(solution)/shard_map/all_to_all | solution.py:343
  13.8 3.5 %collective-permute-start = (f32[3,8,128]{2,1,0:T(8,128)S(1)}, f32[3,8,128]{2,1,0:T(8,128)S(1)}, u32[]{:S(2)}, u32[]{:S(2)}) collective-permute-start(f32[3,8,128]{2,1,0:T(8,128)S(1)} %get-tuple-element.25), channel_id=1, source_target_pairs={{16,0},{17,1},{18,2},{19,3},{20,4},{21,5},{22,6},{23,7},{24,8},{25... | collective-permute-start | bytes 36872 | tf_op jit(solution)/shard_map/ppermute | solution.py:346
  20.6 43.8 %copy-start.9 = (f32[256]{0:T(256)S(1)}, f32[256]{0:T(256)}, u32[]{:S(2)}) copy-start(f32[256]{0:T(256)} %constant.30.clone) | copy-start | bytes 3076
  57.8 8.3 %collective-permute-start.1 = (f32[4,80,256]{2,1,0:T(8,128)S(1)}, f32[4,80,256]{2,1,0:T(8,128)S(1)}, u32[]{:S(2)}, u32[]{:S(2)}) collective-permute-start(f32[4,80,256]{2,1,0:T(8,128)S(1)} %get-tuple-element.34), channel_id=1, source_target_pairs={{16,0},{17,1},{18,2},{19,3},{20,4},{21,5},{22,6},{23,7},{24,8},{25... | collective-permute-start | bytes 983048 | tf_op jit(solution)/shard_map/ppermute | solution.py:404
  58.3 7.8 %collective-permute-start.2 = (f32[4,24,256]{2,1,0:T(8,128)S(1)}, f32[4,24,256]{2,1,0:T(8,128)S(1)}, u32[]{:S(2)}, u32[]{:S(2)}) collective-permute-start(f32[4,24,256]{2,1,0:T(8,128)S(1)} %get-tuple-element.35), channel_id=1, source_target_pairs={{0,1},{1,2},{2,3},{3,4},{4,5},{5,6},{6,7},{7,8},{8,9},{9,10},{10,1... | collective-permute-start | bytes 294920 | tf_op jit(solution)/shard_map/ppermute | solution.py:405
  60.2 5.8 %collective-permute-start.3 = (f32[4,8,256]{2,1,0:T(8,128)S(1)}, f32[4,8,256]{2,1,0:T(8,128)S(1)}, u32[]{:S(2)}, u32[]{:S(2)}) collective-permute-start(f32[4,8,256]{2,1,0:T(8,128)S(1)} %get-tuple-element.36), channel_id=1, source_target_pairs={{16,1},{17,2},{18,3},{19,4},{20,5},{21,6},{22,7},{23,8},{24,9},{25... | collective-permute-start | bytes 98312 | tf_op jit(solution)/shard_map/ppermute | solution.py:406
  88.8 4.6 %collective-permute-start.5 = (f32[216,8,128]{2,1,0:T(8,128)S(1)}, f32[216,8,128]{2,1,0:T(8,128)S(1)}, u32[]{:S(2)}, u32[]{:S(2)}) collective-permute-start(f32[216,8,128]{2,1,0:T(8,128)S(1)} %get-tuple-element.40), channel_id=1, source_target_pairs={{16,0},{17,1},{18,2},{19,3},{20,4},{21,5},{22,6},{23,7},{24,8},{25... | collective-permute-start | bytes 2654216 | tf_op jit(solution)/shard_map/ppermute | solution.py:437
  91.4 4.1 %collective-permute-start.4 = (f32[216,8,128]{2,1,0:T(8,128)S(1)}, f32[216,8,128]{2,1,0:T(8,128)S(1)}, u32[]{:S(2)}, u32[]{:S(2)}) collective-permute-start(f32[216,8,128]{2,1,0:T(8,128)S(1)} %get-tuple-element.38), channel_id=1, source_target_pairs={{16,0},{17,1},{18,2},{19,3},{20,4},{21,5},{22,6},{23,7},{24,8},{25... | collective-permute-start | bytes 2654216 | tf_op jit(solution)/shard_map/ppermute | solution.py:437

commit v9 on v8

--- a/solution.py
+++ b/solution.py
@@ -37,12 +37,11 @@
     return jnp.pad(array, widths, constant_values=value)
 
 
-def pack_kernel(shifts, col_count, rows, comps, dest_hbm, spectra_hbm, wind_hbm, dir_hbm, class_hbm,
+def pack_kernel(total_bits, col_bits, rows, comps, dest_hbm, spectra_hbm, wind_hbm, dir_hbm, class_hbm,
                 out_ref, held_ref, dest_ref, spectra_ref, class_ref, high, low, slots, sems):
     step = pl.program_id(0)
     points = dest_ref.shape[1]
     load = out_ref.shape[1]
-    total_bits, row_bits, col_bits = shifts
 
     @pl.when(step == 0)
     def _():
@@ -56,13 +55,11 @@
         dest = dest_ref[...]
         grid_row = lax.shift_right_logical(dest, total_bits)
         grid_col = dest & (2**total_bits - 1)
-        local_row = grid_row & (2**row_bits - 1)
-        local_col = grid_col & (2**col_bits - 1)
-        owner = (lax.shift_right_logical(grid_row, row_bits) * col_count
-                 + lax.shift_right_logical(grid_col, col_bits))
-        on_row = (grid_row == 0) | (grid_row == rows - 1)
-        on_left = jnp.where(grid_col == 0, 2**col_bits, 2**col_bits + 2**row_bits) + local_row
-        code = jnp.where(on_row, local_col, on_left) + 1
+        owner = lax.shift_right_logical(grid_col, col_bits)
+        cols_dev = 2**col_bits
+        on_row = jnp.where(grid_row == 0, 0, cols_dev) + (grid_col & (cols_dev - 1))
+        on_side = 2 * cols_dev + jnp.where(grid_col == 0, 0, rows) + grid_row
+        code = jnp.where((grid_row == 0) | (grid_row == rows - 1), on_row, on_side) + 1
         lanes = jnp.concatenate(
             [owner.astype(jnp.float32), code.astype(jnp.float32), jnp.zeros((6, points), jnp.float32)],
             axis=0)
@@ -71,7 +68,7 @@
         above = (lax.broadcasted_iota(jnp.int32, (points, points), 0)
                  < lax.broadcasted_iota(jnp.int32, (points, points), 1))
         rank = jnp.sum(jnp.where(same & above, 1.0, 0.0), axis=0, keepdims=True)
-        slots[...] = owner * CAP + rank.astype(jnp.int32)
+        slots[...] = owner * (2 * CAP) + rank.astype(jnp.int32)
         for copy in copies[1:]:
             copy.wait()
         held_ref[2] = class_ref[...].astype(jnp.float32)
@@ -87,29 +84,25 @@
                     + lax.dot_general(place, low[...], over_points, preferred_element_type=jnp.float32))
 
 
-def rim_kernel(own, rows_dev, comps, quad_size, info, arrived_ref, far_ref, own_ref, send_ref, same_ref,
-               cross_ref):
+def rim_kernel(own, rows, comps, quad_size, info, arrived_ref, own_ref, send_ref):
     half = info[ITERS * QUADS]
-    cols_dev = 2 * own
     cells = own + HALO
-    block = cells + rows_dev
+    block = 2 * cells + rows
     width = own_ref.shape[2]
     load = arrived_ref.shape[1]
-    spots = -(-(2 * block + 2 * HALO) // LANES) * LANES
+    spots = -(-2 * block // LANES) * LANES
     lane = lax.broadcasted_iota(jnp.int32, (1, spots), 1)
     at_send = lane >= block
     spot = jnp.where(at_send, lane - block, lane)
     side_at = jnp.where(at_send, 1 - half, half)
-    want = jnp.where(spot < own, own * side_at + spot, -1)
-    want = jnp.where((spot == own) & (side_at == 0), own, want)
-    want = jnp.where((spot == cells - 1) & (side_at == 1), own - 1, want)
-    want = jnp.where(spot >= cells, cols_dev + rows_dev * side_at + spot - cells, want)
-    rest = lane - 2 * block
-    to_left = jnp.where((rest == HALO - 1) & (half == 0), cols_dev - 1, -1)
-    to_left = jnp.where((rest == 0) & (half == 1), 0, to_left)
-    to_left = jnp.where((rest == HALO) & (half == 0), 0, to_left)
-    to_left = jnp.where((rest == 2 * HALO - 1) & (half == 1), cols_dev - 1, to_left)
-    want = jnp.where(rest >= 0, to_left, want)
+    second = spot >= cells
+    cell = jnp.where(second, spot - cells, spot)
+    col = jnp.where(cell < own, own * side_at + cell, -1)
+    col = jnp.where((cell == own) & (side_at == 0), own, col)
+    col = jnp.where((cell == cells - 1) & (side_at == 1), own - 1, col)
+    want = jnp.where(col >= 0, col + jnp.where(second, 2 * own, 0), -1)
+    want = jnp.where(spot >= 2 * cells, 4 * own + rows * side_at + spot - 2 * cells, want)
+    want = jnp.where(lane < 2 * block, want, -1)
     code = arrived_ref[:, comps:comps + 1]
     gather = jnp.where(code == (want + 1).astype(jnp.float32), 1.0, 0.0)
     gather = jnp.where(want >= 0, gather, 0.0).astype(jnp.bfloat16)
@@ -122,13 +115,22 @@
         part = summed if quad == 0 else pltpu.roll(summed, load - start, 1)
         own_ref[quad] = part[:block, :width]
         send_ref[quad] = part[block:2 * block, :width]
-        same_ref[quad, :HALO] = part[2 * block:2 * block + HALO, :width]
-        same_ref[quad, HALO:] = far_ref[quad]
-        cross_ref[quad] = part[2 * block + HALO:2 * block + 2 * HALO, :width]
+
+
+def edge_kernel(own, info, own_ref, par_ref, far_ref, out_ref):
+    low = info[ITERS * QUADS] == 0
+    cells = own + HALO
+    total = own_ref[...] + par_ref[...]
+    out_ref[...] = jnp.zeros_like(out_ref)
+    for row in range(2):
+        first = total[:, cells * row:cells * row + 1]
+        last = total[:, cells * row + own - 1:cells * row + own]
+        out_ref[:, row:row + 1] = jnp.where(low, first, last)
+    out_ref[:, HALO:] = far_ref[...]
 
 
 def sweeps_kernel(rows, own, cells, quad_size, class_count, info, ax_ref, ay_ref, base_ref,
-                  wind_ref, mt_ref, const_ref, own_ref, par_ref, same_ref, cross_ref, *rest):
+                  wind_ref, mt_ref, const_ref, own_ref, par_ref, far_ref, *rest):
     pairs = QUADS // 2
     keep_refs, send_refs = rest[:pairs], rest[pairs:2 * pairs]
     state, power, rim, side = rest[2 * pairs:]
@@ -150,19 +152,17 @@
     def _():
         power[...] = jnp.zeros_like(power)
 
-    rim[0] = own_ref[quad, 0:cells]
-    rim[0, own:cells] = own_ref[quad, own:cells] + same_ref[quad, :HALO]
-    rim[1] = par_ref[quad, 0:cells]
-    rim[1, own:cells] = par_ref[quad, own:cells] + cross_ref[quad]
     far_at = jnp.where(half == 0, HALO - 1, 0)
     at_far = lax.broadcasted_iota(jnp.int32, (HALO, width), 0) == far_at
+    for j in range(2):
+        here = own_ref[quad, j * cells:(j + 1) * cells] + par_ref[quad, j * cells:(j + 1) * cells]
+        rim[j, :own] = here[:own]
+        rim[j, own:] = here[own:] + jnp.where(at_far, far_ref[quad, j:j + 1], 0.0)
     edge_at = jnp.where(half == 0, 0, 2 * HALO - 1)
     at_edge = lax.broadcasted_iota(jnp.int32, (2 * HALO, width), 0) == edge_at
-    for j in range(rows_dev):
-        mine = jnp.where(at_edge, own_ref[quad, cells + j:cells + j + 1], 0.0)
-        theirs = jnp.where(at_edge, par_ref[quad, cells + j:cells + j + 1], 0.0)
-        side[j + rows_dev * half] = mine
-        side[j + rows_dev * (1 - half)] = theirs
+    beside_edge = own_ref[quad, 2 * cells:] + par_ref[quad, 2 * cells:]
+    for j in range(rows):
+        side[j] = jnp.where(at_edge, beside_edge[j:j + 1], 0.0)
 
     def run(count, second):
         def patched(block, far_row):
@@ -173,7 +173,7 @@
         def factors(i, low, high):
             row = first_row + i * step_x
             kind, strength, far_cos, far_sin = [
-                same_ref[feat, pl.ds(HALO + row, 1), :] for feat in range(4)]
+                far_ref[feat, pl.ds(HALO + row, 1), :] for feat in range(4)]
             far_ax = jnp.zeros((1, width), jnp.float32)
             far_base = jnp.zeros((1, width), jnp.float32)
             for each in range(class_count):
@@ -196,7 +196,7 @@
                 parts.append(source[own:])
             source = jnp.concatenate(parts, axis=0)
             if i == 0 or i == rows - 1:
-                here = jnp.where(row // rows_dev == half, 0, 1)
+                here = jnp.where(row == 0, 0, 1)
                 source = source + rim[here, low:high]
             if second:
                 before = state[quad, row]
@@ -285,7 +285,6 @@
     row_count = lax.axis_size("rows")
     col_count = lax.axis_size("cols")
     assert row_count == 2
-    devices = row_count * col_count
     rows = rows_dev * row_count
     own = cols_dev // 2
     cells = own + HALO
@@ -302,22 +301,19 @@
 
     span = range(col_count)
     swap_route = [(device(1 - h, c), device(h, c)) for h in range(2) for c in span]
-    same_route = [(device(0, c - 1), device(0, c)) for c in span if c > 0]
-    same_route += [(device(1, c + 1), device(1, c)) for c in span if c + 1 < col_count]
     cross_route = [(device(1, c - 1), device(0, c)) for c in span if c > 0]
     cross_route += [(device(0, c + 1), device(1, c)) for c in span if c + 1 < col_count]
 
     points = dest_cell.shape[0]
     load = -(-(comps + 1) // LANES) * LANES
-    sizes = (cols_dev * col_count, rows_dev, cols_dev)
-    shifts = tuple(size.bit_length() - 1 for size in sizes)
-    assert all(size == 2**shift for size, shift in zip(sizes, shifts))
-    slot_total = devices * CAP
+    total_bits, col_bits = [(size.bit_length() - 1) for size in (cols_dev * col_count, cols_dev)]
+    assert cols_dev == 2**col_bits and cols_dev * col_count == 2**total_bits
+    slot_total = col_count * 2 * CAP
     steps = 4
     in_vmem = pl.BlockSpec(memory_space=pltpu.VMEM)
     anywhere = pl.BlockSpec(memory_space=pl.ANY)
     outgoing, held = pl.pallas_call(
-        partial(pack_kernel, shifts, col_count, rows, comps),
+        partial(pack_kernel, total_bits, col_bits, rows, comps),
         grid=(steps,),
         in_specs=[anywhere] * 5,
         out_specs=[pl.BlockSpec((slot_total // steps, load), lambda s: (s, 0)), in_vmem],
@@ -331,7 +327,7 @@
         out_shape=[jax.ShapeDtypeStruct((slot_total, load), jnp.float32),
                    jax.ShapeDtypeStruct((3, rows_dev, cols_dev), jnp.float32)],
         compiler_params=pltpu.CompilerParams(
-            dimension_semantics=("arbitrary",), vmem_limit_bytes=48 * 2**20),
+            dimension_semantics=("arbitrary",), vmem_limit_bytes=60 * 2**20),
     )(dest_cell.reshape(1, points), outer_spectra.T, wind_speed, wind_dir, depth_class)
     outgoing, refraction_inverse = lax.optimization_barrier((outgoing, refraction_inverse))
     scale = jnp.asarray(lane_scale(width))
@@ -340,7 +336,7 @@
     on_diag = jnp.eye(width, dtype=bool)[None]
     matrices = jnp.where(on_diag, 0.0, scaled).astype(jnp.bfloat16)
     diagonal = jnp.sum(jnp.where(on_diag, scaled, 0.0), axis=1, keepdims=True)
-    arrived = lax.all_to_all(outgoing.reshape(devices, CAP, load), axes, split_axis=0,
+    arrived = lax.all_to_all(outgoing.reshape(col_count, 2 * CAP, load), "cols", split_axis=0,
                              concat_axis=0, tiled=True).reshape(slot_total, load)
 
     partner = lax.ppermute(held, axes, swap_route)
@@ -350,7 +346,7 @@
     strength = (chip[0] * 0.1) ** 2
     feats = jnp.stack([chip[2], strength, jnp.cos(chip[1]), jnp.sin(chip[1])])
     far_out = jnp.broadcast_to(
-        jnp.where(is_low, feats[:, :, cols_dev - 1:], feats[:, :, :1]), (QUADS, rows, width))
+        jnp.where(is_low, feats[:, :, :1], feats[:, :, cols_dev - 1:]), (QUADS, rows, width))
     mine = jnp.where(is_low, feats[:, :, :own], feats[:, :, own:])
     right = jnp.where(is_low, feats[:, :, own], 0.0)
     left = jnp.where(is_low, 0.0, feats[:, :, own - 1])
@@ -391,19 +387,24 @@
         (arrived, ax, ay, base, wind, matrices))
 
     info = jnp.concatenate([sweep_order.reshape(-1), half[None].astype(jnp.int32)])
-    block = cells + rows_dev
-    rim_shapes = [jax.ShapeDtypeStruct((QUADS, size, width), jnp.float32)
-                  for size in (block, block, HALO + rows, HALO)]
-    rim_own, rim_send, out_same, out_cross = pl.pallas_call(
-        partial(rim_kernel, own, rows_dev, comps, quad_size),
-        in_specs=[pl.BlockSpec(memory_space=pltpu.SMEM), in_vmem, in_vmem],
-        out_specs=[in_vmem] * len(rim_shapes),
-        out_shape=rim_shapes,
+    block = 2 * cells + rows
+    in_smem = pl.BlockSpec(memory_space=pltpu.SMEM)
+    rim_shape = jax.ShapeDtypeStruct((QUADS, block, width), jnp.float32)
+    rim_own, rim_send = pl.pallas_call(
+        partial(rim_kernel, own, rows, comps, quad_size),
+        in_specs=[in_smem, in_vmem],
+        out_specs=[in_vmem] * 2,
+        out_shape=[rim_shape] * 2,
         compiler_params=pltpu.CompilerParams(vmem_limit_bytes=40 * 2**20),
-    )(info, arrived, far_out)
+    )(info, arrived)
     rim_partner = lax.ppermute(rim_send, axes, swap_route)
-    rim_same = lax.ppermute(out_same, axes, same_route)
-    rim_cross = lax.ppermute(out_cross, axes, cross_route)
+    edge = pl.pallas_call(
+        partial(edge_kernel, own),
+        in_specs=[in_smem] + [in_vmem] * 3,
+        out_specs=in_vmem,
+        out_shape=jax.ShapeDtypeStruct((QUADS, HALO + rows, width), jnp.float32),
+    )(info, rim_own, rim_partner, far_out)
+    far = lax.ppermute(edge, axes, cross_route)
 
     turns = ITERS * QUADS
 
@@ -420,7 +421,7 @@
             grid=(turns,),
             in_specs=[quad_block((rows, cells, width))] * 4
             + [quad_block((width, width)), quad_block(consts.shape[1:])]
-            + [in_vmem] * 4,
+            + [in_vmem] * 3,
             out_specs=[in_vmem] * (2 * pairs),
             scratch_shapes=[
                 pltpu.VMEM((QUADS, rows, cells, width), jnp.float32),
@@ -432,7 +433,7 @@
         out_shape=[packed] * (2 * pairs),
         compiler_params=pltpu.CompilerParams(
             dimension_semantics=("arbitrary",), vmem_limit_bytes=49 * 2**20),
-    )(info, ax, ay, base, wind, matrices, consts, rim_own, rim_partner, rim_same, rim_cross)
+    )(info, ax, ay, base, wind, matrices, consts, rim_own, rim_partner, far)
 
     got = [lax.ppermute(half_out, axes, swap_route) for half_out in halves[pairs:]]
     chunks = 4
@@ -440,7 +441,7 @@
     for pair in range(pairs):
         merged = [pl.pallas_call(
             partial(merge_kernel, own, pair, chunks),
-            in_specs=[pl.BlockSpec(memory_space=pltpu.SMEM), in_vmem, in_vmem]
+            in_specs=[in_smem, in_vmem, in_vmem]
             + [pl.BlockSpec(memory_space=pl.ANY)] * len(merged),
             out_specs=pl.BlockSpec(memory_space=pl.ANY),
             scratch_shapes=[

time: 98.9 us -> 104 us (1.052); the launches traced: 97.6 us -> 104 us
  Pallas kernels: 30.6 us -> 35.7 us
  waiting for transfers between devices: 32.5 us -> 34.9 us
    pallas_call x4 -> x5, Pallas kernels: 7.88 us -> 12 us  [the longest x1 4.24 us: body(): pl.pallas_call(partial(pack_kernel, total_bits, col_bits, rows, comps), g...]
    ppermute x2 -> x1, starting transfers between devices: 6.04 us -> 3.14 us  [body(): far = lax.ppermute(edge, axes, cross_route)]
    all_to_all x1, waiting for transfers between devices: 29 us -> 27.1 us  [body(): lax.all_to_all(outgoing.reshape(col_count, 2 * CAP, load), 'cols', split_...]
    ppermute x1, waiting for transfers between devices: 0.01 us -> 1.72 us  [body(): rim_partner = lax.ppermute(rim_send, axes, swap_route)]
    ppermute x1, starting transfers between devices: 0.51 us -> 2.07 us  [body(): rim_partner = lax.ppermute(rim_send, axes, swap_route)]
    unnamed x36 -> x38, local copies, waits for them, and re-layouts: 5.2 us -> 3.81 us
    ppermute x2, waiting for transfers between devices: 1.98 us -> 3.29 us  [body(): lax.ppermute(half_out, axes, swap_route)]
    ppermute x2 -> x1, waiting for transfers between devices: 1.54 us -> 2.83 us  [body(): far = lax.ppermute(edge, axes, cross_route)]
  transfers between devices with their start and end apart: 7 -> 6, of which waited for: 3 -> 4; matrix products, arithmetic and copies ran while one was open for 13% -> 12% of each run, Pallas kernels for 2% -> 2%
where the time goes in v9:
time: 104 us
  Pallas kernels  35.7 us (34%)
  waiting for transfers between devices  34.9 us (34%)
  starting transfers between devices  15.2 us (15%)
  other arithmetic  10.4 us (10%)
  local copies, waits for them, and re-layouts  6.99 us (7%)
    all_to_all x1, waiting for transfers between devices, body(): lax.all_to_all(outgoing.reshape(col_count, 2 * CAP, load), 'cols', split_...  27.1 us
    pallas_call x1, Pallas kernels, body(): pl.pallas_call(partial(sweeps_kernel, rows, own, cells, quad_size, class_...  23.7 us
    select_n x1, other arithmetic, by_class(): jnp.where((class_here == kind)[None, :, :, None], table[:, None, None, ki...  6.65 us
    all_to_all x1, starting transfers between devices, body(): lax.all_to_all(outgoing.reshape(col_count, 2 * CAP, load), 'cols', split_...  6.56 us
    pallas_call x1, Pallas kernels, body(): pl.pallas_call(partial(pack_kernel, total_bits, col_bits, rows, comps), g...  4.24 us
    pallas_call x2, Pallas kernels, body(): pl.pallas_call(partial(merge_kernel, own, pair, chunks), in_specs=[in_sme...  4 us
    unnamed x38, local copies, waits for them, and re-layouts  3.81 us
    ppermute x2, waiting for transfers between devices, body(): lax.ppermute(half_out, axes, swap_route)  3.29 us
  transfers between devices with their start and end apart: 6, of which 4 were waited for; matrix products, arithmetic and copies ran while one was open for 12% of the time, Pallas kernels for 2%

profile of v9, /device:TPU:17, one launch (start us, length us, event | category | flops | bytes accessed | tf_op | source)
XLA Modules:
  0.0 103.8 jit_solution(11508041695785953831)
XLA Ops:
  0.0 4.2 %shard_map.109 = (f32[512,896]{1,0:T(8,128)}, f32[3,8,128]{2,1,0:T(8,128)}) custom-call(s32[1,256]{1,0:T(1,128)} %bitcast.71, f32[864,256]{1,0:T(8,128)} %bitcast.58, f32[8,128]{1,0:T(8,128)} %wind_hbm.1, f32[8,128]{1,0:T(8,128)} %dir_hbm.1, s32[8,128]{1,0:T(8,128)} %class_hbm.1), custom_call_target="tpu_custom_call" | custom-call | tf_op jit(solution)/shard_map/pallas_call | solution.py:315
  4.3 6.6 %all-to-all-start = ((f32[16,32,896]{2,1,0:T(8,128)}), f32[16,32,896]{2,1,0:T(8,128)S(1)}, u32[]{:S(2)}, u32[]{:S(2)}) async-start(f32[16,32,896]{2,1,0:T(8,128)} %bitcast.57), calls=%async_computation | async-start | bytes 3670016 | tf_op jit(solution)/shard_map/all_to_all | solution.py:339
  10.8 1.2 %collective-permute-start = (f32[3,8,128]{2,1,0:T(8,128)}, f32[3,8,128]{2,1,0:T(8,128)S(1)}, u32[]{:S(2)}, u32[]{:S(2)}) collective-permute-start(f32[3,8,128]{2,1,0:T(8,128)} %get-tuple-element.23), channel_id=1, source_target_pairs={{16,0},{17,1},{18,2},{19,3},{20,4},{21,5},{22,6},{23,7},{24,8},{25... | collective-permute-start | bytes 36872 | tf_op jit(solution)/shard_map/ppermute | solution.py:342
  12.3 0.1 broadcast_in_dim.215
  12.4 0.1 broadcast_in_dim.203
  12.9 0.1 reshape.87
  12.9 1.5 %copy.14 = f32[4,216,216]{1,2,0:T(8,128)S(1)} copy(f32[4,216,216]{2,1,0:T(8,128)} %param.19) | data formatting | bytes 1492992 | tf_op jit(solution)/shard_map/optimization_barrier | solution.py:332
  14.5 0.2 select_reduce_fusion
  14.7 0.1 pad_add_fusion.info
  14.8 0.1 tile.32
  15.3 0.2 fusion
  15.4 0.1 pad_maximum_fusion.1
  15.6 0.2 broadcast_multiply_fusion
  15.8 2.7 %multiply_multiply_fusion.wind_ref = f32[4,16,72,256]{3,2,1,0:T(8,128)} fusion(f32[4,256]{1,0:T(4,128)S(1)} %get-tuple-element.77, f32[16,72]{1,0:T(8,128)S(1)} %get-tuple-element.43, f32[4,256]{1,0:T(4,128)S(1)} %get-tuple-element.72, f32[16,72]{1,0:T(8,128)S(1)} %get-tuple-element.44, f32[16,72,256]{2,1,0:T(8,128)S(1)} %broadcast_multiply_fusion), kind=kLoop, calls=%fused_computation | loop fusion | flops 7077888 | bytes 5915648 | tf_op jit(solution)/shard_map/mul | solution.py:384
  18.4 6.7 %select_select_fusion = (f32[4,16,72,256]{3,2,1,0:T(8,128)}, f32[4,16,72,256]{3,2,1,0:T(8,128)}, f32[4,16,72,256]{3,2,1,0:T(8,128)}) fusion(f32[4,256]{1,0:T(4,128)S(1)} %bitcast.64, f32[4,256]{1,0:T(4,128)S(1)} %bitcast.65, f32[4,256]{1,0:T(4,128)S(1)} %bitcast.66, f32[4,256]{1,0:T(4,128)S(1)} %bitcast.63, pred[16,72]{1,0:T(8,128)(4,1)S(1)} %get-tuple-element.47, ...), kind=kLoop, calls=%fused_computation.1 | loop fusion | flops 10616832 | bytes 14208384 | tf_op jit(solution)/shard_map/jit(_where)/select_n | solution.py:375
  25.1 27.1 %all-to-all-done = f32[16,32,896]{2,1,0:T(8,128)S(1)} async-done(((f32[16,32,896]{2,1,0:T(8,128)}), f32[16,32,896]{2,1,0:T(8,128)S(1)}, u32[]{:S(2)}, u32[]{:S(2)}) %all-to-all-start) | async-done | bytes 1835040 | tf_op jit(solution)/shard_map/all_to_all | solution.py:339
  52.2 1.8 %shard_map.110 = (f32[4,160,256]{2,1,0:T(8,128)S(1)}, f32[4,160,256]{2,1,0:T(8,128)S(1)}) custom-call(s32[9]{0:T(128)S(1)} %pad_add_fusion.info, f32[512,896]{1,0:T(8,128)S(1)} %bitcast.55), custom_call_target="tpu_custom_call" | custom-call | tf_op jit(solution)/shard_map/pallas_call | solution.py:393
  54.0 0.8 copy-done
  54.8 2.1 %collective-permute-start.1 = (f32[4,160,256]{2,1,0:T(8,128)S(1)}, f32[4,160,256]{2,1,0:T(8,128)S(1)}, u32[]{:S(2)}, u32[]{:S(2)}) collective-permute-start(f32[4,160,256]{2,1,0:T(8,128)S(1)} %get-tuple-element.32), channel_id=1, source_target_pairs={{16,0},{17,1},{18,2},{19,3},{20,4},{21,5},{22,6},{23,7},{24,8},{25... | collective-permute-start | bytes 1966088 | tf_op jit(solution)/shard_map/ppermute | solution.py:400
  56.9 1.7 %collective-permute-done.1.par_ref = f32[4,160,256]{2,1,0:T(8,128)S(1)} collective-permute-done((f32[4,160,256]{2,1,0:T(8,128)S(1)}, f32[4,160,256]{2,1,0:T(8,128)S(1)}, u32[]{:S(2)}, u32[]{:S(2)}) %collective-permute-start.1) | collective-permute-done | bytes 655392 | tf_op jit(solution)/shard_map/ppermute | solution.py:400
  58.6 0.8 broadcast_in_dim.236.far_ref
  59.5 1.9 %shard_map.111 = f32[4,24,256]{2,1,0:T(8,128)} custom-call(s32[9]{0:T(128)} %copy-done.4, f32[4,160,256]{2,1,0:T(8,128)} %copy-done, f32[4,160,256]{2,1,0:T(8,128)} %copy-done.2, f32[4,16,256]{2,1,0:T(8,128)} %broadcast_in_dim.236.far_ref), custom_call_target="tpu_custom_call" | custom-call | tf_op jit(solution)/shard_map/pallas_call | solution.py:401
  61.5 3.1 %collective-permute-start.2 = (f32[4,24,256]{2,1,0:T(8,128)}, f32[4,24,256]{2,1,0:T(8,128)S(1)}, u32[]{:S(2)}, u32[]{:S(2)}) collective-permute-start(f32[4,24,256]{2,1,0:T(8,128)} %shard_map.111), channel_id=1, source_target_pairs={{16,1},{17,2},{18,3},{19,4},{20,5},{21,6},{22,7},{23,8},{24,9},{25... | collective-permute-start | bytes 294920 | tf_op jit(solution)/shard_map/ppermute | solution.py:407
  64.8 2.8 %collective-permute-done.2.far_ref = f32[4,24,256]{2,1,0:T(8,128)S(1)} collective-permute-done((f32[4,24,256]{2,1,0:T(8,128)}, f32[4,24,256]{2,1,0:T(8,128)S(1)}, u32[]{:S(2)}, u32[]{:S(2)}) %collective-permute-start.2) | collective-permute-done | bytes 98336 | tf_op jit(solution)/shard_map/ppermute | solution.py:407
  67.6 1.1 %copy-done.1 = f32[4,160,256]{2,1,0:T(8,128)S(1)} copy-done((f32[4,160,256]{2,1,0:T(8,128)S(1)}, f32[4,160,256]{2,1,0:T(8,128)}, u32[]{:S(2)}) %copy-start.1) | copy-done | bytes 655384
  68.7 1.1 %copy-done.3 = f32[4,160,256]{2,1,0:T(8,128)S(1)} copy-done((f32[4,160,256]{2,1,0:T(8,128)S(1)}, f32[4,160,256]{2,1,0:T(8,128)}, u32[]{:S(2)}) %copy-start.3) | copy-done | bytes 655384
  69.8 0.7 copy-done.5
  70.4 23.7 %shard_map.112 = (f32[216,8,128]{2,1,0:T(8,128)S(1)}, f32[216,8,128]{2,1,0:T(8,128)S(1)}, f32[216,8,128]{2,1,0:T(8,128)S(1)}, f32[216,8,128]{2,1,0:T(8,128)}) custom-call(s32[9]{0:T(128)S(1)} %copy-done.5, f32[4,16,72,256]{3,2,1,0:T(8,128)} %get-tuple-element.25.ax_ref, f32[4,16,72,256]{3,2,1,0:T(8,128)} %get-tuple-element.26.ay_ref, ...), custom_call_target="tpu_custom_call" | custom-call | tf_op jit(solution)/shard_map/pallas_call | solution.py:417
  94.1 2.2 %collective-permute-start.4 = (f32[216,8,128]{2,1,0:T(8,128)S(1)}, f32[216,8,128]{2,1,0:T(8,128)S(1)}, u32[]{:S(2)}, u32[]{:S(2)}) collective-permute-start(f32[216,8,128]{2,1,0:T(8,128)S(1)} %get-tuple-element.36), channel_id=1, source_target_pairs={{16,0},{17,1},{18,2},{19,3},{20,4},{21,5},{22,6},{23,7},{24,8},{25... | collective-permute-start | bytes 2654216 | tf_op jit(solution)/shard_map/ppermute | solution.py:438
  96.3 3.3 %collective-permute-done.4.got_ref = f32[216,8,128]{2,1,0:T(8,128)S(1)} collective-permute-done((f32[216,8,128]{2,1,0:T(8,128)S(1)}, f32[216,8,128]{2,1,0:T(8,128)S(1)}, u32[]{:S(2)}, u32[]{:S(2)}) %collective-permute-start.4) | collective-permute-done | bytes 884768 | tf_op jit(solution)/shard_map/ppermute | solution.py:438
  99.6 2.0 %shard_map.113.rest_0_ = f32[4,216,8,128]{3,2,1,0:T(8,128)} custom-call(s32[9]{0:T(128)S(1)} %copy-done.5, f32[216,8,128]{2,1,0:T(8,128)S(1)} %get-tuple-element.35.keep_ref, f32[216,8,128]{2,1,0:T(8,128)S(1)} %collective-permute-done.4.got_ref), custom_call_target="tpu_custom_call" | custom-call | tf_op jit(solution)/shard_map/pallas_call | solution.py:442
  101.6 2.0 %shard_map.114 = f32[4,216,8,128]{3,2,1,0:T(8,128)} custom-call(s32[9]{0:T(128)S(1)} %copy-done.5, f32[216,8,128]{2,1,0:T(8,128)S(1)} %get-tuple-element.33.keep_ref, f32[216,8,128]{2,1,0:T(8,128)S(1)} %collective-permute-done.3.got_ref, f32[4,216,8,128]{3,2,1,0:T(8,128)} %shard_map.113.rest_0_), custom_call_target="tpu_custom_call", output_to_operand_aliasing={{}: (3, {})} | custom-call | tf_op jit(solution)/shard_map/pallas_call | solution.py:442
  (70 shorter events, 1.0 us)
Async XLA Ops:
  0.0 14.5 %copy-start.9 = (f32[256]{0:T(256)S(1)}, f32[256]{0:T(256)}, u32[]{:S(2)}) copy-start(f32[256]{0:T(256)} %constant.47) | copy-start | bytes 3076
  0.0 12.5 %copy-start.7 = (f32[4,24]{1,0:T(4,128)S(1)}, f32[4,24]{1,0:T(4,128)}, u32[]{:S(2)}) copy-start(f32[4,24]{1,0:T(4,128)} %param.14) | copy-start | bytes 1156
  0.0 12.6 %copy-start.8 = (f32[4,24]{1,0:T(4,128)S(1)}, f32[4,24]{1,0:T(4,128)}, u32[]{:S(2)}) copy-start(f32[4,24]{1,0:T(4,128)} %param.15) | copy-start | bytes 1156
  0.0 12.8 %copy-start.12 = (s32[2,4]{1,0:T(2,128)S(1)}, s32[2,4]{1,0:T(2,128)}, u32[]{:S(2)}) copy-start(s32[2,4]{1,0:T(2,128)} %param.20) | copy-start | bytes 100
  0.0 14.8 %copy-start.11 = (f32[24]{0:T(128)S(1)}, f32[24]{0:T(128)}, u32[]{:S(2)}) copy-start(f32[24]{0:T(128)} %param.16) | copy-start | bytes 292
  4.3 10.8 %copy-start.6 = (f32[3,8,128]{2,1,0:T(8,128)S(1)}, f32[3,8,128]{2,1,0:T(8,128)}, u32[]{:S(2)}) copy-start(f32[3,8,128]{2,1,0:T(8,128)} %get-tuple-element.23) | copy-start | bytes 36868
  4.3 47.9 %all-to-all-start = ((f32[16,32,896]{2,1,0:T(8,128)}), f32[16,32,896]{2,1,0:T(8,128)S(1)}, u32[]{:S(2)}, u32[]{:S(2)}) async-start(f32[16,32,896]{2,1,0:T(8,128)} %bitcast.57), calls=%async_computation | async-start | bytes 3670016 | tf_op jit(solution)/shard_map/all_to_all | solution.py:339
  10.8 4.3 %collective-permute-start = (f32[3,8,128]{2,1,0:T(8,128)}, f32[3,8,128]{2,1,0:T(8,128)S(1)}, u32[]{:S(2)}, u32[]{:S(2)}) collective-permute-start(f32[3,8,128]{2,1,0:T(8,128)} %get-tuple-element.23), channel_id=1, source_target_pairs={{16,0},{17,1},{18,2},{19,3},{20,4},{21,5},{22,6},{23,7},{24,8},{25... | collective-permute-start | bytes 36872 | tf_op jit(solution)/shard_map/ppermute | solution.py:342
  14.8 37.4 %copy-start.4 = (s32[9]{0:T(128)}, s32[9]{0:T(128)S(1)}, u32[]{:S(2)}) copy-start(s32[9]{0:T(128)S(1)} %pad_add_fusion.info) | copy-start | bytes 112
  18.4 46.2 %copy-start.10 = (f32[256]{0:T(256)S(1)}, f32[256]{0:T(256)}, u32[]{:S(2)}) copy-start(f32[256]{0:T(256)} %constant.30.clone) | copy-start | bytes 3076
  54.0 0.8 copy-start
  54.8 3.8 %collective-permute-start.1 = (f32[4,160,256]{2,1,0:T(8,128)S(1)}, f32[4,160,256]{2,1,0:T(8,128)S(1)}, u32[]{:S(2)}, u32[]{:S(2)}) collective-permute-start(f32[4,160,256]{2,1,0:T(8,128)S(1)} %get-tuple-element.32), channel_id=1, source_target_pairs={{16,0},{17,1},{18,2},{19,3},{20,4},{21,5},{22,6},{23,7},{24,8},{25... | collective-permute-start | bytes 1966088 | tf_op jit(solution)/shard_map/ppermute | solution.py:400
  58.6 0.9 copy-start.2
  61.5 6.1 %collective-permute-start.2 = (f32[4,24,256]{2,1,0:T(8,128)}, f32[4,24,256]{2,1,0:T(8,128)S(1)}, u32[]{:S(2)}, u32[]{:S(2)}) collective-permute-start(f32[4,24,256]{2,1,0:T(8,128)} %shard_map.111), channel_id=1, source_target_pairs={{16,1},{17,2},{18,3},{19,4},{20,5},{21,6},{22,7},{23,8},{24,9},{25... | collective-permute-start | bytes 294920 | tf_op jit(solution)/shard_map/ppermute | solution.py:407
  67.6 1.1 %copy-start.1 = (f32[4,160,256]{2,1,0:T(8,128)S(1)}, f32[4,160,256]{2,1,0:T(8,128)}, u32[]{:S(2)}) copy-start(f32[4,160,256]{2,1,0:T(8,128)} %copy-done) | copy-start | bytes 1966084
  68.7 1.1 %copy-start.3 = (f32[4,160,256]{2,1,0:T(8,128)S(1)}, f32[4,160,256]{2,1,0:T(8,128)}, u32[]{:S(2)}) copy-start(f32[4,160,256]{2,1,0:T(8,128)} %copy-done.2) | copy-start | bytes 1966084
  69.8 0.7 copy-start.5
  94.1 5.5 %collective-permute-start.4 = (f32[216,8,128]{2,1,0:T(8,128)S(1)}, f32[216,8,128]{2,1,0:T(8,128)S(1)}, u32[]{:S(2)}, u32[]{:S(2)}) collective-permute-start(f32[216,8,128]{2,1,0:T(8,128)S(1)} %get-tuple-element.36), channel_id=1, source_target_pairs={{16,0},{17,1},{18,2},{19,3},{20,4},{21,5},{22,6},{23,7},{24,8},{25... | collective-permute-start | bytes 2654216 | tf_op jit(solution)/shard_map/ppermute | solution.py:438
  96.3 5.3 %collective-permute-start.3 = (f32[216,8,128]{2,1,0:T(8,128)}, f32[216,8,128]{2,1,0:T(8,128)S(1)}, u32[]{:S(2)}, u32[]{:S(2)}) collective-permute-start(f32[216,8,128]{2,1,0:T(8,128)} %get-tuple-element.34), channel_id=1, source_target_pairs={{16,0},{17,1},{18,2},{19,3},{20,4},{21,5},{22,6},{23,7},{24,8},{25... | collective-permute-start | bytes 2654216 | tf_op jit(solution)/shard_map/ppermute | solution.py:438

commit v10 on v8

--- a/solution.py
+++ b/solution.py
@@ -122,16 +122,17 @@
         part = summed if quad == 0 else pltpu.roll(summed, load - start, 1)
         own_ref[quad] = part[:block, :width]
         send_ref[quad] = part[block:2 * block, :width]
-        same_ref[quad, :HALO] = part[2 * block:2 * block + HALO, :width]
-        same_ref[quad, HALO:] = far_ref[quad]
+        halo = part[2 * block:2 * block + HALO, :width]
+        free = lax.broadcasted_iota(jnp.int32, halo.shape, 1) >= quad_size
+        same_ref[quad] = jnp.where(free, far_ref[quad], halo)
         cross_ref[quad] = part[2 * block + HALO:2 * block + 2 * HALO, :width]
 
 
-def sweeps_kernel(rows, own, cells, quad_size, class_count, info, ax_ref, ay_ref, base_ref,
+def sweeps_kernel(rows, own, cells, quad_size, class_count, info, ax_ref, base_ref,
                   wind_ref, mt_ref, const_ref, own_ref, par_ref, same_ref, cross_ref, *rest):
     pairs = QUADS // 2
     keep_refs, send_refs = rest[:pairs], rest[pairs:2 * pairs]
-    state, power, rim, side = rest[2 * pairs:]
+    state, power, rim, side, far_rows = rest[2 * pairs:]
     turn = pl.program_id(0)
     quad = info[turn]
     half = info[ITERS * QUADS]
@@ -139,8 +140,8 @@
     rows_dev = rows // 2
     ax_table = const_ref[0, :class_count]
     base_table = const_ref[0, class_count:2 * class_count]
-    rate_lane, cos_lane, sin_lane, scale_lane, diag_lane = [
-        const_ref[0, 2 * class_count + each:2 * class_count + each + 1] for each in range(5)]
+    rate_lane, cos_lane, sin_lane, scale_lane, ratio_lane, diag_lane = [
+        const_ref[0, 2 * class_count + each:2 * class_count + each + 1] for each in range(6)]
     down = (quad == 0) | (quad == 3)
     step_x = jnp.where(down, 1, -1)
     first_row = jnp.where(down, 0, rows - 1)
@@ -149,9 +150,15 @@
     @pl.when(turn == 0)
     def _():
         power[...] = jnp.zeros_like(power)
+        numbers = jnp.concatenate(
+            [same_ref[feat, 0:1, width - LANES:] for feat in range(4)]
+            + [jnp.zeros((4, LANES), jnp.float32)], axis=0).T
+        for feat in range(4):
+            far_rows[feat] = jnp.broadcast_to(
+                numbers[LANES - rows:, feat:feat + 1], (rows, width))
 
     rim[0] = own_ref[quad, 0:cells]
-    rim[0, own:cells] = own_ref[quad, own:cells] + same_ref[quad, :HALO]
+    rim[0, own:cells] = own_ref[quad, own:cells] + same_ref[quad]
     rim[1] = par_ref[quad, 0:cells]
     rim[1, own:cells] = par_ref[quad, own:cells] + cross_ref[quad]
     far_at = jnp.where(half == 0, HALO - 1, 0)
@@ -173,7 +180,7 @@
         def factors(i, low, high):
             row = first_row + i * step_x
             kind, strength, far_cos, far_sin = [
-                same_ref[feat, pl.ds(HALO + row, 1), :] for feat in range(4)]
+                far_rows[feat, pl.ds(row, 1), :] for feat in range(4)]
             far_ax = jnp.zeros((1, width), jnp.float32)
             far_base = jnp.zeros((1, width), jnp.float32)
             for each in range(class_count):
@@ -201,7 +208,7 @@
             if second:
                 before = state[quad, row]
                 shifted = jnp.where(up_y, pltpu.roll(before, 1, 0), pltpu.roll(before, cells - 1, 0))
-                source = source + ay_ref[0, row, low:high] * shifted[low:high]
+                source = source + ax_ref[0, row, low:high] * (ratio_lane * shifted[low:high])
             return patched(ax_ref[0, row, low:high], far_ax) * inverse, source * inverse
 
         def store(i, value):
@@ -214,18 +221,18 @@
             power[quad, row, :count] = jnp.broadcast_to(
                 jnp.sum(folded, axis=1, keepdims=True), (count, LANES))
 
-        along, known = factors(0, 0, count)
+        balance = factors(0, 0, count)[1]
         upwind = None
         for i in range(rows):
-            balance = known if upwind is None else along * upwind + known
             mixed = jnp.dot(balance.astype(jnp.bfloat16), mt_ref[0],
                             preferred_element_type=jnp.float32)
-            updated = diag_lane * balance + mixed
+            direct = diag_lane * balance
             if i + 1 < rows:
                 along, known = factors(i + 1, 0, count)
+                balance = along * mixed + (along * direct + known)
             if i > 0:
                 store(i - 1, upwind)
-            upwind = updated
+            upwind = direct + mixed
         store(rows - 1, upwind)
 
     @pl.when(turn < QUADS)
@@ -331,7 +338,7 @@
         out_shape=[jax.ShapeDtypeStruct((slot_total, load), jnp.float32),
                    jax.ShapeDtypeStruct((3, rows_dev, cols_dev), jnp.float32)],
         compiler_params=pltpu.CompilerParams(
-            dimension_semantics=("arbitrary",), vmem_limit_bytes=48 * 2**20),
+            dimension_semantics=("arbitrary",), vmem_limit_bytes=60 * 2**20),
     )(dest_cell.reshape(1, points), outer_spectra.T, wind_speed, wind_dir, depth_class)
     outgoing, refraction_inverse = lax.optimization_barrier((outgoing, refraction_inverse))
     scale = jnp.asarray(lane_scale(width))
@@ -349,8 +356,10 @@
         [jnp.where(is_low, held, partner), jnp.where(is_low, partner, held)], axis=1)
     strength = (chip[0] * 0.1) ** 2
     feats = jnp.stack([chip[2], strength, jnp.cos(chip[1]), jnp.sin(chip[1])])
-    far_out = jnp.broadcast_to(
-        jnp.where(is_low, feats[:, :, cols_dev - 1:], feats[:, :, :1]), (QUADS, rows, width))
+    assert width - rows >= quad_size and rows <= LANES
+    far_out = jnp.pad(
+        jnp.where(is_low, feats[:, :, cols_dev - 1], feats[:, :, 0])[:, None],
+        ((0, 0), (0, 0), (width - rows, 0)))
     mine = jnp.where(is_low, feats[:, :, :own], feats[:, :, own:])
     right = jnp.where(is_low, feats[:, :, own], 0.0)
     left = jnp.where(is_low, 0.0, feats[:, :, own - 1])
@@ -368,8 +377,9 @@
     ay_table = jnp.abs(sin_lane)[:, None] * speed_lane[None]
     base_table = ax_table + ay_table + loss_lane[None]
 
+    ratio_lane = jnp.abs(sin_lane) / jnp.where(cos_lane == 0.0, 1.0, jnp.abs(cos_lane))
     lanes = jnp.stack([jnp.broadcast_to(rate_lane, (QUADS, width)), cos_lane, sin_lane,
-                       jnp.broadcast_to(scale, (QUADS, width))], axis=1)
+                       jnp.broadcast_to(scale, (QUADS, width)), ratio_lane], axis=1)
     consts = jnp.concatenate([ax_table, base_table, lanes, diagonal], axis=1)
     consts = pad_to(consts, 1, -(-consts.shape[1] // 8) * 8)
 
@@ -380,20 +390,19 @@
         return chosen
 
     ax = by_class(ax_table)
-    ay = by_class(ay_table)
     base = by_class(base_table)
     spread = jnp.maximum(
         cos_here[None, :, :, None] * cos_lane[:, None, None]
         + sin_here[None, :, :, None] * sin_lane[:, None, None], 0.0)
     wind = (rate_lane[None, None, None] * strength[None, :, :, None]) * (spread * spread)
 
-    arrived, ax, ay, base, wind, matrices = lax.optimization_barrier(
-        (arrived, ax, ay, base, wind, matrices))
+    arrived, ax, base, wind, matrices = lax.optimization_barrier(
+        (arrived, ax, base, wind, matrices))
 
     info = jnp.concatenate([sweep_order.reshape(-1), half[None].astype(jnp.int32)])
     block = cells + rows_dev
     rim_shapes = [jax.ShapeDtypeStruct((QUADS, size, width), jnp.float32)
-                  for size in (block, block, HALO + rows, HALO)]
+                  for size in (block, block, HALO, HALO)]
     rim_own, rim_send, out_same, out_cross = pl.pallas_call(
         partial(rim_kernel, own, rows_dev, comps, quad_size),
         in_specs=[pl.BlockSpec(memory_space=pltpu.SMEM), in_vmem, in_vmem],
@@ -418,7 +427,7 @@
         grid_spec=pltpu.PrefetchScalarGridSpec(
             num_scalar_prefetch=1,
             grid=(turns,),
-            in_specs=[quad_block((rows, cells, width))] * 4
+            in_specs=[quad_block((rows, cells, width))] * 3
             + [quad_block((width, width)), quad_block(consts.shape[1:])]
             + [in_vmem] * 4,
             out_specs=[in_vmem] * (2 * pairs),
@@ -427,12 +436,13 @@
                 pltpu.VMEM((QUADS, rows, cells, LANES), jnp.float32),
                 pltpu.VMEM((2, cells, width), jnp.float32),
                 pltpu.VMEM((rows, 2 * HALO, width), jnp.float32),
+                pltpu.VMEM((4, rows, width), jnp.float32),
             ],
         ),
         out_shape=[packed] * (2 * pairs),
         compiler_params=pltpu.CompilerParams(
-            dimension_semantics=("arbitrary",), vmem_limit_bytes=49 * 2**20),
-    )(info, ax, ay, base, wind, matrices, consts, rim_own, rim_partner, rim_same, rim_cross)
+            dimension_semantics=("arbitrary",), vmem_limit_bytes=48 * 2**20),
+    )(info, ax, base, wind, matrices, consts, rim_own, rim_partner, rim_same, rim_cross)
 
     got = [lax.ppermute(half_out, axes, swap_route) for half_out in halves[pairs:]]
     chunks = 4

time: 98.9 us -> 94.1 us (0.951)
  local copies, waits for them, and re-layouts: 7.65 us -> 3.17 us
  other arithmetic: 10.4 us -> 8.7 us
    unnamed x36 -> x20, local copies, waits for them, and re-layouts: 5.2 us -> 0.05 us
    pallas_call x1, Pallas kernels: 2.39 us -> 4.23 us  [body(): pl.pallas_call(partial(pack_kernel, shifts, col_count, rows, comps), grid...]
    select_n x1, other arithmetic: 6.65 us -> 4.84 us  [by_class(): jnp.where((class_here == kind)[None, :, :, None], table[:, None, None, ki...]
    pallas_call x1, Pallas kernels: 22.7 us -> 21.6 us  [body(): pl.pallas_call(partial(sweeps_kernel, rows, own, cells, quad_size, class_...]
    all_to_all x1, waiting for transfers between devices: 29 us -> 30 us  [body(): lax.all_to_all(outgoing.reshape(devices, CAP, load), axes, split_axis=0,...]
where the time goes in v10:
time: 94.1 us; the launch traced here: 92.9 us
  waiting for transfers between devices  33.3 us (35%)
  Pallas kernels  31.3 us (33%)
  starting transfers between devices  15.9 us (17%)
  other arithmetic  8.7 us (9%)
  local copies, waits for them, and re-layouts  3.17 us (3%)
    all_to_all x1, waiting for transfers between devices, body(): lax.all_to_all(outgoing.reshape(devices, CAP, load), axes, split_axis=0,...  30 us
    pallas_call x1, Pallas kernels, body(): pl.pallas_call(partial(sweeps_kernel, rows, own, cells, quad_size, class_...  21.6 us
    all_to_all x1, starting transfers between devices, body(): lax.all_to_all(outgoing.reshape(devices, CAP, load), axes, split_axis=0,...  6.25 us
    select_n x1, other arithmetic, by_class(): jnp.where((class_here == kind)[None, :, :, None], table[:, None, None, ki...  4.84 us
    pallas_call x1, Pallas kernels, body(): pl.pallas_call(partial(pack_kernel, shifts, col_count, rows, comps), grid...  4.23 us
    pallas_call x2, Pallas kernels, body(): pl.pallas_call(partial(merge_kernel, own, pair, chunks), in_specs=[pl.Blo...  3.99 us
    ppermute x1, starting transfers between devices, body(): rim_cross = lax.ppermute(out_cross, axes, cross_route)  3.95 us
    ppermute x2, starting transfers between devices, body(): lax.ppermute(half_out, axes, swap_route)  2.9 us
  transfers between devices with their start and end apart: 7, of which 3 were waited for; matrix products, arithmetic and copies ran while one was open for 13% of the time, Pallas kernels for 2%

profile of v10, /device:TPU:17, one launch (start us, length us, event | category | flops | bytes accessed | tf_op | source)
XLA Modules:
  0.0 92.9 jit_solution(10923760232271930185)
XLA Ops:
  0.0 4.2 %shard_map.109 = (f32[512,896]{1,0:T(8,128)}, f32[3,8,128]{2,1,0:T(8,128)}) custom-call(s32[1,256]{1,0:T(1,128)} %bitcast.63, f32[864,256]{1,0:T(8,128)} %bitcast.53, f32[8,128]{1,0:T(8,128)} %wind_hbm.1, f32[8,128]{1,0:T(8,128)} %dir_hbm.1, s32[8,128]{1,0:T(8,128)} %class_hbm.1), custom_call_target="tpu_custom_call" | custom-call | tf_op jit(solution)/shard_map/pallas_call | solution.py:326
  4.3 6.3 %all-to-all-start = ((f32[32,16,896]{2,1,0:T(8,128)}), f32[32,16,896]{2,1,0:T(8,128)S(1)}, u32[]{:S(2)}, u32[]{:S(2)}) async-start(f32[32,16,896]{2,1,0:T(8,128)} %bitcast.52), calls=%async_computation | async-start | bytes 3670016 | tf_op jit(solution)/shard_map/all_to_all | solution.py:350
  10.5 0.4 collective-permute-start
  11.1 0.8 reshape.102
  11.9 0.1 broadcast_in_dim.173
  12.1 0.1 broadcast_in_dim.161
  12.2 0.1 tile.13
  12.3 0.1 tile.30
  12.4 1.5 %copy.17 = f32[4,216,216]{1,2,0:T(8,128)S(1)} copy(f32[4,216,216]{2,1,0:T(8,128)} %param.19) | data formatting | bytes 1492992 | tf_op jit(solution)/shard_map/optimization_barrier | solution.py:343
  14.0 0.2 select_reduce_fusion
  14.2 0.1 pad_add_fusion.info
  14.3 0.1 tile.32
  14.5 0.1 pad.44.clone
  14.7 0.2 fusion
  14.8 0.1 pad.41.far_ref
  15.0 0.1 pad_maximum_fusion.1
  15.1 0.2 broadcast_multiply_fusion
  15.3 2.8 %multiply_multiply_fusion.wind_ref = f32[4,16,72,256]{3,2,1,0:T(8,128)} fusion(f32[4,256]{1,0:T(4,128)S(1)} %get-tuple-element.74, f32[16,72]{1,0:T(8,128)S(1)} %get-tuple-element.45, f32[4,256]{1,0:T(4,128)S(1)} %get-tuple-element.71, f32[16,72]{1,0:T(8,128)S(1)} %get-tuple-element.46, f32[16,72,256]{2,1,0:T(8,128)S(1)} %broadcast_multiply_fusion), kind=kLoop, calls=%fused_computation | loop fusion | flops 7077888 | bytes 5915648 | tf_op jit(solution)/shard_map/mul | solution.py:397
  18.1 4.8 %select_select_fusion = (f32[4,16,72,256]{3,2,1,0:T(8,128)}, f32[4,16,72,256]{3,2,1,0:T(8,128)}) fusion(f32[4,256]{1,0:T(4,128)S(1)} %bitcast.55, f32[4,256]{1,0:T(4,128)S(1)} %bitcast.56, f32[4,256]{1,0:T(4,128)S(1)} %bitcast.57, f32[4,256]{1,0:T(4,128)S(1)} %bitcast.54, pred[16,72]{1,0:T(8,128)(4,1)S(1)} %get-tuple-element.49, ...), kind=kLoop, calls=%fused_computation.1 | loop fusion | flops 7077888 | bytes 9473408 | tf_op jit(solution)/shard_map/jit(_where)/select_n | solution.py:389
  22.9 30.0 %all-to-all-done = f32[32,16,896]{2,1,0:T(8,128)S(1)} async-done(((f32[32,16,896]{2,1,0:T(8,128)}), f32[32,16,896]{2,1,0:T(8,128)S(1)}, u32[]{:S(2)}, u32[]{:S(2)}) %all-to-all-start) | async-done | bytes 1835040 | tf_op jit(solution)/shard_map/all_to_all | solution.py:350
  52.9 1.5 %shard_map.110 = (f32[4,80,256]{2,1,0:T(8,128)S(1)}, f32[4,80,256]{2,1,0:T(8,128)S(1)}, f32[4,8,256]{2,1,0:T(8,128)S(1)}, f32[4,8,256]{2,1,0:T(8,128)S(1)}) custom-call(s32[9]{0:T(128)S(1)} %pad_add_fusion.info, f32[512,896]{1,0:T(8,128)S(1)} %bitcast.50, f32[4,1,256]{2,1,0:T(1,128)S(1)} %pad.41.far_ref), custom_call_target="tpu_custom_call" | custom-call | tf_op jit(solution)/shard_map/pallas_call | solution.py:406
  54.4 0.5 collective-permute-start.1
  54.9 1.9 %collective-permute-start.2 = (f32[4,8,256]{2,1,0:T(8,128)S(1)}, f32[4,8,256]{2,1,0:T(8,128)S(1)}, u32[]{:S(2)}, u32[]{:S(2)}) collective-permute-start(f32[4,8,256]{2,1,0:T(8,128)S(1)} %get-tuple-element.33), channel_id=1, source_target_pairs={{0,1},{1,2},{2,3},{3,4},{4,5},{5,6},{6,7},{7,8},{8,9},{9,10},{10,1... | collective-permute-start | bytes 98312 | tf_op jit(solution)/shard_map/ppermute | solution.py:414
  56.8 3.9 %collective-permute-start.3 = (f32[4,8,256]{2,1,0:T(8,128)S(1)}, f32[4,8,256]{2,1,0:T(8,128)S(1)}, u32[]{:S(2)}, u32[]{:S(2)}) collective-permute-start(f32[4,8,256]{2,1,0:T(8,128)S(1)} %get-tuple-element.34), channel_id=1, source_target_pairs={{16,1},{17,2},{18,3},{19,4},{20,5},{21,6},{22,7},{23,8},{24,9},{25... | collective-permute-start | bytes 98312 | tf_op jit(solution)/shard_map/ppermute | solution.py:415
  60.9 0.1 concatenate.15
  61.0 1.4 %collective-permute-done.3.cross_ref = f32[4,8,256]{2,1,0:T(8,128)S(1)} collective-permute-done((f32[4,8,256]{2,1,0:T(8,128)S(1)}, f32[4,8,256]{2,1,0:T(8,128)S(1)}, u32[]{:S(2)}, u32[]{:S(2)}) %collective-permute-start.3) | collective-permute-done | bytes 32800 | tf_op jit(solution)/shard_map/ppermute | solution.py:415
  62.4 21.6 %shard_map.111 = (f32[216,8,128]{2,1,0:T(8,128)S(1)}, f32[216,8,128]{2,1,0:T(8,128)S(1)}, f32[216,8,128]{2,1,0:T(8,128)S(1)}, f32[216,8,128]{2,1,0:T(8,128)S(1)}) custom-call(s32[9]{0:T(128)S(1)} %pad_add_fusion.info, f32[4,16,72,256]{3,2,1,0:T(8,128)} %get-tuple-element.26.ax_ref, f32[4,16,72,256]{3,2,1,0:T(8,128)} %get-tuple-element.27.base_ref, ...), custom_call_target="tpu_custom_call" | custom-call | tf_op jit(solution)/shard_map/pallas_call | solution.py:425
  84.0 2.8 %collective-permute-start.5 = (f32[216,8,128]{2,1,0:T(8,128)S(1)}, f32[216,8,128]{2,1,0:T(8,128)S(1)}, u32[]{:S(2)}, u32[]{:S(2)}) collective-permute-start(f32[216,8,128]{2,1,0:T(8,128)S(1)} %get-tuple-element.38), channel_id=1, source_target_pairs={{16,0},{17,1},{18,2},{19,3},{20,4},{21,5},{22,6},{23,7},{24,8},{25... | collective-permute-start | bytes 2654216 | tf_op jit(solution)/shard_map/ppermute | solution.py:447
  86.8 0.1 collective-permute-start.4
  86.9 2.0 %collective-permute-done.5.got_ref = f32[216,8,128]{2,1,0:T(8,128)S(1)} collective-permute-done((f32[216,8,128]{2,1,0:T(8,128)S(1)}, f32[216,8,128]{2,1,0:T(8,128)S(1)}, u32[]{:S(2)}, u32[]{:S(2)}) %collective-permute-start.5) | collective-permute-done | bytes 884768 | tf_op jit(solution)/shard_map/ppermute | solution.py:447
  88.9 2.0 %shard_map.112.rest_0_ = f32[4,216,8,128]{3,2,1,0:T(8,128)} custom-call(s32[9]{0:T(128)S(1)} %pad_add_fusion.info, f32[216,8,128]{2,1,0:T(8,128)S(1)} %get-tuple-element.37.keep_ref, f32[216,8,128]{2,1,0:T(8,128)S(1)} %collective-permute-done.5.got_ref), custom_call_target="tpu_custom_call" | custom-call | tf_op jit(solution)/shard_map/pallas_call | solution.py:451
  90.9 2.0 %shard_map.113 = f32[4,216,8,128]{3,2,1,0:T(8,128)} custom-call(s32[9]{0:T(128)S(1)} %pad_add_fusion.info, f32[216,8,128]{2,1,0:T(8,128)S(1)} %get-tuple-element.35.keep_ref, f32[216,8,128]{2,1,0:T(8,128)S(1)} %collective-permute-done.4.got_ref, f32[4,216,8,128]{3,2,1,0:T(8,128)} %shard_map.112.rest_0_), custom_call_target="tpu_custom_call", output_to_operand_aliasing={{}: (3, {})} | custom-call | tf_op jit(solution)/shard_map/pallas_call | solution.py:451
  (52 shorter events, 0.6 us)
Async XLA Ops:
  0.0 14.0 %copy-start.3 = (f32[256]{0:T(256)S(1)}, f32[256]{0:T(256)}, u32[]{:S(2)}) copy-start(f32[256]{0:T(256)} %constant.51) | copy-start | bytes 3076
  0.0 12.2 %copy-start.1 = (f32[4,24]{1,0:T(4,128)S(1)}, f32[4,24]{1,0:T(4,128)}, u32[]{:S(2)}) copy-start(f32[4,24]{1,0:T(4,128)} %param.14) | copy-start | bytes 1156
  0.0 12.3 %copy-start.2 = (f32[4,24]{1,0:T(4,128)S(1)}, f32[4,24]{1,0:T(4,128)}, u32[]{:S(2)}) copy-start(f32[4,24]{1,0:T(4,128)} %param.15) | copy-start | bytes 1156
  0.0 14.3 %copy-start.5 = (f32[24]{0:T(128)S(1)}, f32[24]{0:T(128)}, u32[]{:S(2)}) copy-start(f32[24]{0:T(128)} %param.16) | copy-start | bytes 292
  4.3 10.3 %copy-start = (f32[3,8,128]{2,1,0:T(8,128)S(1)}, f32[3,8,128]{2,1,0:T(8,128)}, u32[]{:S(2)}) copy-start(f32[3,8,128]{2,1,0:T(8,128)} %get-tuple-element.24) | copy-start | bytes 36868
  4.3 48.6 %all-to-all-start = ((f32[32,16,896]{2,1,0:T(8,128)}), f32[32,16,896]{2,1,0:T(8,128)S(1)}, u32[]{:S(2)}, u32[]{:S(2)}) async-start(f32[32,16,896]{2,1,0:T(8,128)} %bitcast.52), calls=%async_computation | async-start | bytes 3670016 | tf_op jit(solution)/shard_map/all_to_all | solution.py:350
  10.5 4.0 %collective-permute-start = (f32[3,8,128]{2,1,0:T(8,128)}, f32[3,8,128]{2,1,0:T(8,128)S(1)}, u32[]{:S(2)}, u32[]{:S(2)}) collective-permute-start(f32[3,8,128]{2,1,0:T(8,128)} %get-tuple-element.24), channel_id=1, source_target_pairs={{16,0},{17,1},{18,2},{19,3},{20,4},{21,5},{22,6},{23,7},{24,8},{25... | collective-permute-start | bytes 36872 | tf_op jit(solution)/shard_map/ppermute | solution.py:353
  18.1 42.8 %copy-start.4 = (f32[256]{0:T(256)S(1)}, f32[256]{0:T(256)}, u32[]{:S(2)}) copy-start(f32[256]{0:T(256)} %constant.32.clone) | copy-start | bytes 3076
  54.4 8.0 %collective-permute-start.1 = (f32[4,80,256]{2,1,0:T(8,128)S(1)}, f32[4,80,256]{2,1,0:T(8,128)S(1)}, u32[]{:S(2)}, u32[]{:S(2)}) collective-permute-start(f32[4,80,256]{2,1,0:T(8,128)S(1)} %get-tuple-element.32), channel_id=1, source_target_pairs={{16,0},{17,1},{18,2},{19,3},{20,4},{21,5},{22,6},{23,7},{24,8},{25... | collective-permute-start | bytes 983048 | tf_op jit(solution)/shard_map/ppermute | solution.py:413
  54.9 6.1 %collective-permute-start.2 = (f32[4,8,256]{2,1,0:T(8,128)S(1)}, f32[4,8,256]{2,1,0:T(8,128)S(1)}, u32[]{:S(2)}, u32[]{:S(2)}) collective-permute-start(f32[4,8,256]{2,1,0:T(8,128)S(1)} %get-tuple-element.33), channel_id=1, source_target_pairs={{0,1},{1,2},{2,3},{3,4},{4,5},{5,6},{6,7},{7,8},{8,9},{9,10},{10,1... | collective-permute-start | bytes 98312 | tf_op jit(solution)/shard_map/ppermute | solution.py:414
  56.8 5.5 %collective-permute-start.3 = (f32[4,8,256]{2,1,0:T(8,128)S(1)}, f32[4,8,256]{2,1,0:T(8,128)S(1)}, u32[]{:S(2)}, u32[]{:S(2)}) collective-permute-start(f32[4,8,256]{2,1,0:T(8,128)S(1)} %get-tuple-element.34), channel_id=1, source_target_pairs={{16,1},{17,2},{18,3},{19,4},{20,5},{21,6},{22,7},{23,8},{24,9},{25... | collective-permute-start | bytes 98312 | tf_op jit(solution)/shard_map/ppermute | solution.py:415
  84.0 4.9 %collective-permute-start.5 = (f32[216,8,128]{2,1,0:T(8,128)S(1)}, f32[216,8,128]{2,1,0:T(8,128)S(1)}, u32[]{:S(2)}, u32[]{:S(2)}) collective-permute-start(f32[216,8,128]{2,1,0:T(8,128)S(1)} %get-tuple-element.38), channel_id=1, source_target_pairs={{16,0},{17,1},{18,2},{19,3},{20,4},{21,5},{22,6},{23,7},{24,8},{25... | collective-permute-start | bytes 2654216 | tf_op jit(solution)/shard_map/ppermute | solution.py:447
  86.8 4.1 %collective-permute-start.4 = (f32[216,8,128]{2,1,0:T(8,128)S(1)}, f32[216,8,128]{2,1,0:T(8,128)S(1)}, u32[]{:S(2)}, u32[]{:S(2)}) collective-permute-start(f32[216,8,128]{2,1,0:T(8,128)S(1)} %get-tuple-element.36), channel_id=1, source_target_pairs={{16,0},{17,1},{18,2},{19,3},{20,4},{21,5},{22,6},{23,7},{24,8},{25... | collective-permute-start | bytes 2654216 | tf_op jit(solution)/shard_map/ppermute | solution.py:447

commit v11 on v10

--- a/solution.py
+++ b/solution.py
@@ -133,45 +133,41 @@
     pairs = QUADS // 2
     keep_refs, send_refs = rest[:pairs], rest[pairs:2 * pairs]
     state, power, rim, side, far_rows = rest[2 * pairs:]
-    turn = pl.program_id(0)
-    quad = info[turn]
     half = info[ITERS * QUADS]
     width = mt_ref.shape[2]
     rows_dev = rows // 2
-    ax_table = const_ref[0, :class_count]
-    base_table = const_ref[0, class_count:2 * class_count]
-    rate_lane, cos_lane, sin_lane, scale_lane, ratio_lane, diag_lane = [
-        const_ref[0, 2 * class_count + each:2 * class_count + each + 1] for each in range(6)]
-    down = (quad == 0) | (quad == 3)
-    step_x = jnp.where(down, 1, -1)
-    first_row = jnp.where(down, 0, rows - 1)
-    up_y = quad < 2
-
-    @pl.when(turn == 0)
-    def _():
-        power[...] = jnp.zeros_like(power)
-        numbers = jnp.concatenate(
-            [same_ref[feat, 0:1, width - LANES:] for feat in range(4)]
-            + [jnp.zeros((4, LANES), jnp.float32)], axis=0).T
-        for feat in range(4):
-            far_rows[feat] = jnp.broadcast_to(
-                numbers[LANES - rows:, feat:feat + 1], (rows, width))
-
-    rim[0] = own_ref[quad, 0:cells]
-    rim[0, own:cells] = own_ref[quad, own:cells] + same_ref[quad]
-    rim[1] = par_ref[quad, 0:cells]
-    rim[1, own:cells] = par_ref[quad, own:cells] + cross_ref[quad]
-    far_at = jnp.where(half == 0, HALO - 1, 0)
-    at_far = lax.broadcasted_iota(jnp.int32, (HALO, width), 0) == far_at
-    edge_at = jnp.where(half == 0, 0, 2 * HALO - 1)
-    at_edge = lax.broadcasted_iota(jnp.int32, (2 * HALO, width), 0) == edge_at
-    for j in range(rows_dev):
-        mine = jnp.where(at_edge, own_ref[quad, cells + j:cells + j + 1], 0.0)
-        theirs = jnp.where(at_edge, par_ref[quad, cells + j:cells + j + 1], 0.0)
-        side[j + rows_dev * half] = mine
-        side[j + rows_dev * (1 - half)] = theirs
-
-    def run(count, second):
+    power[...] = jnp.zeros_like(power)
+    numbers = jnp.concatenate(
+        [same_ref[feat, 0:1, width - LANES:] for feat in range(4)]
+        + [jnp.zeros((4, LANES), jnp.float32)], axis=0).T
+    for feat in range(4):
+        far_rows[feat] = jnp.broadcast_to(
+            numbers[LANES - rows:, feat:feat + 1], (rows, width))
+
+    def sweep(turn, count, second):
+        quad = info[turn]
+        ax_table = const_ref[quad, :class_count]
+        base_table = const_ref[quad, class_count:2 * class_count]
+        rate_lane, cos_lane, sin_lane, scale_lane, ratio_lane, diag_lane = [
+            const_ref[quad, 2 * class_count + each:2 * class_count + each + 1] for each in range(6)]
+        down = (quad == 0) | (quad == 3)
+        step_x = jnp.where(down, 1, -1)
+        first_row = jnp.where(down, 0, rows - 1)
+        up_y = quad < 2
+        rim[0] = own_ref[quad, 0:cells]
+        rim[0, own:cells] = own_ref[quad, own:cells] + same_ref[quad]
+        rim[1] = par_ref[quad, 0:cells]
+        rim[1, own:cells] = par_ref[quad, own:cells] + cross_ref[quad]
+        far_at = jnp.where(half == 0, HALO - 1, 0)
+        at_far = lax.broadcasted_iota(jnp.int32, (HALO, width), 0) == far_at
+        edge_at = jnp.where(half == 0, 0, 2 * HALO - 1)
+        at_edge = lax.broadcasted_iota(jnp.int32, (2 * HALO, width), 0) == edge_at
+        for j in range(rows_dev):
+            mine = jnp.where(at_edge, own_ref[quad, cells + j:cells + j + 1], 0.0)
+            theirs = jnp.where(at_edge, par_ref[quad, cells + j:cells + j + 1], 0.0)
+            side[j + rows_dev * half] = mine
+            side[j + rows_dev * (1 - half)] = theirs
+
         def patched(block, far_row):
             if second:
                 return block
@@ -193,9 +189,9 @@
                 total = total + power[other, row, low:high]
             level = total * (1.0 / (QUADS * quad_size))
             damping = whitecap_rate * level / (1.0 + level)
-            den = patched(base_ref[0, row, low:high], far_base) + jnp.concatenate([damping] * (width // LANES), axis=1)
+            den = patched(base_ref[quad, row, low:high], far_base) + jnp.concatenate([damping] * (width // LANES), axis=1)
             inverse = scale_lane / den
-            source = patched(wind_ref[0, row, low:high], far_wind)
+            source = patched(wind_ref[quad, row, low:high], far_wind)
             edge = side[row]
             parts = [source[:HALO] + edge[:HALO], source[HALO:own - HALO],
                      source[own - HALO:own] + edge[HALO:]]
@@ -208,8 +204,8 @@
             if second:
                 before = state[quad, row]
                 shifted = jnp.where(up_y, pltpu.roll(before, 1, 0), pltpu.roll(before, cells - 1, 0))
-                source = source + ax_ref[0, row, low:high] * (ratio_lane * shifted[low:high])
-            return patched(ax_ref[0, row, low:high], far_ax) * inverse, source * inverse
+                source = source + ax_ref[quad, row, low:high] * (ratio_lane * shifted[low:high])
+            return patched(ax_ref[quad, row, low:high], far_ax) * inverse, source * inverse
 
         def store(i, value):
             row = first_row + i * step_x
@@ -224,7 +220,7 @@
         balance = factors(0, 0, count)[1]
         upwind = None
         for i in range(rows):
-            mixed = jnp.dot(balance.astype(jnp.bfloat16), mt_ref[0],
+            mixed = jnp.dot(balance.astype(jnp.bfloat16), mt_ref[quad],
                             preferred_element_type=jnp.float32)
             direct = diag_lane * balance
             if i + 1 < rows:
@@ -235,23 +231,21 @@
             upwind = direct + mixed
         store(rows - 1, upwind)
 
-    @pl.when(turn < QUADS)
-    def _():
-        run(cells, False)
-
-    @pl.when(turn >= QUADS)
-    def _():
-        run(own, True)
-
-    @pl.when(turn == ITERS * QUADS - 1)
-    def _():
-        for pair in range(pairs):
-            for j in range(rows_dev):
-                for out_ref, side_at in ((keep_refs[pair], half), (send_refs[pair], 1 - half)):
-                    row = rows_dev * side_at + j
-                    both = jnp.concatenate(
-                        [state[2 * pair, row, :own], state[2 * pair + 1, row, :own]], axis=0)
-                    out_ref[:, j, :] = both.T[:quad_size]
+    @pl.loop(0, QUADS)
+    def _(turn):
+        sweep(turn, cells, False)
+
+    @pl.loop(QUADS, ITERS * QUADS)
+    def _(turn):
+        sweep(turn, own, True)
+
+    for pair in range(pairs):
+        for j in range(rows_dev):
+            for out_ref, side_at in ((keep_refs[pair], half), (send_refs[pair], 1 - half)):
+                row = rows_dev * side_at + j
+                both = jnp.concatenate(
+                    [state[2 * pair, row, :own], state[2 * pair + 1, row, :own]], axis=0)
+                out_ref[:, j, :] = both.T[:quad_size]
 
 
 def merge_kernel(own, pair, chunks, info, keep_ref, got_ref, *rest):
@@ -408,40 +402,27 @@
         in_specs=[pl.BlockSpec(memory_space=pltpu.SMEM), in_vmem, in_vmem],
         out_specs=[in_vmem] * len(rim_shapes),
         out_shape=rim_shapes,
-        compiler_params=pltpu.CompilerParams(vmem_limit_bytes=40 * 2**20),
+        compiler_params=pltpu.CompilerParams(vmem_limit_bytes=24 * 2**20),
     )(info, arrived, far_out)
     rim_partner = lax.ppermute(rim_send, axes, swap_route)
     rim_same = lax.ppermute(out_same, axes, same_route)
     rim_cross = lax.ppermute(out_cross, axes, cross_route)
 
-    turns = ITERS * QUADS
-
-    def quad_block(shape):
-        zeros = (0,) * len(shape)
-        return pl.BlockSpec((1,) + shape, lambda t, info: (info[t],) + zeros)
-
     pairs = QUADS // 2
     packed = jax.ShapeDtypeStruct((quad_size, rows_dev, cols_dev), jnp.float32)
     halves = pl.pallas_call(
         partial(sweeps_kernel, rows, own, cells, quad_size, class_count),
-        grid_spec=pltpu.PrefetchScalarGridSpec(
-            num_scalar_prefetch=1,
-            grid=(turns,),
-            in_specs=[quad_block((rows, cells, width))] * 3
-            + [quad_block((width, width)), quad_block(consts.shape[1:])]
-            + [in_vmem] * 4,
-            out_specs=[in_vmem] * (2 * pairs),
-            scratch_shapes=[
-                pltpu.VMEM((QUADS, rows, cells, width), jnp.float32),
-                pltpu.VMEM((QUADS, rows, cells, LANES), jnp.float32),
-                pltpu.VMEM((2, cells, width), jnp.float32),
-                pltpu.VMEM((rows, 2 * HALO, width), jnp.float32),
-                pltpu.VMEM((4, rows, width), jnp.float32),
-            ],
-        ),
+        in_specs=[pl.BlockSpec(memory_space=pltpu.SMEM)] + [in_vmem] * 9,
+        out_specs=[in_vmem] * (2 * pairs),
+        scratch_shapes=[
+            pltpu.VMEM((QUADS, rows, cells, width), jnp.float32),
+            pltpu.VMEM((QUADS, rows, cells, LANES), jnp.float32),
+            pltpu.VMEM((2, cells, width), jnp.float32),
+            pltpu.VMEM((rows, 2 * HALO, width), jnp.float32),
+            pltpu.VMEM((4, rows, width), jnp.float32),
+        ],
         out_shape=[packed] * (2 * pairs),
-        compiler_params=pltpu.CompilerParams(
-            dimension_semantics=("arbitrary",), vmem_limit_bytes=48 * 2**20),
+        compiler_params=pltpu.CompilerParams(vmem_limit_bytes=24 * 2**20),
     )(info, ax, base, wind, matrices, consts, rim_own, rim_partner, rim_same, rim_cross)
 
     got = [lax.ppermute(half_out, axes, swap_route) for half_out in halves[pairs:]]

time: 94.1 us -> 99 us (1.052)
  local copies, waits for them, and re-layouts: 3.17 us -> 10.2 us
  Pallas kernels: 31.3 us -> 29.1 us
    unnamed x20 -> x26, local copies, waits for them, and re-layouts: 0.05 us -> 7.06 us
    pallas_call x1, Pallas kernels: 21.6 us -> 19.4 us  [body(): pl.pallas_call(partial(sweeps_kernel, rows, own, cells, quad_size, class_...]
  transfers between devices with their start and end apart: 7 -> 7, of which waited for: 3 -> 3; matrix products, arithmetic and copies ran while one was open for 13% -> 12% of each run, Pallas kernels for 2% -> 2%
where the time goes in v11:
time: 99 us; the launch traced here: 97.7 us
  waiting for transfers between devices  33.3 us (34%)
  Pallas kernels  29.1 us (29%)
  starting transfers between devices  16 us (16%)
  local copies, waits for them, and re-layouts  10.2 us (10%)
  other arithmetic  8.72 us (9%)
    all_to_all x1, waiting for transfers between devices, body(): lax.all_to_all(outgoing.reshape(devices, CAP, load), axes, split_axis=0,...  29.9 us
    pallas_call x1, Pallas kernels, body(): pl.pallas_call(partial(sweeps_kernel, rows, own, cells, quad_size, class_...  19.4 us
    unnamed x26, local copies, waits for them, and re-layouts  7.06 us
    all_to_all x1, starting transfers between devices, body(): lax.all_to_all(outgoing.reshape(devices, CAP, load), axes, split_axis=0,...  6.25 us
    select_n x1, other arithmetic, by_class(): jnp.where((class_here == kind)[None, :, :, None], table[:, None, None, ki...  4.85 us
    pallas_call x1, Pallas kernels, body(): pl.pallas_call(partial(pack_kernel, shifts, col_count, rows, comps), grid...  4.23 us
    pallas_call x2, Pallas kernels, body(): pl.pallas_call(partial(merge_kernel, own, pair, chunks), in_specs=[pl.Blo...  3.99 us
    ppermute x1, starting transfers between devices, body(): rim_cross = lax.ppermute(out_cross, axes, cross_route)  3.95 us
  transfers between devices with their start and end apart: 7, of which 3 were waited for; matrix products, arithmetic and copies ran while one was open for 12% of the time, Pallas kernels for 2%

profile of v11, /device:TPU:17, one launch (start us, length us, event | category | flops | bytes accessed | tf_op | source)
XLA Modules:
  0.0 97.7 jit_solution(7898858970435535940)
XLA Ops:
  0.0 4.2 %shard_map.109 = (f32[512,896]{1,0:T(8,128)}, f32[3,8,128]{2,1,0:T(8,128)}) custom-call(s32[1,256]{1,0:T(1,128)} %bitcast.63, f32[864,256]{1,0:T(8,128)} %bitcast.53, f32[8,128]{1,0:T(8,128)} %wind_hbm.1, f32[8,128]{1,0:T(8,128)} %dir_hbm.1, s32[8,128]{1,0:T(8,128)} %class_hbm.1), custom_call_target="tpu_custom_call" | custom-call | tf_op jit(solution)/shard_map/pallas_call | solution.py:320
  4.3 6.3 %all-to-all-start = ((f32[32,16,896]{2,1,0:T(8,128)}), f32[32,16,896]{2,1,0:T(8,128)S(1)}, u32[]{:S(2)}, u32[]{:S(2)}) async-start(f32[32,16,896]{2,1,0:T(8,128)} %bitcast.52), calls=%async_computation | async-start | bytes 3670016 | tf_op jit(solution)/shard_map/all_to_all | solution.py:344
  10.5 0.4 collective-permute-start
  11.1 0.8 reshape.102
  11.9 0.1 broadcast_in_dim.173
  12.1 0.1 broadcast_in_dim.161
  12.2 0.1 tile.13
  12.3 0.1 tile.30
  12.4 1.5 %copy.17 = f32[4,216,216]{1,2,0:T(8,128)S(1)} copy(f32[4,216,216]{2,1,0:T(8,128)} %param.19) | data formatting | bytes 1492992 | tf_op jit(solution)/shard_map/optimization_barrier | solution.py:337
  14.0 0.2 select_reduce_fusion
  14.3 0.1 tile.32
  14.7 0.2 fusion
  15.0 0.1 pad_maximum_fusion.1
  15.1 0.2 broadcast_multiply_fusion
  15.3 2.8 %multiply_multiply_fusion.wind_ref = f32[4,16,72,256]{3,2,1,0:T(8,128)} fusion(f32[4,256]{1,0:T(4,128)S(1)} %get-tuple-element.74, f32[16,72]{1,0:T(8,128)S(1)} %get-tuple-element.45, f32[4,256]{1,0:T(4,128)S(1)} %get-tuple-element.71, f32[16,72]{1,0:T(8,128)S(1)} %get-tuple-element.46, f32[16,72,256]{2,1,0:T(8,128)S(1)} %broadcast_multiply_fusion), kind=kLoop, calls=%fused_computation | loop fusion | flops 7077888 | bytes 5915648 | tf_op jit(solution)/shard_map/mul | solution.py:391
  18.1 4.9 %select_select_fusion = (f32[4,16,72,256]{3,2,1,0:T(8,128)}, f32[4,16,72,256]{3,2,1,0:T(8,128)}) fusion(f32[4,256]{1,0:T(4,128)S(1)} %bitcast.55, f32[4,256]{1,0:T(4,128)S(1)} %bitcast.56, f32[4,256]{1,0:T(4,128)S(1)} %bitcast.57, f32[4,256]{1,0:T(4,128)S(1)} %bitcast.54, pred[16,72]{1,0:T(8,128)(4,1)S(1)} %get-tuple-element.49, ...), kind=kLoop, calls=%fused_computation.1 | loop fusion | flops 7077888 | bytes 9473408 | tf_op jit(solution)/shard_map/jit(_where)/select_n | solution.py:383
  23.0 29.9 %all-to-all-done = f32[32,16,896]{2,1,0:T(8,128)S(1)} async-done(((f32[32,16,896]{2,1,0:T(8,128)}), f32[32,16,896]{2,1,0:T(8,128)S(1)}, u32[]{:S(2)}, u32[]{:S(2)}) %all-to-all-start) | async-done | bytes 1835040 | tf_op jit(solution)/shard_map/all_to_all | solution.py:344
  52.9 1.5 %shard_map.110 = (f32[4,80,256]{2,1,0:T(8,128)S(1)}, f32[4,80,256]{2,1,0:T(8,128)S(1)}, f32[4,8,256]{2,1,0:T(8,128)S(1)}, f32[4,8,256]{2,1,0:T(8,128)S(1)}) custom-call(s32[9]{0:T(128)S(1)} %pad_add_fusion.info, f32[512,896]{1,0:T(8,128)S(1)} %bitcast.50, f32[4,1,256]{2,1,0:T(1,128)S(1)} %pad.41.far_ref), custom_call_target="tpu_custom_call" | custom-call | tf_op jit(solution)/shard_map/pallas_call | solution.py:400
  54.4 0.5 collective-permute-start.1
  54.9 1.9 %collective-permute-start.2 = (f32[4,8,256]{2,1,0:T(8,128)S(1)}, f32[4,8,256]{2,1,0:T(8,128)S(1)}, u32[]{:S(2)}, u32[]{:S(2)}) collective-permute-start(f32[4,8,256]{2,1,0:T(8,128)S(1)} %get-tuple-element.33), channel_id=1, source_target_pairs={{0,1},{1,2},{2,3},{3,4},{4,5},{5,6},{6,7},{7,8},{8,9},{9,10},{10,1... | collective-permute-start | bytes 98312 | tf_op jit(solution)/shard_map/ppermute | solution.py:408
  56.8 3.9 %collective-permute-start.3 = (f32[4,8,256]{2,1,0:T(8,128)S(1)}, f32[4,8,256]{2,1,0:T(8,128)S(1)}, u32[]{:S(2)}, u32[]{:S(2)}) collective-permute-start(f32[4,8,256]{2,1,0:T(8,128)S(1)} %get-tuple-element.34), channel_id=1, source_target_pairs={{16,1},{17,2},{18,3},{19,4},{20,5},{21,6},{22,7},{23,8},{24,9},{25... | collective-permute-start | bytes 98312 | tf_op jit(solution)/shard_map/ppermute | solution.py:409
  60.9 0.1 concatenate.15
  61.0 1.4 %collective-permute-done.3.cross_ref = f32[4,8,256]{2,1,0:T(8,128)S(1)} collective-permute-done((f32[4,8,256]{2,1,0:T(8,128)S(1)}, f32[4,8,256]{2,1,0:T(8,128)S(1)}, u32[]{:S(2)}, u32[]{:S(2)}) %collective-permute-start.3) | collective-permute-done | bytes 32800 | tf_op jit(solution)/shard_map/ppermute | solution.py:409
  62.4 2.3 %copy-done = f32[4,16,72,256]{3,2,1,0:T(8,128)S(1)} copy-done((f32[4,16,72,256]{3,2,1,0:T(8,128)S(1)}, f32[4,16,72,256]{3,2,1,0:T(8,128)}, u32[]{:S(2)}) %copy-start) | copy-done | bytes 4718616
  64.7 2.3 %copy-done.1 = f32[4,16,72,256]{3,2,1,0:T(8,128)S(1)} copy-done((f32[4,16,72,256]{3,2,1,0:T(8,128)S(1)}, f32[4,16,72,256]{3,2,1,0:T(8,128)}, u32[]{:S(2)}) %copy-start.1) | copy-done | bytes 4718616
  67.1 2.3 %copy-done.2 = f32[4,16,72,256]{3,2,1,0:T(8,128)S(1)} copy-done((f32[4,16,72,256]{3,2,1,0:T(8,128)S(1)}, f32[4,16,72,256]{3,2,1,0:T(8,128)}, u32[]{:S(2)}) %copy-start.2) | copy-done | bytes 4718616
  69.4 19.4 %shard_map.111 = (f32[216,8,128]{2,1,0:T(8,128)S(1)}, f32[216,8,128]{2,1,0:T(8,128)S(1)}, f32[216,8,128]{2,1,0:T(8,128)S(1)}, f32[216,8,128]{2,1,0:T(8,128)S(1)}) custom-call(s32[9]{0:T(128)S(1)} %pad_add_fusion.info, f32[4,16,72,256]{3,2,1,0:T(8,128)S(1)} %copy-done.2, f32[4,16,72,256]{3,2,1,0:T(8,128)S(1)} %copy-done.1, f32[4,16,72,256]{3,2,1,0:T(8,128)S(1)} %copy-done, ...), custom_call_target="tpu_custom_call" | custom-call | tf_op jit(solution)/shard_map/pallas_call | solution.py:413
  88.8 2.8 %collective-permute-start.5 = (f32[216,8,128]{2,1,0:T(8,128)S(1)}, f32[216,8,128]{2,1,0:T(8,128)S(1)}, u32[]{:S(2)}, u32[]{:S(2)}) collective-permute-start(f32[216,8,128]{2,1,0:T(8,128)S(1)} %get-tuple-element.38), channel_id=1, source_target_pairs={{16,0},{17,1},{18,2},{19,3},{20,4},{21,5},{22,6},{23,7},{24,8},{25... | collective-permute-start | bytes 2654216 | tf_op jit(solution)/shard_map/ppermute | solution.py:428
  91.7 0.1 collective-permute-start.4
  91.8 2.0 %collective-permute-done.5.got_ref = f32[216,8,128]{2,1,0:T(8,128)S(1)} collective-permute-done((f32[216,8,128]{2,1,0:T(8,128)S(1)}, f32[216,8,128]{2,1,0:T(8,128)S(1)}, u32[]{:S(2)}, u32[]{:S(2)}) %collective-permute-start.5) | collective-permute-done | bytes 884768 | tf_op jit(solution)/shard_map/ppermute | solution.py:428
  93.7 2.0 %shard_map.112.rest_0_ = f32[4,216,8,128]{3,2,1,0:T(8,128)} custom-call(s32[9]{0:T(128)S(1)} %pad_add_fusion.info, f32[216,8,128]{2,1,0:T(8,128)S(1)} %get-tuple-element.37.keep_ref, f32[216,8,128]{2,1,0:T(8,128)S(1)} %collective-permute-done.5.got_ref), custom_call_target="tpu_custom_call" | custom-call | tf_op jit(solution)/shard_map/pallas_call | solution.py:432
  95.7 2.0 %shard_map.113 = f32[4,216,8,128]{3,2,1,0:T(8,128)} custom-call(s32[9]{0:T(128)S(1)} %pad_add_fusion.info, f32[216,8,128]{2,1,0:T(8,128)S(1)} %get-tuple-element.35.keep_ref, f32[216,8,128]{2,1,0:T(8,128)S(1)} %collective-permute-done.4.got_ref, f32[4,216,8,128]{3,2,1,0:T(8,128)} %shard_map.112.rest_0_), custom_call_target="tpu_custom_call", output_to_operand_aliasing={{}: (3, {})} | custom-call | tf_op jit(solution)/shard_map/pallas_call | solution.py:432
  (58 shorter events, 0.8 us)
Async XLA Ops:
  0.0 14.0 %copy-start.6 = (f32[256]{0:T(256)S(1)}, f32[256]{0:T(256)}, u32[]{:S(2)}) copy-start(f32[256]{0:T(256)} %constant.51) | copy-start | bytes 3076
  0.0 12.2 %copy-start.4 = (f32[4,24]{1,0:T(4,128)S(1)}, f32[4,24]{1,0:T(4,128)}, u32[]{:S(2)}) copy-start(f32[4,24]{1,0:T(4,128)} %param.14) | copy-start | bytes 1156
  0.0 12.3 %copy-start.5 = (f32[4,24]{1,0:T(4,128)S(1)}, f32[4,24]{1,0:T(4,128)}, u32[]{:S(2)}) copy-start(f32[4,24]{1,0:T(4,128)} %param.15) | copy-start | bytes 1156
  0.0 14.3 %copy-start.8 = (f32[24]{0:T(128)S(1)}, f32[24]{0:T(128)}, u32[]{:S(2)}) copy-start(f32[24]{0:T(128)} %param.16) | copy-start | bytes 292
  4.3 10.3 %copy-start.3 = (f32[3,8,128]{2,1,0:T(8,128)S(1)}, f32[3,8,128]{2,1,0:T(8,128)}, u32[]{:S(2)}) copy-start(f32[3,8,128]{2,1,0:T(8,128)} %get-tuple-element.24) | copy-start | bytes 36868
  4.3 48.6 %all-to-all-start = ((f32[32,16,896]{2,1,0:T(8,128)}), f32[32,16,896]{2,1,0:T(8,128)S(1)}, u32[]{:S(2)}, u32[]{:S(2)}) async-start(f32[32,16,896]{2,1,0:T(8,128)} %bitcast.52), calls=%async_computation | async-start | bytes 3670016 | tf_op jit(solution)/shard_map/all_to_all | solution.py:344
  10.5 4.0 %collective-permute-start = (f32[3,8,128]{2,1,0:T(8,128)}, f32[3,8,128]{2,1,0:T(8,128)S(1)}, u32[]{:S(2)}, u32[]{:S(2)}) collective-permute-start(f32[3,8,128]{2,1,0:T(8,128)} %get-tuple-element.24), channel_id=1, source_target_pairs={{16,0},{17,1},{18,2},{19,3},{20,4},{21,5},{22,6},{23,7},{24,8},{25... | collective-permute-start | bytes 36872 | tf_op jit(solution)/shard_map/ppermute | solution.py:347
  18.1 42.8 %copy-start.7 = (f32[256]{0:T(256)S(1)}, f32[256]{0:T(256)}, u32[]{:S(2)}) copy-start(f32[256]{0:T(256)} %constant.32.clone) | copy-start | bytes 3076
  54.4 8.0 %collective-permute-start.1 = (f32[4,80,256]{2,1,0:T(8,128)S(1)}, f32[4,80,256]{2,1,0:T(8,128)S(1)}, u32[]{:S(2)}, u32[]{:S(2)}) collective-permute-start(f32[4,80,256]{2,1,0:T(8,128)S(1)} %get-tuple-element.32), channel_id=1, source_target_pairs={{16,0},{17,1},{18,2},{19,3},{20,4},{21,5},{22,6},{23,7},{24,8},{25... | collective-permute-start | bytes 983048 | tf_op jit(solution)/shard_map/ppermute | solution.py:407
  54.9 6.1 %collective-permute-start.2 = (f32[4,8,256]{2,1,0:T(8,128)S(1)}, f32[4,8,256]{2,1,0:T(8,128)S(1)}, u32[]{:S(2)}, u32[]{:S(2)}) collective-permute-start(f32[4,8,256]{2,1,0:T(8,128)S(1)} %get-tuple-element.33), channel_id=1, source_target_pairs={{0,1},{1,2},{2,3},{3,4},{4,5},{5,6},{6,7},{7,8},{8,9},{9,10},{10,1... | collective-permute-start | bytes 98312 | tf_op jit(solution)/shard_map/ppermute | solution.py:408
  56.8 5.5 %collective-permute-start.3 = (f32[4,8,256]{2,1,0:T(8,128)S(1)}, f32[4,8,256]{2,1,0:T(8,128)S(1)}, u32[]{:S(2)}, u32[]{:S(2)}) collective-permute-start(f32[4,8,256]{2,1,0:T(8,128)S(1)} %get-tuple-element.34), channel_id=1, source_target_pairs={{16,1},{17,2},{18,3},{19,4},{20,5},{21,6},{22,7},{23,8},{24,9},{25... | collective-permute-start | bytes 98312 | tf_op jit(solution)/shard_map/ppermute | solution.py:409
  62.4 2.3 %copy-start = (f32[4,16,72,256]{3,2,1,0:T(8,128)S(1)}, f32[4,16,72,256]{3,2,1,0:T(8,128)}, u32[]{:S(2)}) copy-start(f32[4,16,72,256]{3,2,1,0:T(8,128)} %multiply_multiply_fusion.wind_ref) | copy-start | bytes 14155780
  64.7 2.3 %copy-start.1 = (f32[4,16,72,256]{3,2,1,0:T(8,128)S(1)}, f32[4,16,72,256]{3,2,1,0:T(8,128)}, u32[]{:S(2)}) copy-start(f32[4,16,72,256]{3,2,1,0:T(8,128)} %get-tuple-element.27.base_ref) | copy-start | bytes 14155780
  67.1 2.3 %copy-start.2 = (f32[4,16,72,256]{3,2,1,0:T(8,128)S(1)}, f32[4,16,72,256]{3,2,1,0:T(8,128)}, u32[]{:S(2)}) copy-start(f32[4,16,72,256]{3,2,1,0:T(8,128)} %get-tuple-element.26.ax_ref) | copy-start | bytes 14155780
  88.8 4.9 %collective-permute-start.5 = (f32[216,8,128]{2,1,0:T(8,128)S(1)}, f32[216,8,128]{2,1,0:T(8,128)S(1)}, u32[]{:S(2)}, u32[]{:S(2)}) collective-permute-start(f32[216,8,128]{2,1,0:T(8,128)S(1)} %get-tuple-element.38), channel_id=1, source_target_pairs={{16,0},{17,1},{18,2},{19,3},{20,4},{21,5},{22,6},{23,7},{24,8},{25... | collective-permute-start | bytes 2654216 | tf_op jit(solution)/shard_map/ppermute | solution.py:428
  91.7 4.1 %collective-permute-start.4 = (f32[216,8,128]{2,1,0:T(8,128)S(1)}, f32[216,8,128]{2,1,0:T(8,128)S(1)}, u32[]{:S(2)}, u32[]{:S(2)}) collective-permute-start(f32[216,8,128]{2,1,0:T(8,128)S(1)} %get-tuple-element.36), channel_id=1, source_target_pairs={{16,0},{17,1},{18,2},{19,3},{20,4},{21,5},{22,6},{23,7},{24,8},{25... | collective-permute-start | bytes 2654216 | tf_op jit(solution)/shard_map/ppermute | solution.py:428

commit v12 on v11

--- a/solution.py
+++ b/solution.py
@@ -128,14 +128,23 @@
         cross_ref[quad] = part[2 * block + HALO:2 * block + 2 * HALO, :width]
 
 
-def sweeps_kernel(rows, own, cells, quad_size, class_count, info, ax_ref, base_ref,
-                  wind_ref, mt_ref, const_ref, own_ref, par_ref, same_ref, cross_ref, *rest):
+def sweeps_kernel(rows, own, cells, quad_size, class_count, info, ax_hbm, base_hbm,
+                  wind_hbm, mt_ref, const_ref, own_ref, par_ref, same_ref, cross_ref, *rest):
     pairs = QUADS // 2
     keep_refs, send_refs = rest[:pairs], rest[pairs:2 * pairs]
-    state, power, rim, side, far_rows = rest[2 * pairs:]
+    state, power, rim, side, far_rows, ax_ref, base_ref, wind_ref, sems = rest[2 * pairs:]
     half = info[ITERS * QUADS]
     width = mt_ref.shape[2]
     rows_dev = rows // 2
+
+    def fetch(turn):
+        quad = info[turn]
+        return [pltpu.make_async_copy(source.at[quad], target.at[quad], sems.at[index, turn])
+                for index, (source, target) in enumerate(
+                    ((ax_hbm, ax_ref), (base_hbm, base_ref), (wind_hbm, wind_ref)))]
+
+    for copy in fetch(0):
+        copy.start()
     power[...] = jnp.zeros_like(power)
     numbers = jnp.concatenate(
         [same_ref[feat, 0:1, width - LANES:] for feat in range(4)]
@@ -143,6 +152,20 @@
     for feat in range(4):
         far_rows[feat] = jnp.broadcast_to(
             numbers[LANES - rows:, feat:feat + 1], (rows, width))
+    far_at = jnp.where(half == 0, HALO - 1, 0)
+    at_far = lax.broadcasted_iota(jnp.int32, (HALO, width), 0) == far_at
+    edge_at = jnp.where(half == 0, 0, 2 * HALO - 1)
+    at_edge = lax.broadcasted_iota(jnp.int32, (2 * HALO, width), 0) == edge_at
+    for quad in range(QUADS):
+        rim[quad, 0] = own_ref[quad, 0:cells]
+        rim[quad, 0, own:cells] = own_ref[quad, own:cells] + same_ref[quad]
+        rim[quad, 1] = par_ref[quad, 0:cells]
+        rim[quad, 1, own:cells] = par_ref[quad, own:cells] + cross_ref[quad]
+        for j in range(rows_dev):
+            mine = jnp.where(at_edge, own_ref[quad, cells + j:cells + j + 1], 0.0)
+            theirs = jnp.where(at_edge, par_ref[quad, cells + j:cells + j + 1], 0.0)
+            side[quad, j + rows_dev * half] = mine
+            side[quad, j + rows_dev * (1 - half)] = theirs
 
     def sweep(turn, count, second):
         quad = info[turn]
@@ -154,19 +177,6 @@
         step_x = jnp.where(down, 1, -1)
         first_row = jnp.where(down, 0, rows - 1)
         up_y = quad < 2
-        rim[0] = own_ref[quad, 0:cells]
-        rim[0, own:cells] = own_ref[quad, own:cells] + same_ref[quad]
-        rim[1] = par_ref[quad, 0:cells]
-        rim[1, own:cells] = par_ref[quad, own:cells] + cross_ref[quad]
-        far_at = jnp.where(half == 0, HALO - 1, 0)
-        at_far = lax.broadcasted_iota(jnp.int32, (HALO, width), 0) == far_at
-        edge_at = jnp.where(half == 0, 0, 2 * HALO - 1)
-        at_edge = lax.broadcasted_iota(jnp.int32, (2 * HALO, width), 0) == edge_at
-        for j in range(rows_dev):
-            mine = jnp.where(at_edge, own_ref[quad, cells + j:cells + j + 1], 0.0)
-            theirs = jnp.where(at_edge, par_ref[quad, cells + j:cells + j + 1], 0.0)
-            side[j + rows_dev * half] = mine
-            side[j + rows_dev * (1 - half)] = theirs
 
         def patched(block, far_row):
             if second:
@@ -192,7 +202,7 @@
             den = patched(base_ref[quad, row, low:high], far_base) + jnp.concatenate([damping] * (width // LANES), axis=1)
             inverse = scale_lane / den
             source = patched(wind_ref[quad, row, low:high], far_wind)
-            edge = side[row]
+            edge = side[quad, row]
             parts = [source[:HALO] + edge[:HALO], source[HALO:own - HALO],
                      source[own - HALO:own] + edge[HALO:]]
             if high > own:
@@ -200,7 +210,7 @@
             source = jnp.concatenate(parts, axis=0)
             if i == 0 or i == rows - 1:
                 here = jnp.where(row // rows_dev == half, 0, 1)
-                source = source + rim[here, low:high]
+                source = source + rim[quad, here, low:high]
             if second:
                 before = state[quad, row]
                 shifted = jnp.where(up_y, pltpu.roll(before, 1, 0), pltpu.roll(before, cells - 1, 0))
@@ -233,6 +243,14 @@
 
     @pl.loop(0, QUADS)
     def _(turn):
+        for copy in fetch(turn):
+            copy.wait()
+
+        @pl.when(turn + 1 < QUADS)
+        def _():
+            for copy in fetch(turn + 1):
+                copy.start()
+
         sweep(turn, cells, False)
 
     @pl.loop(QUADS, ITERS * QUADS)
@@ -402,7 +420,7 @@
         in_specs=[pl.BlockSpec(memory_space=pltpu.SMEM), in_vmem, in_vmem],
         out_specs=[in_vmem] * len(rim_shapes),
         out_shape=rim_shapes,
-        compiler_params=pltpu.CompilerParams(vmem_limit_bytes=24 * 2**20),
+        compiler_params=pltpu.CompilerParams(vmem_limit_bytes=40 * 2**20),
     )(info, arrived, far_out)
     rim_partner = lax.ppermute(rim_send, axes, swap_route)
     rim_same = lax.ppermute(out_same, axes, same_route)
@@ -412,17 +430,21 @@
     packed = jax.ShapeDtypeStruct((quad_size, rows_dev, cols_dev), jnp.float32)
     halves = pl.pallas_call(
         partial(sweeps_kernel, rows, own, cells, quad_size, class_count),
-        in_specs=[pl.BlockSpec(memory_space=pltpu.SMEM)] + [in_vmem] * 9,
+        in_specs=[pl.BlockSpec(memory_space=pltpu.SMEM)] + [anywhere] * 3 + [in_vmem] * 6,
         out_specs=[in_vmem] * (2 * pairs),
         scratch_shapes=[
             pltpu.VMEM((QUADS, rows, cells, width), jnp.float32),
             pltpu.VMEM((QUADS, rows, cells, LANES), jnp.float32),
-            pltpu.VMEM((2, cells, width), jnp.float32),
-            pltpu.VMEM((rows, 2 * HALO, width), jnp.float32),
+            pltpu.VMEM((QUADS, 2, cells, width), jnp.float32),
+            pltpu.VMEM((QUADS, rows, 2 * HALO, width), jnp.float32),
             pltpu.VMEM((4, rows, width), jnp.float32),
+            pltpu.VMEM((QUADS, rows, cells, width), jnp.float32),
+            pltpu.VMEM((QUADS, rows, cells, width), jnp.float32),
+            pltpu.VMEM((QUADS, rows, cells, width), jnp.float32),
+            pltpu.SemaphoreType.DMA((3, QUADS)),
         ],
         out_shape=[packed] * (2 * pairs),
-        compiler_params=pltpu.CompilerParams(vmem_limit_bytes=24 * 2**20),
+        compiler_params=pltpu.CompilerParams(vmem_limit_bytes=48 * 2**20),
     )(info, ax, base, wind, matrices, consts, rim_own, rim_partner, rim_same, rim_cross)
 
     got = [lax.ppermute(half_out, axes, swap_route) for half_out in halves[pairs:]]

time: 99 us -> 93.6 us (0.945)
  local copies, waits for them, and re-layouts: 10.2 us -> 3.17 us
  Pallas kernels: 29.1 us -> 30.9 us
    unnamed x26 -> x20, local copies, waits for them, and re-layouts: 7.06 us -> 0.05 us
    pallas_call x1, Pallas kernels: 19.4 us -> 21.1 us  [body(): pl.pallas_call(partial(sweeps_kernel, rows, own, cells, quad_size, class_...]
  transfers between devices with their start and end apart: 7 -> 7, of which waited for: 3 -> 3; matrix products, arithmetic and copies ran while one was open for 12% -> 13% of each run, Pallas kernels for 2% -> 2%
where the time goes in v12:
time: 93.6 us; the launch traced here: 92.4 us
  waiting for transfers between devices  33.3 us (36%)
  Pallas kernels  30.9 us (33%)
  starting transfers between devices  16 us (17%)
  other arithmetic  8.7 us (9%)
  local copies, waits for them, and re-layouts  3.17 us (3%)
    all_to_all x1, waiting for transfers between devices, body(): lax.all_to_all(outgoing.reshape(devices, CAP, load), axes, split_axis=0,...  30 us
    pallas_call x1, Pallas kernels, body(): pl.pallas_call(partial(sweeps_kernel, rows, own, cells, quad_size, class_...  21.1 us
    all_to_all x1, starting transfers between devices, body(): lax.all_to_all(outgoing.reshape(devices, CAP, load), axes, split_axis=0,...  6.25 us
    select_n x1, other arithmetic, by_class(): jnp.where((class_here == kind)[None, :, :, None], table[:, None, None, ki...  4.84 us
    pallas_call x1, Pallas kernels, body(): pl.pallas_call(partial(pack_kernel, shifts, col_count, rows, comps), grid...  4.23 us
    pallas_call x2, Pallas kernels, body(): pl.pallas_call(partial(merge_kernel, own, pair, chunks), in_specs=[pl.Blo...  3.99 us
    ppermute x1, starting transfers between devices, body(): rim_cross = lax.ppermute(out_cross, axes, cross_route)  3.95 us
    ppermute x2, starting transfers between devices, body(): lax.ppermute(half_out, axes, swap_route)  2.92 us
  transfers between devices with their start and end apart: 7, of which 3 were waited for; matrix products, arithmetic and copies ran while one was open for 13% of the time, Pallas kernels for 2%

profile of v12, /device:TPU:17, one launch (start us, length us, event | category | flops | bytes accessed | tf_op | source)
XLA Modules:
  0.0 92.4 jit_solution(11476092831444736026)
XLA Ops:
  0.0 4.2 %shard_map.109 = (f32[512,896]{1,0:T(8,128)}, f32[3,8,128]{2,1,0:T(8,128)}) custom-call(s32[1,256]{1,0:T(1,128)} %bitcast.63, f32[864,256]{1,0:T(8,128)} %bitcast.53, f32[8,128]{1,0:T(8,128)} %wind_hbm.1, f32[8,128]{1,0:T(8,128)} %dir_hbm.1, s32[8,128]{1,0:T(8,128)} %class_hbm.1), custom_call_target="tpu_custom_call" | custom-call | tf_op jit(solution)/shard_map/pallas_call | solution.py:338
  4.3 6.3 %all-to-all-start = ((f32[32,16,896]{2,1,0:T(8,128)}), f32[32,16,896]{2,1,0:T(8,128)S(1)}, u32[]{:S(2)}, u32[]{:S(2)}) async-start(f32[32,16,896]{2,1,0:T(8,128)} %bitcast.52), calls=%async_computation | async-start | bytes 3670016 | tf_op jit(solution)/shard_map/all_to_all | solution.py:362
  10.5 0.4 collective-permute-start
  11.1 0.8 reshape.102
  11.9 0.1 broadcast_in_dim.173
  12.1 0.1 broadcast_in_dim.161
  12.2 0.1 tile.13
  12.3 0.1 tile.30
  12.4 1.5 %copy.17 = f32[4,216,216]{1,2,0:T(8,128)S(1)} copy(f32[4,216,216]{2,1,0:T(8,128)} %param.19) | data formatting | bytes 1492992 | tf_op jit(solution)/shard_map/optimization_barrier | solution.py:355
  14.0 0.2 select_reduce_fusion
  14.2 0.1 pad_add_fusion.info
  14.3 0.1 tile.32
  14.5 0.1 pad.44.clone
  14.7 0.2 fusion
  14.8 0.1 pad.41.far_ref
  15.0 0.1 pad_maximum_fusion.1
  15.1 0.2 broadcast_multiply_fusion
  15.3 2.8 %multiply_multiply_fusion.wind_hbm = f32[4,16,72,256]{3,2,1,0:T(8,128)} fusion(f32[4,256]{1,0:T(4,128)S(1)} %get-tuple-element.74, f32[16,72]{1,0:T(8,128)S(1)} %get-tuple-element.45, f32[4,256]{1,0:T(4,128)S(1)} %get-tuple-element.71, f32[16,72]{1,0:T(8,128)S(1)} %get-tuple-element.46, f32[16,72,256]{2,1,0:T(8,128)S(1)} %broadcast_multiply_fusion), kind=kLoop, calls=%fused_computation | loop fusion | flops 7077888 | bytes 5915648 | tf_op jit(solution)/shard_map/mul | solution.py:409
  18.1 4.8 %select_select_fusion = (f32[4,16,72,256]{3,2,1,0:T(8,128)}, f32[4,16,72,256]{3,2,1,0:T(8,128)}) fusion(f32[4,256]{1,0:T(4,128)S(1)} %bitcast.55, f32[4,256]{1,0:T(4,128)S(1)} %bitcast.56, f32[4,256]{1,0:T(4,128)S(1)} %bitcast.57, f32[4,256]{1,0:T(4,128)S(1)} %bitcast.54, pred[16,72]{1,0:T(8,128)(4,1)S(1)} %get-tuple-element.49, ...), kind=kLoop, calls=%fused_computation.1 | loop fusion | flops 7077888 | bytes 9473408 | tf_op jit(solution)/shard_map/jit(_where)/select_n | solution.py:401
  22.9 30.0 %all-to-all-done = f32[32,16,896]{2,1,0:T(8,128)S(1)} async-done(((f32[32,16,896]{2,1,0:T(8,128)}), f32[32,16,896]{2,1,0:T(8,128)S(1)}, u32[]{:S(2)}, u32[]{:S(2)}) %all-to-all-start) | async-done | bytes 1835040 | tf_op jit(solution)/shard_map/all_to_all | solution.py:362
  52.9 1.5 %shard_map.110 = (f32[4,80,256]{2,1,0:T(8,128)S(1)}, f32[4,80,256]{2,1,0:T(8,128)S(1)}, f32[4,8,256]{2,1,0:T(8,128)S(1)}, f32[4,8,256]{2,1,0:T(8,128)S(1)}) custom-call(s32[9]{0:T(128)S(1)} %pad_add_fusion.info, f32[512,896]{1,0:T(8,128)S(1)} %bitcast.50, f32[4,1,256]{2,1,0:T(1,128)S(1)} %pad.41.far_ref), custom_call_target="tpu_custom_call" | custom-call | tf_op jit(solution)/shard_map/pallas_call | solution.py:418
  54.4 0.5 collective-permute-start.1
  54.9 1.9 %collective-permute-start.2 = (f32[4,8,256]{2,1,0:T(8,128)S(1)}, f32[4,8,256]{2,1,0:T(8,128)S(1)}, u32[]{:S(2)}, u32[]{:S(2)}) collective-permute-start(f32[4,8,256]{2,1,0:T(8,128)S(1)} %get-tuple-element.33), channel_id=1, source_target_pairs={{0,1},{1,2},{2,3},{3,4},{4,5},{5,6},{6,7},{7,8},{8,9},{9,10},{10,1... | collective-permute-start | bytes 98312 | tf_op jit(solution)/shard_map/ppermute | solution.py:426
  56.8 3.9 %collective-permute-start.3 = (f32[4,8,256]{2,1,0:T(8,128)S(1)}, f32[4,8,256]{2,1,0:T(8,128)S(1)}, u32[]{:S(2)}, u32[]{:S(2)}) collective-permute-start(f32[4,8,256]{2,1,0:T(8,128)S(1)} %get-tuple-element.34), channel_id=1, source_target_pairs={{16,1},{17,2},{18,3},{19,4},{20,5},{21,6},{22,7},{23,8},{24,9},{25... | collective-permute-start | bytes 98312 | tf_op jit(solution)/shard_map/ppermute | solution.py:427
  60.9 0.1 concatenate.15
  61.0 1.4 %collective-permute-done.3.cross_ref = f32[4,8,256]{2,1,0:T(8,128)S(1)} collective-permute-done((f32[4,8,256]{2,1,0:T(8,128)S(1)}, f32[4,8,256]{2,1,0:T(8,128)S(1)}, u32[]{:S(2)}, u32[]{:S(2)}) %collective-permute-start.3) | collective-permute-done | bytes 32800 | tf_op jit(solution)/shard_map/ppermute | solution.py:427
  62.4 21.1 %shard_map.111 = (f32[216,8,128]{2,1,0:T(8,128)S(1)}, f32[216,8,128]{2,1,0:T(8,128)S(1)}, f32[216,8,128]{2,1,0:T(8,128)S(1)}, f32[216,8,128]{2,1,0:T(8,128)S(1)}) custom-call(s32[9]{0:T(128)S(1)} %pad_add_fusion.info, f32[4,16,72,256]{3,2,1,0:T(8,128)} %get-tuple-element.26.ax_hbm, f32[4,16,72,256]{3,2,1,0:T(8,128)} %get-tuple-element.27.base_hbm, ...), custom_call_target="tpu_custom_call" | custom-call | tf_op jit(solution)/shard_map/pallas_call | solution.py:431
  83.5 2.8 %collective-permute-start.5 = (f32[216,8,128]{2,1,0:T(8,128)S(1)}, f32[216,8,128]{2,1,0:T(8,128)S(1)}, u32[]{:S(2)}, u32[]{:S(2)}) collective-permute-start(f32[216,8,128]{2,1,0:T(8,128)S(1)} %get-tuple-element.38), channel_id=1, source_target_pairs={{16,0},{17,1},{18,2},{19,3},{20,4},{21,5},{22,6},{23,7},{24,8},{25... | collective-permute-start | bytes 2654216 | tf_op jit(solution)/shard_map/ppermute | solution.py:450
  86.4 0.1 collective-permute-start.4
  86.5 2.0 %collective-permute-done.5.got_ref = f32[216,8,128]{2,1,0:T(8,128)S(1)} collective-permute-done((f32[216,8,128]{2,1,0:T(8,128)S(1)}, f32[216,8,128]{2,1,0:T(8,128)S(1)}, u32[]{:S(2)}, u32[]{:S(2)}) %collective-permute-start.5) | collective-permute-done | bytes 884768 | tf_op jit(solution)/shard_map/ppermute | solution.py:450
  88.4 2.0 %shard_map.112.rest_0_ = f32[4,216,8,128]{3,2,1,0:T(8,128)} custom-call(s32[9]{0:T(128)S(1)} %pad_add_fusion.info, f32[216,8,128]{2,1,0:T(8,128)S(1)} %get-tuple-element.37.keep_ref, f32[216,8,128]{2,1,0:T(8,128)S(1)} %collective-permute-done.5.got_ref), custom_call_target="tpu_custom_call" | custom-call | tf_op jit(solution)/shard_map/pallas_call | solution.py:454
  90.4 2.0 %shard_map.113 = f32[4,216,8,128]{3,2,1,0:T(8,128)} custom-call(s32[9]{0:T(128)S(1)} %pad_add_fusion.info, f32[216,8,128]{2,1,0:T(8,128)S(1)} %get-tuple-element.35.keep_ref, f32[216,8,128]{2,1,0:T(8,128)S(1)} %collective-permute-done.4.got_ref, f32[4,216,8,128]{3,2,1,0:T(8,128)} %shard_map.112.rest_0_), custom_call_target="tpu_custom_call", output_to_operand_aliasing={{}: (3, {})} | custom-call | tf_op jit(solution)/shard_map/pallas_call | solution.py:454
  (52 shorter events, 0.6 us)
Async XLA Ops:
  0.0 14.0 %copy-start.3 = (f32[256]{0:T(256)S(1)}, f32[256]{0:T(256)}, u32[]{:S(2)}) copy-start(f32[256]{0:T(256)} %constant.51) | copy-start | bytes 3076
  0.0 12.2 %copy-start.1 = (f32[4,24]{1,0:T(4,128)S(1)}, f32[4,24]{1,0:T(4,128)}, u32[]{:S(2)}) copy-start(f32[4,24]{1,0:T(4,128)} %param.14) | copy-start | bytes 1156
  0.0 12.3 %copy-start.2 = (f32[4,24]{1,0:T(4,128)S(1)}, f32[4,24]{1,0:T(4,128)}, u32[]{:S(2)}) copy-start(f32[4,24]{1,0:T(4,128)} %param.15) | copy-start | bytes 1156
  0.0 14.3 %copy-start.5 = (f32[24]{0:T(128)S(1)}, f32[24]{0:T(128)}, u32[]{:S(2)}) copy-start(f32[24]{0:T(128)} %param.16) | copy-start | bytes 292
  4.3 10.3 %copy-start = (f32[3,8,128]{2,1,0:T(8,128)S(1)}, f32[3,8,128]{2,1,0:T(8,128)}, u32[]{:S(2)}) copy-start(f32[3,8,128]{2,1,0:T(8,128)} %get-tuple-element.24) | copy-start | bytes 36868
  4.3 48.6 %all-to-all-start = ((f32[32,16,896]{2,1,0:T(8,128)}), f32[32,16,896]{2,1,0:T(8,128)S(1)}, u32[]{:S(2)}, u32[]{:S(2)}) async-start(f32[32,16,896]{2,1,0:T(8,128)} %bitcast.52), calls=%async_computation | async-start | bytes 3670016 | tf_op jit(solution)/shard_map/all_to_all | solution.py:362
  10.5 4.0 %collective-permute-start = (f32[3,8,128]{2,1,0:T(8,128)}, f32[3,8,128]{2,1,0:T(8,128)S(1)}, u32[]{:S(2)}, u32[]{:S(2)}) collective-permute-start(f32[3,8,128]{2,1,0:T(8,128)} %get-tuple-element.24), channel_id=1, source_target_pairs={{16,0},{17,1},{18,2},{19,3},{20,4},{21,5},{22,6},{23,7},{24,8},{25... | collective-permute-start | bytes 36872 | tf_op jit(solution)/shard_map/ppermute | solution.py:365
  18.1 42.8 %copy-start.4 = (f32[256]{0:T(256)S(1)}, f32[256]{0:T(256)}, u32[]{:S(2)}) copy-start(f32[256]{0:T(256)} %constant.32.clone) | copy-start | bytes 3076
  54.4 8.0 %collective-permute-start.1 = (f32[4,80,256]{2,1,0:T(8,128)S(1)}, f32[4,80,256]{2,1,0:T(8,128)S(1)}, u32[]{:S(2)}, u32[]{:S(2)}) collective-permute-start(f32[4,80,256]{2,1,0:T(8,128)S(1)} %get-tuple-element.32), channel_id=1, source_target_pairs={{16,0},{17,1},{18,2},{19,3},{20,4},{21,5},{22,6},{23,7},{24,8},{25... | collective-permute-start | bytes 983048 | tf_op jit(solution)/shard_map/ppermute | solution.py:425
  54.9 6.1 %collective-permute-start.2 = (f32[4,8,256]{2,1,0:T(8,128)S(1)}, f32[4,8,256]{2,1,0:T(8,128)S(1)}, u32[]{:S(2)}, u32[]{:S(2)}) collective-permute-start(f32[4,8,256]{2,1,0:T(8,128)S(1)} %get-tuple-element.33), channel_id=1, source_target_pairs={{0,1},{1,2},{2,3},{3,4},{4,5},{5,6},{6,7},{7,8},{8,9},{9,10},{10,1... | collective-permute-start | bytes 98312 | tf_op jit(solution)/shard_map/ppermute | solution.py:426
  56.8 5.5 %collective-permute-start.3 = (f32[4,8,256]{2,1,0:T(8,128)S(1)}, f32[4,8,256]{2,1,0:T(8,128)S(1)}, u32[]{:S(2)}, u32[]{:S(2)}) collective-permute-start(f32[4,8,256]{2,1,0:T(8,128)S(1)} %get-tuple-element.34), channel_id=1, source_target_pairs={{16,1},{17,2},{18,3},{19,4},{20,5},{21,6},{22,7},{23,8},{24,9},{25... | collective-permute-start | bytes 98312 | tf_op jit(solution)/shard_map/ppermute | solution.py:427
  83.5 4.9 %collective-permute-start.5 = (f32[216,8,128]{2,1,0:T(8,128)S(1)}, f32[216,8,128]{2,1,0:T(8,128)S(1)}, u32[]{:S(2)}, u32[]{:S(2)}) collective-permute-start(f32[216,8,128]{2,1,0:T(8,128)S(1)} %get-tuple-element.38), channel_id=1, source_target_pairs={{16,0},{17,1},{18,2},{19,3},{20,4},{21,5},{22,6},{23,7},{24,8},{25... | collective-permute-start | bytes 2654216 | tf_op jit(solution)/shard_map/ppermute | solution.py:450
  86.4 4.1 %collective-permute-start.4 = (f32[216,8,128]{2,1,0:T(8,128)S(1)}, f32[216,8,128]{2,1,0:T(8,128)S(1)}, u32[]{:S(2)}, u32[]{:S(2)}) collective-permute-start(f32[216,8,128]{2,1,0:T(8,128)S(1)} %get-tuple-element.36), channel_id=1, source_target_pairs={{16,0},{17,1},{18,2},{19,3},{20,4},{21,5},{22,6},{23,7},{24,8},{25... | collective-permute-start | bytes 2654216 | tf_op jit(solution)/shard_map/ppermute | solution.py:450

commit v13 on v12

--- a/solution.py
+++ b/solution.py
@@ -167,7 +167,15 @@
             side[quad, j + rows_dev * half] = mine
             side[quad, j + rows_dev * (1 - half)] = theirs
 
-    def sweep(turn, count, second):
+    def pack_rows(pair, j, lane, out_ref, side_at):
+        row = rows_dev * side_at + j
+        first, other = info[QUADS + 2 * pair], info[QUADS + 2 * pair + 1]
+        span = pl.ds(lane, LANES)
+        both = jnp.concatenate([state[first, row, :own, span], state[other, row, :own, span]], axis=0)
+        stop = min(quad_size - lane, LANES)
+        out_ref[lane:lane + stop, j, :] = both.T[:stop]
+
+    def sweep(turn, count, second, extra=None):
         quad = info[turn]
         ax_table = const_ref[quad, :class_count]
         base_table = const_ref[quad, class_count:2 * class_count]
@@ -236,6 +244,8 @@
             if i + 1 < rows:
                 along, known = factors(i + 1, 0, count)
                 balance = along * mixed + (along * direct + known)
+            if extra is not None:
+                extra(i)
             if i > 0:
                 store(i - 1, upwind)
             upwind = direct + mixed
@@ -253,17 +263,22 @@
 
         sweep(turn, cells, False)
 
-    @pl.loop(QUADS, ITERS * QUADS)
+    @pl.loop(QUADS, ITERS * QUADS - 2)
     def _(turn):
         sweep(turn, own, True)
 
-    for pair in range(pairs):
-        for j in range(rows_dev):
-            for out_ref, side_at in ((keep_refs[pair], half), (send_refs[pair], 1 - half)):
-                row = rows_dev * side_at + j
-                both = jnp.concatenate(
-                    [state[2 * pair, row, :own], state[2 * pair + 1, row, :own]], axis=0)
-                out_ref[:, j, :] = both.T[:quad_size]
+    tiles = width // LANES
+    assert rows == rows_dev * tiles
+
+    def between(out_ref, side_at):
+        return lambda i: pack_rows(0, i // tiles, i % tiles * LANES, out_ref, side_at)
+
+    sweep(ITERS * QUADS - 2, own, True, between(keep_refs[0], half))
+    sweep(ITERS * QUADS - 1, own, True, between(send_refs[0], 1 - half))
+    for j in range(rows_dev):
+        for lane in range(0, width, LANES):
+            pack_rows(1, j, lane, keep_refs[1], half)
+            pack_rows(1, j, lane, send_refs[1], 1 - half)
 
 
 def merge_kernel(own, pair, chunks, info, keep_ref, got_ref, *rest):
@@ -282,7 +297,7 @@
         stage[chunk, 1] = jnp.where(low, pltpu.roll(left, own, 2), right)
         for member in range(2):
             copies.append(pltpu.make_async_copy(
-                stage.at[chunk, member], out_ref.at[2 * pair + member, span], sems.at[chunk, member]))
+                stage.at[chunk, member], out_ref.at[info[QUADS + 2 * pair + member], span], sems.at[chunk, member]))
             copies[-1].start()
     for copy in copies:
         copy.wait()
@@ -332,7 +347,7 @@
     shifts = tuple(size.bit_length() - 1 for size in sizes)
     assert all(size == 2**shift for size, shift in zip(sizes, shifts))
     slot_total = devices * CAP
-    steps = 4
+    steps = 2
     in_vmem = pl.BlockSpec(memory_space=pltpu.VMEM)
     anywhere = pl.BlockSpec(memory_space=pl.ANY)
     outgoing, held = pl.pallas_call(

time: 93.6 us -> 92.3 us (0.986)
  Pallas kernels: 30.9 us -> 29.4 us
    pallas_call x1, Pallas kernels: 4.23 us -> 3.25 us  [body(): pl.pallas_call(partial(pack_kernel, shifts, col_count, rows, comps), grid...]
where the time goes in v13:
time: 92.3 us; the launch traced here: 91.1 us
  waiting for transfers between devices  33.2 us (36%)
  Pallas kernels  29.4 us (32%)
  starting transfers between devices  16.1 us (17%)
  other arithmetic  8.7 us (9%)
  local copies, waits for them, and re-layouts  3.17 us (3%)
    all_to_all x1, waiting for transfers between devices, body(): lax.all_to_all(outgoing.reshape(devices, CAP, load), axes, split_axis=0,...  30 us
    pallas_call x1, Pallas kernels, body(): pl.pallas_call(partial(sweeps_kernel, rows, own, cells, quad_size, class_...  20.7 us
    all_to_all x1, starting transfers between devices, body(): lax.all_to_all(outgoing.reshape(devices, CAP, load), axes, split_axis=0,...  6.26 us
    select_n x1, other arithmetic, by_class(): jnp.where((class_here == kind)[None, :, :, None], table[:, None, None, ki...  4.84 us
    ppermute x1, starting transfers between devices, body(): rim_cross = lax.ppermute(out_cross, axes, cross_route)  4.13 us
    pallas_call x2, Pallas kernels, body(): pl.pallas_call(partial(merge_kernel, own, pair, chunks), in_specs=[pl.Blo...  3.99 us
    pallas_call x1, Pallas kernels, body(): pl.pallas_call(partial(pack_kernel, shifts, col_count, rows, comps), grid...  3.25 us
    ppermute x2, starting transfers between devices, body(): lax.ppermute(half_out, axes, swap_route)  2.92 us
  transfers between devices with their start and end apart: 7, of which 3 were waited for; matrix products, arithmetic and copies ran while one was open for 13% of the time, Pallas kernels for 2%

profile of v13, /device:TPU:17, one launch (start us, length us, event | category | flops | bytes accessed | tf_op | source)
XLA Modules:
  0.0 91.1 jit_solution(17079528827755724293)
XLA Ops:
  0.0 3.2 %shard_map.109 = (f32[512,896]{1,0:T(8,128)}, f32[3,8,128]{2,1,0:T(8,128)}) custom-call(s32[1,256]{1,0:T(1,128)} %bitcast.63, f32[864,256]{1,0:T(8,128)} %bitcast.53, f32[8,128]{1,0:T(8,128)} %wind_hbm.1, f32[8,128]{1,0:T(8,128)} %dir_hbm.1, s32[8,128]{1,0:T(8,128)} %class_hbm.1), custom_call_target="tpu_custom_call" | custom-call | tf_op jit(solution)/shard_map/pallas_call | solution.py:353
  3.3 6.3 %all-to-all-start = ((f32[32,16,896]{2,1,0:T(8,128)}), f32[32,16,896]{2,1,0:T(8,128)S(1)}, u32[]{:S(2)}, u32[]{:S(2)}) async-start(f32[32,16,896]{2,1,0:T(8,128)} %bitcast.52), calls=%async_computation | async-start | bytes 3670016 | tf_op jit(solution)/shard_map/all_to_all | solution.py:377
  9.6 0.4 collective-permute-start
  10.1 0.8 reshape.102
  11.0 0.1 broadcast_in_dim.173
  11.1 0.1 broadcast_in_dim.161
  11.2 0.1 tile.13
  11.3 0.1 tile.30
  11.4 1.5 %copy.17 = f32[4,216,216]{1,2,0:T(8,128)S(1)} copy(f32[4,216,216]{2,1,0:T(8,128)} %param.19) | data formatting | bytes 1492992 | tf_op jit(solution)/shard_map/optimization_barrier | solution.py:370
  13.0 0.2 select_reduce_fusion
  13.3 0.1 pad_add_fusion.info
  13.3 0.1 tile.32
  13.5 0.1 pad.44.clone
  13.7 0.2 fusion
  13.8 0.1 pad.41.far_ref
  14.0 0.1 pad_maximum_fusion.1
  14.1 0.2 broadcast_multiply_fusion
  14.3 2.8 %multiply_multiply_fusion.wind_hbm = f32[4,16,72,256]{3,2,1,0:T(8,128)} fusion(f32[4,256]{1,0:T(4,128)S(1)} %get-tuple-element.74, f32[16,72]{1,0:T(8,128)S(1)} %get-tuple-element.45, f32[4,256]{1,0:T(4,128)S(1)} %get-tuple-element.71, f32[16,72]{1,0:T(8,128)S(1)} %get-tuple-element.46, f32[16,72,256]{2,1,0:T(8,128)S(1)} %broadcast_multiply_fusion), kind=kLoop, calls=%fused_computation | loop fusion | flops 7077888 | bytes 5915648 | tf_op jit(solution)/shard_map/mul | solution.py:424
  17.1 4.8 %select_select_fusion = (f32[4,16,72,256]{3,2,1,0:T(8,128)}, f32[4,16,72,256]{3,2,1,0:T(8,128)}) fusion(f32[4,256]{1,0:T(4,128)S(1)} %bitcast.55, f32[4,256]{1,0:T(4,128)S(1)} %bitcast.56, f32[4,256]{1,0:T(4,128)S(1)} %bitcast.57, f32[4,256]{1,0:T(4,128)S(1)} %bitcast.54, pred[16,72]{1,0:T(8,128)(4,1)S(1)} %get-tuple-element.49, ...), kind=kLoop, calls=%fused_computation.1 | loop fusion | flops 7077888 | bytes 9473408 | tf_op jit(solution)/shard_map/jit(_where)/select_n | solution.py:416
  22.0 30.0 %all-to-all-done = f32[32,16,896]{2,1,0:T(8,128)S(1)} async-done(((f32[32,16,896]{2,1,0:T(8,128)}), f32[32,16,896]{2,1,0:T(8,128)S(1)}, u32[]{:S(2)}, u32[]{:S(2)}) %all-to-all-start) | async-done | bytes 1835040 | tf_op jit(solution)/shard_map/all_to_all | solution.py:377
  51.9 1.5 %shard_map.110 = (f32[4,80,256]{2,1,0:T(8,128)S(1)}, f32[4,80,256]{2,1,0:T(8,128)S(1)}, f32[4,8,256]{2,1,0:T(8,128)S(1)}, f32[4,8,256]{2,1,0:T(8,128)S(1)}) custom-call(s32[9]{0:T(128)S(1)} %pad_add_fusion.info, f32[512,896]{1,0:T(8,128)S(1)} %bitcast.50, f32[4,1,256]{2,1,0:T(1,128)S(1)} %pad.41.far_ref), custom_call_target="tpu_custom_call" | custom-call | tf_op jit(solution)/shard_map/pallas_call | solution.py:433
  53.4 0.5 collective-permute-start.1
  53.9 1.9 %collective-permute-start.2 = (f32[4,8,256]{2,1,0:T(8,128)S(1)}, f32[4,8,256]{2,1,0:T(8,128)S(1)}, u32[]{:S(2)}, u32[]{:S(2)}) collective-permute-start(f32[4,8,256]{2,1,0:T(8,128)S(1)} %get-tuple-element.33), channel_id=1, source_target_pairs={{0,1},{1,2},{2,3},{3,4},{4,5},{5,6},{6,7},{7,8},{8,9},{9,10},{10,1... | collective-permute-start | bytes 98312 | tf_op jit(solution)/shard_map/ppermute | solution.py:441
  55.9 4.1 %collective-permute-start.3 = (f32[4,8,256]{2,1,0:T(8,128)S(1)}, f32[4,8,256]{2,1,0:T(8,128)S(1)}, u32[]{:S(2)}, u32[]{:S(2)}) collective-permute-start(f32[4,8,256]{2,1,0:T(8,128)S(1)} %get-tuple-element.34), channel_id=1, source_target_pairs={{16,1},{17,2},{18,3},{19,4},{20,5},{21,6},{22,7},{23,8},{24,9},{25... | collective-permute-start | bytes 98312 | tf_op jit(solution)/shard_map/ppermute | solution.py:442
  60.1 0.1 concatenate.15
  60.2 1.2 %collective-permute-done.3.cross_ref = f32[4,8,256]{2,1,0:T(8,128)S(1)} collective-permute-done((f32[4,8,256]{2,1,0:T(8,128)S(1)}, f32[4,8,256]{2,1,0:T(8,128)S(1)}, u32[]{:S(2)}, u32[]{:S(2)}) %collective-permute-start.3) | collective-permute-done | bytes 32800 | tf_op jit(solution)/shard_map/ppermute | solution.py:442
  61.4 20.7 %shard_map.111 = (f32[216,8,128]{2,1,0:T(8,128)S(1)}, f32[216,8,128]{2,1,0:T(8,128)S(1)}, f32[216,8,128]{2,1,0:T(8,128)S(1)}, f32[216,8,128]{2,1,0:T(8,128)S(1)}) custom-call(s32[9]{0:T(128)S(1)} %pad_add_fusion.info, f32[4,16,72,256]{3,2,1,0:T(8,128)} %get-tuple-element.26.ax_hbm, f32[4,16,72,256]{3,2,1,0:T(8,128)} %get-tuple-element.27.base_hbm, ...), custom_call_target="tpu_custom_call" | custom-call | tf_op jit(solution)/shard_map/pallas_call | solution.py:446
  82.1 2.8 %collective-permute-start.5 = (f32[216,8,128]{2,1,0:T(8,128)S(1)}, f32[216,8,128]{2,1,0:T(8,128)S(1)}, u32[]{:S(2)}, u32[]{:S(2)}) collective-permute-start(f32[216,8,128]{2,1,0:T(8,128)S(1)} %get-tuple-element.38), channel_id=1, source_target_pairs={{16,0},{17,1},{18,2},{19,3},{20,4},{21,5},{22,6},{23,7},{24,8},{25... | collective-permute-start | bytes 2654216 | tf_op jit(solution)/shard_map/ppermute | solution.py:465
  84.9 0.1 collective-permute-start.4
  85.0 2.0 %collective-permute-done.5.got_ref = f32[216,8,128]{2,1,0:T(8,128)S(1)} collective-permute-done((f32[216,8,128]{2,1,0:T(8,128)S(1)}, f32[216,8,128]{2,1,0:T(8,128)S(1)}, u32[]{:S(2)}, u32[]{:S(2)}) %collective-permute-start.5) | collective-permute-done | bytes 884768 | tf_op jit(solution)/shard_map/ppermute | solution.py:465
  87.0 2.0 %shard_map.112.rest_0_ = f32[4,216,8,128]{3,2,1,0:T(8,128)} custom-call(s32[9]{0:T(128)S(1)} %pad_add_fusion.info, f32[216,8,128]{2,1,0:T(8,128)S(1)} %get-tuple-element.37.keep_ref, f32[216,8,128]{2,1,0:T(8,128)S(1)} %collective-permute-done.5.got_ref), custom_call_target="tpu_custom_call" | custom-call | tf_op jit(solution)/shard_map/pallas_call | solution.py:469
  89.0 2.0 %shard_map.113 = f32[4,216,8,128]{3,2,1,0:T(8,128)} custom-call(s32[9]{0:T(128)S(1)} %pad_add_fusion.info, f32[216,8,128]{2,1,0:T(8,128)S(1)} %get-tuple-element.35.keep_ref, f32[216,8,128]{2,1,0:T(8,128)S(1)} %collective-permute-done.4.got_ref, f32[4,216,8,128]{3,2,1,0:T(8,128)} %shard_map.112.rest_0_), custom_call_target="tpu_custom_call", output_to_operand_aliasing={{}: (3, {})} | custom-call | tf_op jit(solution)/shard_map/pallas_call | solution.py:469
  (52 shorter events, 0.6 us)
Async XLA Ops:
  0.0 13.0 %copy-start.3 = (f32[256]{0:T(256)S(1)}, f32[256]{0:T(256)}, u32[]{:S(2)}) copy-start(f32[256]{0:T(256)} %constant.51) | copy-start | bytes 3076
  0.0 11.2 %copy-start.1 = (f32[4,24]{1,0:T(4,128)S(1)}, f32[4,24]{1,0:T(4,128)}, u32[]{:S(2)}) copy-start(f32[4,24]{1,0:T(4,128)} %param.14) | copy-start | bytes 1156
  0.0 11.3 %copy-start.2 = (f32[4,24]{1,0:T(4,128)S(1)}, f32[4,24]{1,0:T(4,128)}, u32[]{:S(2)}) copy-start(f32[4,24]{1,0:T(4,128)} %param.15) | copy-start | bytes 1156
  0.0 13.3 %copy-start.5 = (f32[24]{0:T(128)S(1)}, f32[24]{0:T(128)}, u32[]{:S(2)}) copy-start(f32[24]{0:T(128)} %param.16) | copy-start | bytes 292
  3.3 10.3 %copy-start = (f32[3,8,128]{2,1,0:T(8,128)S(1)}, f32[3,8,128]{2,1,0:T(8,128)}, u32[]{:S(2)}) copy-start(f32[3,8,128]{2,1,0:T(8,128)} %get-tuple-element.24) | copy-start | bytes 36868
  3.3 48.6 %all-to-all-start = ((f32[32,16,896]{2,1,0:T(8,128)}), f32[32,16,896]{2,1,0:T(8,128)S(1)}, u32[]{:S(2)}, u32[]{:S(2)}) async-start(f32[32,16,896]{2,1,0:T(8,128)} %bitcast.52), calls=%async_computation | async-start | bytes 3670016 | tf_op jit(solution)/shard_map/all_to_all | solution.py:377
  9.6 4.0 %collective-permute-start = (f32[3,8,128]{2,1,0:T(8,128)}, f32[3,8,128]{2,1,0:T(8,128)S(1)}, u32[]{:S(2)}, u32[]{:S(2)}) collective-permute-start(f32[3,8,128]{2,1,0:T(8,128)} %get-tuple-element.24), channel_id=1, source_target_pairs={{16,0},{17,1},{18,2},{19,3},{20,4},{21,5},{22,6},{23,7},{24,8},{25... | collective-permute-start | bytes 36872 | tf_op jit(solution)/shard_map/ppermute | solution.py:380
  17.1 42.9 %copy-start.4 = (f32[256]{0:T(256)S(1)}, f32[256]{0:T(256)}, u32[]{:S(2)}) copy-start(f32[256]{0:T(256)} %constant.32.clone) | copy-start | bytes 3076
  53.4 8.0 %collective-permute-start.1 = (f32[4,80,256]{2,1,0:T(8,128)S(1)}, f32[4,80,256]{2,1,0:T(8,128)S(1)}, u32[]{:S(2)}, u32[]{:S(2)}) collective-permute-start(f32[4,80,256]{2,1,0:T(8,128)S(1)} %get-tuple-element.32), channel_id=1, source_target_pairs={{16,0},{17,1},{18,2},{19,3},{20,4},{21,5},{22,6},{23,7},{24,8},{25... | collective-permute-start | bytes 983048 | tf_op jit(solution)/shard_map/ppermute | solution.py:440
  53.9 6.2 %collective-permute-start.2 = (f32[4,8,256]{2,1,0:T(8,128)S(1)}, f32[4,8,256]{2,1,0:T(8,128)S(1)}, u32[]{:S(2)}, u32[]{:S(2)}) collective-permute-start(f32[4,8,256]{2,1,0:T(8,128)S(1)} %get-tuple-element.33), channel_id=1, source_target_pairs={{0,1},{1,2},{2,3},{3,4},{4,5},{5,6},{6,7},{7,8},{8,9},{9,10},{10,1... | collective-permute-start | bytes 98312 | tf_op jit(solution)/shard_map/ppermute | solution.py:441
  55.9 5.5 %collective-permute-start.3 = (f32[4,8,256]{2,1,0:T(8,128)S(1)}, f32[4,8,256]{2,1,0:T(8,128)S(1)}, u32[]{:S(2)}, u32[]{:S(2)}) collective-permute-start(f32[4,8,256]{2,1,0:T(8,128)S(1)} %get-tuple-element.34), channel_id=1, source_target_pairs={{16,1},{17,2},{18,3},{19,4},{20,5},{21,6},{22,7},{23,8},{24,9},{25... | collective-permute-start | bytes 98312 | tf_op jit(solution)/shard_map/ppermute | solution.py:442
  82.1 4.9 %collective-permute-start.5 = (f32[216,8,128]{2,1,0:T(8,128)S(1)}, f32[216,8,128]{2,1,0:T(8,128)S(1)}, u32[]{:S(2)}, u32[]{:S(2)}) collective-permute-start(f32[216,8,128]{2,1,0:T(8,128)S(1)} %get-tuple-element.38), channel_id=1, source_target_pairs={{16,0},{17,1},{18,2},{19,3},{20,4},{21,5},{22,6},{23,7},{24,8},{25... | collective-permute-start | bytes 2654216 | tf_op jit(solution)/shard_map/ppermute | solution.py:465
  84.9 4.1 %collective-permute-start.4 = (f32[216,8,128]{2,1,0:T(8,128)S(1)}, f32[216,8,128]{2,1,0:T(8,128)S(1)}, u32[]{:S(2)}, u32[]{:S(2)}) collective-permute-start(f32[216,8,128]{2,1,0:T(8,128)S(1)} %get-tuple-element.36), channel_id=1, source_target_pairs={{16,0},{17,1},{18,2},{19,3},{20,4},{21,5},{22,6},{23,7},{24,8},{25... | collective-permute-start | bytes 2654216 | tf_op jit(solution)/shard_map/ppermute | solution.py:465
